TPU v7x, 32 devices: a whole 2x2x4 slice. The times are simulated.
32 devices in a mesh: section: 2 (over x), seq: 8 (over z, core), rep: 2 (over y).
Axes of the slice: x: 2, y: 2, z: 4, core: 2. Of those that a mesh axis runs over, the one named last changes fastest.
Arguments:
- signal: bfloat16 [2, 64, 4, 4096], P(None, 'seq', None, 'rep'), may hold values from -200 to 200, as said below
- head_proj: bfloat16 [2, 32, 128, 384], P('section', 'rep'), may hold values from -2 to 6, as said below
- record_start: int32 [2, 4], replicated, may hold values from 0 to 15
- record_pad: int32 [2, 4], replicated, may hold values from 0 to 15
Outputs:
- layer_out: bfloat16 [2, 2, 64, 4, 4096], P('section', None, 'seq', None, 'rep')
Inputs may be any that keep to these rules, and one draw needn't show every extreme that they name: `signal`: finite. `head_proj`: finite.
All inputs are finite; a program needn't handle non-finite values.
Results may differ from a plain program's by a relative error of at most 0.015.
The roundings to bfloat16 on the way count: a program that leaves them out, or rounds other values in their place, can miss the bound.
Values may be sent and summed in bfloat16 or wider, within the bound.
No kernel may reach another device: no remote copies, remote signals or barrier semaphores. Data moves between devices by JAX's collectives and lax.ppermute only.
A program may use at most 64 MiB of HBM per device.

v0:
```python
import math

import jax
import jax.numpy as jnp
from jax import lax
from jax.sharding import PartitionSpec as P

HEADS = 32
HEAD = 128


def extended(cells, sides, width):
    for axis, dim in sides:
        count = lax.axis_size(axis)
        ends = count - 1
        head = lax.slice_in_dim(cells, 0, width, axis=dim)
        tail = lax.slice_in_dim(cells, cells.shape[dim] - width, cells.shape[dim], axis=dim)
        cells = jnp.concatenate(
            [
                lax.ppermute(tail, axis, [(i, (i + 1) % count) for i in range(ends)]),
                cells,
                lax.ppermute(head, axis, [((i + 1) % count, i) for i in range(ends)]),
            ],
            axis=dim,
        )
    return cells


def passed_along(block, axis, distance):
    devices = range(lax.axis_size(axis))
    route = [(i - distance, i) for i in devices if i - distance in devices]
    return lax.ppermute(block, axis, route)


def masked_softmax(scores, allowed):
    scores = jnp.where(allowed, scores, -1e30)
    row_top = jnp.max(scores, axis=-1, keepdims=True)
    weights = jnp.where(allowed, jnp.exp(scores - row_top), 0.0)
    return (weights / jnp.sum(weights, axis=-1, keepdims=True)).astype(jnp.bfloat16)


def project_rows(normed, weights):
    time_rows, stations, feature_width = normed.shape
    heads_dev = weights.shape[0]
    split_rows = normed.reshape(time_rows, stations, heads_dev, feature_width // heads_dev)
    return jnp.einsum(
        "tshd,hde->tshe", split_rows, weights, preferred_element_type=jnp.float32
    ).astype(jnp.bfloat16)


def axial_layer(hidden, weights, first_step, pad_steps, time_base, total_steps):
    time_dev, stations, feature_width = hidden.shape
    head_size = weights.shape[1]
    reach = time_dev // 2
    widened = hidden.astype(jnp.float32)
    local_squares = jnp.sum(widened * widened, axis=-1, keepdims=True)
    squares = lax.psum(local_squares, "rep")
    normed = (widened * lax.rsqrt(squares / (HEADS * HEAD) + 1e-06)).astype(jnp.bfloat16)
    projected = project_rows(normed, weights)
    queries = projected[..., :head_size]
    key_value = extended(projected[..., head_size:], (("seq", 0),), reach)
    keys_all = key_value[..., :head_size]
    values_all = key_value[..., head_size:]
    scale = math.sqrt(head_size)
    scores = (
        jnp.einsum("tshd,ushd->shtu", queries, keys_all, preferred_element_type=jnp.float32) / scale
    )
    key_steps = time_base - reach + jnp.arange(time_dev + 2 * reach, dtype=jnp.int32)
    key_valid = (key_steps[None, :] >= first_step[:, None]) & (
        key_steps[None, :] < total_steps - pad_steps[:, None]
    )
    offset = jnp.arange(time_dev + 2 * reach)[None, :] - jnp.arange(time_dev)[:, None]
    in_band = (offset >= 0) & (offset <= 2 * reach)
    centre = offset == reach
    allowed = in_band[None, None] & key_valid[:, None, None, :] | centre[None, None]
    time_weights = masked_softmax(scores, allowed)
    along_time = jnp.einsum(
        "shtu,ushd->tshd", time_weights, values_all, preferred_element_type=jnp.float32
    )
    query_steps = time_base + jnp.arange(time_dev, dtype=jnp.int32)
    own_valid = (query_steps[:, None] >= first_step[None, :]) & (
        query_steps[:, None] < total_steps - pad_steps[None, :]
    )
    keys_own = projected[..., head_size : 2 * head_size]
    values_own = projected[..., 2 * head_size :]
    station_scores = (
        jnp.einsum("tshd,tzhd->thsz", queries, keys_own, preferred_element_type=jnp.float32) / scale
    )
    station_allowed = own_valid[:, None, None, :] | jnp.eye(stations, dtype=bool)[None, None]
    station_weights = masked_softmax(station_scores, station_allowed)
    across = jnp.einsum(
        "thsz,tzhd->tshd", station_weights, values_own, preferred_element_type=jnp.float32
    )
    updates = (along_time + across).reshape(time_dev, stations, feature_width)
    return (widened + updates).astype(jnp.bfloat16)


def body(signal, head_proj, record_start, record_pad):
    section_count = lax.axis_size("section")
    section_index = lax.axis_index("section")
    micro_count = signal.shape[0]
    time_dev = signal.shape[1]
    total_steps = time_dev * lax.axis_size("seq")
    time_base = lax.axis_index("seq") * time_dev
    weights = head_proj[0]
    outputs = jnp.zeros(signal.shape, jnp.bfloat16)
    arriving = jnp.zeros(signal.shape[1:], jnp.bfloat16)
    tick_count = section_count + micro_count - 1
    for tick_index in range(tick_count):
        micro_index = tick_index - section_index
        slot_index = jnp.clip(micro_index, 0, micro_count - 1)
        entering = signal[min(tick_index, micro_count - 1)]
        current = jnp.where(section_index == 0, entering, arriving)
        first_step = lax.dynamic_index_in_dim(record_start, slot_index, 0, keepdims=False)
        pad_steps = lax.dynamic_index_in_dim(record_pad, slot_index, 0, keepdims=False)
        result = axial_layer(current, weights, first_step, pad_steps, time_base, total_steps)
        chosen = (jnp.arange(micro_count) == micro_index)[:, None, None, None]
        outputs = jnp.where(chosen, result[None], outputs)
        if tick_index + 1 < tick_count:
            arriving = passed_along(result, "section", 1)
    return outputs[None]


def solution(mesh):
    return jax.shard_map(
        body,
        mesh=mesh,
        in_specs=(P(None, "seq", None, "rep"), P("section", "rep", None, None), P(), P()),
        out_specs=P("section", None, "seq", None, "rep"),
        check_vma=False,
    )
```

profile of v0, /device:TPU:11, one launch (start us, length us, event | category | flops | bytes accessed | tf_op | source)
XLA Modules:
  0.0 63.7 jit_solution(7699737242537784098)
XLA Ops:
  0.0 1.2 %fusion.120 = (bf16[1,8,4,2048]{3,2,1,0:T(4,128)(2,1)S(1)}, bf16[1,8,4,2048]{3,2,1,0:T(4,128)(2,1)S(1)}) fusion(bf16[2,8,4,2048]{3,2,1,0:T(4,128)(2,1)} %param.4), kind=kLoop, calls=%fused_computation.169 | loop fusion | bytes 524288 | tf_op jit(solution)/shard_map/slice | solution.py:112
  1.4 3.8 %psum.21 = f32[8,4,1]{0,1,2:T(4,128)S(1)} all-reduce(f32[8,4,1]{0,1,2:T(4,128)S(1)} %bitcast.134), channel_id=1, replica_groups=mesh['section'=2,'seq'=8,'rep'=2] {'rep'}, use_global_device_ids=true, to_apply=%region_1.2 | all-reduce | flops 32 | bytes 256 | tf_op jit(solution)/shard_map/psum | solution.py:57
  5.2 0.4 fusion.27
  5.8 3.7 %collective-permute-start.1 = (bf16[4,4,16,256]{3,0,1,2:T(4,128)(2,1)S(1)}, bf16[4,4,16,256]{3,0,1,2:T(4,128)(2,1)S(1)}, u32[]{:S(2)}, u32[]{:S(2)}) collective-permute-start(bf16[4,4,16,256]{3,0,1,2:T(4,128)(2,1)S(1)} %get-tuple-element.26), channel_id=1, source_target_pairs={{2,0},{4,2},{6,4},{8,6},{10,8},{12,10},{14,12},{3,1},{5,3},{7,5},{... | collective-permute-start | bytes 393224 | tf_op jit(solution)/shard_map/ppermute | solution.py:22
  9.5 3.1 %collective-permute-start = (bf16[4,4,16,256]{3,0,1,2:T(4,128)(2,1)S(1)}, bf16[4,4,16,256]{3,0,1,2:T(4,128)(2,1)S(1)}, u32[]{:S(2)}, u32[]{:S(2)}) collective-permute-start(bf16[4,4,16,256]{3,0,1,2:T(4,128)(2,1)S(1)} %get-tuple-element.25), channel_id=1, source_target_pairs={{0,2},{2,4},{4,6},{6,8},{8,10},{10,12},{12,14},{1,3},{3,5},{5,7},{... | collective-permute-start | bytes 393224 | tf_op jit(solution)/shard_map/ppermute | solution.py:20
  14.6 0.3 pad_maximum_fusion
  15.1 0.4 fusion.121
  15.5 0.5 fusion.51
  16.0 1.3 %collective-permute-start.2 = (bf16[8,4,2048]{2,0,1:T(8,128)(2,1)S(1)}, bf16[8,4,2048]{2,0,1:T(8,128)(2,1)S(1)}, u32[]{:S(2)}, u32[]{:S(2)}) collective-permute-start(bf16[8,4,2048]{2,0,1:T(8,128)(2,1)S(1)} %get-tuple-element.52), channel_id=1, source_target_pairs={{0,16},{1,17},{2,18},{3,19},{4,20},{5,21},{6,22},{7,23},{8,24},{9,... | collective-permute-start | bytes 393224 | tf_op jit(solution)/shard_map/ppermute | solution.py:32
  17.3 0.6 iota_compare_fusion.3
  17.9 0.5 iota_compare_fusion.1
  18.4 3.3 %collective-permute-done.2 = bf16[8,4,2048]{2,0,1:T(8,128)(2,1)S(1)} collective-permute-done((bf16[8,4,2048]{2,0,1:T(8,128)(2,1)S(1)}, bf16[8,4,2048]{2,0,1:T(8,128)(2,1)S(1)}, u32[]{:S(2)}, u32[]{:S(2)}) %collective-permute-start.2) | collective-permute-done | bytes 131104 | tf_op jit(solution)/shard_map/ppermute | solution.py:32
  21.9 3.8 %psum.22 = f32[8,4,1]{0,1,2:T(4,128)S(1)} all-reduce(f32[8,4,1]{0,1,2:T(4,128)S(1)} %bitcast.133), channel_id=1, replica_groups=mesh['section'=2,'seq'=8,'rep'=2] {'rep'}, use_global_device_ids=true, to_apply=%region_7.8 | all-reduce | flops 32 | bytes 256 | tf_op jit(solution)/shard_map/psum | solution.py:57
  25.7 0.4 fusion.24
  27.5 5.4 %collective-permute-start.4 = (bf16[4,4,16,256]{3,0,1,2:T(4,128)(2,1)S(1)}, bf16[4,4,16,256]{3,0,1,2:T(4,128)(2,1)S(1)}, u32[]{:S(2)}, u32[]{:S(2)}) collective-permute-start(bf16[4,4,16,256]{3,0,1,2:T(4,128)(2,1)S(1)} %get-tuple-element.21), channel_id=1, source_target_pairs={{2,0},{4,2},{6,4},{8,6},{10,8},{12,10},{14,12},{3,1},{5,3},{7,5},{... | collective-permute-start | bytes 393224 | tf_op jit(solution)/shard_map/ppermute | solution.py:22
  33.0 3.1 %collective-permute-start.3 = (bf16[4,4,16,256]{3,0,1,2:T(4,128)(2,1)S(1)}, bf16[4,4,16,256]{3,0,1,2:T(4,128)(2,1)S(1)}, u32[]{:S(2)}, u32[]{:S(2)}) collective-permute-start(bf16[4,4,16,256]{3,0,1,2:T(4,128)(2,1)S(1)} %get-tuple-element.20), channel_id=1, source_target_pairs={{0,2},{2,4},{4,6},{6,8},{8,10},{10,12},{12,14},{1,3},{3,5},{5,7},{... | collective-permute-start | bytes 393224 | tf_op jit(solution)/shard_map/ppermute | solution.py:20
  36.4 0.4 collective-permute-done.4
  36.8 1.2 %collective-permute-done.3 = bf16[4,4,16,256]{3,0,1,2:T(4,128)(2,1)S(1)} collective-permute-done((bf16[4,4,16,256]{3,0,1,2:T(4,128)(2,1)S(1)}, bf16[4,4,16,256]{3,0,1,2:T(4,128)(2,1)S(1)}, u32[]{:S(2)}, u32[]{:S(2)}) %collective-permute-start.3) | collective-permute-done | bytes 131104 | tf_op jit(solution)/shard_map/ppermute | solution.py:20
  38.0 0.3 pad_maximum_fusion.1
  38.5 0.4 fusion.122
  38.9 0.3 fusion.38
  39.2 1.3 %collective-permute-start.5 = (bf16[8,4,2048]{2,0,1:T(8,128)(2,1)S(1)}, bf16[8,4,2048]{2,0,1:T(8,128)(2,1)S(1)}, u32[]{:S(2)}, u32[]{:S(2)}) collective-permute-start(bf16[8,4,2048]{2,0,1:T(8,128)(2,1)S(1)} %fusion.38), channel_id=1, source_target_pairs={{0,16},{1,17},{2,18},{3,19},{4,20},{5,21},{6,22},{7,23},{8,24},{9,... | collective-permute-start | bytes 393224 | tf_op jit(solution)/shard_map/ppermute | solution.py:32
  40.9 4.1 %collective-permute-done.5 = bf16[8,4,2048]{2,0,1:T(8,128)(2,1)S(1)} collective-permute-done((bf16[8,4,2048]{2,0,1:T(8,128)(2,1)S(1)}, bf16[8,4,2048]{2,0,1:T(8,128)(2,1)S(1)}, u32[]{:S(2)}, u32[]{:S(2)}) %collective-permute-start.5) | collective-permute-done | bytes 131104 | tf_op jit(solution)/shard_map/ppermute | solution.py:32
  45.2 3.8 %psum.23 = f32[8,4,1]{0,1,2:T(4,128)S(1)} all-reduce(f32[8,4,1]{0,1,2:T(4,128)S(1)} %bitcast.132), channel_id=1, replica_groups=mesh['section'=2,'seq'=8,'rep'=2] {'rep'}, use_global_device_ids=true, to_apply=%region_13.14 | all-reduce | flops 32 | bytes 256 | tf_op jit(solution)/shard_map/psum | solution.py:57
  49.0 0.4 fusion.21
  50.8 5.5 %collective-permute-start.7 = (bf16[4,4,16,256]{3,0,1,2:T(4,128)(2,1)S(1)}, bf16[4,4,16,256]{3,0,1,2:T(4,128)(2,1)S(1)}, u32[]{:S(2)}, u32[]{:S(2)}) collective-permute-start(bf16[4,4,16,256]{3,0,1,2:T(4,128)(2,1)S(1)} %get-tuple-element.16), channel_id=1, source_target_pairs={{2,0},{4,2},{6,4},{8,6},{10,8},{12,10},{14,12},{3,1},{5,3},{7,5},{... | collective-permute-start | bytes 393224 | tf_op jit(solution)/shard_map/ppermute | solution.py:22
  56.3 3.1 %collective-permute-start.6 = (bf16[4,4,16,256]{3,0,1,2:T(4,128)(2,1)S(1)}, bf16[4,4,16,256]{3,0,1,2:T(4,128)(2,1)S(1)}, u32[]{:S(2)}, u32[]{:S(2)}) collective-permute-start(bf16[4,4,16,256]{3,0,1,2:T(4,128)(2,1)S(1)} %get-tuple-element.15), channel_id=1, source_target_pairs={{0,2},{2,4},{4,6},{6,8},{8,10},{10,12},{12,14},{1,3},{3,5},{5,7},{... | collective-permute-start | bytes 393224 | tf_op jit(solution)/shard_map/ppermute | solution.py:20
  59.7 0.4 collective-permute-done.7
  60.1 1.2 %collective-permute-done.6 = bf16[4,4,16,256]{3,0,1,2:T(4,128)(2,1)S(1)} collective-permute-done((bf16[4,4,16,256]{3,0,1,2:T(4,128)(2,1)S(1)}, bf16[4,4,16,256]{3,0,1,2:T(4,128)(2,1)S(1)}, u32[]{:S(2)}, u32[]{:S(2)}) %collective-permute-start.6) | collective-permute-done | bytes 131104 | tf_op jit(solution)/shard_map/ppermute | solution.py:20
  61.3 0.3 pad_maximum_fusion.2
  61.8 0.4 fusion.123
  62.7 0.9 %select_select_fusion = bf16[1,2,8,4,2048]{4,3,2,1,0:T(4,128)(2,1)} fusion(pred[2]{0:T(512)(128)(4,1)S(1)} %copy-done.4, pred[2]{0:T(512)(128)(4,1)S(1)} %copy-done.5, pred[2]{0:T(512)(128)(4,1)S(1)} %copy-done.3, bf16[8,4,2048]{2,1,0:T(4,128)(2,1)S(1)} %copy.100, bf16[8,4,2048]{2,1,0:T(4,128)(2,1)S(1)} %copy.99, bf16[8,4,2048]{2,1,0:T(4,128)(2,1)S(1)} %copy.98), kind=kLoop, calls=%fused_computation.69 | loop fusion | flops 393216 | bytes 655366 | tf_op jit(solution)/shard_map/jit(_where)/select_n | solution.py:118
  (67 shorter events, 7.0 us)
Async XLA Ops:
  0.0 5.2 %copy-start = (bf16[1,16,128,384]{3,2,1,0:T(8,128)(2,1)S(1)}, bf16[1,16,128,384]{3,2,1,0:T(8,128)(2,1)}, u32[]{:S(2)}) copy-start(bf16[1,16,128,384]{3,2,1,0:T(8,128)(2,1)} %param.5) | copy-start | bytes 4718596
  5.7 7.7 %copy-start.1 = (s32[2,4]{1,0:T(2,128)S(1)}, s32[2,4]{1,0:T(2,128)}, u32[]{:S(2)}) copy-start(s32[2,4]{1,0:T(2,128)} %param.6) | copy-start | bytes 100
  5.7 7.7 %copy-start.2 = (s32[2,4]{1,0:T(2,128)S(1)}, s32[2,4]{1,0:T(2,128)}, u32[]{:S(2)}) copy-start(s32[2,4]{1,0:T(2,128)} %param.7) | copy-start | bytes 100
  5.8 8.8 %collective-permute-start.1 = (bf16[4,4,16,256]{3,0,1,2:T(4,128)(2,1)S(1)}, bf16[4,4,16,256]{3,0,1,2:T(4,128)(2,1)S(1)}, u32[]{:S(2)}, u32[]{:S(2)}) collective-permute-start(bf16[4,4,16,256]{3,0,1,2:T(4,128)(2,1)S(1)} %get-tuple-element.26), channel_id=1, source_target_pairs={{2,0},{4,2},{6,4},{8,6},{10,8},{12,10},{14,12},{3,1},{5,3},{7,5},{... | collective-permute-start | bytes 393224 | tf_op jit(solution)/shard_map/ppermute | solution.py:22
  9.5 5.1 %collective-permute-start = (bf16[4,4,16,256]{3,0,1,2:T(4,128)(2,1)S(1)}, bf16[4,4,16,256]{3,0,1,2:T(4,128)(2,1)S(1)}, u32[]{:S(2)}, u32[]{:S(2)}) collective-permute-start(bf16[4,4,16,256]{3,0,1,2:T(4,128)(2,1)S(1)} %get-tuple-element.25), channel_id=1, source_target_pairs={{0,2},{2,4},{4,6},{6,8},{8,10},{10,12},{12,14},{1,3},{3,5},{5,7},{... | collective-permute-start | bytes 393224 | tf_op jit(solution)/shard_map/ppermute | solution.py:20
  16.0 5.7 %collective-permute-start.2 = (bf16[8,4,2048]{2,0,1:T(8,128)(2,1)S(1)}, bf16[8,4,2048]{2,0,1:T(8,128)(2,1)S(1)}, u32[]{:S(2)}, u32[]{:S(2)}) collective-permute-start(bf16[8,4,2048]{2,0,1:T(8,128)(2,1)S(1)} %get-tuple-element.52), channel_id=1, source_target_pairs={{0,16},{1,17},{2,18},{3,19},{4,20},{5,21},{6,22},{7,23},{8,24},{9,... | collective-permute-start | bytes 393224 | tf_op jit(solution)/shard_map/ppermute | solution.py:32
  27.5 9.3 %collective-permute-start.4 = (bf16[4,4,16,256]{3,0,1,2:T(4,128)(2,1)S(1)}, bf16[4,4,16,256]{3,0,1,2:T(4,128)(2,1)S(1)}, u32[]{:S(2)}, u32[]{:S(2)}) collective-permute-start(bf16[4,4,16,256]{3,0,1,2:T(4,128)(2,1)S(1)} %get-tuple-element.21), channel_id=1, source_target_pairs={{2,0},{4,2},{6,4},{8,6},{10,8},{12,10},{14,12},{3,1},{5,3},{7,5},{... | collective-permute-start | bytes 393224 | tf_op jit(solution)/shard_map/ppermute | solution.py:22
  33.0 5.0 %collective-permute-start.3 = (bf16[4,4,16,256]{3,0,1,2:T(4,128)(2,1)S(1)}, bf16[4,4,16,256]{3,0,1,2:T(4,128)(2,1)S(1)}, u32[]{:S(2)}, u32[]{:S(2)}) collective-permute-start(bf16[4,4,16,256]{3,0,1,2:T(4,128)(2,1)S(1)} %get-tuple-element.20), channel_id=1, source_target_pairs={{0,2},{2,4},{4,6},{6,8},{8,10},{10,12},{12,14},{1,3},{3,5},{5,7},{... | collective-permute-start | bytes 393224 | tf_op jit(solution)/shard_map/ppermute | solution.py:20
  39.2 5.7 %collective-permute-start.5 = (bf16[8,4,2048]{2,0,1:T(8,128)(2,1)S(1)}, bf16[8,4,2048]{2,0,1:T(8,128)(2,1)S(1)}, u32[]{:S(2)}, u32[]{:S(2)}) collective-permute-start(bf16[8,4,2048]{2,0,1:T(8,128)(2,1)S(1)} %fusion.38), channel_id=1, source_target_pairs={{0,16},{1,17},{2,18},{3,19},{4,20},{5,21},{6,22},{7,23},{8,24},{9,... | collective-permute-start | bytes 393224 | tf_op jit(solution)/shard_map/ppermute | solution.py:32
  50.8 9.3 %collective-permute-start.7 = (bf16[4,4,16,256]{3,0,1,2:T(4,128)(2,1)S(1)}, bf16[4,4,16,256]{3,0,1,2:T(4,128)(2,1)S(1)}, u32[]{:S(2)}, u32[]{:S(2)}) collective-permute-start(bf16[4,4,16,256]{3,0,1,2:T(4,128)(2,1)S(1)} %get-tuple-element.16), channel_id=1, source_target_pairs={{2,0},{4,2},{6,4},{8,6},{10,8},{12,10},{14,12},{3,1},{5,3},{7,5},{... | collective-permute-start | bytes 393224 | tf_op jit(solution)/shard_map/ppermute | solution.py:22
  56.3 5.0 %collective-permute-start.6 = (bf16[4,4,16,256]{3,0,1,2:T(4,128)(2,1)S(1)}, bf16[4,4,16,256]{3,0,1,2:T(4,128)(2,1)S(1)}, u32[]{:S(2)}, u32[]{:S(2)}) collective-permute-start(bf16[4,4,16,256]{3,0,1,2:T(4,128)(2,1)S(1)} %get-tuple-element.15), channel_id=1, source_target_pairs={{0,2},{2,4},{4,6},{6,8},{8,10},{10,12},{12,14},{1,3},{3,5},{5,7},{... | collective-permute-start | bytes 393224 | tf_op jit(solution)/shard_map/ppermute | solution.py:20
  61.8 0.9 %copy-start.3 = (pred[2]{0:T(512)(128)(4,1)S(1)}, pred[2]{0:T(512)(128)(4,1)}, u32[]{:S(2)}) copy-start(pred[2]{0:T(512)(128)(4,1)} %get-tuple-element.63) | copy-start | bytes 10
  61.8 0.9 %copy-start.4 = (pred[2]{0:T(512)(128)(4,1)S(1)}, pred[2]{0:T(512)(128)(4,1)}, u32[]{:S(2)}) copy-start(pred[2]{0:T(512)(128)(4,1)} %get-tuple-element.64) | copy-start | bytes 10
  61.8 0.9 %copy-start.5 = (pred[2]{0:T(512)(128)(4,1)S(1)}, pred[2]{0:T(512)(128)(4,1)}, u32[]{:S(2)}) copy-start(pred[2]{0:T(512)(128)(4,1)} %iota_compare_fusion.3) | copy-start | bytes 10
where the time goes:
time: 64.6 us; the launch traced here: 63.7 us
  starting transfers between devices  26.5 us (41%)
  blocking collectives  11.3 us (17%)
  waiting for transfers between devices  10.7 us (17%)
  matrix products  5.28 us (8%)
  other arithmetic  5.06 us (8%)
  local copies, waits for them, and re-layouts  4.25 us (7%)
    ppermute x3, starting transfers between devices, extended(): lax.ppermute(head, axis, [((i + 1) % count, i) for i in range(ends)])  14.6 us
    psum x3, blocking collectives, axial_layer(): squares = lax.psum(local_squares, 'rep')  11.3 us
    ppermute x3, starting transfers between devices, extended(): lax.ppermute(tail, axis, [(i, (i + 1) % count) for i in range(ends)])  9.31 us
    ppermute x2, waiting for transfers between devices, passed_along(): return lax.ppermute(block, axis, route)  7.39 us
    ppermute x2, starting transfers between devices, passed_along(): return lax.ppermute(block, axis, route)  2.58 us
    ppermute x3, waiting for transfers between devices, extended(): lax.ppermute(tail, axis, [(i, (i + 1) % count) for i in range(ends)])  2.44 us
    dot_general x3, matrix products, project_rows(): jnp.einsum('tshd,hde->tshe', split_rows, weights, preferred_element_type=...  1.31 us
  transfers between devices with their start and end apart: 8, of which 6 were waited for; matrix products, arithmetic and copies ran while one was open for 6% of the time, Pallas kernels for 0%

commit v1 on v0

v1 whole, which is shorter than its diff:
```python
import math

import jax
import jax.numpy as jnp
from jax import lax
from jax.experimental import pallas as pl
from jax.experimental.pallas import tpu as pltpu
from jax.sharding import PartitionSpec as P

HEADS = 32
HEAD = 128
WIN = 4
GROUP = 4
EPS = 1e-06
BIG = 1e30

VMEM = pl.BlockSpec(memory_space=pltpu.VMEM)
SMEM = pl.BlockSpec(memory_space=pltpu.SMEM)
PARAMS = pltpu.CompilerParams(vmem_limit_bytes=48 * 1024 * 1024)


def cost(flops, moved):
    return pl.CostEstimate(flops=flops, bytes_accessed=moved, transcendentals=0)


def eye(rows):
    return (
        lax.broadcasted_iota(jnp.int32, (rows, rows), 0)
        == lax.broadcasted_iota(jnp.int32, (rows, rows), 1)
    ).astype(jnp.float32)


def squares_row(rows):
    gram = lax.dot_general(
        rows, rows, (((1,), (1,)), ((), ())), preferred_element_type=jnp.float32
    )
    return jnp.sum(gram * eye(rows.shape[0]), axis=0, keepdims=True)


def first_kernel(signal_ref, own_ref, squares_ref):
    micro, steps, stations, _ = signal_ref.shape
    rows_micro = steps * stations
    for m in range(micro):
        for t in range(0, steps, 2):
            own_ref[pl.ds(m * rows_micro + t * stations, 2 * stations), :] = jnp.concatenate(
                [signal_ref[m, t].astype(jnp.float32), signal_ref[m, t + 1].astype(jnp.float32)],
                axis=0,
            ).astype(jnp.bfloat16)
    squares_ref[...] = jnp.zeros(squares_ref.shape, jnp.float32)
    rows = own_ref[...]
    squares_ref[0:1, 0 : rows.shape[0]] = squares_row(rows)


def norm_kernel(own_ref, partner_ref, normed_ref, head_ref, tail_ref, *, micro, edge):
    rows = own_ref[...]
    count = rows.shape[0]
    total = squares_row(rows) + partner_ref[0:1, 0:count]
    factor = lax.rsqrt(total / (HEADS * HEAD) + EPS)
    column = jnp.sum(eye(count) * factor, axis=1, keepdims=True)
    normed = (rows.astype(jnp.float32) * column).astype(jnp.bfloat16)
    normed_ref[...] = normed
    rows_micro = count // micro
    for m in range(micro):
        base = m * rows_micro
        head_ref[m * edge : (m + 1) * edge, :] = normed[base : base + edge]
        tail_ref[m * edge : (m + 1) * edge, :] = normed[base + rows_micro - edge : base + rows_micro]


def masks(first_step_ref, pad_ref, m, time_base, total_steps, steps, stations):
    keys = (steps + 2 * WIN) * stations
    columns = GROUP * steps * stations
    key = lax.broadcasted_iota(jnp.int32, (keys, columns), 0)
    query = lax.broadcasted_iota(jnp.int32, (keys, columns), 1) % (steps * stations)
    key_station, query_station = key % stations, query % stations
    key_time, query_time = key // stations - WIN, query // stations
    first = jnp.zeros((keys, columns), jnp.int32)
    last = jnp.zeros((keys, columns), jnp.int32)
    for s in range(stations):
        first = jnp.where(key_station == s, first_step_ref[m, s], first)
        last = jnp.where(key_station == s, total_steps - pad_ref[m, s], last)
    step = time_base + key_time
    recorded = (step >= first) & (step < last)
    same_station = key_station == query_station
    same_time = key_time == query_time
    near = jnp.abs(key_time - query_time) <= WIN
    time_bias = jnp.where(same_station & near & (recorded | same_time), 0.0, -BIG)
    station_bias = jnp.where(same_time & (recorded | same_station), 0.0, -BIG)
    own = slice(WIN * stations, (WIN + steps) * stations)
    return time_bias, station_bias[own]


def softmax_columns(scores):
    grown = jnp.exp(scores - jnp.max(scores, axis=0, keepdims=True))
    return (grown * (1.0 / jnp.sum(grown, axis=0, keepdims=True))).astype(jnp.bfloat16)


def layer_kernel(
    place_ref, first_ref, pad_ref, hidden_ref, normed_ref, left_ref, right_ref, weights_ref,
    kept_ref, out_ref, squares_ref, *, tick, micro, steps, stations, total_steps, last,
):
    rows_micro = steps * stations
    edge = WIN * stations
    own_rows = micro * rows_micro
    heads_dev = weights_ref.shape[1]

    def write(m, head, values):
        lanes = slice(head * HEAD, (head + 1) * HEAD)
        if last:
            for t in range(steps):
                out_ref[0, m, t, :, lanes] = values[t * stations : (t + 1) * stations].astype(jnp.bfloat16)
        else:
            out_ref[m * rows_micro : (m + 1) * rows_micro, lanes] = values.astype(jnp.bfloat16)

    @pl.when(place_ref[0] == tick)
    def _():
        time_base = place_ref[1]
        bias = [
            masks(first_ref, pad_ref, m, time_base, total_steps, steps, stations)
            for m in range(micro)
        ]
        sums = [jnp.zeros((rows_micro, HEAD), jnp.float32) for _ in range(micro)]
        for group in range(heads_dev // GROUP):
            queries, keys, values = [], [], []
            for j in range(GROUP):
                head = group * GROUP + j
                lanes = slice(head * HEAD, (head + 1) * HEAD)
                tokens = jnp.concatenate(
                    [normed_ref[:, lanes], left_ref[:, lanes], right_ref[:, lanes]], axis=0
                )
                projected = jnp.dot(
                    tokens, weights_ref[0, head], preferred_element_type=jnp.float32
                ).astype(jnp.bfloat16)
                queries.append(projected[:own_rows, :HEAD])
                keys.append(projected[:, HEAD : 2 * HEAD])
                values.append(projected[:, 2 * HEAD :])
            for m in range(micro):
                time_bias, station_bias = bias[m]
                own = slice(m * rows_micro, (m + 1) * rows_micro)
                left = slice(own_rows + m * edge, own_rows + (m + 1) * edge)
                right = slice(own_rows + (micro + m) * edge, own_rows + (micro + m + 1) * edge)
                blank = jnp.zeros((rows_micro, HEAD), jnp.bfloat16)
                spread = jnp.concatenate(
                    [
                        jnp.concatenate(
                            [queries[j][own] if i == j else blank for i in range(GROUP)], axis=1
                        )
                        for j in range(GROUP)
                    ],
                    axis=0,
                )
                all_keys = jnp.concatenate(
                    [
                        jnp.concatenate([k[left], k[own], k[right]], axis=0) for k in keys
                    ],
                    axis=1,
                )
                scores = lax.dot_general(
                    all_keys, spread, (((1,), (1,)), ((), ())), preferred_element_type=jnp.float32
                ) * (1.0 / math.sqrt(HEAD))
                time_weights = softmax_columns(scores + time_bias)
                station_weights = softmax_columns(scores[edge : edge + rows_micro] + station_bias)
                both = jnp.concatenate([time_weights, station_weights], axis=0).T
                for j in range(GROUP):
                    head = group * GROUP + j
                    v = values[j]
                    mixed = jnp.dot(
                        both[j * rows_micro : (j + 1) * rows_micro],
                        jnp.concatenate([v[left], v[own], v[right], v[own]], axis=0),
                        preferred_element_type=jnp.float32,
                    )
                    lanes = slice(head * HEAD, (head + 1) * HEAD)
                    result = hidden_ref[own, lanes].astype(jnp.float32) + mixed
                    write(m, head, result)
                    if not last:
                        rounded = result.astype(jnp.bfloat16).astype(jnp.float32)
                        sums[m] = sums[m] + rounded * rounded
        if not last:
            column = jnp.sum(jnp.concatenate(sums, axis=0), axis=1, keepdims=True)
            squares_ref[...] = jnp.zeros(squares_ref.shape, jnp.float32)
            squares_ref[0:1, 0:own_rows] = jnp.sum(eye(own_rows) * column, axis=0, keepdims=True)

    @pl.when(place_ref[0] != tick)
    def _():
        for m in range(micro):
            for head in range(heads_dev):
                lanes = slice(head * HEAD, (head + 1) * HEAD)
                write(m, head, kept_ref[m * rows_micro : (m + 1) * rows_micro, lanes].astype(jnp.float32))
        if not last:
            squares_ref[...] = jnp.zeros(squares_ref.shape, jnp.float32)


def body(signal, head_proj, record_start, record_pad):
    section_count = lax.axis_size("section")
    seq_count = lax.axis_size("seq")
    rep_count = lax.axis_size("rep")
    section_index = lax.axis_index("section")
    micro, steps, stations, features = signal.shape
    total_steps = steps * seq_count
    own_rows = micro * steps * stations
    edge = WIN * stations
    place = jnp.stack([section_index, lax.axis_index("seq") * steps]).astype(jnp.int32)
    bf16, f32 = jnp.bfloat16, jnp.float32
    own_shape = jax.ShapeDtypeStruct((own_rows, features), bf16)
    edge_shape = jax.ShapeDtypeStruct((micro * edge, features), bf16)
    squares_shape = jax.ShapeDtypeStruct((8, 128), f32)
    own_bytes = own_rows * features * 2

    own, squares = pl.pallas_call(
        first_kernel,
        in_specs=[VMEM],
        out_specs=[VMEM, VMEM],
        out_shape=[own_shape, squares_shape],
        compiler_params=PARAMS,
        cost_estimate=cost(2 * own_rows * own_rows * features, 2 * own_bytes),
        name="first",
    )(signal)
    kept = own
    partner = lax.ppermute(
        squares, ("section", "rep"), [(r, (r + 1) % rep_count) for r in range(rep_count)]
    )
    for tick in range(section_count):
        last = tick + 1 == section_count
        normed, head_rows, tail_rows = pl.pallas_call(
            lambda *refs: norm_kernel(*refs, micro=micro, edge=edge),
            in_specs=[VMEM, VMEM],
            out_specs=[VMEM] * 3,
            out_shape=[own_shape, edge_shape, edge_shape],
            compiler_params=PARAMS,
            cost_estimate=cost(2 * own_rows * own_rows * features, 3 * own_bytes),
            name="norm",
        )(own, partner)
        base = tick * seq_count
        left = lax.ppermute(
            tail_rows, ("section", "seq"), [(base + i, base + i + 1) for i in range(seq_count - 1)]
        )
        right = lax.ppermute(
            head_rows, ("section", "seq"), [(base + i + 1, base + i) for i in range(seq_count - 1)]
        )
        out_shape = (
            [jax.ShapeDtypeStruct((1,) + signal.shape, bf16)] if last else [own_shape]
        ) + [squares_shape]

        def kernel(*refs, tick=tick, last=last):
            layer_kernel(
                *refs, tick=tick, micro=micro, steps=steps, stations=stations,
                total_steps=total_steps, last=last,
            )

        kept, squares = pl.pallas_call(
            kernel,
            in_specs=[SMEM] * 3 + [VMEM] * 6,
            out_specs=[VMEM, VMEM],
            out_shape=out_shape,
            compiler_params=PARAMS,
            cost_estimate=cost(4 * own_rows * features * 3 * HEAD, 16 * own_bytes),
            name="layer",
        )(place, record_start, record_pad, own, normed, left, right, head_proj, kept)
        if not last:
            across = [(tick * rep_count + r, (tick + 1) * rep_count + r) for r in range(rep_count)]
            own = lax.ppermute(
                kept, "section", [(tick, tick + 1)]
            )
            partner = lax.ppermute(
                squares,
                ("section", "rep"),
                [(a, (tick + 1) * rep_count + (b + 1) % rep_count) for a, b in across],
            )
    return kept


def solution(mesh):
    return jax.shard_map(
        body,
        mesh=mesh,
        in_specs=(P(None, "seq", None, "rep"), P("section", "rep", None, None), P(), P()),
        out_specs=P("section", None, "seq", None, "rep"),
        check_vma=False,
    )
```

time: 64.6 us -> 44.6 us (0.69)
  starting transfers between devices: 26.5 us -> 9.12 us
  waiting for transfers between devices: 10.7 us -> 25.8 us
  blocking collectives: 11.3 us -> 0 us
  Pallas kernels: 0 us -> 5.43 us
  matrix products: 5.28 us -> 0 us
  other arithmetic: 5.06 us -> 0.08 us
    ppermute x8 -> x7, starting transfers between devices: 26.5 us -> 9.12 us  [the longest x2 3.29 us: body(): lax.ppermute(tail_rows, ('section', 'seq'), [(base + i, base + i + 1) for...]
    ppermute x8 -> x7, waiting for transfers between devices: 10.7 us -> 25.8 us  [the longest x1 21.5 us: body(): lax.ppermute(squares, ('section', 'rep'), [(a, (tick + 1) * rep_count + (...]
    psum x3 -> x0, blocking collectives: 11.3 us -> none  [axial_layer(): squares = lax.psum(local_squares, 'rep')]
    pallas_call x0 -> x5, Pallas kernels: none -> 5.43 us  [the longest x2 4.48 us: body(): pl.pallas_call(kernel, in_specs=[SMEM] * 3 + [VMEM] * 6, out_specs=[VMEM,...]
    dot_general x12 -> x0, matrix products: 4.04 us -> none  [the longest x3 1.31 us: project_rows(): jnp.einsum('tshd,hde->tshe', split_rows, weights, preferred_element_type=...]
    unnamed x12, local copies, waits for them, and re-layouts: 0.03 us -> 3.72 us
    slice x13 -> x0, local copies, waits for them, and re-layouts: 2.13 us -> none  [the longest x1 1.18 us: body(): entering = signal[min(tick_index, micro_count - 1)]]
    sub x3 -> x0, matrix products: 1.24 us -> none  [masked_softmax(): weights = jnp.where(allowed, jnp.exp(scores - row_top), 0.0)]
  transfers between devices with their start and end apart: 8 -> 7, of which waited for: 6 -> 2; matrix products, arithmetic and copies ran while one was open for 6% -> 0% of each run, Pallas kernels for 0% -> 0%
where the time goes in v1:
time: 44.6 us; the launch traced here: 44.3 us
  waiting for transfers between devices  25.8 us (58%)
  starting transfers between devices  9.12 us (20%)
  Pallas kernels  5.43 us (12%)
  local copies, waits for them, and re-layouts  3.72 us (8%)
    ppermute x1, waiting for transfers between devices, body(): lax.ppermute(squares, ('section', 'rep'), [(a, (tick + 1) * rep_count + (...  21.5 us
    pallas_call x2, Pallas kernels, body(): pl.pallas_call(kernel, in_specs=[SMEM] * 3 + [VMEM] * 6, out_specs=[VMEM,...  4.48 us
    ppermute x2, waiting for transfers between devices, body(): lax.ppermute(head_rows, ('section', 'seq'), [(base + i + 1, base + i) for...  4.35 us
    unnamed x12, local copies, waits for them, and re-layouts  3.72 us
    ppermute x2, starting transfers between devices, body(): lax.ppermute(tail_rows, ('section', 'seq'), [(base + i, base + i + 1) for...  3.29 us
    ppermute x2, starting transfers between devices, body(): lax.ppermute(head_rows, ('section', 'seq'), [(base + i + 1, base + i) for...  2.59 us
    ppermute x1, starting transfers between devices, body(): own = lax.ppermute(kept, 'section', [(tick, tick + 1)])  1.29 us
    ppermute x1, starting transfers between devices, body(): lax.ppermute(squares, ('section', 'rep'), [(a, (tick + 1) * rep_count + (...  1.29 us
  transfers between devices with their start and end apart: 7, of which 2 were waited for; matrix products, arithmetic and copies ran while one was open for 0% of the time, Pallas kernels for 0%

profile of v1, /device:TPU:11, one launch (start us, length us, event | category | flops | bytes accessed | tf_op | source)
XLA Modules:
  0.0 44.3 jit_solution(7717501174700518738)
XLA Ops:
  0.0 0.0 copy-start.2
  0.0 0.9 %copy-done.2 = bf16[2,8,4,2048]{3,2,1,0:T(4,128)(2,1)S(1)} copy-done((bf16[2,8,4,2048]{3,2,1,0:T(4,128)(2,1)S(1)}, bf16[2,8,4,2048]{3,2,1,0:T(4,128)(2,1)}, u32[]{:S(2)}) %copy-start.2) | copy-done | bytes 262168
  1.0 0.2 first.1
  1.2 0.7 %collective-permute-start = (f32[8,128]{1,0:T(8,128)S(1)}, f32[8,128]{1,0:T(8,128)S(1)}, u32[]{:S(2)}, u32[]{:S(2)}) collective-permute-start(f32[8,128]{1,0:T(8,128)S(1)} %get-tuple-element.17), channel_id=1, source_target_pairs={{0,1},{1,0},{2,3},{3,2},{4,5},{5,4},{6,7},{7,6},{8,9},{9,8},{10,11... | collective-permute-start | bytes 12296 | tf_op jit(solution)/shard_map/ppermute | solution.py:218
  1.9 0.0 collective-permute-done.refs_1_
  1.9 0.0 copy-start.4
  1.9 0.4 norm.2
  2.3 0.7 %collective-permute-start.1 = (bf16[32,2048]{1,0:T(8,128)(2,1)S(1)}, bf16[32,2048]{1,0:T(8,128)(2,1)S(1)}, u32[]{:S(2)}, u32[]{:S(2)}) collective-permute-start(bf16[32,2048]{1,0:T(8,128)(2,1)S(1)} %get-tuple-element.19), channel_id=1, source_target_pairs={{0,2},{2,4},{4,6},{6,8},{8,10},{10,12},{12,14},{1,3},{3,5},{5,7},{... | collective-permute-start | bytes 393224 | tf_op jit(solution)/shard_map/ppermute | solution.py:233
  2.9 0.7 %collective-permute-start.2 = (bf16[32,2048]{1,0:T(8,128)(2,1)S(1)}, bf16[32,2048]{1,0:T(8,128)(2,1)S(1)}, u32[]{:S(2)}, u32[]{:S(2)}) collective-permute-start(bf16[32,2048]{1,0:T(8,128)(2,1)S(1)} %get-tuple-element.20), channel_id=1, source_target_pairs={{2,0},{4,2},{6,4},{8,6},{10,8},{12,10},{14,12},{3,1},{5,3},{7,5},{... | collective-permute-start | bytes 393224 | tf_op jit(solution)/shard_map/ppermute | solution.py:236
  3.6 0.1 pad_add_fusion.refs_0_
  3.7 0.0 collective-permute-done.1.refs_5_
  3.7 0.0 collective-permute-done.2.refs_6_
  3.7 0.0 copy-start
  3.7 1.4 %copy-done = bf16[1,16,128,384]{3,2,1,0:T(8,128)(2,1)S(1)} copy-done((bf16[1,16,128,384]{3,2,1,0:T(8,128)(2,1)S(1)}, bf16[1,16,128,384]{3,2,1,0:T(8,128)(2,1)}, u32[]{:S(2)}) %copy-start) | copy-done | bytes 1572888
  5.1 0.0 copy-start.3
  5.1 0.7 %copy-done.3 = s32[2,4]{1,0:T(2,128)S(1)} copy-done((s32[2,4]{1,0:T(2,128)S(1)}, s32[2,4]{1,0:T(2,128)}, u32[]{:S(2)}) %copy-start.3) | copy-done | bytes 56
  5.8 0.0 copy-start.5
  5.8 0.7 %copy-done.5 = s32[2,4]{1,0:T(2,128)S(1)} copy-done((s32[2,4]{1,0:T(2,128)S(1)}, s32[2,4]{1,0:T(2,128)}, u32[]{:S(2)}) %copy-start.5) | copy-done | bytes 56
  6.5 0.0 copy-start.1
  6.5 0.6 %layer.2 = (bf16[64,2048]{1,0:T(8,128)(2,1)S(1)}, f32[8,128]{1,0:T(8,128)S(1)}) custom-call(s32[2]{0:T(128)S(1)} %pad_add_fusion.refs_0_, s32[2,4]{1,0:T(2,128)S(1)} %copy-done.3, s32[2,4]{1,0:T(2,128)S(1)} %copy-done.5, bf16[64,2048]{1,0:T(8,128)(2,1)S(1)} %get-tuple-element.16.refs_0_.refs_3_.refs_8_, bf16[64,2048]{1,0:T(8,128)(2,1)S(1)} %get-tuple-element.18.refs_4_, ...), custom_call_target="tpu_custom_call" | custom-call | flops 201326592 | bytes 4194304 | tf_op jit(solution)/shard_map/layer/pallas_call | solution.py:249
  7.1 1.3 %collective-permute-start.3 = (bf16[64,2048]{1,0:T(8,128)(2,1)S(1)}, bf16[64,2048]{1,0:T(8,128)(2,1)S(1)}, u32[]{:S(2)}, u32[]{:S(2)}) collective-permute-start(bf16[64,2048]{1,0:T(8,128)(2,1)S(1)} %get-tuple-element.21.refs_8_), channel_id=1, source_target_pairs={{0,16},{1,17},{2,18},{3,19},{4,20},{5,21},{6,22},{7,23},{8,24},{9,... | collective-permute-start | bytes 786440 | tf_op jit(solution)/shard_map/ppermute | solution.py:260
  8.4 1.3 %collective-permute-start.4 = (f32[8,128]{1,0:T(8,128)S(1)}, f32[8,128]{1,0:T(8,128)S(1)}, u32[]{:S(2)}, u32[]{:S(2)}) collective-permute-start(f32[8,128]{1,0:T(8,128)S(1)} %get-tuple-element.22), channel_id=1, source_target_pairs={{0,17},{1,16},{2,19},{3,18},{4,21},{5,20},{6,23},{7,22},{8,25},{9,... | collective-permute-start | bytes 12296 | tf_op jit(solution)/shard_map/ppermute | solution.py:263
  9.7 21.5 %collective-permute-done.4.refs_1_ = f32[8,128]{1,0:T(8,128)S(1)} collective-permute-done((f32[8,128]{1,0:T(8,128)S(1)}, f32[8,128]{1,0:T(8,128)S(1)}, u32[]{:S(2)}, u32[]{:S(2)}) %collective-permute-start.4) | collective-permute-done | bytes 4128 | tf_op jit(solution)/shard_map/ppermute | solution.py:263
  31.1 0.0 collective-permute-done.3.refs_0_.refs_3_
  31.2 0.4 norm.3
  31.5 2.6 %collective-permute-start.5 = (bf16[32,2048]{1,0:T(8,128)(2,1)S(1)}, bf16[32,2048]{1,0:T(8,128)(2,1)S(1)}, u32[]{:S(2)}, u32[]{:S(2)}) collective-permute-start(bf16[32,2048]{1,0:T(8,128)(2,1)S(1)} %get-tuple-element.24), channel_id=1, source_target_pairs={{16,18},{18,20},{20,22},{22,24},{24,26},{26,28},{28,30},{17,19},{1... | collective-permute-start | bytes 393224 | tf_op jit(solution)/shard_map/ppermute | solution.py:233
  34.1 1.9 %collective-permute-start.6 = (bf16[32,2048]{1,0:T(8,128)(2,1)S(1)}, bf16[32,2048]{1,0:T(8,128)(2,1)S(1)}, u32[]{:S(2)}, u32[]{:S(2)}) collective-permute-start(bf16[32,2048]{1,0:T(8,128)(2,1)S(1)} %get-tuple-element.25), channel_id=1, source_target_pairs={{18,16},{20,18},{22,20},{24,22},{26,24},{28,26},{30,28},{19,17},{2... | collective-permute-start | bytes 393224 | tf_op jit(solution)/shard_map/ppermute | solution.py:236
  36.1 0.0 collective-permute-done.5.refs_5_
  36.1 4.3 %collective-permute-done.6.refs_6_ = bf16[32,2048]{1,0:T(8,128)(2,1)S(1)} collective-permute-done((bf16[32,2048]{1,0:T(8,128)(2,1)S(1)}, bf16[32,2048]{1,0:T(8,128)(2,1)S(1)}, u32[]{:S(2)}, u32[]{:S(2)}) %collective-permute-start.6) | collective-permute-done | bytes 131104 | tf_op jit(solution)/shard_map/ppermute | solution.py:236
  40.4 0.0 copy-done.4
  40.4 0.0 copy-done.1
  40.4 3.9 %layer.3 = (bf16[1,2,8,4,2048]{4,3,2,1,0:T(4,128)(2,1)}, f32[8,128]{1,0:T(8,128)}) custom-call(s32[2]{0:T(128)S(1)} %pad_add_fusion.refs_0_, s32[2,4]{1,0:T(2,128)S(1)} %copy-done.4, s32[2,4]{1,0:T(2,128)S(1)} %copy-done.5, bf16[64,2048]{1,0:T(8,128)(2,1)S(1)} %collective-permute-done.3.refs_0_.refs_3_, bf16[64,2048]{1,0:T(8,128)(2,1)S(1)} %get-tuple-element.23.refs_4_, ...), custom_call_target="tpu_custom_call" | custom-call | flops 201326592 | bytes 4194304 | tf_op jit(solution)/shard_map/layer/pallas_call | solution.py:249
Async XLA Ops:
  0.0 0.9 %copy-start.2 = (bf16[2,8,4,2048]{3,2,1,0:T(4,128)(2,1)S(1)}, bf16[2,8,4,2048]{3,2,1,0:T(4,128)(2,1)}, u32[]{:S(2)}) copy-start(bf16[2,8,4,2048]{3,2,1,0:T(4,128)(2,1)} %signal_ref.1) | copy-start | bytes 786436
  1.2 0.7 %collective-permute-start = (f32[8,128]{1,0:T(8,128)S(1)}, f32[8,128]{1,0:T(8,128)S(1)}, u32[]{:S(2)}, u32[]{:S(2)}) collective-permute-start(f32[8,128]{1,0:T(8,128)S(1)} %get-tuple-element.17), channel_id=1, source_target_pairs={{0,1},{1,0},{2,3},{3,2},{4,5},{5,4},{6,7},{7,6},{8,9},{9,8},{10,11... | collective-permute-start | bytes 12296 | tf_op jit(solution)/shard_map/ppermute | solution.py:218
  1.9 38.6 %copy-start.4 = (s32[2,4]{1,0:T(2,128)S(1)}, s32[2,4]{1,0:T(2,128)}, u32[]{:S(2)}) copy-start(s32[2,4]{1,0:T(2,128)} %refs_1_.3) | copy-start | bytes 100
  2.3 1.4 %collective-permute-start.1 = (bf16[32,2048]{1,0:T(8,128)(2,1)S(1)}, bf16[32,2048]{1,0:T(8,128)(2,1)S(1)}, u32[]{:S(2)}, u32[]{:S(2)}) collective-permute-start(bf16[32,2048]{1,0:T(8,128)(2,1)S(1)} %get-tuple-element.19), channel_id=1, source_target_pairs={{0,2},{2,4},{4,6},{6,8},{8,10},{10,12},{12,14},{1,3},{3,5},{5,7},{... | collective-permute-start | bytes 393224 | tf_op jit(solution)/shard_map/ppermute | solution.py:233
  2.9 0.8 %collective-permute-start.2 = (bf16[32,2048]{1,0:T(8,128)(2,1)S(1)}, bf16[32,2048]{1,0:T(8,128)(2,1)S(1)}, u32[]{:S(2)}, u32[]{:S(2)}) collective-permute-start(bf16[32,2048]{1,0:T(8,128)(2,1)S(1)} %get-tuple-element.20), channel_id=1, source_target_pairs={{2,0},{4,2},{6,4},{8,6},{10,8},{12,10},{14,12},{3,1},{5,3},{7,5},{... | collective-permute-start | bytes 393224 | tf_op jit(solution)/shard_map/ppermute | solution.py:236
  3.7 1.4 %copy-start = (bf16[1,16,128,384]{3,2,1,0:T(8,128)(2,1)S(1)}, bf16[1,16,128,384]{3,2,1,0:T(8,128)(2,1)}, u32[]{:S(2)}) copy-start(bf16[1,16,128,384]{3,2,1,0:T(8,128)(2,1)} %refs_7_.3) | copy-start | bytes 4718596
  5.1 0.7 %copy-start.3 = (s32[2,4]{1,0:T(2,128)S(1)}, s32[2,4]{1,0:T(2,128)}, u32[]{:S(2)}) copy-start(s32[2,4]{1,0:T(2,128)} %refs_1_.3) | copy-start | bytes 100
  5.8 0.7 %copy-start.5 = (s32[2,4]{1,0:T(2,128)S(1)}, s32[2,4]{1,0:T(2,128)}, u32[]{:S(2)}) copy-start(s32[2,4]{1,0:T(2,128)} %refs_2_.3) | copy-start | bytes 100
  6.5 34.0 %copy-start.1 = (bf16[1,16,128,384]{3,2,1,0:T(8,128)(2,1)S(1)}, bf16[1,16,128,384]{3,2,1,0:T(8,128)(2,1)}, u32[]{:S(2)}) copy-start(bf16[1,16,128,384]{3,2,1,0:T(8,128)(2,1)} %refs_7_.3) | copy-start | bytes 4718596
  7.1 24.1 %collective-permute-start.3 = (bf16[64,2048]{1,0:T(8,128)(2,1)S(1)}, bf16[64,2048]{1,0:T(8,128)(2,1)S(1)}, u32[]{:S(2)}, u32[]{:S(2)}) collective-permute-start(bf16[64,2048]{1,0:T(8,128)(2,1)S(1)} %get-tuple-element.21.refs_8_), channel_id=1, source_target_pairs={{0,16},{1,17},{2,18},{3,19},{4,20},{5,21},{6,22},{7,23},{8,24},{9,... | collective-permute-start | bytes 786440 | tf_op jit(solution)/shard_map/ppermute | solution.py:260
  8.4 22.8 %collective-permute-start.4 = (f32[8,128]{1,0:T(8,128)S(1)}, f32[8,128]{1,0:T(8,128)S(1)}, u32[]{:S(2)}, u32[]{:S(2)}) collective-permute-start(f32[8,128]{1,0:T(8,128)S(1)} %get-tuple-element.22), channel_id=1, source_target_pairs={{0,17},{1,16},{2,19},{3,18},{4,21},{5,20},{6,23},{7,22},{8,25},{9,... | collective-permute-start | bytes 12296 | tf_op jit(solution)/shard_map/ppermute | solution.py:263
  31.5 4.6 %collective-permute-start.5 = (bf16[32,2048]{1,0:T(8,128)(2,1)S(1)}, bf16[32,2048]{1,0:T(8,128)(2,1)S(1)}, u32[]{:S(2)}, u32[]{:S(2)}) collective-permute-start(bf16[32,2048]{1,0:T(8,128)(2,1)S(1)} %get-tuple-element.24), channel_id=1, source_target_pairs={{16,18},{18,20},{20,22},{22,24},{24,26},{26,28},{28,30},{17,19},{1... | collective-permute-start | bytes 393224 | tf_op jit(solution)/shard_map/ppermute | solution.py:233
  34.1 6.3 %collective-permute-start.6 = (bf16[32,2048]{1,0:T(8,128)(2,1)S(1)}, bf16[32,2048]{1,0:T(8,128)(2,1)S(1)}, u32[]{:S(2)}, u32[]{:S(2)}) collective-permute-start(bf16[32,2048]{1,0:T(8,128)(2,1)S(1)} %get-tuple-element.25), channel_id=1, source_target_pairs={{18,16},{20,18},{22,20},{24,22},{26,24},{28,26},{30,28},{19,17},{2... | collective-permute-start | bytes 393224 | tf_op jit(solution)/shard_map/ppermute | solution.py:236

commit v2 on v1

v2 whole, which is shorter than its diff:
```python
import math

import jax
import jax.numpy as jnp
from jax import lax
from jax.experimental import pallas as pl
from jax.experimental.pallas import tpu as pltpu
from jax.sharding import PartitionSpec as P

HEADS = 32
HEAD = 128
WIN = 4
GROUP = 4
EPS = 1e-06
BIG = 1e30

HBM = pl.BlockSpec(memory_space=pltpu.HBM)
VMEM = pl.BlockSpec(memory_space=pltpu.VMEM)
PARAMS = pltpu.CompilerParams(vmem_limit_bytes=16 * 1024 * 1024)


def cost(flops, moved):
    return pl.CostEstimate(flops=flops, bytes_accessed=moved, transcendentals=0)


def first_kernel(
    signal_hbm, weights_hbm, first_hbm, pad_hbm, own_ref, head_ref, tail_ref, squares_ref,
    weights_ref, time_ref, station_ref, signal_ref, first_ref, pad_ref, arrived,
    *, total_steps,
):
    copies = [
        pltpu.make_async_copy(signal_hbm, signal_ref, arrived.at[0]),
        pltpu.make_async_copy(first_hbm, first_ref, arrived.at[1]),
        pltpu.make_async_copy(pad_hbm, pad_ref, arrived.at[2]),
        pltpu.make_async_copy(weights_hbm, weights_ref, arrived.at[3]),
    ]
    for copy in copies:
        copy.start()
    micro, steps, stations, _ = signal_ref.shape
    rows_micro = steps * stations
    edge = WIN * stations
    copies[0].wait()
    for m in range(micro):
        for t in range(0, steps, 2):
            own_ref[pl.ds(m * rows_micro + t * stations, 2 * stations), :] = jnp.concatenate(
                [signal_ref[m, t].astype(jnp.float32), signal_ref[m, t + 1].astype(jnp.float32)],
                axis=0,
            ).astype(jnp.bfloat16)
    for m in range(micro):
        base = m * rows_micro
        head_ref[m * edge : (m + 1) * edge, :] = own_ref[base : base + edge, :]
        tail_ref[m * edge : (m + 1) * edge, :] = own_ref[base + rows_micro - edge : base + rows_micro, :]
    rows = own_ref[...]
    count = rows.shape[0]
    gram = lax.dot_general(
        rows, rows, (((1,), (1,)), ((), ())), preferred_element_type=jnp.float32
    )
    squares_ref[...] = jnp.zeros(squares_ref.shape, jnp.float32)
    squares_ref[pl.ds(lax.axis_index("seq"), 1), 0:count] = jnp.sum(
        jnp.where(same(count), gram, 0.0), axis=0, keepdims=True
    )
    copies[1].wait()
    copies[2].wait()
    fill_masks(first_ref, pad_ref, time_ref, station_ref, steps, stations, total_steps)
    copies[3].wait()


def same(count):
    return lax.broadcasted_iota(jnp.int32, (count, count), 0) == lax.broadcasted_iota(
        jnp.int32, (count, count), 1
    )


def fill_masks(first_ref, pad_ref, time_ref, station_ref, steps, stations, total_steps):
    time_base = lax.axis_index("seq") * steps
    keys = (steps + 2 * WIN) * stations
    columns = GROUP * steps * stations
    key = lax.broadcasted_iota(jnp.int32, (keys, columns), 0)
    query = lax.broadcasted_iota(jnp.int32, (keys, columns), 1) % (steps * stations)
    key_station, query_station = key % stations, query % stations
    key_time, query_time = key // stations - WIN, query // stations
    same_station = key_station == query_station
    same_time = key_time == query_time
    near = jnp.abs(key_time - query_time) <= WIN
    step = time_base + key_time
    for m in range(time_ref.shape[0]):
        first = jnp.zeros((keys, columns), jnp.int32)
        pad = jnp.zeros((keys, columns), jnp.int32)
        for s in range(stations):
            first = jnp.where(key_station == s, first_ref[m, s], first)
            pad = jnp.where(key_station == s, pad_ref[m, s], pad)
        recorded = (step >= first) & (step < total_steps - pad)
        time_ref[m] = jnp.where(same_station & near & (recorded | same_time), 0.0, -BIG)
        station_ref[m] = jnp.where(same_time & (recorded | same_station), 0.0, -BIG)[
            WIN * stations : (WIN + steps) * stations
        ]


def softmax_columns(scores):
    grown = jnp.exp(scores - jnp.max(scores, axis=0, keepdims=True))
    return (grown * (1.0 / jnp.sum(grown, axis=0, keepdims=True))).astype(jnp.bfloat16)


def layer_kernel(
    own_ref, left_ref, right_ref, own_squares_ref, left_squares_ref, right_squares_ref,
    time_ref, station_ref, weights_ref, kept_ref, out_ref, *refs, tick, micro, steps, stations, last,
):
    if last:
        normed_ref, projected_ref = refs
    else:
        head_ref, tail_ref, squares_ref, normed_ref, projected_ref = refs
    rows_micro = steps * stations
    edge = WIN * stations
    reach = rows_micro + 2 * edge
    own_rows = micro * rows_micro
    all_rows = micro * reach
    heads_dev = weights_ref.shape[1]
    active = lax.axis_index("section") == tick
    bf16, f32 = jnp.bfloat16, jnp.float32

    def write(m, lanes, values):
        if last:
            for t in range(steps):
                out_ref[0, m, t, :, lanes] = values[t * stations : (t + 1) * stations].astype(bf16)
        else:
            values = values.astype(bf16)
            out_ref[m * rows_micro : (m + 1) * rows_micro, lanes] = values
            head_ref[m * edge : (m + 1) * edge, lanes] = values[:edge]
            tail_ref[m * edge : (m + 1) * edge, lanes] = values[rows_micro - edge :]

    def column_squares():
        seq = lax.axis_index("seq")
        if tick == 0:
            before, after = jnp.maximum(seq - 1, 0), jnp.minimum(seq + 1, lax.axis_size("seq") - 1)
            sources = (
                left_squares_ref[pl.ds(before, 1), :],
                own_squares_ref[pl.ds(seq, 1), :],
                right_squares_ref[pl.ds(after, 1), :],
            )
        else:
            sources = (left_squares_ref[0:1, :], own_squares_ref[0:1, :], right_squares_ref[0:1, :])
        row = lax.broadcasted_iota(jnp.int32, (all_rows, 128), 0)
        lane = lax.broadcasted_iota(jnp.int32, (all_rows, 128), 1)
        place, base = row % reach, (row // reach) * rows_micro
        picked = jnp.where(
            place < edge,
            jnp.where(lane == base + place + rows_micro - edge, sources[0], 0.0),
            jnp.where(
                place < edge + rows_micro,
                jnp.where(lane == base + place - edge, sources[1], 0.0),
                jnp.where(lane == base + place - edge - rows_micro, sources[2], 0.0),
            ),
        )
        return jnp.sum(picked, axis=1, keepdims=True)

    @pl.when(active)
    def _():
        raw = []
        for m in range(micro):
            raw += [
                left_ref[m * edge : (m + 1) * edge, :],
                own_ref[m * rows_micro : (m + 1) * rows_micro, :],
                right_ref[m * edge : (m + 1) * edge, :],
            ]
        raw = jnp.concatenate(raw, axis=0)
        total = column_squares()
        if tick > 0:
            mine = jnp.zeros((all_rows, HEAD), f32)
            for head in range(heads_dev):
                part = raw[:, head * HEAD : (head + 1) * HEAD].astype(f32)
                mine = mine + part * part
            total = total + jnp.sum(mine, axis=1, keepdims=True)
        factor = lax.rsqrt(total / (HEADS * HEAD) + EPS)
        for head in range(heads_dev):
            lanes = slice(head * HEAD, (head + 1) * HEAD)
            normed_ref[:, lanes] = (raw[:, lanes].astype(f32) * factor).astype(bf16)
        width = 3 * HEAD
        for head in range(heads_dev):
            projected_ref[:, head * width : (head + 1) * width] = jnp.dot(
                normed_ref[:, head * HEAD : (head + 1) * HEAD],
                weights_ref[0, head],
                preferred_element_type=f32,
            ).astype(bf16)
        pairs = [(g, m) for g in range(heads_dev // GROUP) for m in range(micro)]
        blank = jnp.zeros((rows_micro, HEAD), bf16)
        scores = []
        for g, m in pairs:
            at = [(g * GROUP + j) * width for j in range(GROUP)]
            first = m * reach
            spread = jnp.concatenate(
                [
                    jnp.concatenate(
                        [
                            projected_ref[first + edge : first + edge + rows_micro, at[j] : at[j] + HEAD]
                            if i == j
                            else blank
                            for i in range(GROUP)
                        ],
                        axis=1,
                    )
                    for j in range(GROUP)
                ],
                axis=0,
            )
            keys = jnp.concatenate(
                [projected_ref[first : first + reach, a + HEAD : a + 2 * HEAD] for a in at], axis=1
            )
            scores.append(
                lax.dot_general(
                    keys, spread, (((1,), (1,)), ((), ())), preferred_element_type=f32
                )
                * (1.0 / math.sqrt(HEAD))
            )
        mixes = []
        for (g, m), score in zip(pairs, scores):
            time_weights = softmax_columns(score + time_ref[m])
            station_weights = softmax_columns(score[edge : edge + rows_micro] + station_ref[m])
            mixes.append(jnp.concatenate([time_weights, station_weights], axis=0).T)
        sums = [jnp.zeros((rows_micro, HEAD), f32) for _ in range(micro)]
        for (g, m), mix in zip(pairs, mixes):
            first = m * reach
            for j in range(GROUP):
                head = g * GROUP + j
                at = head * width + 2 * HEAD
                mixed = jnp.dot(
                    mix[j * rows_micro : (j + 1) * rows_micro],
                    jnp.concatenate(
                        [
                            projected_ref[first : first + reach, at : at + HEAD],
                            projected_ref[first + edge : first + edge + rows_micro, at : at + HEAD],
                        ],
                        axis=0,
                    ),
                    preferred_element_type=f32,
                )
                lanes = slice(head * HEAD, (head + 1) * HEAD)
                own = slice(m * rows_micro, (m + 1) * rows_micro)
                result = own_ref[own, lanes].astype(f32) + mixed
                write(m, lanes, result)
                if not last:
                    rounded = result.astype(bf16).astype(f32)
                    sums[m] = sums[m] + rounded * rounded
        if not last:
            column = jnp.sum(jnp.concatenate(sums, axis=0), axis=1, keepdims=True)
            squares_ref[...] = jnp.zeros(squares_ref.shape, f32)
            squares_ref[0:1, 0:own_rows] = jnp.sum(
                jnp.where(same(own_rows), column, 0.0), axis=0, keepdims=True
            )

    @pl.when(jnp.logical_not(active))
    def _():
        for m in range(micro):
            for head in range(heads_dev):
                lanes = slice(head * HEAD, (head + 1) * HEAD)
                write(m, lanes, kept_ref[m * rows_micro : (m + 1) * rows_micro, lanes].astype(f32))
        if not last:
            squares_ref[...] = jnp.zeros(squares_ref.shape, f32)


def body(signal, head_proj, record_start, record_pad):
    section_count = lax.axis_size("section")
    seq_count = lax.axis_size("seq")
    rep_count = lax.axis_size("rep")
    micro, steps, stations, features = signal.shape
    heads_dev = head_proj.shape[1]
    rows_micro = steps * stations
    own_rows = micro * rows_micro
    edge = WIN * stations
    reach = rows_micro + 2 * edge
    bf16, f32 = jnp.bfloat16, jnp.float32
    own_shape = jax.ShapeDtypeStruct((own_rows, features), bf16)
    edge_shape = jax.ShapeDtypeStruct((micro * edge, features), bf16)
    squares_shape = jax.ShapeDtypeStruct((8, 128), f32)
    own_bytes = own_rows * features * 2
    columns = GROUP * rows_micro

    own, head_rows, tail_rows, squares, weights, time_bias, station_bias = pl.pallas_call(
        lambda *refs: first_kernel(*refs, total_steps=steps * seq_count),
        in_specs=[HBM] * 4,
        out_specs=[VMEM] * 7,
        out_shape=[
            own_shape,
            edge_shape,
            edge_shape,
            jax.ShapeDtypeStruct((seq_count, 128), f32),
            jax.ShapeDtypeStruct(head_proj.shape, bf16),
            jax.ShapeDtypeStruct((micro, reach, columns), f32),
            jax.ShapeDtypeStruct((micro, rows_micro, columns), f32),
        ],
        scratch_shapes=[
            pltpu.VMEM(signal.shape, bf16),
            pltpu.SMEM(record_start.shape, jnp.int32),
            pltpu.SMEM(record_pad.shape, jnp.int32),
            pltpu.SemaphoreType.DMA((4,)),
        ],
        compiler_params=PARAMS,
        cost_estimate=cost(2 * own_rows * own_rows * features, 3 * own_bytes),
        name="first",
    )(*[pltpu.with_memory_space_constraint(x, pltpu.HBM) for x in (signal, head_proj, record_start, record_pad)])

    def to_next(block, source, target, step):
        route = [
            (source * seq_count + i, target * seq_count + i + step)
            for i in range(seq_count)
            if 0 <= i + step < seq_count
        ]
        return lax.ppermute(block, ("section", "seq"), route)

    def to_next_other(block, source, target, step):
        route = [
            (
                (source * seq_count + i) * rep_count + r,
                (target * seq_count + i + step) * rep_count + (r + 1) % rep_count,
            )
            for i in range(seq_count)
            if 0 <= i + step < seq_count
            for r in range(rep_count)
        ]
        return lax.ppermute(block, ("section", "seq", "rep"), route)

    helper = 1 if section_count > 1 else 0
    left = to_next(tail_rows, helper, 0, 1)
    right = to_next(head_rows, helper, 0, -1)
    own_squares = left_squares = right_squares = lax.psum(squares, ("seq", "rep"))
    kept = own
    for tick in range(section_count):
        last = tick + 1 == section_count

        def kernel(*refs, tick=tick, last=last):
            layer_kernel(*refs, tick=tick, micro=micro, steps=steps, stations=stations, last=last)

        out_shape = (
            [jax.ShapeDtypeStruct((1,) + signal.shape, bf16)]
            if last
            else [own_shape, edge_shape, edge_shape, squares_shape]
        )
        kept, *sent = pl.pallas_call(
            kernel,
            in_specs=[VMEM] * 10,
            out_specs=[VMEM] * len(out_shape),
            out_shape=out_shape,
            scratch_shapes=[
                pltpu.VMEM((micro * reach, features), bf16),
                pltpu.VMEM((micro * reach, heads_dev * 3 * HEAD), bf16),
            ],
            compiler_params=PARAMS,
            cost_estimate=cost(4 * own_rows * features * 3 * HEAD, 16 * own_bytes),
            name="layer",
        )(
            own, left, right, own_squares, left_squares, right_squares,
            time_bias, station_bias, weights, kept,
        )
        if not last:
            head_rows, tail_rows, squares = sent
            own = to_next(kept, tick, tick + 1, 0)
            left = to_next(tail_rows, tick, tick + 1, 1)
            right = to_next(head_rows, tick, tick + 1, -1)
            own_squares = to_next_other(squares, tick, tick + 1, 0)
            left_squares = to_next_other(squares, tick, tick + 1, 1)
            right_squares = to_next_other(squares, tick, tick + 1, -1)
    return kept


def solution(mesh):
    return jax.shard_map(
        body,
        mesh=mesh,
        in_specs=(P(None, "seq", None, "rep"), P("section", "rep", None, None), P(), P()),
        out_specs=P("section", None, "seq", None, "rep"),
        check_vma=False,
    )
```

time: 44.6 us -> 58.8 us (1.32)
  the two profiles are of different devices: /device:TPU:11 before, /device:TPU:6 now
where the time goes in v2:
time: 58.8 us; the launch traced here: 58.5 us
  blocking collectives  31.5 us (54%)
  waiting for transfers between devices  14.3 us (24%)
  starting transfers between devices  9.04 us (15%)
  Pallas kernels  3.55 us (6%)
    psum x1, blocking collectives, body(): lax.psum(squares, ('seq', 'rep'))  31.5 us
    ppermute x3, waiting for transfers between devices, to_next_other(): return lax.ppermute(block, ('section', 'seq', 'rep'), route)  14.3 us
    ppermute x5, starting transfers between devices, to_next(): return lax.ppermute(block, ('section', 'seq'), route)  5.81 us
    ppermute x3, starting transfers between devices, to_next_other(): return lax.ppermute(block, ('section', 'seq', 'rep'), route)  3.23 us
    pallas_call x2, Pallas kernels, body(): pl.pallas_call(kernel, in_specs=[VMEM] * 10, out_specs=[VMEM] * len(out_s...  2.01 us
    pallas_call x1, Pallas kernels, body(): pl.pallas_call(lambda *refs: first_kernel(*refs, total_steps=steps * seq_...  1.54 us
  transfers between devices with their start and end apart: 8, of which 2 were waited for; matrix products, arithmetic and copies ran while one was open for 0% of the time, Pallas kernels for 0%

profile of v2, /device:TPU:6, one launch (start us, length us, event | category | flops | bytes accessed | tf_op | source)
XLA Modules:
  0.0 58.5 jit_solution(10858092924929288842)
XLA Ops:
  0.0 1.5 %first.1 = (bf16[64,2048]{1,0:T(8,128)(2,1)S(1)}, bf16[32,2048]{1,0:T(8,128)(2,1)S(1)}, bf16[32,2048]{1,0:T(8,128)(2,1)S(1)}, f32[8,128]{1,0:T(8,128)S(1)}, bf16...) custom-call(bf16[2,8,4,2048]{3,2,1,0:T(4,128)(2,1)} %refs_0_.1, ...), custom_call_target="tpu_custom_call" | custom-call | flops 16777216 | bytes 786432 | tf_op jit(solution)/shard_map/first/pallas_call | solution.py:277
  1.5 1.9 %collective-permute-start = (bf16[32,2048]{1,0:T(8,128)(2,1)S(1)}, bf16[32,2048]{1,0:T(8,128)(2,1)S(1)}, u32[]{:S(2)}, u32[]{:S(2)}) collective-permute-start(bf16[32,2048]{1,0:T(8,128)(2,1)S(1)} %get-tuple-element.17), channel_id=1, source_target_pairs={{16,2},{18,4},{20,6},{22,8},{24,10},{26,12},{28,14},{17,3},{19,5},... | collective-permute-start | bytes 393224 | tf_op jit(solution)/shard_map/ppermute | solution.py:307
  3.4 0.7 %collective-permute-start.1 = (bf16[32,2048]{1,0:T(8,128)(2,1)S(1)}, bf16[32,2048]{1,0:T(8,128)(2,1)S(1)}, u32[]{:S(2)}, u32[]{:S(2)}) collective-permute-start(bf16[32,2048]{1,0:T(8,128)(2,1)S(1)} %get-tuple-element.18), channel_id=1, source_target_pairs={{18,0},{20,2},{22,4},{24,6},{26,8},{28,10},{30,12},{19,1},{21,3},{... | collective-permute-start | bytes 393224 | tf_op jit(solution)/shard_map/ppermute | solution.py:307
  4.1 31.5 %psum.7.refs_3_.refs_4_.refs_5_ = f32[8,128]{1,0:T(8,128)S(1)} all-reduce(f32[8,128]{1,0:T(8,128)S(1)} %get-tuple-element.19), channel_id=1, replica_groups=mesh['section'=2,'seq'=8,'rep'=2] {'seq','rep'}, use_global_device_ids=true, to_apply=%region_0.0 | all-reduce | flops 1024 | bytes 8192 | tf_op jit(solution)/shard_map/psum | solution.py:324
  35.6 0.0 collective-permute-done.refs_1_
  35.7 0.0 collective-permute-done.1.refs_2_
  35.7 0.1 layer.2
  35.8 1.3 %collective-permute-start.2 = (bf16[64,2048]{1,0:T(8,128)(2,1)S(1)}, bf16[64,2048]{1,0:T(8,128)(2,1)S(1)}, u32[]{:S(2)}, u32[]{:S(2)}) collective-permute-start(bf16[64,2048]{1,0:T(8,128)(2,1)S(1)} %get-tuple-element.23.refs_9_), channel_id=1, source_target_pairs={{0,16},{2,18},{4,20},{6,22},{8,24},{10,26},{12,28},{14,30},{1,17},... | collective-permute-start | bytes 786440 | tf_op jit(solution)/shard_map/ppermute | solution.py:307
  37.1 0.7 %collective-permute-start.3 = (bf16[32,2048]{1,0:T(8,128)(2,1)S(1)}, bf16[32,2048]{1,0:T(8,128)(2,1)S(1)}, u32[]{:S(2)}, u32[]{:S(2)}) collective-permute-start(bf16[32,2048]{1,0:T(8,128)(2,1)S(1)} %get-tuple-element.24), channel_id=1, source_target_pairs={{0,18},{2,20},{4,22},{6,24},{8,26},{10,28},{12,30},{1,19},{3,21},{... | collective-permute-start | bytes 393224 | tf_op jit(solution)/shard_map/ppermute | solution.py:307
  37.7 1.3 %collective-permute-start.4 = (bf16[32,2048]{1,0:T(8,128)(2,1)S(1)}, bf16[32,2048]{1,0:T(8,128)(2,1)S(1)}, u32[]{:S(2)}, u32[]{:S(2)}) collective-permute-start(bf16[32,2048]{1,0:T(8,128)(2,1)S(1)} %get-tuple-element.25), channel_id=1, source_target_pairs={{2,16},{4,18},{6,20},{8,22},{10,24},{12,26},{14,28},{3,17},{5,19},... | collective-permute-start | bytes 393224 | tf_op jit(solution)/shard_map/ppermute | solution.py:307
  39.0 1.3 %collective-permute-start.7 = (f32[8,128]{1,0:T(8,128)S(1)}, f32[8,128]{1,0:T(8,128)S(1)}, u32[]{:S(2)}, u32[]{:S(2)}) collective-permute-start(f32[8,128]{1,0:T(8,128)S(1)} %get-tuple-element.26), channel_id=1, source_target_pairs={{2,17},{3,16},{4,19},{5,18},{6,21},{7,20},{8,23},{9,22},{10,25},{1... | collective-permute-start | bytes 12296 | tf_op jit(solution)/shard_map/ppermute | solution.py:319
  40.3 0.7 %collective-permute-start.6 = (f32[8,128]{1,0:T(8,128)S(1)}, f32[8,128]{1,0:T(8,128)S(1)}, u32[]{:S(2)}, u32[]{:S(2)}) collective-permute-start(f32[8,128]{1,0:T(8,128)S(1)} %get-tuple-element.26), channel_id=1, source_target_pairs={{0,19},{1,18},{2,21},{3,20},{4,23},{5,22},{6,25},{7,24},{8,27},{9,... | collective-permute-start | bytes 12296 | tf_op jit(solution)/shard_map/ppermute | solution.py:319
  41.0 9.2 %collective-permute-done.7.refs_5_ = f32[8,128]{1,0:T(8,128)S(1)} collective-permute-done((f32[8,128]{1,0:T(8,128)S(1)}, f32[8,128]{1,0:T(8,128)S(1)}, u32[]{:S(2)}, u32[]{:S(2)}) %collective-permute-start.7) | collective-permute-done | bytes 4128 | tf_op jit(solution)/shard_map/ppermute | solution.py:319
  50.2 1.3 %collective-permute-start.5 = (f32[8,128]{1,0:T(8,128)S(1)}, f32[8,128]{1,0:T(8,128)S(1)}, u32[]{:S(2)}, u32[]{:S(2)}) collective-permute-start(f32[8,128]{1,0:T(8,128)S(1)} %get-tuple-element.26), channel_id=1, source_target_pairs={{0,17},{1,16},{2,19},{3,18},{4,21},{5,20},{6,23},{7,22},{8,25},{9,... | collective-permute-start | bytes 12296 | tf_op jit(solution)/shard_map/ppermute | solution.py:319
  51.4 0.0 collective-permute-done.6.refs_4_
  51.5 5.1 %collective-permute-done.5.refs_3_ = f32[8,128]{1,0:T(8,128)S(1)} collective-permute-done((f32[8,128]{1,0:T(8,128)S(1)}, f32[8,128]{1,0:T(8,128)S(1)}, u32[]{:S(2)}, u32[]{:S(2)}) %collective-permute-start.5) | collective-permute-done | bytes 4128 | tf_op jit(solution)/shard_map/ppermute | solution.py:319
  56.5 0.0 collective-permute-done.3.refs_1_
  56.6 0.0 collective-permute-done.4.refs_2_
  56.6 0.0 collective-permute-done.2.refs_0_
  56.6 1.9 %layer.3 = bf16[1,2,8,4,2048]{4,3,2,1,0:T(4,128)(2,1)} custom-call(bf16[64,2048]{1,0:T(8,128)(2,1)S(1)} %collective-permute-done.2.refs_0_, bf16[32,2048]{1,0:T(8,128)(2,1)S(1)} %collective-permute-done.3.refs_1_, bf16[32,2048]{1,0:T(8,128)(2,1)S(1)} %collective-permute-done.4.refs_2_, f32[8,128]{1,0:T(8,128)S(1)} %collective-permute-done.5.refs_3_, ...), custom_call_target="tpu_custom_call" | custom-call | flops 201326592 | bytes 4194304 | tf_op jit(solution)/shard_map/layer/pallas_call | solution.py:337
Async XLA Ops:
  1.5 34.1 %collective-permute-start = (bf16[32,2048]{1,0:T(8,128)(2,1)S(1)}, bf16[32,2048]{1,0:T(8,128)(2,1)S(1)}, u32[]{:S(2)}, u32[]{:S(2)}) collective-permute-start(bf16[32,2048]{1,0:T(8,128)(2,1)S(1)} %get-tuple-element.17), channel_id=1, source_target_pairs={{16,2},{18,4},{20,6},{22,8},{24,10},{26,12},{28,14},{17,3},{19,5},... | collective-permute-start | bytes 393224 | tf_op jit(solution)/shard_map/ppermute | solution.py:307
  3.4 32.2 %collective-permute-start.1 = (bf16[32,2048]{1,0:T(8,128)(2,1)S(1)}, bf16[32,2048]{1,0:T(8,128)(2,1)S(1)}, u32[]{:S(2)}, u32[]{:S(2)}) collective-permute-start(bf16[32,2048]{1,0:T(8,128)(2,1)S(1)} %get-tuple-element.18), channel_id=1, source_target_pairs={{18,0},{20,2},{22,4},{24,6},{26,8},{28,10},{30,12},{19,1},{21,3},{... | collective-permute-start | bytes 393224 | tf_op jit(solution)/shard_map/ppermute | solution.py:307
  35.8 20.8 %collective-permute-start.2 = (bf16[64,2048]{1,0:T(8,128)(2,1)S(1)}, bf16[64,2048]{1,0:T(8,128)(2,1)S(1)}, u32[]{:S(2)}, u32[]{:S(2)}) collective-permute-start(bf16[64,2048]{1,0:T(8,128)(2,1)S(1)} %get-tuple-element.23.refs_9_), channel_id=1, source_target_pairs={{0,16},{2,18},{4,20},{6,22},{8,24},{10,26},{12,28},{14,30},{1,17},... | collective-permute-start | bytes 786440 | tf_op jit(solution)/shard_map/ppermute | solution.py:307
  37.1 19.5 %collective-permute-start.3 = (bf16[32,2048]{1,0:T(8,128)(2,1)S(1)}, bf16[32,2048]{1,0:T(8,128)(2,1)S(1)}, u32[]{:S(2)}, u32[]{:S(2)}) collective-permute-start(bf16[32,2048]{1,0:T(8,128)(2,1)S(1)} %get-tuple-element.24), channel_id=1, source_target_pairs={{0,18},{2,20},{4,22},{6,24},{8,26},{10,28},{12,30},{1,19},{3,21},{... | collective-permute-start | bytes 393224 | tf_op jit(solution)/shard_map/ppermute | solution.py:307
  37.7 18.8 %collective-permute-start.4 = (bf16[32,2048]{1,0:T(8,128)(2,1)S(1)}, bf16[32,2048]{1,0:T(8,128)(2,1)S(1)}, u32[]{:S(2)}, u32[]{:S(2)}) collective-permute-start(bf16[32,2048]{1,0:T(8,128)(2,1)S(1)} %get-tuple-element.25), channel_id=1, source_target_pairs={{2,16},{4,18},{6,20},{8,22},{10,24},{12,26},{14,28},{3,17},{5,19},... | collective-permute-start | bytes 393224 | tf_op jit(solution)/shard_map/ppermute | solution.py:307
  39.0 11.1 %collective-permute-start.7 = (f32[8,128]{1,0:T(8,128)S(1)}, f32[8,128]{1,0:T(8,128)S(1)}, u32[]{:S(2)}, u32[]{:S(2)}) collective-permute-start(f32[8,128]{1,0:T(8,128)S(1)} %get-tuple-element.26), channel_id=1, source_target_pairs={{2,17},{3,16},{4,19},{5,18},{6,21},{7,20},{8,23},{9,22},{10,25},{1... | collective-permute-start | bytes 12296 | tf_op jit(solution)/shard_map/ppermute | solution.py:319
  40.3 11.1 %collective-permute-start.6 = (f32[8,128]{1,0:T(8,128)S(1)}, f32[8,128]{1,0:T(8,128)S(1)}, u32[]{:S(2)}, u32[]{:S(2)}) collective-permute-start(f32[8,128]{1,0:T(8,128)S(1)} %get-tuple-element.26), channel_id=1, source_target_pairs={{0,19},{1,18},{2,21},{3,20},{4,23},{5,22},{6,25},{7,24},{8,27},{9,... | collective-permute-start | bytes 12296 | tf_op jit(solution)/shard_map/ppermute | solution.py:319
  50.2 6.4 %collective-permute-start.5 = (f32[8,128]{1,0:T(8,128)S(1)}, f32[8,128]{1,0:T(8,128)S(1)}, u32[]{:S(2)}, u32[]{:S(2)}) collective-permute-start(f32[8,128]{1,0:T(8,128)S(1)} %get-tuple-element.26), channel_id=1, source_target_pairs={{0,17},{1,16},{2,19},{3,18},{4,21},{5,20},{6,23},{7,22},{8,25},{9,... | collective-permute-start | bytes 12296 | tf_op jit(solution)/shard_map/ppermute | solution.py:319

commit v3 on v2

--- a/solution.py
+++ b/solution.py
@@ -24,7 +24,7 @@
 
 
 def first_kernel(
-    signal_hbm, weights_hbm, first_hbm, pad_hbm, own_ref, head_ref, tail_ref, squares_ref,
+    signal_hbm, weights_hbm, first_hbm, pad_hbm, own_ref, chip_ref, far_ref, squares_ref,
     weights_ref, time_ref, station_ref, signal_ref, first_ref, pad_ref, arrived,
     *, total_steps,
 ):
@@ -46,23 +46,30 @@
                 [signal_ref[m, t].astype(jnp.float32), signal_ref[m, t + 1].astype(jnp.float32)],
                 axis=0,
             ).astype(jnp.bfloat16)
+    odd = lax.axis_index("seq") % 2
     for m in range(micro):
-        base = m * rows_micro
-        head_ref[m * edge : (m + 1) * edge, :] = own_ref[base : base + edge, :]
-        tail_ref[m * edge : (m + 1) * edge, :] = own_ref[base + rows_micro - edge : base + rows_micro, :]
-    rows = own_ref[...]
-    count = rows.shape[0]
-    gram = lax.dot_general(
-        rows, rows, (((1,), (1,)), ((), ())), preferred_element_type=jnp.float32
-    )
+        chip = m * rows_micro + (1 - odd) * (rows_micro - edge)
+        far = m * rows_micro + odd * (rows_micro - edge)
+        chip_ref[m * edge : (m + 1) * edge, :] = own_ref[pl.ds(pl.multiple_of(chip, edge), edge), :]
+        far_ref[m * edge : (m + 1) * edge, :] = own_ref[pl.ds(pl.multiple_of(far, edge), edge), :]
     squares_ref[...] = jnp.zeros(squares_ref.shape, jnp.float32)
-    squares_ref[pl.ds(lax.axis_index("seq"), 1), 0:count] = jnp.sum(
-        jnp.where(same(count), gram, 0.0), axis=0, keepdims=True
-    )
+    squares_ref[0:1, 0 : micro * rows_micro] = squares_row(own_ref[...])
     copies[1].wait()
     copies[2].wait()
     fill_masks(first_ref, pad_ref, time_ref, station_ref, steps, stations, total_steps)
     copies[3].wait()
+
+
+def squares_row(rows):
+    gram = lax.dot_general(
+        rows, rows, (((1,), (1,)), ((), ())), preferred_element_type=jnp.float32
+    )
+    return jnp.sum(jnp.where(same(rows.shape[0]), gram, 0.0), axis=0, keepdims=True)
+
+
+def edge_kernel(edge_ref, squares_ref, out_ref):
+    out_ref[...] = squares_ref[...]
+    out_ref[1:2, 0 : edge_ref.shape[0]] = squares_row(edge_ref[...])
 
 
 def same(count):
@@ -78,7 +85,18 @@
     key = lax.broadcasted_iota(jnp.int32, (keys, columns), 0)
     query = lax.broadcasted_iota(jnp.int32, (keys, columns), 1) % (steps * stations)
     key_station, query_station = key % stations, query % stations
-    key_time, query_time = key // stations - WIN, query // stations
+    query_time = query // stations
+    odd = lax.axis_index("seq") % 2
+    after_first = steps * (1 - odd) - WIN * odd
+    after_second = steps * odd - WIN * (1 - odd)
+    step_of = key // stations
+    key_time = jnp.where(
+        step_of < steps,
+        step_of,
+        jnp.where(
+            step_of < steps + WIN, step_of - steps + after_first, step_of - steps - WIN + after_second
+        ),
+    )
     same_station = key_station == query_station
     same_time = key_time == query_time
     near = jnp.abs(key_time - query_time) <= WIN
@@ -91,9 +109,7 @@
             pad = jnp.where(key_station == s, pad_ref[m, s], pad)
         recorded = (step >= first) & (step < total_steps - pad)
         time_ref[m] = jnp.where(same_station & near & (recorded | same_time), 0.0, -BIG)
-        station_ref[m] = jnp.where(same_time & (recorded | same_station), 0.0, -BIG)[
-            WIN * stations : (WIN + steps) * stations
-        ]
+        station_ref[m] = jnp.where(same_time & (recorded | same_station), 0.0, -BIG)[: steps * stations]
 
 
 def softmax_columns(scores):
@@ -102,13 +118,13 @@
 
 
 def layer_kernel(
-    own_ref, left_ref, right_ref, own_squares_ref, left_squares_ref, right_squares_ref,
+    own_ref, chip_ref, far_ref, own_squares_ref, chip_squares_ref, far_squares_ref,
     time_ref, station_ref, weights_ref, kept_ref, out_ref, *refs, tick, micro, steps, stations, last,
 ):
     if last:
         normed_ref, projected_ref = refs
     else:
-        head_ref, tail_ref, squares_ref, normed_ref, projected_ref = refs
+        next_chip_ref, next_far_ref, squares_ref, normed_ref, projected_ref = refs
     rows_micro = steps * stations
     edge = WIN * stations
     reach = rows_micro + 2 * edge
@@ -116,6 +132,7 @@
     all_rows = micro * reach
     heads_dev = weights_ref.shape[1]
     active = lax.axis_index("section") == tick
+    odd = lax.axis_index("seq") % 2
     bf16, f32 = jnp.bfloat16, jnp.float32
 
     def write(m, lanes, values):
@@ -125,30 +142,29 @@
         else:
             values = values.astype(bf16)
             out_ref[m * rows_micro : (m + 1) * rows_micro, lanes] = values
-            head_ref[m * edge : (m + 1) * edge, lanes] = values[:edge]
-            tail_ref[m * edge : (m + 1) * edge, lanes] = values[rows_micro - edge :]
+            head, tail = values[:edge], values[rows_micro - edge :]
+            next_chip_ref[m * edge : (m + 1) * edge, lanes] = jnp.where(odd == 1, head, tail)
+            next_far_ref[m * edge : (m + 1) * edge, lanes] = jnp.where(odd == 1, tail, head)
+
+    row = lax.broadcasted_iota(jnp.int32, (all_rows, 128), 0)
+    lane = lax.broadcasted_iota(jnp.int32, (all_rows, 128), 1)
+    place, of_micro = row % reach, row // reach
 
     def column_squares():
-        seq = lax.axis_index("seq")
+        base = of_micro * rows_micro
+        chip_lane = base + place - rows_micro + odd * (rows_micro - edge)
+        far_lane = base + place - rows_micro - edge + (1 - odd) * (rows_micro - edge)
+        chip_row = chip_squares_ref[0:1, :]
         if tick == 0:
-            before, after = jnp.maximum(seq - 1, 0), jnp.minimum(seq + 1, lax.axis_size("seq") - 1)
-            sources = (
-                left_squares_ref[pl.ds(before, 1), :],
-                own_squares_ref[pl.ds(seq, 1), :],
-                right_squares_ref[pl.ds(after, 1), :],
-            )
-        else:
-            sources = (left_squares_ref[0:1, :], own_squares_ref[0:1, :], right_squares_ref[0:1, :])
-        row = lax.broadcasted_iota(jnp.int32, (all_rows, 128), 0)
-        lane = lax.broadcasted_iota(jnp.int32, (all_rows, 128), 1)
-        place, base = row % reach, (row // reach) * rows_micro
+            chip_row = chip_squares_ref[1:2, :]
+            chip_lane = of_micro * edge + place - rows_micro
         picked = jnp.where(
-            place < edge,
-            jnp.where(lane == base + place + rows_micro - edge, sources[0], 0.0),
+            place < rows_micro,
+            jnp.where(lane == base + place, own_squares_ref[0:1, :], 0.0),
             jnp.where(
-                place < edge + rows_micro,
-                jnp.where(lane == base + place - edge, sources[1], 0.0),
-                jnp.where(lane == base + place - edge - rows_micro, sources[2], 0.0),
+                place < rows_micro + edge,
+                jnp.where(lane == chip_lane, chip_row, 0.0),
+                jnp.where(lane == far_lane, far_squares_ref[0:1, :], 0.0),
             ),
         )
         return jnp.sum(picked, axis=1, keepdims=True)
@@ -158,18 +174,19 @@
         raw = []
         for m in range(micro):
             raw += [
-                left_ref[m * edge : (m + 1) * edge, :],
                 own_ref[m * rows_micro : (m + 1) * rows_micro, :],
-                right_ref[m * edge : (m + 1) * edge, :],
+                chip_ref[m * edge : (m + 1) * edge, :],
+                far_ref[m * edge : (m + 1) * edge, :],
             ]
         raw = jnp.concatenate(raw, axis=0)
         total = column_squares()
-        if tick > 0:
-            mine = jnp.zeros((all_rows, HEAD), f32)
-            for head in range(heads_dev):
-                part = raw[:, head * HEAD : (head + 1) * HEAD].astype(f32)
-                mine = mine + part * part
-            total = total + jnp.sum(mine, axis=1, keepdims=True)
+        mine = jnp.zeros((all_rows, HEAD), f32)
+        for head in range(heads_dev):
+            part = raw[:, head * HEAD : (head + 1) * HEAD].astype(f32)
+            mine = mine + part * part
+        if tick == 0:
+            mine = jnp.where(place < rows_micro + edge, 0.0, mine)
+        total = total + jnp.sum(mine, axis=1, keepdims=True)
         factor = lax.rsqrt(total / (HEADS * HEAD) + EPS)
         for head in range(heads_dev):
             lanes = slice(head * HEAD, (head + 1) * HEAD)
@@ -191,7 +208,7 @@
                 [
                     jnp.concatenate(
                         [
-                            projected_ref[first + edge : first + edge + rows_micro, at[j] : at[j] + HEAD]
+                            projected_ref[first : first + rows_micro, at[j] : at[j] + HEAD]
                             if i == j
                             else blank
                             for i in range(GROUP)
@@ -214,7 +231,7 @@
         mixes = []
         for (g, m), score in zip(pairs, scores):
             time_weights = softmax_columns(score + time_ref[m])
-            station_weights = softmax_columns(score[edge : edge + rows_micro] + station_ref[m])
+            station_weights = softmax_columns(score[:rows_micro] + station_ref[m])
             mixes.append(jnp.concatenate([time_weights, station_weights], axis=0).T)
         sums = [jnp.zeros((rows_micro, HEAD), f32) for _ in range(micro)]
         for (g, m), mix in zip(pairs, mixes):
@@ -227,7 +244,7 @@
                     jnp.concatenate(
                         [
                             projected_ref[first : first + reach, at : at + HEAD],
-                            projected_ref[first + edge : first + edge + rows_micro, at : at + HEAD],
+                            projected_ref[first : first + rows_micro, at : at + HEAD],
                         ],
                         axis=0,
                     ),
@@ -274,7 +291,7 @@
     own_bytes = own_rows * features * 2
     columns = GROUP * rows_micro
 
-    own, head_rows, tail_rows, squares, weights, time_bias, station_bias = pl.pallas_call(
+    own, chip_rows, far_rows, squares, weights, time_bias, station_bias = pl.pallas_call(
         lambda *refs: first_kernel(*refs, total_steps=steps * seq_count),
         in_specs=[HBM] * 4,
         out_specs=[VMEM] * 7,
@@ -282,7 +299,7 @@
             own_shape,
             edge_shape,
             edge_shape,
-            jax.ShapeDtypeStruct((seq_count, 128), f32),
+            squares_shape,
             jax.ShapeDtypeStruct(head_proj.shape, bf16),
             jax.ShapeDtypeStruct((micro, reach, columns), f32),
             jax.ShapeDtypeStruct((micro, rows_micro, columns), f32),
@@ -298,30 +315,34 @@
         name="first",
     )(*[pltpu.with_memory_space_constraint(x, pltpu.HBM) for x in (signal, head_proj, record_start, record_pad)])
 
-    def to_next(block, source, target, step):
-        route = [
-            (source * seq_count + i, target * seq_count + i + step)
-            for i in range(seq_count)
-            if 0 <= i + step < seq_count
-        ]
-        return lax.ppermute(block, ("section", "seq"), route)
-
-    def to_next_other(block, source, target, step):
-        route = [
-            (
-                (source * seq_count + i) * rep_count + r,
-                (target * seq_count + i + step) * rep_count + (r + 1) % rep_count,
-            )
-            for i in range(seq_count)
-            if 0 <= i + step < seq_count
-            for r in range(rep_count)
-        ]
+    def moved(block, source, target, hop, other=False):
+        route = []
+        for i in range(seq_count):
+            to = i if hop == 0 else i + 1 - 2 * (i % 2) if hop == 1 else i - 1 + 2 * (i % 2)
+            if 0 <= to < seq_count:
+                for r in range(rep_count):
+                    route.append(
+                        (
+                            (source * seq_count + i) * rep_count + r,
+                            (target * seq_count + to) * rep_count
+                            + ((r + 1) % rep_count if other else r),
+                        )
+                    )
         return lax.ppermute(block, ("section", "seq", "rep"), route)
 
     helper = 1 if section_count > 1 else 0
-    left = to_next(tail_rows, helper, 0, 1)
-    right = to_next(head_rows, helper, 0, -1)
-    own_squares = left_squares = right_squares = lax.psum(squares, ("seq", "rep"))
+    chip_edge = moved(chip_rows, 0, 0, 1)
+    far_edge = moved(far_rows, helper, 0, 2)
+    far_squares = moved(squares, helper, 0, 2, other=True)
+    both = pl.pallas_call(
+        edge_kernel,
+        in_specs=[VMEM] * 2,
+        out_specs=VMEM,
+        out_shape=squares_shape,
+        compiler_params=PARAMS,
+        name="edge",
+    )(chip_edge, squares)
+    own_squares = chip_squares = lax.psum(both, "rep")
     kept = own
     for tick in range(section_count):
         last = tick + 1 == section_count
@@ -347,17 +368,18 @@
             cost_estimate=cost(4 * own_rows * features * 3 * HEAD, 16 * own_bytes),
             name="layer",
         )(
-            own, left, right, own_squares, left_squares, right_squares,
+            own, chip_edge, far_edge, own_squares, chip_squares, far_squares,
             time_bias, station_bias, weights, kept,
         )
         if not last:
-            head_rows, tail_rows, squares = sent
-            own = to_next(kept, tick, tick + 1, 0)
-            left = to_next(tail_rows, tick, tick + 1, 1)
-            right = to_next(head_rows, tick, tick + 1, -1)
-            own_squares = to_next_other(squares, tick, tick + 1, 0)
-            left_squares = to_next_other(squares, tick, tick + 1, 1)
-            right_squares = to_next_other(squares, tick, tick + 1, -1)
+            chip_rows, far_rows, squares = sent
+            own_squares = moved(squares, tick, tick + 1, 0, other=True)
+            own = moved(kept, tick, tick + 1, 0)
+            chip_edge = moved(chip_rows, tick, tick + 1, 1)
+            far_edge = moved(far_rows, tick, tick + 1, 2)
+            chip_squares = moved(squares, tick, tick + 1, 1, other=True)
+            squares, _ = lax.optimization_barrier((squares, own_squares))
+            far_squares = moved(squares, tick, tick + 1, 2, other=True)
     return kept
 
 

time: 58.8 us -> 38.3 us (0.65)
  the two profiles are of different devices: /device:TPU:6 before, /device:TPU:18 now
where the time goes in v3:
time: 38.3 us; the launch traced here: 38 us
  waiting for transfers between devices  14.9 us (39%)
  starting transfers between devices  14.3 us (37%)
  blocking collectives  4.95 us (13%)
  Pallas kernels  3.72 us (10%)
    ppermute x9, waiting for transfers between devices, moved(): return lax.ppermute(block, ('section', 'seq', 'rep'), route)  14.9 us
    ppermute x9, starting transfers between devices, moved(): return lax.ppermute(block, ('section', 'seq', 'rep'), route)  14.3 us
    psum x1, blocking collectives, body(): own_squares = chip_squares = lax.psum(both, 'rep')  4.95 us
    pallas_call x2, Pallas kernels, body(): pl.pallas_call(kernel, in_specs=[VMEM] * 10, out_specs=[VMEM] * len(out_s...  2.01 us
    pallas_call x1, Pallas kernels, body(): pl.pallas_call(lambda *refs: first_kernel(*refs, total_steps=steps * seq_...  1.54 us
  transfers between devices with their start and end apart: 9, of which 2 were waited for; matrix products, arithmetic and copies ran while one was open for 0% of the time, Pallas kernels for 0%

profile of v3, /device:TPU:18, one launch (start us, length us, event | category | flops | bytes accessed | tf_op | source)
XLA Modules:
  0.0 38.0 jit_solution(15282909187004322348)
XLA Ops:
  0.0 1.5 %first.1 = (bf16[64,2048]{1,0:T(8,128)(2,1)S(1)}, bf16[32,2048]{1,0:T(8,128)(2,1)S(1)}, bf16[32,2048]{1,0:T(8,128)(2,1)S(1)}, f32[8,128]{1,0:T(8,128)S(1)}, bf16...) custom-call(bf16[2,8,4,2048]{3,2,1,0:T(4,128)(2,1)} %refs_0_.1, ...), custom_call_target="tpu_custom_call" | custom-call | flops 16777216 | bytes 786432 | tf_op jit(solution)/shard_map/first/pallas_call | solution.py:294
  1.5 0.7 %collective-permute-start = (bf16[32,2048]{1,0:T(8,128)(2,1)S(1)}, bf16[32,2048]{1,0:T(8,128)(2,1)S(1)}, u32[]{:S(2)}, u32[]{:S(2)}) collective-permute-start(bf16[32,2048]{1,0:T(8,128)(2,1)S(1)} %get-tuple-element.18), channel_id=1, source_target_pairs={{0,2},{1,3},{2,0},{3,1},{4,6},{5,7},{6,4},{7,5},{8,10},{9,11},{10,... | collective-permute-start | bytes 393224 | tf_op jit(solution)/shard_map/ppermute | solution.py:331
  2.2 3.7 %collective-permute-start.1 = (bf16[32,2048]{1,0:T(8,128)(2,1)S(1)}, bf16[32,2048]{1,0:T(8,128)(2,1)S(1)}, u32[]{:S(2)}, u32[]{:S(2)}) collective-permute-start(bf16[32,2048]{1,0:T(8,128)(2,1)S(1)} %get-tuple-element.19), channel_id=1, source_target_pairs={{18,4},{19,5},{20,2},{21,3},{22,8},{23,9},{24,6},{25,7},{26,12},{2... | collective-permute-start | bytes 393224 | tf_op jit(solution)/shard_map/ppermute | solution.py:331
  5.9 2.2 %collective-permute-start.2 = (f32[8,128]{1,0:T(8,128)S(1)}, f32[8,128]{1,0:T(8,128)S(1)}, u32[]{:S(2)}, u32[]{:S(2)}) collective-permute-start(f32[8,128]{1,0:T(8,128)S(1)} %get-tuple-element.20.squares_ref), channel_id=1, source_target_pairs={{18,5},{19,4},{20,3},{21,2},{22,9},{23,8},{24,7},{25,6},{26,13},{2... | collective-permute-start | bytes 12296 | tf_op jit(solution)/shard_map/ppermute | solution.py:331
  8.2 0.0 collective-permute-done.edge_ref.refs_1_
  8.2 0.2 edge.1
  8.4 4.9 %psum.7.refs_3_.refs_4_ = f32[8,128]{1,0:T(8,128)S(1)} all-reduce(f32[8,128]{1,0:T(8,128)S(1)} %edge.1), channel_id=1, replica_groups=mesh['section'=2,'seq'=8,'rep'=2] {'rep'}, use_global_device_ids=true, to_apply=%region_0.0 | all-reduce | flops 1024 | bytes 8192 | tf_op jit(solution)/shard_map/psum | solution.py:345
  13.3 0.0 collective-permute-done.2.refs_5_
  13.3 0.0 collective-permute-done.1.refs_2_
  13.3 0.1 layer.2
  13.4 1.3 %collective-permute-start.3 = (bf16[64,2048]{1,0:T(8,128)(2,1)S(1)}, bf16[64,2048]{1,0:T(8,128)(2,1)S(1)}, u32[]{:S(2)}, u32[]{:S(2)}) collective-permute-start(bf16[64,2048]{1,0:T(8,128)(2,1)S(1)} %get-tuple-element.24.refs_9_), channel_id=1, source_target_pairs={{0,16},{1,17},{2,18},{3,19},{4,20},{5,21},{6,22},{7,23},{8,24},{9,... | collective-permute-start | bytes 786440 | tf_op jit(solution)/shard_map/ppermute | solution.py:331
  14.7 1.3 %collective-permute-start.4 = (bf16[32,2048]{1,0:T(8,128)(2,1)S(1)}, bf16[32,2048]{1,0:T(8,128)(2,1)S(1)}, u32[]{:S(2)}, u32[]{:S(2)}) collective-permute-start(bf16[32,2048]{1,0:T(8,128)(2,1)S(1)} %get-tuple-element.25), channel_id=1, source_target_pairs={{0,18},{1,19},{2,16},{3,17},{4,22},{5,23},{6,20},{7,21},{8,26},{9,... | collective-permute-start | bytes 393224 | tf_op jit(solution)/shard_map/ppermute | solution.py:331
  16.0 1.3 %collective-permute-start.5 = (bf16[32,2048]{1,0:T(8,128)(2,1)S(1)}, bf16[32,2048]{1,0:T(8,128)(2,1)S(1)}, u32[]{:S(2)}, u32[]{:S(2)}) collective-permute-start(bf16[32,2048]{1,0:T(8,128)(2,1)S(1)} %get-tuple-element.26), channel_id=1, source_target_pairs={{2,20},{3,21},{4,18},{5,19},{6,24},{7,25},{8,22},{9,23},{10,28},{1... | collective-permute-start | bytes 393224 | tf_op jit(solution)/shard_map/ppermute | solution.py:331
  17.3 1.3 %collective-permute-start.6 = (f32[8,128]{1,0:T(8,128)S(1)}, f32[8,128]{1,0:T(8,128)S(1)}, u32[]{:S(2)}, u32[]{:S(2)}) collective-permute-start(f32[8,128]{1,0:T(8,128)S(1)} %get-tuple-element.28), channel_id=1, source_target_pairs={{0,17},{1,16},{2,19},{3,18},{4,21},{5,20},{6,23},{7,22},{8,25},{9,... | collective-permute-start | bytes 12296 | tf_op jit(solution)/shard_map/ppermute | solution.py:331
  18.6 1.3 %collective-permute-start.7 = (f32[8,128]{1,0:T(8,128)S(1)}, f32[8,128]{1,0:T(8,128)S(1)}, u32[]{:S(2)}, u32[]{:S(2)}) collective-permute-start(f32[8,128]{1,0:T(8,128)S(1)} %get-tuple-element.28), channel_id=1, source_target_pairs={{0,19},{1,18},{2,17},{3,16},{4,23},{5,22},{6,21},{7,20},{8,27},{9,... | collective-permute-start | bytes 12296 | tf_op jit(solution)/shard_map/ppermute | solution.py:331
  19.9 9.5 %collective-permute-done.6.refs_3_ = f32[8,128]{1,0:T(8,128)S(1)} collective-permute-done((f32[8,128]{1,0:T(8,128)S(1)}, f32[8,128]{1,0:T(8,128)S(1)}, u32[]{:S(2)}, u32[]{:S(2)}) %collective-permute-start.6) | collective-permute-done | bytes 4128 | tf_op jit(solution)/shard_map/ppermute | solution.py:331
  29.4 1.3 %collective-permute-start.8 = (f32[8,128]{1,0:T(8,128)S(1)}, f32[8,128]{1,0:T(8,128)S(1)}, u32[]{:S(2)}, u32[]{:S(2)}) collective-permute-start(f32[8,128]{1,0:T(8,128)S(1)} %get-tuple-element.28), channel_id=1, source_target_pairs={{2,21},{3,20},{4,19},{5,18},{6,25},{7,24},{8,23},{9,22},{10,29},{1... | collective-permute-start | bytes 12296 | tf_op jit(solution)/shard_map/ppermute | solution.py:331
  30.7 0.0 collective-permute-done.7.refs_4_
  30.7 5.4 %collective-permute-done.8.refs_5_ = f32[8,128]{1,0:T(8,128)S(1)} collective-permute-done((f32[8,128]{1,0:T(8,128)S(1)}, f32[8,128]{1,0:T(8,128)S(1)}, u32[]{:S(2)}, u32[]{:S(2)}) %collective-permute-start.8) | collective-permute-done | bytes 4128 | tf_op jit(solution)/shard_map/ppermute | solution.py:331
  36.1 0.0 collective-permute-done.4.refs_1_
  36.1 0.0 collective-permute-done.5.refs_2_
  36.1 0.0 collective-permute-done.3.refs_0_
  36.1 1.9 %layer.3 = bf16[1,2,8,4,2048]{4,3,2,1,0:T(4,128)(2,1)} custom-call(bf16[64,2048]{1,0:T(8,128)(2,1)S(1)} %collective-permute-done.3.refs_0_, bf16[32,2048]{1,0:T(8,128)(2,1)S(1)} %collective-permute-done.4.refs_1_, bf16[32,2048]{1,0:T(8,128)(2,1)S(1)} %collective-permute-done.5.refs_2_, f32[8,128]{1,0:T(8,128)S(1)} %collective-permute-done.6.refs_3_, ...), custom_call_target="tpu_custom_call" | custom-call | flops 201326592 | bytes 4194304 | tf_op jit(solution)/shard_map/layer/pallas_call | solution.py:358
Async XLA Ops:
  1.5 6.6 %collective-permute-start = (bf16[32,2048]{1,0:T(8,128)(2,1)S(1)}, bf16[32,2048]{1,0:T(8,128)(2,1)S(1)}, u32[]{:S(2)}, u32[]{:S(2)}) collective-permute-start(bf16[32,2048]{1,0:T(8,128)(2,1)S(1)} %get-tuple-element.18), channel_id=1, source_target_pairs={{0,2},{1,3},{2,0},{3,1},{4,6},{5,7},{6,4},{7,5},{8,10},{9,11},{10,... | collective-permute-start | bytes 393224 | tf_op jit(solution)/shard_map/ppermute | solution.py:331
  2.2 11.1 %collective-permute-start.1 = (bf16[32,2048]{1,0:T(8,128)(2,1)S(1)}, bf16[32,2048]{1,0:T(8,128)(2,1)S(1)}, u32[]{:S(2)}, u32[]{:S(2)}) collective-permute-start(bf16[32,2048]{1,0:T(8,128)(2,1)S(1)} %get-tuple-element.19), channel_id=1, source_target_pairs={{18,4},{19,5},{20,2},{21,3},{22,8},{23,9},{24,6},{25,7},{26,12},{2... | collective-permute-start | bytes 393224 | tf_op jit(solution)/shard_map/ppermute | solution.py:331
  5.9 7.4 %collective-permute-start.2 = (f32[8,128]{1,0:T(8,128)S(1)}, f32[8,128]{1,0:T(8,128)S(1)}, u32[]{:S(2)}, u32[]{:S(2)}) collective-permute-start(f32[8,128]{1,0:T(8,128)S(1)} %get-tuple-element.20.squares_ref), channel_id=1, source_target_pairs={{18,5},{19,4},{20,3},{21,2},{22,9},{23,8},{24,7},{25,6},{26,13},{2... | collective-permute-start | bytes 12296 | tf_op jit(solution)/shard_map/ppermute | solution.py:331
  13.4 22.7 %collective-permute-start.3 = (bf16[64,2048]{1,0:T(8,128)(2,1)S(1)}, bf16[64,2048]{1,0:T(8,128)(2,1)S(1)}, u32[]{:S(2)}, u32[]{:S(2)}) collective-permute-start(bf16[64,2048]{1,0:T(8,128)(2,1)S(1)} %get-tuple-element.24.refs_9_), channel_id=1, source_target_pairs={{0,16},{1,17},{2,18},{3,19},{4,20},{5,21},{6,22},{7,23},{8,24},{9,... | collective-permute-start | bytes 786440 | tf_op jit(solution)/shard_map/ppermute | solution.py:331
  14.7 21.4 %collective-permute-start.4 = (bf16[32,2048]{1,0:T(8,128)(2,1)S(1)}, bf16[32,2048]{1,0:T(8,128)(2,1)S(1)}, u32[]{:S(2)}, u32[]{:S(2)}) collective-permute-start(bf16[32,2048]{1,0:T(8,128)(2,1)S(1)} %get-tuple-element.25), channel_id=1, source_target_pairs={{0,18},{1,19},{2,16},{3,17},{4,22},{5,23},{6,20},{7,21},{8,26},{9,... | collective-permute-start | bytes 393224 | tf_op jit(solution)/shard_map/ppermute | solution.py:331
  16.0 20.1 %collective-permute-start.5 = (bf16[32,2048]{1,0:T(8,128)(2,1)S(1)}, bf16[32,2048]{1,0:T(8,128)(2,1)S(1)}, u32[]{:S(2)}, u32[]{:S(2)}) collective-permute-start(bf16[32,2048]{1,0:T(8,128)(2,1)S(1)} %get-tuple-element.26), channel_id=1, source_target_pairs={{2,20},{3,21},{4,18},{5,19},{6,24},{7,25},{8,22},{9,23},{10,28},{1... | collective-permute-start | bytes 393224 | tf_op jit(solution)/shard_map/ppermute | solution.py:331
  17.3 12.1 %collective-permute-start.6 = (f32[8,128]{1,0:T(8,128)S(1)}, f32[8,128]{1,0:T(8,128)S(1)}, u32[]{:S(2)}, u32[]{:S(2)}) collective-permute-start(f32[8,128]{1,0:T(8,128)S(1)} %get-tuple-element.28), channel_id=1, source_target_pairs={{0,17},{1,16},{2,19},{3,18},{4,21},{5,20},{6,23},{7,22},{8,25},{9,... | collective-permute-start | bytes 12296 | tf_op jit(solution)/shard_map/ppermute | solution.py:331
  18.6 12.1 %collective-permute-start.7 = (f32[8,128]{1,0:T(8,128)S(1)}, f32[8,128]{1,0:T(8,128)S(1)}, u32[]{:S(2)}, u32[]{:S(2)}) collective-permute-start(f32[8,128]{1,0:T(8,128)S(1)} %get-tuple-element.28), channel_id=1, source_target_pairs={{0,19},{1,18},{2,17},{3,16},{4,23},{5,22},{6,21},{7,20},{8,27},{9,... | collective-permute-start | bytes 12296 | tf_op jit(solution)/shard_map/ppermute | solution.py:331
  29.4 6.7 %collective-permute-start.8 = (f32[8,128]{1,0:T(8,128)S(1)}, f32[8,128]{1,0:T(8,128)S(1)}, u32[]{:S(2)}, u32[]{:S(2)}) collective-permute-start(f32[8,128]{1,0:T(8,128)S(1)} %get-tuple-element.28), channel_id=1, source_target_pairs={{2,21},{3,20},{4,19},{5,18},{6,25},{7,24},{8,23},{9,22},{10,29},{1... | collective-permute-start | bytes 12296 | tf_op jit(solution)/shard_map/ppermute | solution.py:331

commit v4 on v3

v4 whole, which is shorter than its diff:
```python
import math

import jax
import jax.numpy as jnp
from jax import lax
from jax.experimental import pallas as pl
from jax.experimental.pallas import tpu as pltpu
from jax.sharding import PartitionSpec as P

HEADS = 32
HEAD = 128
WIN = 4
GROUP = 4
EPS = 1e-06
BIG = 1e30
CHIP, FAR, NEXT_CHIP, NEXT_FAR = range(4)

HBM = pl.BlockSpec(memory_space=pltpu.HBM)
VMEM = pl.BlockSpec(memory_space=pltpu.VMEM)
PARAMS = pltpu.CompilerParams(vmem_limit_bytes=16 * 1024 * 1024)


def cost(flops, moved):
    return pl.CostEstimate(flops=flops, bytes_accessed=moved, transcendentals=0)


def odd_device():
    return lax.axis_index("seq") % 2


def first_step(half):
    odd = odd_device()
    return {
        CHIP: WIN * (1 - odd),
        FAR: WIN * odd,
        NEXT_CHIP: 2 * WIN * (1 - odd) - WIN * odd,
        NEXT_FAR: 2 * WIN * odd - WIN * (1 - odd),
    }[half]


def same(count):
    return lax.broadcasted_iota(jnp.int32, (count, count), 0) == lax.broadcasted_iota(
        jnp.int32, (count, count), 1
    )


def squares_row(rows):
    gram = lax.dot_general(
        rows, rows, (((1,), (1,)), ((), ())), preferred_element_type=jnp.float32
    )
    return jnp.sum(jnp.where(same(rows.shape[0]), gram, 0.0), axis=0, keepdims=True)


def fill_masks(first_ref, pad_ref, time_ref, station_ref, stations, total_steps):
    own = 2 * WIN * stations
    keys, columns = 2 * own, GROUP * own
    key = lax.broadcasted_iota(jnp.int32, (keys, columns), 0)
    query = lax.broadcasted_iota(jnp.int32, (keys, columns), 1) % own

    def time_of(row):
        half, step = row // (WIN * stations), (row // stations) % WIN
        start = jnp.where(half == CHIP, first_step(CHIP), first_step(FAR))
        start = jnp.where(half == NEXT_CHIP, first_step(NEXT_CHIP), start)
        return step + jnp.where(half == NEXT_FAR, first_step(NEXT_FAR), start)

    key_station, query_station = key % stations, query % stations
    key_time, query_time = time_of(key), time_of(query)
    same_station = key_station == query_station
    same_time = key_time == query_time
    near = jnp.abs(key_time - query_time) <= WIN
    step = lax.axis_index("seq") * (2 * WIN) + key_time
    for m in range(time_ref.shape[0]):
        first = jnp.zeros((keys, columns), jnp.int32)
        pad = jnp.zeros((keys, columns), jnp.int32)
        for s in range(stations):
            first = jnp.where(key_station == s, first_ref[m, s], first)
            pad = jnp.where(key_station == s, pad_ref[m, s], pad)
        recorded = (step >= first) & (step < total_steps - pad)
        time_ref[m] = jnp.where(same_station & near & (recorded | same_time), 0.0, -BIG)
        station_ref[m] = jnp.where(same_time & (recorded | same_station), 0.0, -BIG)[:own]


def first_kernel(
    signal_hbm, weights_hbm, first_hbm, pad_hbm, chip_ref, far_ref, squares_ref,
    weights_ref, time_ref, station_ref, signal_ref, first_ref, pad_ref, arrived,
    *, total_steps,
):
    copies = [
        pltpu.make_async_copy(signal_hbm, signal_ref, arrived.at[0]),
        pltpu.make_async_copy(first_hbm, first_ref, arrived.at[1]),
        pltpu.make_async_copy(pad_hbm, pad_ref, arrived.at[2]),
        pltpu.make_async_copy(weights_hbm, weights_ref, arrived.at[3]),
    ]
    for copy in copies:
        copy.start()
    micro, _, stations, _ = signal_ref.shape
    edge = WIN * stations
    copies[0].wait()
    for half, half_ref in ((CHIP, chip_ref), (FAR, far_ref)):
        start = first_step(half)
        for m in range(micro):
            for t in range(0, WIN, 2):
                pair = [signal_ref[m, start + t + i].astype(jnp.float32) for i in range(2)]
                at = m * edge + t * stations
                half_ref[at : at + 2 * stations, :] = jnp.concatenate(pair, axis=0).astype(
                    jnp.bfloat16
                )
    squares_ref[...] = jnp.zeros(squares_ref.shape, jnp.float32)
    for half, half_ref in ((CHIP, chip_ref), (FAR, far_ref)):
        squares_ref[half : half + 1, 0 : micro * edge] = squares_row(half_ref[...])
    copies[1].wait()
    copies[2].wait()
    fill_masks(first_ref, pad_ref, time_ref, station_ref, stations, total_steps)
    copies[3].wait()


def edge_kernel(next_chip_ref, next_far_ref, squares_ref, out_ref):
    out_ref[...] = squares_ref[...]
    for half, half_ref in ((NEXT_CHIP, next_chip_ref), (NEXT_FAR, next_far_ref)):
        out_ref[half : half + 1, 0 : half_ref.shape[0]] = squares_row(half_ref[...])


def norm_kernel(chip_ref, squares_ref, _, normed_ref):
    rows = chip_ref[...]
    count = rows.shape[0]
    total = squares_row(rows) + squares_ref[CHIP : CHIP + 1, 0:count]
    factor = lax.rsqrt(total / (HEADS * HEAD) + EPS)
    column = jnp.sum(jnp.where(same(count), factor, 0.0), axis=1, keepdims=True)
    normed_ref[...] = (rows.astype(jnp.float32) * column).astype(jnp.bfloat16)


def softmax_columns(scores):
    grown = jnp.exp(scores - jnp.max(scores, axis=0, keepdims=True))
    return (grown * (1.0 / jnp.sum(grown, axis=0, keepdims=True))).astype(jnp.bfloat16)


def layer_kernel(
    chip_ref, far_ref, next_chip_ref, next_far_ref, squares_ref, far_squares_ref,
    time_ref, station_ref, weights_ref, kept_chip_ref, kept_far_ref, *refs, tick, stations, last,
):
    if last:
        out_ref, normed_ref, projected_ref = refs
    else:
        out_chip_ref, out_far_ref, out_squares_ref, normed_ref, projected_ref = refs
    edge = WIN * stations
    micro = chip_ref.shape[0] // edge
    own, reach = 2 * edge, 4 * edge
    heads_dev = weights_ref.shape[1]
    width = 3 * HEAD
    bf16, f32 = jnp.bfloat16, jnp.float32
    active = lax.axis_index("section") == tick

    def write(m, lanes, values):
        for half in (CHIP, FAR):
            part = values[half * edge : (half + 1) * edge].astype(bf16)
            if last:
                for t in range(WIN):
                    out_ref[0, m, first_step(half) + t, :, lanes] = part[
                        t * stations : (t + 1) * stations
                    ]
            else:
                half_ref = (out_chip_ref, out_far_ref)[half]
                half_ref[m * edge : (m + 1) * edge, lanes] = part

    def norm_rows(half, half_ref, squares_row_ref, complete):
        lane = lax.broadcasted_iota(jnp.int32, (micro * edge, 128), 1)
        row = lax.broadcasted_iota(jnp.int32, (micro * edge, 128), 0)
        total = jnp.where(lane == row, squares_row_ref, 0.0)
        if not complete:
            for head in range(heads_dev):
                part = half_ref[:, head * HEAD : (head + 1) * HEAD].astype(f32)
                total = total + part * part
        factor = lax.rsqrt(jnp.sum(total, axis=1, keepdims=True) / (HEADS * HEAD) + EPS)
        for head in range(heads_dev):
            lanes = slice(head * HEAD, (head + 1) * HEAD)
            put_normed(half, lanes, (half_ref[:, lanes].astype(f32) * factor).astype(bf16))

    def put_normed(half, lanes, rows):
        for m in range(micro):
            at = m * reach + half * edge
            normed_ref[at : at + edge, lanes] = rows[m * edge : (m + 1) * edge]

    @pl.when(active)
    def _():
        if tick == 0:
            for half, half_ref in enumerate((chip_ref, far_ref, next_chip_ref, next_far_ref)):
                norm_rows(half, half_ref, squares_ref[half : half + 1, :], True)
        else:
            norm_rows(CHIP, chip_ref, squares_ref[CHIP : CHIP + 1, :], False)
            norm_rows(FAR, far_ref, squares_ref[FAR : FAR + 1, :], False)
            put_normed(NEXT_CHIP, slice(None), next_chip_ref[...])
            norm_rows(NEXT_FAR, next_far_ref, far_squares_ref[FAR : FAR + 1, :], False)
        for head in range(heads_dev):
            projected_ref[:, head * width : (head + 1) * width] = jnp.dot(
                normed_ref[:, head * HEAD : (head + 1) * HEAD],
                weights_ref[0, head],
                preferred_element_type=f32,
            ).astype(bf16)
        pairs = [(g, m) for g in range(heads_dev // GROUP) for m in range(micro)]
        blank = jnp.zeros((own, HEAD), bf16)
        scores = []
        for g, m in pairs:
            at = [(g * GROUP + j) * width for j in range(GROUP)]
            first = m * reach
            spread = jnp.concatenate(
                [
                    jnp.concatenate(
                        [
                            projected_ref[first : first + own, at[j] : at[j] + HEAD]
                            if i == j
                            else blank
                            for i in range(GROUP)
                        ],
                        axis=1,
                    )
                    for j in range(GROUP)
                ],
                axis=0,
            )
            keys = jnp.concatenate(
                [projected_ref[first : first + reach, a + HEAD : a + 2 * HEAD] for a in at], axis=1
            )
            scores.append(
                lax.dot_general(
                    keys, spread, (((1,), (1,)), ((), ())), preferred_element_type=f32
                )
                * (1.0 / math.sqrt(HEAD))
            )
        mixes = []
        for (g, m), score in zip(pairs, scores):
            time_weights = softmax_columns(score + time_ref[m])
            station_weights = softmax_columns(score[:own] + station_ref[m])
            mixes.append(jnp.concatenate([time_weights, station_weights], axis=0).T)
        sums = [jnp.zeros((own, HEAD), f32) for _ in range(micro)]
        for (g, m), mix in zip(pairs, mixes):
            first = m * reach
            for j in range(GROUP):
                head = g * GROUP + j
                at = head * width + 2 * HEAD
                mixed = jnp.dot(
                    mix[j * own : (j + 1) * own],
                    jnp.concatenate(
                        [
                            projected_ref[first : first + reach, at : at + HEAD],
                            projected_ref[first : first + own, at : at + HEAD],
                        ],
                        axis=0,
                    ),
                    preferred_element_type=f32,
                )
                lanes = slice(head * HEAD, (head + 1) * HEAD)
                hidden = jnp.concatenate(
                    [ref[m * edge : (m + 1) * edge, lanes] for ref in (chip_ref, far_ref)], axis=0
                )
                result = hidden.astype(f32) + mixed
                write(m, lanes, result)
                if not last:
                    rounded = result.astype(bf16).astype(f32)
                    sums[m] = sums[m] + rounded * rounded
        if not last:
            out_squares_ref[...] = jnp.zeros(out_squares_ref.shape, f32)
            for half in (CHIP, FAR):
                parts = [s[half * edge : (half + 1) * edge] for s in sums]
                column = jnp.sum(jnp.concatenate(parts, axis=0), axis=1, keepdims=True)
                out_squares_ref[half : half + 1, 0 : micro * edge] = jnp.sum(
                    jnp.where(same(micro * edge), column, 0.0), axis=0, keepdims=True
                )

    @pl.when(jnp.logical_not(active))
    def _():
        for m in range(micro):
            for head in range(heads_dev):
                lanes = slice(head * HEAD, (head + 1) * HEAD)
                kept = [
                    ref[m * edge : (m + 1) * edge, lanes] for ref in (kept_chip_ref, kept_far_ref)
                ]
                write(m, lanes, jnp.concatenate(kept, axis=0).astype(f32))
        if not last:
            out_squares_ref[...] = jnp.zeros(out_squares_ref.shape, f32)


def body(signal, head_proj, record_start, record_pad):
    section_count = lax.axis_size("section")
    seq_count = lax.axis_size("seq")
    rep_count = lax.axis_size("rep")
    micro, steps, stations, features = signal.shape
    heads_dev = head_proj.shape[1]
    edge = WIN * stations
    own, reach = 2 * edge, 4 * edge
    bf16, f32 = jnp.bfloat16, jnp.float32
    half_shape = jax.ShapeDtypeStruct((micro * edge, features), bf16)
    squares_shape = jax.ShapeDtypeStruct((8, 128), f32)
    signal_bytes = signal.size * 2

    chip, far, squares, weights, time_bias, station_bias = pl.pallas_call(
        lambda *refs: first_kernel(*refs, total_steps=steps * seq_count),
        in_specs=[HBM] * 4,
        out_specs=[VMEM] * 6,
        out_shape=[
            half_shape,
            half_shape,
            squares_shape,
            jax.ShapeDtypeStruct(head_proj.shape, bf16),
            jax.ShapeDtypeStruct((micro, reach, GROUP * own), f32),
            jax.ShapeDtypeStruct((micro, own, GROUP * own), f32),
        ],
        scratch_shapes=[
            pltpu.VMEM(signal.shape, bf16),
            pltpu.SMEM(record_start.shape, jnp.int32),
            pltpu.SMEM(record_pad.shape, jnp.int32),
            pltpu.SemaphoreType.DMA((4,)),
        ],
        compiler_params=PARAMS,
        cost_estimate=cost(2 * micro * own * signal.size, 3 * signal_bytes),
        name="first",
    )(
        *[
            pltpu.with_memory_space_constraint(x, pltpu.HBM)
            for x in (signal, head_proj, record_start, record_pad)
        ]
    )

    def moved(block, source, target, hop, other=False):
        route = []
        for i in range(seq_count):
            to = i if hop == 0 else i + 1 - 2 * (i % 2) if hop == 1 else i - 1 + 2 * (i % 2)
            if 0 <= to < seq_count:
                for r in range(rep_count):
                    route.append(
                        (
                            (source * seq_count + i) * rep_count + r,
                            (target * seq_count + to) * rep_count
                            + ((r + 1) % rep_count if other else r),
                        )
                    )
        return lax.ppermute(block, ("section", "seq", "rep"), route)

    helper = 1 if section_count > 1 else 0
    next_far = moved(far, helper, 0, 2)
    next_chip = moved(chip, 0, 0, 1)
    squares = pl.pallas_call(
        edge_kernel,
        in_specs=[VMEM] * 3,
        out_specs=VMEM,
        out_shape=squares_shape,
        compiler_params=PARAMS,
        name="edge",
    )(next_chip, next_far, squares)
    squares = far_squares = lax.psum(squares, "rep")
    kept = (chip, far)
    for tick in range(section_count):
        last = tick + 1 == section_count

        def kernel(*refs, tick=tick, last=last):
            layer_kernel(*refs, tick=tick, stations=stations, last=last)

        out_shape = (
            [jax.ShapeDtypeStruct((1,) + signal.shape, bf16)]
            if last
            else [half_shape, half_shape, squares_shape]
        )
        outputs = pl.pallas_call(
            kernel,
            in_specs=[VMEM] * 11,
            out_specs=[VMEM] * len(out_shape),
            out_shape=out_shape,
            scratch_shapes=[
                pltpu.VMEM((micro * reach, features), bf16),
                pltpu.VMEM((micro * reach, heads_dev * 3 * HEAD), bf16),
            ],
            compiler_params=PARAMS,
            cost_estimate=cost(8 * signal.size * 3 * HEAD, 16 * signal_bytes),
            name="layer",
        )(
            chip, far, next_chip, next_far, squares, far_squares,
            time_bias, station_bias, weights, *kept,
        )
        if last:
            return outputs[0]
        kept = outputs[:2]
        mine = outputs[2]
        chip = moved(kept[0], tick, tick + 1, 0)
        squares = moved(mine, tick, tick + 1, 0, other=True)
        far = moved(kept[1], tick, tick + 1, 0)
        next_far = moved(kept[1], tick, tick + 1, 2)
        far_squares = moved(mine, tick, tick + 1, 2, other=True)
        normed_chip = pl.pallas_call(
            norm_kernel,
            in_specs=[VMEM] * 3,
            out_specs=VMEM,
            out_shape=half_shape,
            compiler_params=PARAMS,
            name="norm",
        )(chip, squares, far_squares)
        next_chip = moved(normed_chip, tick + 1, tick + 1, 1)


def solution(mesh):
    return jax.shard_map(
        body,
        mesh=mesh,
        in_specs=(P(None, "seq", None, "rep"), P("section", "rep", None, None), P(), P()),
        out_specs=P("section", None, "seq", None, "rep"),
        check_vma=False,
    )
```

time: 38.3 us -> 32.7 us (0.85)
  the two profiles are of different devices: /device:TPU:18 before, /device:TPU:11 now
where the time goes in v4:
time: 32.7 us; the launch traced here: 32.3 us
  starting transfers between devices  15.4 us (47%)
  waiting for transfers between devices  8.85 us (27%)
  blocking collectives  3.97 us (12%)
  Pallas kernels  3.96 us (12%)
    ppermute x8, starting transfers between devices, moved(): return lax.ppermute(block, ('section', 'seq', 'rep'), route)  15.4 us
    ppermute x8, waiting for transfers between devices, moved(): return lax.ppermute(block, ('section', 'seq', 'rep'), route)  8.85 us
    psum x1, blocking collectives, body(): squares = far_squares = lax.psum(squares, 'rep')  3.97 us
    pallas_call x2, Pallas kernels, body(): pl.pallas_call(kernel, in_specs=[VMEM] * 11, out_specs=[VMEM] * len(out_s...  1.93 us
    pallas_call x1, Pallas kernels, body(): pl.pallas_call(lambda *refs: first_kernel(*refs, total_steps=steps * seq_...  1.54 us
  transfers between devices with their start and end apart: 8, of which 3 were waited for; matrix products, arithmetic and copies ran while one was open for 0% of the time, Pallas kernels for 1%

profile of v4, /device:TPU:11, one launch (start us, length us, event | category | flops | bytes accessed | tf_op | source)
XLA Modules:
  0.0 32.3 jit_solution(11385737267939460343)
XLA Ops:
  0.0 1.5 %first.1 = (bf16[32,2048]{1,0:T(8,128)(2,1)S(1)}, bf16[32,2048]{1,0:T(8,128)(2,1)S(1)}, f32[8,128]{1,0:T(8,128)S(1)}, bf16[1,16,128,384]{3,2,1,0:T(8,128)(2,1)S(...) custom-call(bf16[2,8,4,2048]{3,2,1,0:T(4,128)(2,1)} %refs_0_.1, bf16[1,16,128,384]{3,2,1,0:T(8,128)(2,1)} %refs_1_.1, ...), custom_call_target="tpu_custom_call" | custom-call | flops 16777216 | bytes 786432 | tf_op jit(solution)/shard_map/first/pallas_call | solution.py:295
  1.5 0.7 %collective-permute-start = (bf16[32,2048]{1,0:T(8,128)(2,1)S(1)}, bf16[32,2048]{1,0:T(8,128)(2,1)S(1)}, u32[]{:S(2)}, u32[]{:S(2)}) collective-permute-start(bf16[32,2048]{1,0:T(8,128)(2,1)S(1)} %get-tuple-element.14.refs_0_.refs_9_), channel_id=1, source_target_pairs={{0,2},{1,3},{2,0},{3,1},{4,6},{5,7},{6,4},{7,5},{8,10},{9,11},{10,... | collective-permute-start | bytes 393224 | tf_op jit(solution)/shard_map/ppermute | solution.py:336
  2.2 5.0 %collective-permute-start.1 = (bf16[32,2048]{1,0:T(8,128)(2,1)S(1)}, bf16[32,2048]{1,0:T(8,128)(2,1)S(1)}, u32[]{:S(2)}, u32[]{:S(2)}) collective-permute-start(bf16[32,2048]{1,0:T(8,128)(2,1)S(1)} %get-tuple-element.15.refs_1_.refs_10_), channel_id=1, source_target_pairs={{18,4},{19,5},{20,2},{21,3},{22,8},{23,9},{24,6},{25,7},{26,12},{2... | collective-permute-start | bytes 393224 | tf_op jit(solution)/shard_map/ppermute | solution.py:336
  7.2 0.0 collective-permute-done.next_chip_ref.refs_2_
  7.2 1.9 %collective-permute-done.1.next_far_ref.refs_3_ = bf16[32,2048]{1,0:T(8,128)(2,1)S(1)} collective-permute-done((bf16[32,2048]{1,0:T(8,128)(2,1)S(1)}, bf16[32,2048]{1,0:T(8,128)(2,1)S(1)}, u32[]{:S(2)}, u32[]{:S(2)}) %collective-permute-start.1) | collective-permute-done | bytes 131104 | tf_op jit(solution)/shard_map/ppermute | solution.py:336
  9.1 0.2 edge.1
  9.4 4.0 %psum.7.refs_4_.refs_5_ = f32[8,128]{1,0:T(8,128)S(1)} all-reduce(f32[8,128]{1,0:T(8,128)S(1)} %edge.1), channel_id=1, replica_groups=mesh['section'=2,'seq'=8,'rep'=2] {'rep'}, use_global_device_ids=true, to_apply=%region_0.0 | all-reduce | flops 1024 | bytes 8192 | tf_op jit(solution)/shard_map/psum | solution.py:349
  13.4 1.3 %collective-permute-start.2 = (bf16[32,2048]{1,0:T(8,128)(2,1)S(1)}, bf16[32,2048]{1,0:T(8,128)(2,1)S(1)}, u32[]{:S(2)}, u32[]{:S(2)}) collective-permute-start(bf16[32,2048]{1,0:T(8,128)(2,1)S(1)} %get-tuple-element.20.refs_9_), channel_id=1, source_target_pairs={{0,16},{1,17},{2,18},{3,19},{4,20},{5,21},{6,22},{7,23},{8,24},{9,... | collective-permute-start | bytes 393224 | tf_op jit(solution)/shard_map/ppermute | solution.py:336
  14.7 1.3 %collective-permute-start.5 = (f32[8,128]{1,0:T(8,128)S(1)}, f32[8,128]{1,0:T(8,128)S(1)}, u32[]{:S(2)}, u32[]{:S(2)}) collective-permute-start(f32[8,128]{1,0:T(8,128)S(1)} %get-tuple-element.22), channel_id=1, source_target_pairs={{2,21},{3,20},{4,19},{5,18},{6,25},{7,24},{8,23},{9,22},{10,29},{1... | collective-permute-start | bytes 12296 | tf_op jit(solution)/shard_map/ppermute | solution.py:336
  16.0 1.3 %collective-permute-start.4 = (f32[8,128]{1,0:T(8,128)S(1)}, f32[8,128]{1,0:T(8,128)S(1)}, u32[]{:S(2)}, u32[]{:S(2)}) collective-permute-start(f32[8,128]{1,0:T(8,128)S(1)} %get-tuple-element.22), channel_id=1, source_target_pairs={{0,17},{1,16},{2,19},{3,18},{4,21},{5,20},{6,23},{7,22},{8,25},{9,... | collective-permute-start | bytes 12296 | tf_op jit(solution)/shard_map/ppermute | solution.py:336
  17.3 1.3 %collective-permute-start.7 = (bf16[32,2048]{1,0:T(8,128)(2,1)S(1)}, bf16[32,2048]{1,0:T(8,128)(2,1)S(1)}, u32[]{:S(2)}, u32[]{:S(2)}) collective-permute-start(bf16[32,2048]{1,0:T(8,128)(2,1)S(1)} %get-tuple-element.21.refs_10_), channel_id=1, source_target_pairs={{2,20},{3,21},{4,18},{5,19},{6,24},{7,25},{8,22},{9,23},{10,28},{1... | collective-permute-start | bytes 393224 | tf_op jit(solution)/shard_map/ppermute | solution.py:336
  18.6 1.3 %collective-permute-start.3 = (bf16[32,2048]{1,0:T(8,128)(2,1)S(1)}, bf16[32,2048]{1,0:T(8,128)(2,1)S(1)}, u32[]{:S(2)}, u32[]{:S(2)}) collective-permute-start(bf16[32,2048]{1,0:T(8,128)(2,1)S(1)} %get-tuple-element.21.refs_10_), channel_id=1, source_target_pairs={{0,16},{1,17},{2,18},{3,19},{4,20},{5,21},{6,22},{7,23},{8,24},{9,... | collective-permute-start | bytes 393224 | tf_op jit(solution)/shard_map/ppermute | solution.py:336
  19.9 4.7 %collective-permute-done.5._.refs_5_ = f32[8,128]{1,0:T(8,128)S(1)} collective-permute-done((f32[8,128]{1,0:T(8,128)S(1)}, f32[8,128]{1,0:T(8,128)S(1)}, u32[]{:S(2)}, u32[]{:S(2)}) %collective-permute-start.5) | collective-permute-done | bytes 4128 | tf_op jit(solution)/shard_map/ppermute | solution.py:336
  24.5 0.0 collective-permute-done.4.squares_ref.refs_4_
  24.6 0.0 collective-permute-done.2.chip_ref.refs_0_
  24.6 0.3 norm.1
  24.8 3.2 %collective-permute-start.6 = (bf16[32,2048]{1,0:T(8,128)(2,1)S(1)}, bf16[32,2048]{1,0:T(8,128)(2,1)S(1)}, u32[]{:S(2)}, u32[]{:S(2)}) collective-permute-start(bf16[32,2048]{1,0:T(8,128)(2,1)S(1)} %norm.1), channel_id=1, source_target_pairs={{16,18},{17,19},{18,16},{19,17},{20,22},{21,23},{22,20},{23,21},{2... | collective-permute-start | bytes 393224 | tf_op jit(solution)/shard_map/ppermute | solution.py:336
  28.1 0.0 collective-permute-done.7.refs_3_
  28.1 2.3 %collective-permute-done.3.refs_1_ = bf16[32,2048]{1,0:T(8,128)(2,1)S(1)} collective-permute-done((bf16[32,2048]{1,0:T(8,128)(2,1)S(1)}, bf16[32,2048]{1,0:T(8,128)(2,1)S(1)}, u32[]{:S(2)}, u32[]{:S(2)}) %collective-permute-start.3) | collective-permute-done | bytes 131104 | tf_op jit(solution)/shard_map/ppermute | solution.py:336
  30.4 0.0 collective-permute-done.6.refs_2_
  30.4 1.9 %layer.3 = bf16[1,2,8,4,2048]{4,3,2,1,0:T(4,128)(2,1)} custom-call(bf16[32,2048]{1,0:T(8,128)(2,1)S(1)} %collective-permute-done.2.chip_ref.refs_0_, bf16[32,2048]{1,0:T(8,128)(2,1)S(1)} %collective-permute-done.3.refs_1_, bf16[32,2048]{1,0:T(8,128)(2,1)S(1)} %collective-permute-done.6.refs_2_, bf16[32,2048]{1,0:T(8,128)(2,1)S(1)} %collective-permute-done.7.refs_3_, ...), custom_call_target="tpu_custom_call" | custom-call | flops 402653184 | bytes 4194304 | tf_op jit(solution)/shard_map/layer/pallas_call | solution.py:362
  (1 shorter events, 0.0 us)
Async XLA Ops:
  1.5 5.7 %collective-permute-start = (bf16[32,2048]{1,0:T(8,128)(2,1)S(1)}, bf16[32,2048]{1,0:T(8,128)(2,1)S(1)}, u32[]{:S(2)}, u32[]{:S(2)}) collective-permute-start(bf16[32,2048]{1,0:T(8,128)(2,1)S(1)} %get-tuple-element.14.refs_0_.refs_9_), channel_id=1, source_target_pairs={{0,2},{1,3},{2,0},{3,1},{4,6},{5,7},{6,4},{7,5},{8,10},{9,11},{10,... | collective-permute-start | bytes 393224 | tf_op jit(solution)/shard_map/ppermute | solution.py:336
  2.2 6.9 %collective-permute-start.1 = (bf16[32,2048]{1,0:T(8,128)(2,1)S(1)}, bf16[32,2048]{1,0:T(8,128)(2,1)S(1)}, u32[]{:S(2)}, u32[]{:S(2)}) collective-permute-start(bf16[32,2048]{1,0:T(8,128)(2,1)S(1)} %get-tuple-element.15.refs_1_.refs_10_), channel_id=1, source_target_pairs={{18,4},{19,5},{20,2},{21,3},{22,8},{23,9},{24,6},{25,7},{26,12},{2... | collective-permute-start | bytes 393224 | tf_op jit(solution)/shard_map/ppermute | solution.py:336
  13.4 11.2 %collective-permute-start.2 = (bf16[32,2048]{1,0:T(8,128)(2,1)S(1)}, bf16[32,2048]{1,0:T(8,128)(2,1)S(1)}, u32[]{:S(2)}, u32[]{:S(2)}) collective-permute-start(bf16[32,2048]{1,0:T(8,128)(2,1)S(1)} %get-tuple-element.20.refs_9_), channel_id=1, source_target_pairs={{0,16},{1,17},{2,18},{3,19},{4,20},{5,21},{6,22},{7,23},{8,24},{9,... | collective-permute-start | bytes 393224 | tf_op jit(solution)/shard_map/ppermute | solution.py:336
  14.7 9.9 %collective-permute-start.5 = (f32[8,128]{1,0:T(8,128)S(1)}, f32[8,128]{1,0:T(8,128)S(1)}, u32[]{:S(2)}, u32[]{:S(2)}) collective-permute-start(f32[8,128]{1,0:T(8,128)S(1)} %get-tuple-element.22), channel_id=1, source_target_pairs={{2,21},{3,20},{4,19},{5,18},{6,25},{7,24},{8,23},{9,22},{10,29},{1... | collective-permute-start | bytes 12296 | tf_op jit(solution)/shard_map/ppermute | solution.py:336
  16.0 8.6 %collective-permute-start.4 = (f32[8,128]{1,0:T(8,128)S(1)}, f32[8,128]{1,0:T(8,128)S(1)}, u32[]{:S(2)}, u32[]{:S(2)}) collective-permute-start(f32[8,128]{1,0:T(8,128)S(1)} %get-tuple-element.22), channel_id=1, source_target_pairs={{0,17},{1,16},{2,19},{3,18},{4,21},{5,20},{6,23},{7,22},{8,25},{9,... | collective-permute-start | bytes 12296 | tf_op jit(solution)/shard_map/ppermute | solution.py:336
  17.3 10.8 %collective-permute-start.7 = (bf16[32,2048]{1,0:T(8,128)(2,1)S(1)}, bf16[32,2048]{1,0:T(8,128)(2,1)S(1)}, u32[]{:S(2)}, u32[]{:S(2)}) collective-permute-start(bf16[32,2048]{1,0:T(8,128)(2,1)S(1)} %get-tuple-element.21.refs_10_), channel_id=1, source_target_pairs={{2,20},{3,21},{4,18},{5,19},{6,24},{7,25},{8,22},{9,23},{10,28},{1... | collective-permute-start | bytes 393224 | tf_op jit(solution)/shard_map/ppermute | solution.py:336
  18.6 11.8 %collective-permute-start.3 = (bf16[32,2048]{1,0:T(8,128)(2,1)S(1)}, bf16[32,2048]{1,0:T(8,128)(2,1)S(1)}, u32[]{:S(2)}, u32[]{:S(2)}) collective-permute-start(bf16[32,2048]{1,0:T(8,128)(2,1)S(1)} %get-tuple-element.21.refs_10_), channel_id=1, source_target_pairs={{0,16},{1,17},{2,18},{3,19},{4,20},{5,21},{6,22},{7,23},{8,24},{9,... | collective-permute-start | bytes 393224 | tf_op jit(solution)/shard_map/ppermute | solution.py:336
  24.8 5.5 %collective-permute-start.6 = (bf16[32,2048]{1,0:T(8,128)(2,1)S(1)}, bf16[32,2048]{1,0:T(8,128)(2,1)S(1)}, u32[]{:S(2)}, u32[]{:S(2)}) collective-permute-start(bf16[32,2048]{1,0:T(8,128)(2,1)S(1)} %norm.1), channel_id=1, source_target_pairs={{16,18},{17,19},{18,16},{19,17},{20,22},{21,23},{22,20},{23,21},{2... | collective-permute-start | bytes 393224 | tf_op jit(solution)/shard_map/ppermute | solution.py:336

commit v5 on v4

--- a/solution.py
+++ b/solution.py
@@ -80,23 +80,13 @@
         station_ref[m] = jnp.where(same_time & (recorded | same_station), 0.0, -BIG)[:own]
 
 
-def first_kernel(
-    signal_hbm, weights_hbm, first_hbm, pad_hbm, chip_ref, far_ref, squares_ref,
-    weights_ref, time_ref, station_ref, signal_ref, first_ref, pad_ref, arrived,
-    *, total_steps,
-):
-    copies = [
-        pltpu.make_async_copy(signal_hbm, signal_ref, arrived.at[0]),
-        pltpu.make_async_copy(first_hbm, first_ref, arrived.at[1]),
-        pltpu.make_async_copy(pad_hbm, pad_ref, arrived.at[2]),
-        pltpu.make_async_copy(weights_hbm, weights_ref, arrived.at[3]),
-    ]
-    for copy in copies:
-        copy.start()
+def halves_kernel(signal_hbm, chip_ref, far_ref, signal_ref, arrived):
+    copy = pltpu.make_async_copy(signal_hbm, signal_ref, arrived)
+    copy.start()
     micro, _, stations, _ = signal_ref.shape
     edge = WIN * stations
-    copies[0].wait()
-    for half, half_ref in ((CHIP, chip_ref), (FAR, far_ref)):
+    copy.wait()
+    for half, half_ref in ((FAR, far_ref), (CHIP, chip_ref)):
         start = first_step(half)
         for m in range(micro):
             for t in range(0, WIN, 2):
@@ -105,28 +95,39 @@
                 half_ref[at : at + 2 * stations, :] = jnp.concatenate(pair, axis=0).astype(
                     jnp.bfloat16
                 )
-    squares_ref[...] = jnp.zeros(squares_ref.shape, jnp.float32)
-    for half, half_ref in ((CHIP, chip_ref), (FAR, far_ref)):
-        squares_ref[half : half + 1, 0 : micro * edge] = squares_row(half_ref[...])
+
+
+def fixed_kernel(
+    weights_hbm, first_hbm, pad_hbm, _, weights_ref, time_ref, station_ref,
+    first_ref, pad_ref, arrived, *, stations, total_steps,
+):
+    copies = [
+        pltpu.make_async_copy(first_hbm, first_ref, arrived.at[0]),
+        pltpu.make_async_copy(pad_hbm, pad_ref, arrived.at[1]),
+        pltpu.make_async_copy(weights_hbm, weights_ref, arrived.at[2]),
+    ]
+    for copy in copies:
+        copy.start()
+    copies[0].wait()
     copies[1].wait()
+    fill_masks(first_ref, pad_ref, time_ref, station_ref, stations, total_steps)
     copies[2].wait()
-    fill_masks(first_ref, pad_ref, time_ref, station_ref, stations, total_steps)
-    copies[3].wait()
-
-
-def edge_kernel(next_chip_ref, next_far_ref, squares_ref, out_ref):
-    out_ref[...] = squares_ref[...]
-    for half, half_ref in ((NEXT_CHIP, next_chip_ref), (NEXT_FAR, next_far_ref)):
+
+
+def squares_kernel(*refs):
+    out_ref = refs[-1]
+    out_ref[...] = jnp.zeros(out_ref.shape, jnp.float32)
+    for half, half_ref in enumerate(refs[:-1]):
         out_ref[half : half + 1, 0 : half_ref.shape[0]] = squares_row(half_ref[...])
 
 
-def norm_kernel(chip_ref, squares_ref, _, normed_ref):
+def norm_kernel(chip_ref, squares_ref, *refs):
     rows = chip_ref[...]
     count = rows.shape[0]
     total = squares_row(rows) + squares_ref[CHIP : CHIP + 1, 0:count]
     factor = lax.rsqrt(total / (HEADS * HEAD) + EPS)
     column = jnp.sum(jnp.where(same(count), factor, 0.0), axis=1, keepdims=True)
-    normed_ref[...] = (rows.astype(jnp.float32) * column).astype(jnp.bfloat16)
+    refs[-1][...] = (rows.astype(jnp.float32) * column).astype(jnp.bfloat16)
 
 
 def softmax_columns(scores):
@@ -141,7 +142,7 @@
     if last:
         out_ref, normed_ref, projected_ref = refs
     else:
-        out_chip_ref, out_far_ref, out_squares_ref, normed_ref, projected_ref = refs
+        out_chip_ref, out_far_ref, normed_ref, projected_ref = refs
     edge = WIN * stations
     micro = chip_ref.shape[0] // edge
     own, reach = 2 * edge, 4 * edge
@@ -231,7 +232,6 @@
             time_weights = softmax_columns(score + time_ref[m])
             station_weights = softmax_columns(score[:own] + station_ref[m])
             mixes.append(jnp.concatenate([time_weights, station_weights], axis=0).T)
-        sums = [jnp.zeros((own, HEAD), f32) for _ in range(micro)]
         for (g, m), mix in zip(pairs, mixes):
             first = m * reach
             for j in range(GROUP):
@@ -254,17 +254,6 @@
                 )
                 result = hidden.astype(f32) + mixed
                 write(m, lanes, result)
-                if not last:
-                    rounded = result.astype(bf16).astype(f32)
-                    sums[m] = sums[m] + rounded * rounded
-        if not last:
-            out_squares_ref[...] = jnp.zeros(out_squares_ref.shape, f32)
-            for half in (CHIP, FAR):
-                parts = [s[half * edge : (half + 1) * edge] for s in sums]
-                column = jnp.sum(jnp.concatenate(parts, axis=0), axis=1, keepdims=True)
-                out_squares_ref[half : half + 1, 0 : micro * edge] = jnp.sum(
-                    jnp.where(same(micro * edge), column, 0.0), axis=0, keepdims=True
-                )
 
     @pl.when(jnp.logical_not(active))
     def _():
@@ -275,8 +264,6 @@
                     ref[m * edge : (m + 1) * edge, lanes] for ref in (kept_chip_ref, kept_far_ref)
                 ]
                 write(m, lanes, jnp.concatenate(kept, axis=0).astype(f32))
-        if not last:
-            out_squares_ref[...] = jnp.zeros(out_squares_ref.shape, f32)
 
 
 def body(signal, head_proj, record_start, record_pad):
@@ -292,33 +279,47 @@
     squares_shape = jax.ShapeDtypeStruct((8, 128), f32)
     signal_bytes = signal.size * 2
 
-    chip, far, squares, weights, time_bias, station_bias = pl.pallas_call(
-        lambda *refs: first_kernel(*refs, total_steps=steps * seq_count),
-        in_specs=[HBM] * 4,
-        out_specs=[VMEM] * 6,
+    def in_hbm(block):
+        return pltpu.with_memory_space_constraint(block, pltpu.HBM)
+
+    def squares_of(*halves):
+        return pl.pallas_call(
+            squares_kernel,
+            in_specs=[VMEM] * len(halves),
+            out_specs=VMEM,
+            out_shape=squares_shape,
+            compiler_params=PARAMS,
+            name="squares",
+        )(*halves)
+
+    chip, far = pl.pallas_call(
+        halves_kernel,
+        in_specs=[HBM],
+        out_specs=[VMEM] * 2,
+        out_shape=[half_shape] * 2,
+        scratch_shapes=[pltpu.VMEM(signal.shape, bf16), pltpu.SemaphoreType.DMA],
+        compiler_params=PARAMS,
+        cost_estimate=cost(signal.size, 2 * signal_bytes),
+        name="halves",
+    )(in_hbm(signal))
+    weights, time_bias, station_bias = pl.pallas_call(
+        lambda *refs: fixed_kernel(*refs, stations=stations, total_steps=steps * seq_count),
+        in_specs=[HBM] * 3 + [VMEM],
+        out_specs=[VMEM] * 3,
         out_shape=[
-            half_shape,
-            half_shape,
-            squares_shape,
             jax.ShapeDtypeStruct(head_proj.shape, bf16),
             jax.ShapeDtypeStruct((micro, reach, GROUP * own), f32),
             jax.ShapeDtypeStruct((micro, own, GROUP * own), f32),
         ],
         scratch_shapes=[
-            pltpu.VMEM(signal.shape, bf16),
             pltpu.SMEM(record_start.shape, jnp.int32),
             pltpu.SMEM(record_pad.shape, jnp.int32),
-            pltpu.SemaphoreType.DMA((4,)),
+            pltpu.SemaphoreType.DMA((3,)),
         ],
         compiler_params=PARAMS,
-        cost_estimate=cost(2 * micro * own * signal.size, 3 * signal_bytes),
-        name="first",
-    )(
-        *[
-            pltpu.with_memory_space_constraint(x, pltpu.HBM)
-            for x in (signal, head_proj, record_start, record_pad)
-        ]
-    )
+        cost_estimate=cost(signal.size, 2 * head_proj.size),
+        name="fixed",
+    )(in_hbm(head_proj), in_hbm(record_start), in_hbm(record_pad), chip)
 
     def moved(block, source, target, hop, other=False):
         route = []
@@ -338,14 +339,7 @@
     helper = 1 if section_count > 1 else 0
     next_far = moved(far, helper, 0, 2)
     next_chip = moved(chip, 0, 0, 1)
-    squares = pl.pallas_call(
-        edge_kernel,
-        in_specs=[VMEM] * 3,
-        out_specs=VMEM,
-        out_shape=squares_shape,
-        compiler_params=PARAMS,
-        name="edge",
-    )(next_chip, next_far, squares)
+    squares = squares_of(chip, far, next_chip, next_far)
     squares = far_squares = lax.psum(squares, "rep")
     kept = (chip, far)
     for tick in range(section_count):
@@ -357,7 +351,7 @@
         out_shape = (
             [jax.ShapeDtypeStruct((1,) + signal.shape, bf16)]
             if last
-            else [half_shape, half_shape, squares_shape]
+            else [half_shape, half_shape]
         )
         outputs = pl.pallas_call(
             kernel,
@@ -377,21 +371,21 @@
         )
         if last:
             return outputs[0]
-        kept = outputs[:2]
-        mine = outputs[2]
+        kept = outputs
+        mine = squares_of(*kept)
         chip = moved(kept[0], tick, tick + 1, 0)
+        next_far = moved(kept[1], tick, tick + 1, 2)
+        far = moved(kept[1], tick, tick + 1, 0)
         squares = moved(mine, tick, tick + 1, 0, other=True)
-        far = moved(kept[1], tick, tick + 1, 0)
-        next_far = moved(kept[1], tick, tick + 1, 2)
         far_squares = moved(mine, tick, tick + 1, 2, other=True)
         normed_chip = pl.pallas_call(
             norm_kernel,
-            in_specs=[VMEM] * 3,
+            in_specs=[VMEM] * 4,
             out_specs=VMEM,
             out_shape=half_shape,
             compiler_params=PARAMS,
             name="norm",
-        )(chip, squares, far_squares)
+        )(chip, squares, far_squares, next_far)
         next_chip = moved(normed_chip, tick + 1, tick + 1, 1)
 
 

time: 32.7 us -> 30.6 us (0.936)
  starting transfers between devices: 15.4 us -> 13.7 us
  waiting for transfers between devices: 8.85 us -> 7.44 us
  Pallas kernels: 3.96 us -> 5.16 us
    ppermute x8, starting transfers between devices: 15.4 us -> 13.7 us  [moved(): return lax.ppermute(block, ('section', 'seq', 'rep'), route)]
    ppermute x8, waiting for transfers between devices: 8.85 us -> 7.44 us  [moved(): return lax.ppermute(block, ('section', 'seq', 'rep'), route)]
    pallas_call x3 -> x5, Pallas kernels: 2.03 us -> 3.23 us  [the longest x1 1.44 us: body(): pl.pallas_call(lambda *refs: fixed_kernel(*refs, stations=stations, total...]
  transfers between devices with their start and end apart: 8 -> 8, of which waited for: 3 -> 3; matrix products, arithmetic and copies ran while one was open for 0% -> 0% of each run, Pallas kernels for 1% -> 6%
where the time goes in v5:
time: 30.6 us; the launch traced here: 30.3 us
  starting transfers between devices  13.7 us (45%)
  waiting for transfers between devices  7.44 us (24%)
  Pallas kernels  5.16 us (17%)
  blocking collectives  3.8 us (12%)
    ppermute x8, starting transfers between devices, moved(): return lax.ppermute(block, ('section', 'seq', 'rep'), route)  13.7 us
    ppermute x8, waiting for transfers between devices, moved(): return lax.ppermute(block, ('section', 'seq', 'rep'), route)  7.44 us
    psum x1, blocking collectives, body(): squares = far_squares = lax.psum(squares, 'rep')  3.8 us
    pallas_call x2, Pallas kernels, body(): pl.pallas_call(kernel, in_specs=[VMEM] * 11, out_specs=[VMEM] * len(out_s...  1.93 us
    pallas_call x1, Pallas kernels, body(): pl.pallas_call(lambda *refs: fixed_kernel(*refs, stations=stations, total...  1.44 us
    pallas_call x1, Pallas kernels, body(): pl.pallas_call(halves_kernel, in_specs=[HBM], out_specs=[VMEM] * 2, out_s...  1.02 us
  transfers between devices with their start and end apart: 8, of which 3 were waited for; matrix products, arithmetic and copies ran while one was open for 0% of the time, Pallas kernels for 6%

profile of v5, /device:TPU:11, one launch (start us, length us, event | category | flops | bytes accessed | tf_op | source)
XLA Modules:
  0.0 30.3 jit_solution(11369048792654905476)
XLA Ops:
  0.0 1.0 %halves.1 = (bf16[32,2048]{1,0:T(8,128)(2,1)S(1)}, bf16[32,2048]{1,0:T(8,128)(2,1)S(1)}) custom-call(bf16[2,8,4,2048]{3,2,1,0:T(4,128)(2,1)} %signal_hbm.1), custom_call_target="tpu_custom_call" | custom-call | flops 131072 | bytes 524288 | tf_op jit(solution)/shard_map/halves/pallas_call | solution.py:295
  1.0 3.7 %collective-permute-start.1 = (bf16[32,2048]{1,0:T(8,128)(2,1)S(1)}, bf16[32,2048]{1,0:T(8,128)(2,1)S(1)}, u32[]{:S(2)}, u32[]{:S(2)}) collective-permute-start(bf16[32,2048]{1,0:T(8,128)(2,1)S(1)} %get-tuple-element.13.refs_1_.refs_10_), channel_id=1, source_target_pairs={{18,4},{19,5},{20,2},{21,3},{22,8},{23,9},{24,6},{25,7},{26,12},{2... | collective-permute-start | bytes 393224 | tf_op jit(solution)/shard_map/ppermute | solution.py:337
  4.8 0.7 %collective-permute-start = (bf16[32,2048]{1,0:T(8,128)(2,1)S(1)}, bf16[32,2048]{1,0:T(8,128)(2,1)S(1)}, u32[]{:S(2)}, u32[]{:S(2)}) collective-permute-start(bf16[32,2048]{1,0:T(8,128)(2,1)S(1)} %get-tuple-element.12.refs_0_.refs_3_.refs_9_), channel_id=1, source_target_pairs={{0,2},{1,3},{2,0},{3,1},{4,6},{5,7},{6,4},{7,5},{8,10},{9,11},{10,... | collective-permute-start | bytes 393224 | tf_op jit(solution)/shard_map/ppermute | solution.py:337
  5.5 1.4 %fixed.1 = (bf16[1,16,128,384]{3,2,1,0:T(8,128)(2,1)S(1)}, f32[2,64,128]{2,1,0:T(8,128)S(1)}, f32[2,32,128]{2,1,0:T(8,128)S(1)}) custom-call(bf16[1,16,128,384]{3,2,1,0:T(8,128)(2,1)} %refs_0_.1, s32[2,4]{1,0:T(2,128)} %refs_1_.1, s32[2,4]{1,0:T(2,128)} %refs_2_.1, bf16[32,2048]{1,0:T(8,128)(2,1)S(1)} %get-tuple-element.12.refs_0_.refs_3_.refs_9_), custom_call_target="tpu_custom_call" | custom-call | flops 131072 | bytes 1572864 | tf_op jit(solution)/shard_map/fixed/pallas_call | solution.py:305
  6.9 0.1 collective-permute-done.1.refs_3_
  7.0 0.0 collective-permute-done.refs_2_
  7.0 0.3 squares.2
  7.3 3.8 %psum.7.refs_4_.refs_5_ = f32[8,128]{1,0:T(8,128)S(1)} all-reduce(f32[8,128]{1,0:T(8,128)S(1)} %squares.2), channel_id=1, replica_groups=mesh['section'=2,'seq'=8,'rep'=2] {'rep'}, use_global_device_ids=true, to_apply=%region_0.0 | all-reduce | flops 1024 | bytes 8192 | tf_op jit(solution)/shard_map/psum | solution.py:343
  11.2 1.3 %collective-permute-start.2 = (bf16[32,2048]{1,0:T(8,128)(2,1)S(1)}, bf16[32,2048]{1,0:T(8,128)(2,1)S(1)}, u32[]{:S(2)}, u32[]{:S(2)}) collective-permute-start(bf16[32,2048]{1,0:T(8,128)(2,1)S(1)} %get-tuple-element.17.refs_0_.refs_9_), channel_id=1, source_target_pairs={{0,16},{1,17},{2,18},{3,19},{4,20},{5,21},{6,22},{7,23},{8,24},{9,... | collective-permute-start | bytes 393224 | tf_op jit(solution)/shard_map/ppermute | solution.py:337
  12.5 1.3 %collective-permute-start.6 = (bf16[32,2048]{1,0:T(8,128)(2,1)S(1)}, bf16[32,2048]{1,0:T(8,128)(2,1)S(1)}, u32[]{:S(2)}, u32[]{:S(2)}) collective-permute-start(bf16[32,2048]{1,0:T(8,128)(2,1)S(1)} %get-tuple-element.18.refs_1_.refs_10_), channel_id=1, source_target_pairs={{2,20},{3,21},{4,18},{5,19},{6,24},{7,25},{8,22},{9,23},{10,28},{1... | collective-permute-start | bytes 393224 | tf_op jit(solution)/shard_map/ppermute | solution.py:337
  13.8 0.2 squares.3
  14.0 1.3 %collective-permute-start.5 = (f32[8,128]{1,0:T(8,128)S(1)}, f32[8,128]{1,0:T(8,128)S(1)}, u32[]{:S(2)}, u32[]{:S(2)}) collective-permute-start(f32[8,128]{1,0:T(8,128)S(1)} %squares.3), channel_id=1, source_target_pairs={{2,21},{3,20},{4,19},{5,18},{6,25},{7,24},{8,23},{9,22},{10,29},{1... | collective-permute-start | bytes 12296 | tf_op jit(solution)/shard_map/ppermute | solution.py:337
  15.3 1.3 %collective-permute-start.4 = (f32[8,128]{1,0:T(8,128)S(1)}, f32[8,128]{1,0:T(8,128)S(1)}, u32[]{:S(2)}, u32[]{:S(2)}) collective-permute-start(f32[8,128]{1,0:T(8,128)S(1)} %squares.3), channel_id=1, source_target_pairs={{0,17},{1,16},{2,19},{3,18},{4,21},{5,20},{6,23},{7,22},{8,25},{9,... | collective-permute-start | bytes 12296 | tf_op jit(solution)/shard_map/ppermute | solution.py:337
  16.6 1.3 %collective-permute-start.3 = (bf16[32,2048]{1,0:T(8,128)(2,1)S(1)}, bf16[32,2048]{1,0:T(8,128)(2,1)S(1)}, u32[]{:S(2)}, u32[]{:S(2)}) collective-permute-start(bf16[32,2048]{1,0:T(8,128)(2,1)S(1)} %get-tuple-element.18.refs_1_.refs_10_), channel_id=1, source_target_pairs={{0,16},{1,17},{2,18},{3,19},{4,20},{5,21},{6,22},{7,23},{8,24},{9,... | collective-permute-start | bytes 393224 | tf_op jit(solution)/shard_map/ppermute | solution.py:337
  17.9 6.3 %collective-permute-done.5.refs_0_.refs_5_ = f32[8,128]{1,0:T(8,128)S(1)} collective-permute-done((f32[8,128]{1,0:T(8,128)S(1)}, f32[8,128]{1,0:T(8,128)S(1)}, u32[]{:S(2)}, u32[]{:S(2)}) %collective-permute-start.5) | collective-permute-done | bytes 4128 | tf_op jit(solution)/shard_map/ppermute | solution.py:337
  24.2 0.0 collective-permute-done.4.squares_ref.refs_4_
  24.2 0.0 collective-permute-done.2.chip_ref.refs_0_
  24.2 0.0 collective-permute-done.6.refs_1_.refs_3_
  24.2 0.3 norm.1
  24.5 2.9 %collective-permute-start.7 = (bf16[32,2048]{1,0:T(8,128)(2,1)S(1)}, bf16[32,2048]{1,0:T(8,128)(2,1)S(1)}, u32[]{:S(2)}, u32[]{:S(2)}) collective-permute-start(bf16[32,2048]{1,0:T(8,128)(2,1)S(1)} %norm.1), channel_id=1, source_target_pairs={{16,18},{17,19},{18,16},{19,17},{20,22},{21,23},{22,20},{23,21},{2... | collective-permute-start | bytes 393224 | tf_op jit(solution)/shard_map/ppermute | solution.py:337
  27.4 0.0 collective-permute-done.3.refs_1_
  27.4 1.0 %collective-permute-done.7.refs_2_ = bf16[32,2048]{1,0:T(8,128)(2,1)S(1)} collective-permute-done((bf16[32,2048]{1,0:T(8,128)(2,1)S(1)}, bf16[32,2048]{1,0:T(8,128)(2,1)S(1)}, u32[]{:S(2)}, u32[]{:S(2)}) %collective-permute-start.7) | collective-permute-done | bytes 131104 | tf_op jit(solution)/shard_map/ppermute | solution.py:337
  28.4 1.9 %layer.3 = bf16[1,2,8,4,2048]{4,3,2,1,0:T(4,128)(2,1)} custom-call(bf16[32,2048]{1,0:T(8,128)(2,1)S(1)} %collective-permute-done.2.chip_ref.refs_0_, bf16[32,2048]{1,0:T(8,128)(2,1)S(1)} %collective-permute-done.3.refs_1_, bf16[32,2048]{1,0:T(8,128)(2,1)S(1)} %collective-permute-done.7.refs_2_, bf16[32,2048]{1,0:T(8,128)(2,1)S(1)} %collective-permute-done.6.refs_1_.refs_3_, ...), custom_call_target="tpu_custom_call" | custom-call | flops 402653184 | bytes 4194304 | tf_op jit(solution)/shard_map/layer/pallas_call | solution.py:356
  (1 shorter events, 0.0 us)
Async XLA Ops:
  1.0 6.0 %collective-permute-start.1 = (bf16[32,2048]{1,0:T(8,128)(2,1)S(1)}, bf16[32,2048]{1,0:T(8,128)(2,1)S(1)}, u32[]{:S(2)}, u32[]{:S(2)}) collective-permute-start(bf16[32,2048]{1,0:T(8,128)(2,1)S(1)} %get-tuple-element.13.refs_1_.refs_10_), channel_id=1, source_target_pairs={{18,4},{19,5},{20,2},{21,3},{22,8},{23,9},{24,6},{25,7},{26,12},{2... | collective-permute-start | bytes 393224 | tf_op jit(solution)/shard_map/ppermute | solution.py:337
  4.8 2.3 %collective-permute-start = (bf16[32,2048]{1,0:T(8,128)(2,1)S(1)}, bf16[32,2048]{1,0:T(8,128)(2,1)S(1)}, u32[]{:S(2)}, u32[]{:S(2)}) collective-permute-start(bf16[32,2048]{1,0:T(8,128)(2,1)S(1)} %get-tuple-element.12.refs_0_.refs_3_.refs_9_), channel_id=1, source_target_pairs={{0,2},{1,3},{2,0},{3,1},{4,6},{5,7},{6,4},{7,5},{8,10},{9,11},{10,... | collective-permute-start | bytes 393224 | tf_op jit(solution)/shard_map/ppermute | solution.py:337
  11.2 13.1 %collective-permute-start.2 = (bf16[32,2048]{1,0:T(8,128)(2,1)S(1)}, bf16[32,2048]{1,0:T(8,128)(2,1)S(1)}, u32[]{:S(2)}, u32[]{:S(2)}) collective-permute-start(bf16[32,2048]{1,0:T(8,128)(2,1)S(1)} %get-tuple-element.17.refs_0_.refs_9_), channel_id=1, source_target_pairs={{0,16},{1,17},{2,18},{3,19},{4,20},{5,21},{6,22},{7,23},{8,24},{9,... | collective-permute-start | bytes 393224 | tf_op jit(solution)/shard_map/ppermute | solution.py:337
  12.5 11.8 %collective-permute-start.6 = (bf16[32,2048]{1,0:T(8,128)(2,1)S(1)}, bf16[32,2048]{1,0:T(8,128)(2,1)S(1)}, u32[]{:S(2)}, u32[]{:S(2)}) collective-permute-start(bf16[32,2048]{1,0:T(8,128)(2,1)S(1)} %get-tuple-element.18.refs_1_.refs_10_), channel_id=1, source_target_pairs={{2,20},{3,21},{4,18},{5,19},{6,24},{7,25},{8,22},{9,23},{10,28},{1... | collective-permute-start | bytes 393224 | tf_op jit(solution)/shard_map/ppermute | solution.py:337
  14.0 10.2 %collective-permute-start.5 = (f32[8,128]{1,0:T(8,128)S(1)}, f32[8,128]{1,0:T(8,128)S(1)}, u32[]{:S(2)}, u32[]{:S(2)}) collective-permute-start(f32[8,128]{1,0:T(8,128)S(1)} %squares.3), channel_id=1, source_target_pairs={{2,21},{3,20},{4,19},{5,18},{6,25},{7,24},{8,23},{9,22},{10,29},{1... | collective-permute-start | bytes 12296 | tf_op jit(solution)/shard_map/ppermute | solution.py:337
  15.3 8.9 %collective-permute-start.4 = (f32[8,128]{1,0:T(8,128)S(1)}, f32[8,128]{1,0:T(8,128)S(1)}, u32[]{:S(2)}, u32[]{:S(2)}) collective-permute-start(f32[8,128]{1,0:T(8,128)S(1)} %squares.3), channel_id=1, source_target_pairs={{0,17},{1,16},{2,19},{3,18},{4,21},{5,20},{6,23},{7,22},{8,25},{9,... | collective-permute-start | bytes 12296 | tf_op jit(solution)/shard_map/ppermute | solution.py:337
  16.6 10.8 %collective-permute-start.3 = (bf16[32,2048]{1,0:T(8,128)(2,1)S(1)}, bf16[32,2048]{1,0:T(8,128)(2,1)S(1)}, u32[]{:S(2)}, u32[]{:S(2)}) collective-permute-start(bf16[32,2048]{1,0:T(8,128)(2,1)S(1)} %get-tuple-element.18.refs_1_.refs_10_), channel_id=1, source_target_pairs={{0,16},{1,17},{2,18},{3,19},{4,20},{5,21},{6,22},{7,23},{8,24},{9,... | collective-permute-start | bytes 393224 | tf_op jit(solution)/shard_map/ppermute | solution.py:337
  24.5 3.9 %collective-permute-start.7 = (bf16[32,2048]{1,0:T(8,128)(2,1)S(1)}, bf16[32,2048]{1,0:T(8,128)(2,1)S(1)}, u32[]{:S(2)}, u32[]{:S(2)}) collective-permute-start(bf16[32,2048]{1,0:T(8,128)(2,1)S(1)} %norm.1), channel_id=1, source_target_pairs={{16,18},{17,19},{18,16},{19,17},{20,22},{21,23},{22,20},{23,21},{2... | collective-permute-start | bytes 393224 | tf_op jit(solution)/shard_map/ppermute | solution.py:337

commit v6 on v5

--- a/solution.py
+++ b/solution.py
@@ -121,13 +121,13 @@
         out_ref[half : half + 1, 0 : half_ref.shape[0]] = squares_row(half_ref[...])
 
 
-def norm_kernel(chip_ref, squares_ref, *refs):
-    rows = chip_ref[...]
+def norm_kernel(half_ref, squares_ref, normed_ref, *, line):
+    rows = half_ref[...]
     count = rows.shape[0]
-    total = squares_row(rows) + squares_ref[CHIP : CHIP + 1, 0:count]
+    total = squares_row(rows) + squares_ref[line : line + 1, 0:count]
     factor = lax.rsqrt(total / (HEADS * HEAD) + EPS)
     column = jnp.sum(jnp.where(same(count), factor, 0.0), axis=1, keepdims=True)
-    refs[-1][...] = (rows.astype(jnp.float32) * column).astype(jnp.bfloat16)
+    normed_ref[...] = (rows.astype(jnp.float32) * column).astype(jnp.bfloat16)
 
 
 def softmax_columns(scores):
@@ -136,7 +136,7 @@
 
 
 def layer_kernel(
-    chip_ref, far_ref, next_chip_ref, next_far_ref, squares_ref, far_squares_ref,
+    chip_ref, far_ref, next_chip_ref, next_far_ref, squares_ref,
     time_ref, station_ref, weights_ref, kept_chip_ref, kept_far_ref, *refs, tick, stations, last,
 ):
     if last:
@@ -190,7 +190,7 @@
             norm_rows(CHIP, chip_ref, squares_ref[CHIP : CHIP + 1, :], False)
             norm_rows(FAR, far_ref, squares_ref[FAR : FAR + 1, :], False)
             put_normed(NEXT_CHIP, slice(None), next_chip_ref[...])
-            norm_rows(NEXT_FAR, next_far_ref, far_squares_ref[FAR : FAR + 1, :], False)
+            put_normed(NEXT_FAR, slice(None), next_far_ref[...])
         for head in range(heads_dev):
             projected_ref[:, head * width : (head + 1) * width] = jnp.dot(
                 normed_ref[:, head * HEAD : (head + 1) * HEAD],
@@ -292,6 +292,17 @@
             name="squares",
         )(*halves)
 
+    def normed(rows, squares, line):
+        return pl.pallas_call(
+            lambda *refs: norm_kernel(*refs, line=line),
+            in_specs=[VMEM] * 2,
+            out_specs=VMEM,
+            out_shape=half_shape,
+            compiler_params=PARAMS,
+            cost_estimate=cost(2000000000, 4 * half_shape.size),
+            name="norm",
+        )(rows, squares)
+
     chip, far = pl.pallas_call(
         halves_kernel,
         in_specs=[HBM],
@@ -336,11 +347,10 @@
                     )
         return lax.ppermute(block, ("section", "seq", "rep"), route)
 
-    helper = 1 if section_count > 1 else 0
-    next_far = moved(far, helper, 0, 2)
+    next_far = moved(far, 0, 0, 2)
     next_chip = moved(chip, 0, 0, 1)
     squares = squares_of(chip, far, next_chip, next_far)
-    squares = far_squares = lax.psum(squares, "rep")
+    squares = lax.psum(squares, "rep")
     kept = (chip, far)
     for tick in range(section_count):
         last = tick + 1 == section_count
@@ -355,7 +365,7 @@
         )
         outputs = pl.pallas_call(
             kernel,
-            in_specs=[VMEM] * 11,
+            in_specs=[VMEM] * 10,
             out_specs=[VMEM] * len(out_shape),
             out_shape=out_shape,
             scratch_shapes=[
@@ -366,7 +376,7 @@
             cost_estimate=cost(8 * signal.size * 3 * HEAD, 16 * signal_bytes),
             name="layer",
         )(
-            chip, far, next_chip, next_far, squares, far_squares,
+            chip, far, next_chip, next_far, squares,
             time_bias, station_bias, weights, *kept,
         )
         if last:
@@ -378,15 +388,8 @@
         far = moved(kept[1], tick, tick + 1, 0)
         squares = moved(mine, tick, tick + 1, 0, other=True)
         far_squares = moved(mine, tick, tick + 1, 2, other=True)
-        normed_chip = pl.pallas_call(
-            norm_kernel,
-            in_specs=[VMEM] * 4,
-            out_specs=VMEM,
-            out_shape=half_shape,
-            compiler_params=PARAMS,
-            name="norm",
-        )(chip, squares, far_squares, next_far)
-        next_chip = moved(normed_chip, tick + 1, tick + 1, 1)
+        next_chip = moved(normed(chip, squares, CHIP), tick + 1, tick + 1, 1)
+        next_far = normed(next_far, far_squares, FAR)
 
 
 def solution(mesh):

time: 30.6 us -> 28 us (0.915)
  the two profiles are of different devices: /device:TPU:11 before, /device:TPU:14 now
where the time goes in v6:
time: 28 us; the launch traced here: 27.7 us
  starting transfers between devices  9.72 us (35%)
  waiting for transfers between devices  7.37 us (26%)
  Pallas kernels  5.47 us (20%)
  blocking collectives  4.95 us (18%)
    ppermute x8, starting transfers between devices, moved(): return lax.ppermute(block, ('section', 'seq', 'rep'), route)  9.72 us
    ppermute x8, waiting for transfers between devices, moved(): return lax.ppermute(block, ('section', 'seq', 'rep'), route)  7.37 us
    psum x1, blocking collectives, body(): squares = lax.psum(squares, 'rep')  4.95 us
    pallas_call x2, Pallas kernels, body(): pl.pallas_call(kernel, in_specs=[VMEM] * 10, out_specs=[VMEM] * len(out_s...  1.95 us
    pallas_call x1, Pallas kernels, body(): pl.pallas_call(lambda *refs: fixed_kernel(*refs, stations=stations, total...  1.44 us
    pallas_call x1, Pallas kernels, body(): pl.pallas_call(halves_kernel, in_specs=[HBM], out_specs=[VMEM] * 2, out_s...  1.02 us
    pallas_call x2, Pallas kernels, normed(): pl.pallas_call(lambda *refs: norm_kernel(*refs, line=line), in_specs=[VME...  0.57 us
  transfers between devices with their start and end apart: 8, of which 2 were waited for; matrix products, arithmetic and copies ran while one was open for 0% of the time, Pallas kernels for 8%

profile of v6, /device:TPU:14, one launch (start us, length us, event | category | flops | bytes accessed | tf_op | source)
XLA Modules:
  0.0 27.7 jit_solution(3846496959707986511)
XLA Ops:
  0.0 1.0 %halves.1 = (bf16[32,2048]{1,0:T(8,128)(2,1)S(1)}, bf16[32,2048]{1,0:T(8,128)(2,1)S(1)}) custom-call(bf16[2,8,4,2048]{3,2,1,0:T(4,128)(2,1)} %signal_hbm.1), custom_call_target="tpu_custom_call" | custom-call | flops 131072 | bytes 524288 | tf_op jit(solution)/shard_map/halves/pallas_call | solution.py:306
  1.0 0.7 %collective-permute-start.1 = (bf16[32,2048]{1,0:T(8,128)(2,1)S(1)}, bf16[32,2048]{1,0:T(8,128)(2,1)S(1)}, u32[]{:S(2)}, u32[]{:S(2)}) collective-permute-start(bf16[32,2048]{1,0:T(8,128)(2,1)S(1)} %get-tuple-element.13.refs_1_.refs_9_), channel_id=1, source_target_pairs={{2,4},{3,5},{4,2},{5,3},{6,8},{7,9},{8,6},{9,7},{10,12},{11,13},{1... | collective-permute-start | bytes 393224 | tf_op jit(solution)/shard_map/ppermute | solution.py:348
  1.7 0.7 %collective-permute-start = (bf16[32,2048]{1,0:T(8,128)(2,1)S(1)}, bf16[32,2048]{1,0:T(8,128)(2,1)S(1)}, u32[]{:S(2)}, u32[]{:S(2)}) collective-permute-start(bf16[32,2048]{1,0:T(8,128)(2,1)S(1)} %get-tuple-element.12.refs_0_.refs_3_.refs_8_), channel_id=1, source_target_pairs={{0,2},{1,3},{2,0},{3,1},{4,6},{5,7},{6,4},{7,5},{8,10},{9,11},{10,... | collective-permute-start | bytes 393224 | tf_op jit(solution)/shard_map/ppermute | solution.py:348
  2.4 1.4 %fixed.1 = (bf16[1,16,128,384]{3,2,1,0:T(8,128)(2,1)S(1)}, f32[2,64,128]{2,1,0:T(8,128)S(1)}, f32[2,32,128]{2,1,0:T(8,128)S(1)}) custom-call(bf16[1,16,128,384]{3,2,1,0:T(8,128)(2,1)} %refs_0_.1, s32[2,4]{1,0:T(2,128)} %refs_1_.1, s32[2,4]{1,0:T(2,128)} %refs_2_.1, bf16[32,2048]{1,0:T(8,128)(2,1)S(1)} %get-tuple-element.12.refs_0_.refs_3_.refs_8_), custom_call_target="tpu_custom_call" | custom-call | flops 131072 | bytes 1572864 | tf_op jit(solution)/shard_map/fixed/pallas_call | solution.py:316
  3.8 0.0 collective-permute-done.1.refs_3_
  3.8 0.0 collective-permute-done.refs_2_
  3.8 0.3 %squares.2 = f32[8,128]{1,0:T(8,128)S(1)} custom-call(bf16[32,2048]{1,0:T(8,128)(2,1)S(1)} %get-tuple-element.12.refs_0_.refs_3_.refs_8_, bf16[32,2048]{1,0:T(8,128)(2,1)S(1)} %get-tuple-element.13.refs_1_.refs_9_, bf16[32,2048]{1,0:T(8,128)(2,1)S(1)} %collective-permute-done.refs_2_, bf16[32,2048]{1,0:T(8,128)(2,1)S(1)} %collective-permute-done.1.refs_3_), custom_call_target="tpu_custom_call" | custom-call | tf_op jit(solution)/shard_map/squares/pallas_call | solution.py:286
  4.1 5.0 %psum.7.refs_4_ = f32[8,128]{1,0:T(8,128)S(1)} all-reduce(f32[8,128]{1,0:T(8,128)S(1)} %squares.2), channel_id=1, replica_groups=mesh['section'=2,'seq'=8,'rep'=2] {'rep'}, use_global_device_ids=true, to_apply=%region_0.0 | all-reduce | flops 1024 | bytes 8192 | tf_op jit(solution)/shard_map/psum | solution.py:353
  9.1 1.3 %collective-permute-start.2 = (bf16[32,2048]{1,0:T(8,128)(2,1)S(1)}, bf16[32,2048]{1,0:T(8,128)(2,1)S(1)}, u32[]{:S(2)}, u32[]{:S(2)}) collective-permute-start(bf16[32,2048]{1,0:T(8,128)(2,1)S(1)} %get-tuple-element.17.refs_0_.refs_8_), channel_id=1, source_target_pairs={{0,16},{1,17},{2,18},{3,19},{4,20},{5,21},{6,22},{7,23},{8,24},{9,... | collective-permute-start | bytes 393224 | tf_op jit(solution)/shard_map/ppermute | solution.py:348
  10.4 0.2 squares.3
  10.7 1.3 %collective-permute-start.4 = (f32[8,128]{1,0:T(8,128)S(1)}, f32[8,128]{1,0:T(8,128)S(1)}, u32[]{:S(2)}, u32[]{:S(2)}) collective-permute-start(f32[8,128]{1,0:T(8,128)S(1)} %squares.3), channel_id=1, source_target_pairs={{0,17},{1,16},{2,19},{3,18},{4,21},{5,20},{6,23},{7,22},{8,25},{9,... | collective-permute-start | bytes 12296 | tf_op jit(solution)/shard_map/ppermute | solution.py:348
  12.0 1.3 %collective-permute-start.7 = (f32[8,128]{1,0:T(8,128)S(1)}, f32[8,128]{1,0:T(8,128)S(1)}, u32[]{:S(2)}, u32[]{:S(2)}) collective-permute-start(f32[8,128]{1,0:T(8,128)S(1)} %squares.3), channel_id=1, source_target_pairs={{2,21},{3,20},{4,19},{5,18},{6,25},{7,24},{8,23},{9,22},{10,29},{1... | collective-permute-start | bytes 12296 | tf_op jit(solution)/shard_map/ppermute | solution.py:348
  13.3 1.3 %collective-permute-start.6 = (bf16[32,2048]{1,0:T(8,128)(2,1)S(1)}, bf16[32,2048]{1,0:T(8,128)(2,1)S(1)}, u32[]{:S(2)}, u32[]{:S(2)}) collective-permute-start(bf16[32,2048]{1,0:T(8,128)(2,1)S(1)} %get-tuple-element.18.refs_1_.refs_9_), channel_id=1, source_target_pairs={{2,20},{3,21},{4,18},{5,19},{6,24},{7,25},{8,22},{9,23},{10,28},{1... | collective-permute-start | bytes 393224 | tf_op jit(solution)/shard_map/ppermute | solution.py:348
  14.6 1.3 %collective-permute-start.3 = (bf16[32,2048]{1,0:T(8,128)(2,1)S(1)}, bf16[32,2048]{1,0:T(8,128)(2,1)S(1)}, u32[]{:S(2)}, u32[]{:S(2)}) collective-permute-start(bf16[32,2048]{1,0:T(8,128)(2,1)S(1)} %get-tuple-element.18.refs_1_.refs_9_), channel_id=1, source_target_pairs={{0,16},{1,17},{2,18},{3,19},{4,20},{5,21},{6,22},{7,23},{8,24},{9,... | collective-permute-start | bytes 393224 | tf_op jit(solution)/shard_map/ppermute | solution.py:348
  15.9 3.5 %collective-permute-done.4.refs_1_.refs_4_ = f32[8,128]{1,0:T(8,128)S(1)} collective-permute-done((f32[8,128]{1,0:T(8,128)S(1)}, f32[8,128]{1,0:T(8,128)S(1)}, u32[]{:S(2)}, u32[]{:S(2)}) %collective-permute-start.4) | collective-permute-done | bytes 4128 | tf_op jit(solution)/shard_map/ppermute | solution.py:348
  19.3 0.0 collective-permute-done.2.refs_0_
  19.3 0.3 %norm.2 = bf16[32,2048]{1,0:T(8,128)(2,1)S(1)} custom-call(bf16[32,2048]{1,0:T(8,128)(2,1)S(1)} %collective-permute-done.2.refs_0_, f32[8,128]{1,0:T(8,128)S(1)} %collective-permute-done.4.refs_1_.refs_4_), custom_call_target="tpu_custom_call" | custom-call | flops 2000000000 | bytes 262144 | tf_op jit(solution)/shard_map/norm/pallas_call | solution.py:296
  19.6 1.9 %collective-permute-start.5 = (bf16[32,2048]{1,0:T(8,128)(2,1)S(1)}, bf16[32,2048]{1,0:T(8,128)(2,1)S(1)}, u32[]{:S(2)}, u32[]{:S(2)}) collective-permute-start(bf16[32,2048]{1,0:T(8,128)(2,1)S(1)} %norm.2), channel_id=1, source_target_pairs={{16,18},{17,19},{18,16},{19,17},{20,22},{21,23},{22,20},{23,21},{2... | collective-permute-start | bytes 393224 | tf_op jit(solution)/shard_map/ppermute | solution.py:348
  21.5 0.0 collective-permute-done.7.refs_1_
  21.6 0.0 collective-permute-done.6.refs_0_
  21.6 0.3 %norm.3.refs_3_ = bf16[32,2048]{1,0:T(8,128)(2,1)S(1)} custom-call(bf16[32,2048]{1,0:T(8,128)(2,1)S(1)} %collective-permute-done.6.refs_0_, f32[8,128]{1,0:T(8,128)S(1)} %collective-permute-done.7.refs_1_), custom_call_target="tpu_custom_call" | custom-call | flops 2000000000 | bytes 262144 | tf_op jit(solution)/shard_map/norm/pallas_call | solution.py:296
  21.9 3.9 %collective-permute-done.3.refs_1_ = bf16[32,2048]{1,0:T(8,128)(2,1)S(1)} collective-permute-done((bf16[32,2048]{1,0:T(8,128)(2,1)S(1)}, bf16[32,2048]{1,0:T(8,128)(2,1)S(1)}, u32[]{:S(2)}, u32[]{:S(2)}) %collective-permute-start.3) | collective-permute-done | bytes 131104 | tf_op jit(solution)/shard_map/ppermute | solution.py:348
  25.8 0.0 collective-permute-done.5.refs_2_
  25.8 1.9 %layer.3 = bf16[1,2,8,4,2048]{4,3,2,1,0:T(4,128)(2,1)} custom-call(bf16[32,2048]{1,0:T(8,128)(2,1)S(1)} %collective-permute-done.2.refs_0_, bf16[32,2048]{1,0:T(8,128)(2,1)S(1)} %collective-permute-done.3.refs_1_, bf16[32,2048]{1,0:T(8,128)(2,1)S(1)} %collective-permute-done.5.refs_2_, bf16[32,2048]{1,0:T(8,128)(2,1)S(1)} %norm.3.refs_3_, ...), custom_call_target="tpu_custom_call" | custom-call | flops 402653184 | bytes 4194304 | tf_op jit(solution)/shard_map/layer/pallas_call | solution.py:366
  (1 shorter events, 0.0 us)
Async XLA Ops:
  1.0 2.8 %collective-permute-start.1 = (bf16[32,2048]{1,0:T(8,128)(2,1)S(1)}, bf16[32,2048]{1,0:T(8,128)(2,1)S(1)}, u32[]{:S(2)}, u32[]{:S(2)}) collective-permute-start(bf16[32,2048]{1,0:T(8,128)(2,1)S(1)} %get-tuple-element.13.refs_1_.refs_9_), channel_id=1, source_target_pairs={{2,4},{3,5},{4,2},{5,3},{6,8},{7,9},{8,6},{9,7},{10,12},{11,13},{1... | collective-permute-start | bytes 393224 | tf_op jit(solution)/shard_map/ppermute | solution.py:348
  1.7 2.1 %collective-permute-start = (bf16[32,2048]{1,0:T(8,128)(2,1)S(1)}, bf16[32,2048]{1,0:T(8,128)(2,1)S(1)}, u32[]{:S(2)}, u32[]{:S(2)}) collective-permute-start(bf16[32,2048]{1,0:T(8,128)(2,1)S(1)} %get-tuple-element.12.refs_0_.refs_3_.refs_8_), channel_id=1, source_target_pairs={{0,2},{1,3},{2,0},{3,1},{4,6},{5,7},{6,4},{7,5},{8,10},{9,11},{10,... | collective-permute-start | bytes 393224 | tf_op jit(solution)/shard_map/ppermute | solution.py:348
  9.1 10.2 %collective-permute-start.2 = (bf16[32,2048]{1,0:T(8,128)(2,1)S(1)}, bf16[32,2048]{1,0:T(8,128)(2,1)S(1)}, u32[]{:S(2)}, u32[]{:S(2)}) collective-permute-start(bf16[32,2048]{1,0:T(8,128)(2,1)S(1)} %get-tuple-element.17.refs_0_.refs_8_), channel_id=1, source_target_pairs={{0,16},{1,17},{2,18},{3,19},{4,20},{5,21},{6,22},{7,23},{8,24},{9,... | collective-permute-start | bytes 393224 | tf_op jit(solution)/shard_map/ppermute | solution.py:348
  10.7 8.7 %collective-permute-start.4 = (f32[8,128]{1,0:T(8,128)S(1)}, f32[8,128]{1,0:T(8,128)S(1)}, u32[]{:S(2)}, u32[]{:S(2)}) collective-permute-start(f32[8,128]{1,0:T(8,128)S(1)} %squares.3), channel_id=1, source_target_pairs={{0,17},{1,16},{2,19},{3,18},{4,21},{5,20},{6,23},{7,22},{8,25},{9,... | collective-permute-start | bytes 12296 | tf_op jit(solution)/shard_map/ppermute | solution.py:348
  12.0 9.6 %collective-permute-start.7 = (f32[8,128]{1,0:T(8,128)S(1)}, f32[8,128]{1,0:T(8,128)S(1)}, u32[]{:S(2)}, u32[]{:S(2)}) collective-permute-start(f32[8,128]{1,0:T(8,128)S(1)} %squares.3), channel_id=1, source_target_pairs={{2,21},{3,20},{4,19},{5,18},{6,25},{7,24},{8,23},{9,22},{10,29},{1... | collective-permute-start | bytes 12296 | tf_op jit(solution)/shard_map/ppermute | solution.py:348
  13.3 8.3 %collective-permute-start.6 = (bf16[32,2048]{1,0:T(8,128)(2,1)S(1)}, bf16[32,2048]{1,0:T(8,128)(2,1)S(1)}, u32[]{:S(2)}, u32[]{:S(2)}) collective-permute-start(bf16[32,2048]{1,0:T(8,128)(2,1)S(1)} %get-tuple-element.18.refs_1_.refs_9_), channel_id=1, source_target_pairs={{2,20},{3,21},{4,18},{5,19},{6,24},{7,25},{8,22},{9,23},{10,28},{1... | collective-permute-start | bytes 393224 | tf_op jit(solution)/shard_map/ppermute | solution.py:348
  14.6 11.2 %collective-permute-start.3 = (bf16[32,2048]{1,0:T(8,128)(2,1)S(1)}, bf16[32,2048]{1,0:T(8,128)(2,1)S(1)}, u32[]{:S(2)}, u32[]{:S(2)}) collective-permute-start(bf16[32,2048]{1,0:T(8,128)(2,1)S(1)} %get-tuple-element.18.refs_1_.refs_9_), channel_id=1, source_target_pairs={{0,16},{1,17},{2,18},{3,19},{4,20},{5,21},{6,22},{7,23},{8,24},{9,... | collective-permute-start | bytes 393224 | tf_op jit(solution)/shard_map/ppermute | solution.py:348
  19.6 6.1 %collective-permute-start.5 = (bf16[32,2048]{1,0:T(8,128)(2,1)S(1)}, bf16[32,2048]{1,0:T(8,128)(2,1)S(1)}, u32[]{:S(2)}, u32[]{:S(2)}) collective-permute-start(bf16[32,2048]{1,0:T(8,128)(2,1)S(1)} %norm.2), channel_id=1, source_target_pairs={{16,18},{17,19},{18,16},{19,17},{20,22},{21,23},{22,20},{23,21},{2... | collective-permute-start | bytes 393224 | tf_op jit(solution)/shard_map/ppermute | solution.py:348

commit v7 on v6

--- a/solution.py
+++ b/solution.py
@@ -17,6 +17,7 @@
 
 HBM = pl.BlockSpec(memory_space=pltpu.HBM)
 VMEM = pl.BlockSpec(memory_space=pltpu.VMEM)
+BUSY = pl.CostEstimate(flops=2000000000, bytes_accessed=300000, transcendentals=0)
 PARAMS = pltpu.CompilerParams(vmem_limit_bytes=16 * 1024 * 1024)
 
 
@@ -80,7 +81,7 @@
         station_ref[m] = jnp.where(same_time & (recorded | same_station), 0.0, -BIG)[:own]
 
 
-def halves_kernel(signal_hbm, chip_ref, far_ref, signal_ref, arrived):
+def halves_kernel(signal_hbm, chip_ref, far_ref, squares_ref, signal_ref, arrived):
     copy = pltpu.make_async_copy(signal_hbm, signal_ref, arrived)
     copy.start()
     micro, _, stations, _ = signal_ref.shape
@@ -95,6 +96,7 @@
                 half_ref[at : at + 2 * stations, :] = jnp.concatenate(pair, axis=0).astype(
                     jnp.bfloat16
                 )
+    squares_kernel(chip_ref, far_ref, squares_ref)
 
 
 def fixed_kernel(
@@ -121,13 +123,39 @@
         out_ref[half : half + 1, 0 : half_ref.shape[0]] = squares_row(half_ref[...])
 
 
+def scaled(rows, total):
+    count = rows.shape[0]
+    factor = lax.rsqrt(total / (HEADS * HEAD) + EPS)
+    column = jnp.sum(jnp.where(same(count), factor, 0.0), axis=1, keepdims=True)
+    return (rows.astype(jnp.float32) * column).astype(jnp.bfloat16)
+
+
+def first_norm_kernel(half_ref, squares_ref, *refs, line):
+    rows = half_ref[...]
+    refs[-1][...] = scaled(rows, squares_ref[line : line + 1, 0 : rows.shape[0]])
+
+
 def norm_kernel(half_ref, squares_ref, normed_ref, *, line):
     rows = half_ref[...]
-    count = rows.shape[0]
-    total = squares_row(rows) + squares_ref[line : line + 1, 0:count]
-    factor = lax.rsqrt(total / (HEADS * HEAD) + EPS)
-    column = jnp.sum(jnp.where(same(count), factor, 0.0), axis=1, keepdims=True)
-    normed_ref[...] = (rows.astype(jnp.float32) * column).astype(jnp.bfloat16)
+    normed_ref[...] = scaled(
+        rows, squares_row(rows) + squares_ref[line : line + 1, 0 : rows.shape[0]]
+    )
+
+
+def project_kernel(weights_ref, *refs):
+    count = len(refs) // 2
+    halves, outs = refs[:count], refs[count:]
+    rows = halves[0].shape[0]
+    width = 3 * HEAD
+    for head in range(weights_ref.shape[1]):
+        lanes = slice(head * HEAD, (head + 1) * HEAD)
+        projected = jnp.dot(
+            jnp.concatenate([half[:, lanes] for half in halves], axis=0),
+            weights_ref[0, head],
+            preferred_element_type=jnp.float32,
+        ).astype(jnp.bfloat16)
+        for i, out in enumerate(outs):
+            out[:, head * width : (head + 1) * width] = projected[i * rows : (i + 1) * rows]
 
 
 def softmax_columns(scores):
@@ -136,20 +164,29 @@
 
 
 def layer_kernel(
-    chip_ref, far_ref, next_chip_ref, next_far_ref, squares_ref,
-    time_ref, station_ref, weights_ref, kept_chip_ref, kept_far_ref, *refs, tick, stations, last,
+    chip_ref, far_ref, squares_ref, time_ref, station_ref, weights_ref, kept_chip_ref, kept_far_ref,
+    *refs, tick, stations, last,
 ):
-    if last:
-        out_ref, normed_ref, projected_ref = refs
-    else:
-        out_chip_ref, out_far_ref, normed_ref, projected_ref = refs
     edge = WIN * stations
     micro = chip_ref.shape[0] // edge
-    own, reach = 2 * edge, 4 * edge
+    own = 2 * edge
     heads_dev = weights_ref.shape[1]
     width = 3 * HEAD
     bf16, f32 = jnp.bfloat16, jnp.float32
     active = lax.axis_index("section") == tick
+    if tick == 0:
+        projected_chip, projected_far, next_far_ref, next_chip_ref, *refs = refs
+    else:
+        projected_chip, projected_next_chip, projected_next_far, *refs = refs
+    if last:
+        out_ref, *refs = refs
+    else:
+        out_chip_ref, out_far_ref, *refs = refs
+    if tick == 0:
+        projected_next_chip, projected_next_far = refs
+    else:
+        (projected_far,) = refs
+    projected = (projected_chip, projected_far, projected_next_chip, projected_next_far)
 
     def write(m, lanes, values):
         for half in (CHIP, FAR):
@@ -163,55 +200,39 @@
                 half_ref = (out_chip_ref, out_far_ref)[half]
                 half_ref[m * edge : (m + 1) * edge, lanes] = part
 
-    def norm_rows(half, half_ref, squares_row_ref, complete):
-        lane = lax.broadcasted_iota(jnp.int32, (micro * edge, 128), 1)
-        row = lax.broadcasted_iota(jnp.int32, (micro * edge, 128), 0)
-        total = jnp.where(lane == row, squares_row_ref, 0.0)
-        if not complete:
-            for head in range(heads_dev):
-                part = half_ref[:, head * HEAD : (head + 1) * HEAD].astype(f32)
-                total = total + part * part
-        factor = lax.rsqrt(jnp.sum(total, axis=1, keepdims=True) / (HEADS * HEAD) + EPS)
-        for head in range(heads_dev):
-            lanes = slice(head * HEAD, (head + 1) * HEAD)
-            put_normed(half, lanes, (half_ref[:, lanes].astype(f32) * factor).astype(bf16))
-
-    def put_normed(half, lanes, rows):
-        for m in range(micro):
-            at = m * reach + half * edge
-            normed_ref[at : at + edge, lanes] = rows[m * edge : (m + 1) * edge]
+    def rows_of(halves, m, at):
+        return [projected[half][m * edge : (m + 1) * edge, at : at + HEAD] for half in halves]
 
     @pl.when(active)
     def _():
         if tick == 0:
-            for half, half_ref in enumerate((chip_ref, far_ref, next_chip_ref, next_far_ref)):
-                norm_rows(half, half_ref, squares_ref[half : half + 1, :], True)
+            project_kernel(
+                weights_ref, next_chip_ref, next_far_ref, projected_next_chip, projected_next_far
+            )
         else:
-            norm_rows(CHIP, chip_ref, squares_ref[CHIP : CHIP + 1, :], False)
-            norm_rows(FAR, far_ref, squares_ref[FAR : FAR + 1, :], False)
-            put_normed(NEXT_CHIP, slice(None), next_chip_ref[...])
-            put_normed(NEXT_FAR, slice(None), next_far_ref[...])
-        for head in range(heads_dev):
-            projected_ref[:, head * width : (head + 1) * width] = jnp.dot(
-                normed_ref[:, head * HEAD : (head + 1) * HEAD],
-                weights_ref[0, head],
-                preferred_element_type=f32,
-            ).astype(bf16)
+            lane = lax.broadcasted_iota(jnp.int32, (micro * edge, 128), 1)
+            row = lax.broadcasted_iota(jnp.int32, (micro * edge, 128), 0)
+            total = jnp.where(lane == row, squares_ref[FAR : FAR + 1, :], 0.0)
+            for head in range(heads_dev):
+                part = far_ref[:, head * HEAD : (head + 1) * HEAD].astype(f32)
+                total = total + part * part
+            factor = lax.rsqrt(jnp.sum(total, axis=1, keepdims=True) / (HEADS * HEAD) + EPS)
+            for head in range(heads_dev):
+                projected_far[:, head * width : (head + 1) * width] = jnp.dot(
+                    (far_ref[:, head * HEAD : (head + 1) * HEAD].astype(f32) * factor).astype(bf16),
+                    weights_ref[0, head],
+                    preferred_element_type=f32,
+                ).astype(bf16)
         pairs = [(g, m) for g in range(heads_dev // GROUP) for m in range(micro)]
         blank = jnp.zeros((own, HEAD), bf16)
         scores = []
         for g, m in pairs:
             at = [(g * GROUP + j) * width for j in range(GROUP)]
-            first = m * reach
+            queries = [jnp.concatenate(rows_of((CHIP, FAR), m, a), axis=0) for a in at]
             spread = jnp.concatenate(
                 [
                     jnp.concatenate(
-                        [
-                            projected_ref[first : first + own, at[j] : at[j] + HEAD]
-                            if i == j
-                            else blank
-                            for i in range(GROUP)
-                        ],
+                        [queries[j] if i == j else blank for i in range(GROUP)],
                         axis=1,
                     )
                     for j in range(GROUP)
@@ -219,7 +240,7 @@
                 axis=0,
             )
             keys = jnp.concatenate(
-                [projected_ref[first : first + reach, a + HEAD : a + 2 * HEAD] for a in at], axis=1
+                [jnp.concatenate(rows_of(range(4), m, a + HEAD), axis=0) for a in at], axis=1
             )
             scores.append(
                 lax.dot_general(
@@ -233,19 +254,12 @@
             station_weights = softmax_columns(score[:own] + station_ref[m])
             mixes.append(jnp.concatenate([time_weights, station_weights], axis=0).T)
         for (g, m), mix in zip(pairs, mixes):
-            first = m * reach
             for j in range(GROUP):
                 head = g * GROUP + j
                 at = head * width + 2 * HEAD
                 mixed = jnp.dot(
                     mix[j * own : (j + 1) * own],
-                    jnp.concatenate(
-                        [
-                            projected_ref[first : first + reach, at : at + HEAD],
-                            projected_ref[first : first + own, at : at + HEAD],
-                        ],
-                        axis=0,
-                    ),
+                    jnp.concatenate(rows_of((0, 1, 2, 3, CHIP, FAR), m, at), axis=0),
                     preferred_element_type=f32,
                 )
                 lanes = slice(head * HEAD, (head + 1) * HEAD)
@@ -277,6 +291,7 @@
     bf16, f32 = jnp.bfloat16, jnp.float32
     half_shape = jax.ShapeDtypeStruct((micro * edge, features), bf16)
     squares_shape = jax.ShapeDtypeStruct((8, 128), f32)
+    projected_shape = jax.ShapeDtypeStruct((micro * edge, heads_dev * 3 * HEAD), bf16)
     signal_bytes = signal.size * 2
 
     def in_hbm(block):
@@ -299,20 +314,45 @@
             out_specs=VMEM,
             out_shape=half_shape,
             compiler_params=PARAMS,
-            cost_estimate=cost(2000000000, 4 * half_shape.size),
+            cost_estimate=BUSY,
             name="norm",
         )(rows, squares)
 
-    chip, far = pl.pallas_call(
+    def project(*halves):
+        return pl.pallas_call(
+            project_kernel,
+            in_specs=[VMEM] * (1 + len(halves)),
+            out_specs=[VMEM] * len(halves),
+            out_shape=[projected_shape] * len(halves),
+            compiler_params=PARAMS,
+            cost_estimate=BUSY,
+            name="project",
+        )(weights, *halves)
+
+    chip, far, squares = pl.pallas_call(
         halves_kernel,
         in_specs=[HBM],
-        out_specs=[VMEM] * 2,
-        out_shape=[half_shape] * 2,
+        out_specs=[VMEM] * 3,
+        out_shape=[half_shape, half_shape, squares_shape],
         scratch_shapes=[pltpu.VMEM(signal.shape, bf16), pltpu.SemaphoreType.DMA],
         compiler_params=PARAMS,
         cost_estimate=cost(signal.size, 2 * signal_bytes),
         name="halves",
     )(in_hbm(signal))
+    squares = lax.psum(squares, "rep")
+    def first_normed(line, *operands):
+        return pl.pallas_call(
+            lambda *refs: first_norm_kernel(*refs, line=line),
+            in_specs=[VMEM] * len(operands),
+            out_specs=VMEM,
+            out_shape=half_shape,
+            compiler_params=PARAMS,
+            cost_estimate=BUSY,
+            name="norm",
+        )(*operands)
+
+    normed_far = first_normed(FAR, far, squares)
+    normed_chip = first_normed(CHIP, chip, squares, normed_far)
     weights, time_bias, station_bias = pl.pallas_call(
         lambda *refs: fixed_kernel(*refs, stations=stations, total_steps=steps * seq_count),
         in_specs=[HBM] * 3 + [VMEM],
@@ -330,7 +370,7 @@
         compiler_params=PARAMS,
         cost_estimate=cost(signal.size, 2 * head_proj.size),
         name="fixed",
-    )(in_hbm(head_proj), in_hbm(record_start), in_hbm(record_pad), chip)
+    )(in_hbm(head_proj), in_hbm(record_start), in_hbm(record_pad), normed_chip)
 
     def moved(block, source, target, hop, other=False):
         route = []
@@ -347,10 +387,9 @@
                     )
         return lax.ppermute(block, ("section", "seq", "rep"), route)
 
-    next_far = moved(far, 0, 0, 2)
-    next_chip = moved(chip, 0, 0, 1)
-    squares = squares_of(chip, far, next_chip, next_far)
-    squares = lax.psum(squares, "rep")
+    next_far = moved(normed_far, 0, 0, 2)
+    next_chip = moved(normed_chip, 0, 0, 1)
+    inputs = (*project(normed_chip, normed_far), next_far, next_chip)
     kept = (chip, far)
     for tick in range(section_count):
         last = tick + 1 == section_count
@@ -365,19 +404,15 @@
         )
         outputs = pl.pallas_call(
             kernel,
-            in_specs=[VMEM] * 10,
+            in_specs=[VMEM] * (8 + len(inputs)),
             out_specs=[VMEM] * len(out_shape),
             out_shape=out_shape,
-            scratch_shapes=[
-                pltpu.VMEM((micro * reach, features), bf16),
-                pltpu.VMEM((micro * reach, heads_dev * 3 * HEAD), bf16),
-            ],
+            scratch_shapes=[pltpu.VMEM(projected_shape.shape, bf16)] * (2 if tick == 0 else 1),
             compiler_params=PARAMS,
             cost_estimate=cost(8 * signal.size * 3 * HEAD, 16 * signal_bytes),
             name="layer",
         )(
-            chip, far, next_chip, next_far, squares,
-            time_bias, station_bias, weights, *kept,
+            chip, far, squares, time_bias, station_bias, weights, *kept, *inputs,
         )
         if last:
             return outputs[0]
@@ -388,8 +423,10 @@
         far = moved(kept[1], tick, tick + 1, 0)
         squares = moved(mine, tick, tick + 1, 0, other=True)
         far_squares = moved(mine, tick, tick + 1, 2, other=True)
-        next_chip = moved(normed(chip, squares, CHIP), tick + 1, tick + 1, 1)
+        normed_chip = normed(chip, squares, CHIP)
+        next_chip = moved(normed_chip, tick + 1, tick + 1, 1)
         next_far = normed(next_far, far_squares, FAR)
+        inputs = project(normed_chip, next_chip, next_far)
 
 
 def solution(mesh):

time: 28 us -> 29.3 us (1.046)
  the two profiles are of different devices: /device:TPU:14 before, /device:TPU:11 now
where the time goes in v7:
time: 29.3 us; the launch traced here: 28.8 us
  starting transfers between devices  11.1 us (38%)
  waiting for transfers between devices  7.42 us (25%)
  Pallas kernels  6.31 us (22%)
  blocking collectives  3.8 us (13%)
    ppermute x8, starting transfers between devices, moved(): return lax.ppermute(block, ('section', 'seq', 'rep'), route)  11.1 us
    ppermute x8, waiting for transfers between devices, moved(): return lax.ppermute(block, ('section', 'seq', 'rep'), route)  7.42 us
    psum x1, blocking collectives, body(): squares = lax.psum(squares, 'rep')  3.8 us
    pallas_call x2, Pallas kernels, body(): pl.pallas_call(kernel, in_specs=[VMEM] * (8 + len(inputs)), out_specs=[VM...  1.79 us
    pallas_call x1, Pallas kernels, body(): pl.pallas_call(lambda *refs: fixed_kernel(*refs, stations=stations, total...  1.44 us
    pallas_call x1, Pallas kernels, body(): pl.pallas_call(halves_kernel, in_specs=[HBM], out_specs=[VMEM] * 3, out_s...  1.19 us
    pallas_call x2, Pallas kernels, project(): pl.pallas_call(project_kernel, in_specs=[VMEM] * (1 + len(halves)), out_s...  0.91 us
  transfers between devices with their start and end apart: 8, of which 4 were waited for; matrix products, arithmetic and copies ran while one was open for 0% of the time, Pallas kernels for 11%

profile of v7, /device:TPU:11, one launch (start us, length us, event | category | flops | bytes accessed | tf_op | source)
XLA Modules:
  0.0 28.8 jit_solution(16157524496559669842)
XLA Ops:
  0.0 1.2 %halves.1 = (bf16[32,2048]{1,0:T(8,128)(2,1)S(1)}, bf16[32,2048]{1,0:T(8,128)(2,1)S(1)}, f32[8,128]{1,0:T(8,128)S(1)}) custom-call(bf16[2,8,4,2048]{3,2,1,0:T(4,128)(2,1)} %signal_hbm.1), custom_call_target="tpu_custom_call" | custom-call | flops 131072 | bytes 524288 | tf_op jit(solution)/shard_map/halves/pallas_call | solution.py:332
  1.2 3.8 %psum.7.refs_1_.refs_2_ = f32[8,128]{1,0:T(8,128)S(1)} all-reduce(f32[8,128]{1,0:T(8,128)S(1)} %get-tuple-element.20), channel_id=1, replica_groups=mesh['section'=2,'seq'=8,'rep'=2] {'rep'}, use_global_device_ids=true, to_apply=%region_0.0 | all-reduce | flops 1024 | bytes 8192 | tf_op jit(solution)/shard_map/psum | solution.py:342
  5.0 0.1 norm.4.refs_2_.refs_1_
  5.1 0.7 %collective-permute-start = (bf16[32,2048]{1,0:T(8,128)(2,1)S(1)}, bf16[32,2048]{1,0:T(8,128)(2,1)S(1)}, u32[]{:S(2)}, u32[]{:S(2)}) collective-permute-start(bf16[32,2048]{1,0:T(8,128)(2,1)S(1)} %norm.4.refs_2_.refs_1_), channel_id=1, source_target_pairs={{2,4},{3,5},{4,2},{5,3},{6,8},{7,9},{8,6},{9,7},{10,12},{11,13},{1... | collective-permute-start | bytes 393224 | tf_op jit(solution)/shard_map/ppermute | solution.py:388
  5.8 0.1 norm.5.refs_3_.refs_0_
  5.9 0.7 %collective-permute-start.1 = (bf16[32,2048]{1,0:T(8,128)(2,1)S(1)}, bf16[32,2048]{1,0:T(8,128)(2,1)S(1)}, u32[]{:S(2)}, u32[]{:S(2)}) collective-permute-start(bf16[32,2048]{1,0:T(8,128)(2,1)S(1)} %norm.5.refs_3_.refs_0_), channel_id=1, source_target_pairs={{0,2},{1,3},{2,0},{3,1},{4,6},{5,7},{6,4},{7,5},{8,10},{9,11},{10,... | collective-permute-start | bytes 393224 | tf_op jit(solution)/shard_map/ppermute | solution.py:388
  6.6 1.4 %fixed.1 = (bf16[1,16,128,384]{3,2,1,0:T(8,128)(2,1)S(1)}, f32[2,64,128]{2,1,0:T(8,128)S(1)}, f32[2,32,128]{2,1,0:T(8,128)S(1)}) custom-call(bf16[1,16,128,384]{3,2,1,0:T(8,128)(2,1)} %refs_0_.1, s32[2,4]{1,0:T(2,128)} %refs_1_.1, s32[2,4]{1,0:T(2,128)} %refs_2_.1, bf16[32,2048]{1,0:T(8,128)(2,1)S(1)} %norm.5.refs_3_.refs_0_), custom_call_target="tpu_custom_call" | custom-call | flops 131072 | bytes 1572864 | tf_op jit(solution)/shard_map/fixed/pallas_call | solution.py:356
  8.0 0.4 %project.2 = (bf16[32,6144]{1,0:T(8,128)(2,1)S(1)}, bf16[32,6144]{1,0:T(8,128)(2,1)S(1)}) custom-call(bf16[1,16,128,384]{3,2,1,0:T(8,128)(2,1)S(1)} %get-tuple-element.23.weights_ref.refs_5_, bf16[32,2048]{1,0:T(8,128)(2,1)S(1)} %norm.5.refs_3_.refs_0_, bf16[32,2048]{1,0:T(8,128)(2,1)S(1)} %norm.4.refs_2_.refs_1_), custom_call_target="tpu_custom_call" | custom-call | flops 2000000000 | bytes 300000 | tf_op jit(solution)/shard_map/project/pallas_call | solution.py:322
  8.4 0.0 collective-permute-done.1.refs_11_
  8.5 0.0 collective-permute-done.refs_10_
  8.5 0.1 layer.2
  8.5 1.3 %collective-permute-start.2 = (bf16[32,2048]{1,0:T(8,128)(2,1)S(1)}, bf16[32,2048]{1,0:T(8,128)(2,1)S(1)}, u32[]{:S(2)}, u32[]{:S(2)}) collective-permute-start(bf16[32,2048]{1,0:T(8,128)(2,1)S(1)} %get-tuple-element.26.refs_0_.refs_6_), channel_id=1, source_target_pairs={{0,16},{1,17},{2,18},{3,19},{4,20},{5,21},{6,22},{7,23},{8,24},{9,... | collective-permute-start | bytes 393224 | tf_op jit(solution)/shard_map/ppermute | solution.py:388
  9.8 0.2 squares.1
  10.1 1.3 %collective-permute-start.4 = (f32[8,128]{1,0:T(8,128)S(1)}, f32[8,128]{1,0:T(8,128)S(1)}, u32[]{:S(2)}, u32[]{:S(2)}) collective-permute-start(f32[8,128]{1,0:T(8,128)S(1)} %squares.1), channel_id=1, source_target_pairs={{0,17},{1,16},{2,19},{3,18},{4,21},{5,20},{6,23},{7,22},{8,25},{9,... | collective-permute-start | bytes 12296 | tf_op jit(solution)/shard_map/ppermute | solution.py:388
  11.4 1.3 %collective-permute-start.7 = (f32[8,128]{1,0:T(8,128)S(1)}, f32[8,128]{1,0:T(8,128)S(1)}, u32[]{:S(2)}, u32[]{:S(2)}) collective-permute-start(f32[8,128]{1,0:T(8,128)S(1)} %squares.1), channel_id=1, source_target_pairs={{2,21},{3,20},{4,19},{5,18},{6,25},{7,24},{8,23},{9,22},{10,29},{1... | collective-permute-start | bytes 12296 | tf_op jit(solution)/shard_map/ppermute | solution.py:388
  12.7 1.3 %collective-permute-start.6 = (bf16[32,2048]{1,0:T(8,128)(2,1)S(1)}, bf16[32,2048]{1,0:T(8,128)(2,1)S(1)}, u32[]{:S(2)}, u32[]{:S(2)}) collective-permute-start(bf16[32,2048]{1,0:T(8,128)(2,1)S(1)} %get-tuple-element.27.refs_1_.refs_7_), channel_id=1, source_target_pairs={{2,20},{3,21},{4,18},{5,19},{6,24},{7,25},{8,22},{9,23},{10,28},{1... | collective-permute-start | bytes 393224 | tf_op jit(solution)/shard_map/ppermute | solution.py:388
  14.0 1.3 %collective-permute-start.3 = (bf16[32,2048]{1,0:T(8,128)(2,1)S(1)}, bf16[32,2048]{1,0:T(8,128)(2,1)S(1)}, u32[]{:S(2)}, u32[]{:S(2)}) collective-permute-start(bf16[32,2048]{1,0:T(8,128)(2,1)S(1)} %get-tuple-element.27.refs_1_.refs_7_), channel_id=1, source_target_pairs={{0,16},{1,17},{2,18},{3,19},{4,20},{5,21},{6,22},{7,23},{8,24},{9,... | collective-permute-start | bytes 393224 | tf_op jit(solution)/shard_map/ppermute | solution.py:388
  15.3 5.4 %collective-permute-done.4.refs_1_.refs_2_ = f32[8,128]{1,0:T(8,128)S(1)} collective-permute-done((f32[8,128]{1,0:T(8,128)S(1)}, f32[8,128]{1,0:T(8,128)S(1)}, u32[]{:S(2)}, u32[]{:S(2)}) %collective-permute-start.4) | collective-permute-done | bytes 4128 | tf_op jit(solution)/shard_map/ppermute | solution.py:388
  20.7 0.0 collective-permute-done.2.refs_0_
  20.7 0.3 norm.6.refs_0_
  20.9 3.3 %collective-permute-start.5 = (bf16[32,2048]{1,0:T(8,128)(2,1)S(1)}, bf16[32,2048]{1,0:T(8,128)(2,1)S(1)}, u32[]{:S(2)}, u32[]{:S(2)}) collective-permute-start(bf16[32,2048]{1,0:T(8,128)(2,1)S(1)} %norm.6.refs_0_), channel_id=1, source_target_pairs={{16,18},{17,19},{18,16},{19,17},{20,22},{21,23},{22,20},{23,21},{2... | collective-permute-start | bytes 393224 | tf_op jit(solution)/shard_map/ppermute | solution.py:388
  24.2 0.0 collective-permute-done.7.refs_1_
  24.2 0.5 %collective-permute-done.6.refs_0_ = bf16[32,2048]{1,0:T(8,128)(2,1)S(1)} collective-permute-done((bf16[32,2048]{1,0:T(8,128)(2,1)S(1)}, bf16[32,2048]{1,0:T(8,128)(2,1)S(1)}, u32[]{:S(2)}, u32[]{:S(2)}) %collective-permute-start.6) | collective-permute-done | bytes 131104 | tf_op jit(solution)/shard_map/ppermute | solution.py:388
  24.7 0.3 norm.7.refs_2_
  25.0 0.2 collective-permute-done.5.refs_1_
  25.2 0.5 %project.3 = (bf16[32,6144]{1,0:T(8,128)(2,1)S(1)}, bf16[32,6144]{1,0:T(8,128)(2,1)S(1)}, bf16[32,6144]{1,0:T(8,128)(2,1)S(1)}) custom-call(bf16[1,16,128,384]{3,2,1,0:T(8,128)(2,1)S(1)} %get-tuple-element.23.weights_ref.refs_5_, bf16[32,2048]{1,0:T(8,128)(2,1)S(1)} %norm.6.refs_0_, bf16[32,2048]{1,0:T(8,128)(2,1)S(1)} %collective-permute-done.5.refs_1_, ...), custom_call_target="tpu_custom_call" | custom-call | flops 2000000000 | bytes 300000 | tf_op jit(solution)/shard_map/project/pallas_call | solution.py:322
  25.7 1.3 %collective-permute-done.3.refs_1_ = bf16[32,2048]{1,0:T(8,128)(2,1)S(1)} collective-permute-done((bf16[32,2048]{1,0:T(8,128)(2,1)S(1)}, bf16[32,2048]{1,0:T(8,128)(2,1)S(1)}, u32[]{:S(2)}, u32[]{:S(2)}) %collective-permute-start.3) | collective-permute-done | bytes 131104 | tf_op jit(solution)/shard_map/ppermute | solution.py:388
  27.0 1.7 %layer.3 = bf16[1,2,8,4,2048]{4,3,2,1,0:T(4,128)(2,1)} custom-call(bf16[32,2048]{1,0:T(8,128)(2,1)S(1)} %collective-permute-done.2.refs_0_, bf16[32,2048]{1,0:T(8,128)(2,1)S(1)} %collective-permute-done.3.refs_1_, f32[8,128]{1,0:T(8,128)S(1)} %collective-permute-done.4.refs_1_.refs_2_, f32[2,64,128]{2,1,0:T(8,128)S(1)} %get-tuple-element.21.refs_3_, ...), custom_call_target="tpu_custom_call" | custom-call | flops 402653184 | bytes 4194304 | tf_op jit(solution)/shard_map/layer/pallas_call | solution.py:405
Async XLA Ops:
  5.1 3.3 %collective-permute-start = (bf16[32,2048]{1,0:T(8,128)(2,1)S(1)}, bf16[32,2048]{1,0:T(8,128)(2,1)S(1)}, u32[]{:S(2)}, u32[]{:S(2)}) collective-permute-start(bf16[32,2048]{1,0:T(8,128)(2,1)S(1)} %norm.4.refs_2_.refs_1_), channel_id=1, source_target_pairs={{2,4},{3,5},{4,2},{5,3},{6,8},{7,9},{8,6},{9,7},{10,12},{11,13},{1... | collective-permute-start | bytes 393224 | tf_op jit(solution)/shard_map/ppermute | solution.py:388
  5.9 2.5 %collective-permute-start.1 = (bf16[32,2048]{1,0:T(8,128)(2,1)S(1)}, bf16[32,2048]{1,0:T(8,128)(2,1)S(1)}, u32[]{:S(2)}, u32[]{:S(2)}) collective-permute-start(bf16[32,2048]{1,0:T(8,128)(2,1)S(1)} %norm.5.refs_3_.refs_0_), channel_id=1, source_target_pairs={{0,2},{1,3},{2,0},{3,1},{4,6},{5,7},{6,4},{7,5},{8,10},{9,11},{10,... | collective-permute-start | bytes 393224 | tf_op jit(solution)/shard_map/ppermute | solution.py:388
  8.5 12.1 %collective-permute-start.2 = (bf16[32,2048]{1,0:T(8,128)(2,1)S(1)}, bf16[32,2048]{1,0:T(8,128)(2,1)S(1)}, u32[]{:S(2)}, u32[]{:S(2)}) collective-permute-start(bf16[32,2048]{1,0:T(8,128)(2,1)S(1)} %get-tuple-element.26.refs_0_.refs_6_), channel_id=1, source_target_pairs={{0,16},{1,17},{2,18},{3,19},{4,20},{5,21},{6,22},{7,23},{8,24},{9,... | collective-permute-start | bytes 393224 | tf_op jit(solution)/shard_map/ppermute | solution.py:388
  10.1 10.6 %collective-permute-start.4 = (f32[8,128]{1,0:T(8,128)S(1)}, f32[8,128]{1,0:T(8,128)S(1)}, u32[]{:S(2)}, u32[]{:S(2)}) collective-permute-start(f32[8,128]{1,0:T(8,128)S(1)} %squares.1), channel_id=1, source_target_pairs={{0,17},{1,16},{2,19},{3,18},{4,21},{5,20},{6,23},{7,22},{8,25},{9,... | collective-permute-start | bytes 12296 | tf_op jit(solution)/shard_map/ppermute | solution.py:388
  11.4 12.9 %collective-permute-start.7 = (f32[8,128]{1,0:T(8,128)S(1)}, f32[8,128]{1,0:T(8,128)S(1)}, u32[]{:S(2)}, u32[]{:S(2)}) collective-permute-start(f32[8,128]{1,0:T(8,128)S(1)} %squares.1), channel_id=1, source_target_pairs={{2,21},{3,20},{4,19},{5,18},{6,25},{7,24},{8,23},{9,22},{10,29},{1... | collective-permute-start | bytes 12296 | tf_op jit(solution)/shard_map/ppermute | solution.py:388
  12.7 12.0 %collective-permute-start.6 = (bf16[32,2048]{1,0:T(8,128)(2,1)S(1)}, bf16[32,2048]{1,0:T(8,128)(2,1)S(1)}, u32[]{:S(2)}, u32[]{:S(2)}) collective-permute-start(bf16[32,2048]{1,0:T(8,128)(2,1)S(1)} %get-tuple-element.27.refs_1_.refs_7_), channel_id=1, source_target_pairs={{2,20},{3,21},{4,18},{5,19},{6,24},{7,25},{8,22},{9,23},{10,28},{1... | collective-permute-start | bytes 393224 | tf_op jit(solution)/shard_map/ppermute | solution.py:388
  14.0 13.1 %collective-permute-start.3 = (bf16[32,2048]{1,0:T(8,128)(2,1)S(1)}, bf16[32,2048]{1,0:T(8,128)(2,1)S(1)}, u32[]{:S(2)}, u32[]{:S(2)}) collective-permute-start(bf16[32,2048]{1,0:T(8,128)(2,1)S(1)} %get-tuple-element.27.refs_1_.refs_7_), channel_id=1, source_target_pairs={{0,16},{1,17},{2,18},{3,19},{4,20},{5,21},{6,22},{7,23},{8,24},{9,... | collective-permute-start | bytes 393224 | tf_op jit(solution)/shard_map/ppermute | solution.py:388
  20.9 4.2 %collective-permute-start.5 = (bf16[32,2048]{1,0:T(8,128)(2,1)S(1)}, bf16[32,2048]{1,0:T(8,128)(2,1)S(1)}, u32[]{:S(2)}, u32[]{:S(2)}) collective-permute-start(bf16[32,2048]{1,0:T(8,128)(2,1)S(1)} %norm.6.refs_0_), channel_id=1, source_target_pairs={{16,18},{17,19},{18,16},{19,17},{20,22},{21,23},{22,20},{23,21},{2... | collective-permute-start | bytes 393224 | tf_op jit(solution)/shard_map/ppermute | solution.py:388

commit v8 on v7

--- a/solution.py
+++ b/solution.py
@@ -13,7 +13,7 @@
 GROUP = 4
 EPS = 1e-06
 BIG = 1e30
-CHIP, FAR, NEXT_CHIP, NEXT_FAR = range(4)
+CHIP, FAR, NEXT_FAR, NEXT_CHIP = range(4)
 
 HBM = pl.BlockSpec(memory_space=pltpu.HBM)
 VMEM = pl.BlockSpec(memory_space=pltpu.VMEM)
@@ -81,12 +81,24 @@
         station_ref[m] = jnp.where(same_time & (recorded | same_station), 0.0, -BIG)[:own]
 
 
-def halves_kernel(signal_hbm, chip_ref, far_ref, squares_ref, signal_ref, arrived):
-    copy = pltpu.make_async_copy(signal_hbm, signal_ref, arrived)
-    copy.start()
+def first_kernel(
+    signal_hbm, weights_hbm, first_hbm, pad_hbm, chip_ref, far_ref, weights_ref, time_ref, station_ref,
+    signal_ref, first_ref, pad_ref, arrived, *, total_steps,
+):
+    copies = [
+        pltpu.make_async_copy(signal_hbm, signal_ref, arrived.at[0]),
+        pltpu.make_async_copy(first_hbm, first_ref, arrived.at[1]),
+        pltpu.make_async_copy(pad_hbm, pad_ref, arrived.at[2]),
+        pltpu.make_async_copy(weights_hbm, weights_ref, arrived.at[3]),
+    ]
+    for copy in copies:
+        copy.start()
     micro, _, stations, _ = signal_ref.shape
     edge = WIN * stations
-    copy.wait()
+    copies[1].wait()
+    copies[2].wait()
+    fill_masks(first_ref, pad_ref, time_ref, station_ref, stations, total_steps)
+    copies[0].wait()
     for half, half_ref in ((FAR, far_ref), (CHIP, chip_ref)):
         start = first_step(half)
         for m in range(micro):
@@ -96,24 +108,7 @@
                 half_ref[at : at + 2 * stations, :] = jnp.concatenate(pair, axis=0).astype(
                     jnp.bfloat16
                 )
-    squares_kernel(chip_ref, far_ref, squares_ref)
-
-
-def fixed_kernel(
-    weights_hbm, first_hbm, pad_hbm, _, weights_ref, time_ref, station_ref,
-    first_ref, pad_ref, arrived, *, stations, total_steps,
-):
-    copies = [
-        pltpu.make_async_copy(first_hbm, first_ref, arrived.at[0]),
-        pltpu.make_async_copy(pad_hbm, pad_ref, arrived.at[1]),
-        pltpu.make_async_copy(weights_hbm, weights_ref, arrived.at[2]),
-    ]
-    for copy in copies:
-        copy.start()
-    copies[0].wait()
-    copies[1].wait()
-    fill_masks(first_ref, pad_ref, time_ref, station_ref, stations, total_steps)
-    copies[2].wait()
+    copies[3].wait()
 
 
 def squares_kernel(*refs):
@@ -130,16 +125,21 @@
     return (rows.astype(jnp.float32) * column).astype(jnp.bfloat16)
 
 
-def first_norm_kernel(half_ref, squares_ref, *refs, line):
-    rows = half_ref[...]
-    refs[-1][...] = scaled(rows, squares_ref[line : line + 1, 0 : rows.shape[0]])
-
-
 def norm_kernel(half_ref, squares_ref, normed_ref, *, line):
     rows = half_ref[...]
     normed_ref[...] = scaled(
         rows, squares_row(rows) + squares_ref[line : line + 1, 0 : rows.shape[0]]
     )
+
+
+def copy_kernel(squares_ref, half_ref, squares_out_ref, half_out_ref):
+    squares_out_ref[...] = squares_ref[...]
+    half_out_ref[...] = half_ref[...]
+
+
+def add_kernel(mine_ref, other_ref, out_ref):
+    out_ref[...] = jnp.zeros(out_ref.shape, jnp.float32)
+    out_ref[0:1, :] = mine_ref[0:1, :] + other_ref[FAR : FAR + 1, :]
 
 
 def project_kernel(weights_ref, *refs):
@@ -174,55 +174,51 @@
     width = 3 * HEAD
     bf16, f32 = jnp.bfloat16, jnp.float32
     active = lax.axis_index("section") == tick
+    projected = [None] * 4
     if tick == 0:
-        projected_chip, projected_far, next_far_ref, next_chip_ref, *refs = refs
+        next_chip_ref, next_far_ref, *refs = refs
+        late = [
+            (half, half_ref, squares_ref[half : half + 1, :], True)
+            for half, half_ref in enumerate((chip_ref, far_ref, next_far_ref, next_chip_ref))
+        ]
     else:
-        projected_chip, projected_next_chip, projected_next_far, *refs = refs
-    if last:
-        out_ref, *refs = refs
-    else:
-        out_chip_ref, out_far_ref, *refs = refs
-    if tick == 0:
-        projected_next_chip, projected_next_far = refs
-    else:
-        (projected_far,) = refs
-    projected = (projected_chip, projected_far, projected_next_chip, projected_next_far)
+        next_far_ref, far_squares_ref, projected[CHIP], projected[NEXT_CHIP], *refs = refs
+        late = [
+            (FAR, far_ref, squares_ref[FAR : FAR + 1, :], False),
+            (NEXT_FAR, next_far_ref, far_squares_ref[0:1, :], True),
+        ]
+    outs, refs = (refs[:1], refs[1:]) if last else (refs[:2], refs[2:])
+    normed = refs[: len(late)]
+    for (half, *_), half_ref in zip(late, refs[len(late) :]):
+        projected[half] = half_ref
 
     def write(m, lanes, values):
         for half in (CHIP, FAR):
             part = values[half * edge : (half + 1) * edge].astype(bf16)
             if last:
                 for t in range(WIN):
-                    out_ref[0, m, first_step(half) + t, :, lanes] = part[
+                    outs[0][0, m, first_step(half) + t, :, lanes] = part[
                         t * stations : (t + 1) * stations
                     ]
             else:
-                half_ref = (out_chip_ref, out_far_ref)[half]
-                half_ref[m * edge : (m + 1) * edge, lanes] = part
+                outs[half][m * edge : (m + 1) * edge, lanes] = part
 
     def rows_of(halves, m, at):
         return [projected[half][m * edge : (m + 1) * edge, at : at + HEAD] for half in halves]
 
     @pl.when(active)
     def _():
-        if tick == 0:
-            project_kernel(
-                weights_ref, next_chip_ref, next_far_ref, projected_next_chip, projected_next_far
-            )
-        else:
-            lane = lax.broadcasted_iota(jnp.int32, (micro * edge, 128), 1)
-            row = lax.broadcasted_iota(jnp.int32, (micro * edge, 128), 0)
-            total = jnp.where(lane == row, squares_ref[FAR : FAR + 1, :], 0.0)
-            for head in range(heads_dev):
-                part = far_ref[:, head * HEAD : (head + 1) * HEAD].astype(f32)
-                total = total + part * part
+        lane = lax.broadcasted_iota(jnp.int32, (micro * edge, 128), 1)
+        row = lax.broadcasted_iota(jnp.int32, (micro * edge, 128), 0)
+        for (_, half_ref, line, complete), normed_ref in zip(late, normed):
+            total = jnp.where(lane == row, line, 0.0)
+            if not complete:
+                for head in range(heads_dev):
+                    part = half_ref[:, head * HEAD : (head + 1) * HEAD].astype(f32)
+                    total = total + part * part
             factor = lax.rsqrt(jnp.sum(total, axis=1, keepdims=True) / (HEADS * HEAD) + EPS)
-            for head in range(heads_dev):
-                projected_far[:, head * width : (head + 1) * width] = jnp.dot(
-                    (far_ref[:, head * HEAD : (head + 1) * HEAD].astype(f32) * factor).astype(bf16),
-                    weights_ref[0, head],
-                    preferred_element_type=f32,
-                ).astype(bf16)
+            normed_ref[...] = (half_ref[...].astype(f32) * factor).astype(bf16)
+        project_kernel(weights_ref, *normed, *[projected[half] for half, *_ in late])
         pairs = [(g, m) for g in range(heads_dev // GROUP) for m in range(micro)]
         blank = jnp.zeros((own, HEAD), bf16)
         scores = []
@@ -329,48 +325,27 @@
             name="project",
         )(weights, *halves)
 
-    chip, far, squares = pl.pallas_call(
-        halves_kernel,
-        in_specs=[HBM],
-        out_specs=[VMEM] * 3,
-        out_shape=[half_shape, half_shape, squares_shape],
-        scratch_shapes=[pltpu.VMEM(signal.shape, bf16), pltpu.SemaphoreType.DMA],
-        compiler_params=PARAMS,
-        cost_estimate=cost(signal.size, 2 * signal_bytes),
-        name="halves",
-    )(in_hbm(signal))
-    squares = lax.psum(squares, "rep")
-    def first_normed(line, *operands):
-        return pl.pallas_call(
-            lambda *refs: first_norm_kernel(*refs, line=line),
-            in_specs=[VMEM] * len(operands),
-            out_specs=VMEM,
-            out_shape=half_shape,
-            compiler_params=PARAMS,
-            cost_estimate=BUSY,
-            name="norm",
-        )(*operands)
-
-    normed_far = first_normed(FAR, far, squares)
-    normed_chip = first_normed(CHIP, chip, squares, normed_far)
-    weights, time_bias, station_bias = pl.pallas_call(
-        lambda *refs: fixed_kernel(*refs, stations=stations, total_steps=steps * seq_count),
-        in_specs=[HBM] * 3 + [VMEM],
-        out_specs=[VMEM] * 3,
+    chip, far, weights, time_bias, station_bias = pl.pallas_call(
+        lambda *refs: first_kernel(*refs, total_steps=steps * seq_count),
+        in_specs=[HBM] * 4,
+        out_specs=[VMEM] * 5,
         out_shape=[
+            half_shape,
+            half_shape,
             jax.ShapeDtypeStruct(head_proj.shape, bf16),
             jax.ShapeDtypeStruct((micro, reach, GROUP * own), f32),
             jax.ShapeDtypeStruct((micro, own, GROUP * own), f32),
         ],
         scratch_shapes=[
+            pltpu.VMEM(signal.shape, bf16),
             pltpu.SMEM(record_start.shape, jnp.int32),
             pltpu.SMEM(record_pad.shape, jnp.int32),
-            pltpu.SemaphoreType.DMA((3,)),
+            pltpu.SemaphoreType.DMA((4,)),
         ],
         compiler_params=PARAMS,
         cost_estimate=cost(signal.size, 2 * head_proj.size),
-        name="fixed",
-    )(in_hbm(head_proj), in_hbm(record_start), in_hbm(record_pad), normed_chip)
+        name="first",
+    )(in_hbm(signal), in_hbm(head_proj), in_hbm(record_start), in_hbm(record_pad))
 
     def moved(block, source, target, hop, other=False):
         route = []
@@ -387,9 +362,10 @@
                     )
         return lax.ppermute(block, ("section", "seq", "rep"), route)
 
-    next_far = moved(normed_far, 0, 0, 2)
-    next_chip = moved(normed_chip, 0, 0, 1)
-    inputs = (*project(normed_chip, normed_far), next_far, next_chip)
+    next_far = moved(far, 0, 0, 2)
+    next_chip = moved(chip, 0, 0, 1)
+    squares = lax.psum(squares_of(chip, far, next_far, next_chip), "rep")
+    inputs = (next_chip, next_far)
     kept = (chip, far)
     for tick in range(section_count):
         last = tick + 1 == section_count
@@ -407,7 +383,11 @@
             in_specs=[VMEM] * (8 + len(inputs)),
             out_specs=[VMEM] * len(out_shape),
             out_shape=out_shape,
-            scratch_shapes=[pltpu.VMEM(projected_shape.shape, bf16)] * (2 if tick == 0 else 1),
+            scratch_shapes=[
+                pltpu.VMEM(shape.shape, bf16)
+                for shape in (half_shape, projected_shape)
+                for _ in range(4 if tick == 0 else 2)
+            ],
             compiler_params=PARAMS,
             cost_estimate=cost(8 * signal.size * 3 * HEAD, 16 * signal_bytes),
             name="layer",
@@ -420,13 +400,30 @@
         mine = squares_of(*kept)
         chip = moved(kept[0], tick, tick + 1, 0)
         next_far = moved(kept[1], tick, tick + 1, 2)
-        far = moved(kept[1], tick, tick + 1, 0)
         squares = moved(mine, tick, tick + 1, 0, other=True)
-        far_squares = moved(mine, tick, tick + 1, 2, other=True)
+        mine_again, far_again = pl.pallas_call(
+            copy_kernel,
+            in_specs=[VMEM] * 2,
+            out_specs=[VMEM] * 2,
+            out_shape=[squares_shape, half_shape],
+            compiler_params=PARAMS,
+            cost_estimate=BUSY,
+            name="copy",
+        )(mine, kept[1])
+        far = moved(far_again, tick, tick + 1, 0)
+        far_squares = moved(mine_again, tick, tick + 1, 2, other=True)
         normed_chip = normed(chip, squares, CHIP)
         next_chip = moved(normed_chip, tick + 1, tick + 1, 1)
-        next_far = normed(next_far, far_squares, FAR)
-        inputs = project(normed_chip, next_chip, next_far)
+        far_squares = pl.pallas_call(
+            add_kernel,
+            in_specs=[VMEM] * 2,
+            out_specs=VMEM,
+            out_shape=squares_shape,
+            compiler_params=PARAMS,
+            cost_estimate=BUSY,
+            name="add",
+        )(squares_of(next_far), far_squares)
+        inputs = (next_far, far_squares, *project(normed_chip, next_chip))
 
 
 def solution(mesh):

time: 29.3 us -> 28.2 us (0.962)
  starting transfers between devices: 11.1 us -> 13.2 us
  Pallas kernels: 6.31 us -> 4.72 us
  waiting for transfers between devices: 7.42 us -> 5.92 us
    ppermute x8, starting transfers between devices: 11.1 us -> 13.2 us  [moved(): return lax.ppermute(block, ('section', 'seq', 'rep'), route)]
    ppermute x8, waiting for transfers between devices: 7.42 us -> 5.92 us  [moved(): return lax.ppermute(block, ('section', 'seq', 'rep'), route)]
    pallas_call x4 -> x3, Pallas kernels: 2.84 us -> 1.55 us  [the longest x1 1.54 us: body(): pl.pallas_call(lambda *refs: first_kernel(*refs, total_steps=steps * seq_...]
    pallas_call x2 -> x1, Pallas kernels: 0.91 us -> 0.42 us  [project(): pl.pallas_call(project_kernel, in_specs=[VMEM] * (1 + len(halves)), out_s...]
    pallas_call x1 -> x3, Pallas kernels: 0.21 us -> 0.66 us  [squares_of(): pl.pallas_call(squares_kernel, in_specs=[VMEM] * len(halves), out_specs=V...]
  transfers between devices with their start and end apart: 8 -> 8, of which waited for: 4 -> 3; matrix products, arithmetic and copies ran while one was open for 0% -> 0% of each run, Pallas kernels for 11% -> 4%
where the time goes in v8:
time: 28.2 us; the launch traced here: 27.8 us
  starting transfers between devices  13.2 us (47%)
  waiting for transfers between devices  5.92 us (21%)
  Pallas kernels  4.72 us (17%)
  blocking collectives  3.8 us (13%)
    ppermute x8, starting transfers between devices, moved(): return lax.ppermute(block, ('section', 'seq', 'rep'), route)  13.2 us
    ppermute x8, waiting for transfers between devices, moved(): return lax.ppermute(block, ('section', 'seq', 'rep'), route)  5.92 us
    psum x1, blocking collectives, body(): squares = lax.psum(squares_of(chip, far, next_far, next_chip), 'rep')  3.8 us
    pallas_call x2, Pallas kernels, body(): pl.pallas_call(kernel, in_specs=[VMEM] * (8 + len(inputs)), out_specs=[VM...  1.8 us
    pallas_call x1, Pallas kernels, body(): pl.pallas_call(lambda *refs: first_kernel(*refs, total_steps=steps * seq_...  1.54 us
    pallas_call x3, Pallas kernels, squares_of(): pl.pallas_call(squares_kernel, in_specs=[VMEM] * len(halves), out_specs=V...  0.66 us
  transfers between devices with their start and end apart: 8, of which 3 were waited for; matrix products, arithmetic and copies ran while one was open for 0% of the time, Pallas kernels for 4%

profile of v8, /device:TPU:11, one launch (start us, length us, event | category | flops | bytes accessed | tf_op | source)
XLA Modules:
  0.0 27.8 jit_solution(8679730406958637654)
XLA Ops:
  0.0 1.5 %first.1 = (bf16[32,2048]{1,0:T(8,128)(2,1)S(1)}, bf16[32,2048]{1,0:T(8,128)(2,1)S(1)}, bf16[1,16,128,384]{3,2,1,0:T(8,128)(2,1)S(1)}, f32[2,64,128]{2,1,0:T(8,128)S(1)}, f32[2,32,128]{2,1,0:T(8,128)S(1)}) custom-call(bf16[2,8,4,2048]{3,2,1,0:T(4,128)(2,1)} %refs_0_.1, bf16[1,16,128,384]{3,2,1,0:T(8,128)(2,1)} %refs_1_.1, s32[2,4]{1,0:T(2,128)} %refs_2_.1, ...), custom_call_target="tpu_custom_call" | custom-call | flops 131072 | bytes 1572864 | tf_op jit(solution)/shard_map/first/pallas_call | solution.py:328
  1.5 0.7 %collective-permute-start = (bf16[32,2048]{1,0:T(8,128)(2,1)S(1)}, bf16[32,2048]{1,0:T(8,128)(2,1)S(1)}, u32[]{:S(2)}, u32[]{:S(2)}) collective-permute-start(bf16[32,2048]{1,0:T(8,128)(2,1)S(1)} %get-tuple-element.17.refs_1_.refs_7_), channel_id=1, source_target_pairs={{2,4},{3,5},{4,2},{5,3},{6,8},{7,9},{8,6},{9,7},{10,12},{11,13},{1... | collective-permute-start | bytes 393224 | tf_op jit(solution)/shard_map/ppermute | solution.py:363
  2.2 0.7 %collective-permute-start.1 = (bf16[32,2048]{1,0:T(8,128)(2,1)S(1)}, bf16[32,2048]{1,0:T(8,128)(2,1)S(1)}, u32[]{:S(2)}, u32[]{:S(2)}) collective-permute-start(bf16[32,2048]{1,0:T(8,128)(2,1)S(1)} %get-tuple-element.16.refs_0_.refs_6_), channel_id=1, source_target_pairs={{0,2},{1,3},{2,0},{3,1},{4,6},{5,7},{6,4},{7,5},{8,10},{9,11},{10,... | collective-permute-start | bytes 393224 | tf_op jit(solution)/shard_map/ppermute | solution.py:363
  2.9 0.0 collective-permute-done.refs_2_.refs_9_
  2.9 0.0 collective-permute-done.1.refs_3_.refs_8_
  2.9 0.3 %squares.3 = f32[8,128]{1,0:T(8,128)S(1)} custom-call(bf16[32,2048]{1,0:T(8,128)(2,1)S(1)} %get-tuple-element.16.refs_0_.refs_6_, bf16[32,2048]{1,0:T(8,128)(2,1)S(1)} %get-tuple-element.17.refs_1_.refs_7_, bf16[32,2048]{1,0:T(8,128)(2,1)S(1)} %collective-permute-done.refs_2_.refs_9_, bf16[32,2048]{1,0:T(8,128)(2,1)S(1)} %collective-permute-done.1.refs_3_.refs_8_), custom_call_target="tpu_custom_call" | custom-call | tf_op jit(solution)/shard_map/squares/pallas_call | solution.py:297
  3.2 3.8 %psum.7.refs_2_ = f32[8,128]{1,0:T(8,128)S(1)} all-reduce(f32[8,128]{1,0:T(8,128)S(1)} %squares.3), channel_id=1, replica_groups=mesh['section'=2,'seq'=8,'rep'=2] {'rep'}, use_global_device_ids=true, to_apply=%region_0.0 | all-reduce | flops 1024 | bytes 8192 | tf_op jit(solution)/shard_map/psum | solution.py:367
  7.0 0.1 layer.2
  7.1 1.3 %collective-permute-start.2 = (bf16[32,2048]{1,0:T(8,128)(2,1)S(1)}, bf16[32,2048]{1,0:T(8,128)(2,1)S(1)}, u32[]{:S(2)}, u32[]{:S(2)}) collective-permute-start(bf16[32,2048]{1,0:T(8,128)(2,1)S(1)} %get-tuple-element.21.refs_0_.refs_6_), channel_id=1, source_target_pairs={{0,16},{1,17},{2,18},{3,19},{4,20},{5,21},{6,22},{7,23},{8,24},{9,... | collective-permute-start | bytes 393224 | tf_op jit(solution)/shard_map/ppermute | solution.py:363
  8.4 0.2 squares.4.squares_ref
  8.6 1.3 %collective-permute-start.4 = (f32[8,128]{1,0:T(8,128)S(1)}, f32[8,128]{1,0:T(8,128)S(1)}, u32[]{:S(2)}, u32[]{:S(2)}) collective-permute-start(f32[8,128]{1,0:T(8,128)S(1)} %squares.4.squares_ref), channel_id=1, source_target_pairs={{0,17},{1,16},{2,19},{3,18},{4,21},{5,20},{6,23},{7,22},{8,25},{9,... | collective-permute-start | bytes 12296 | tf_op jit(solution)/shard_map/ppermute | solution.py:363
  9.9 1.3 %collective-permute-start.5 = (bf16[32,2048]{1,0:T(8,128)(2,1)S(1)}, bf16[32,2048]{1,0:T(8,128)(2,1)S(1)}, u32[]{:S(2)}, u32[]{:S(2)}) collective-permute-start(bf16[32,2048]{1,0:T(8,128)(2,1)S(1)} %get-tuple-element.22.refs_1_.half_ref.refs_7_), channel_id=1, source_target_pairs={{2,20},{3,21},{4,18},{5,19},{6,24},{7,25},{8,22},{9,23},{10,28},{1... | collective-permute-start | bytes 393224 | tf_op jit(solution)/shard_map/ppermute | solution.py:363
  11.2 1.3 %collective-permute-start.6 = (f32[8,128]{1,0:T(8,128)S(1)}, f32[8,128]{1,0:T(8,128)S(1)}, u32[]{:S(2)}, u32[]{:S(2)}) collective-permute-start(f32[8,128]{1,0:T(8,128)S(1)} %get-tuple-element.24), channel_id=1, source_target_pairs={{2,21},{3,20},{4,19},{5,18},{6,25},{7,24},{8,23},{9,22},{10,29},{1... | collective-permute-start | bytes 12296 | tf_op jit(solution)/shard_map/ppermute | solution.py:363
  12.5 1.3 %collective-permute-start.3 = (bf16[32,2048]{1,0:T(8,128)(2,1)S(1)}, bf16[32,2048]{1,0:T(8,128)(2,1)S(1)}, u32[]{:S(2)}, u32[]{:S(2)}) collective-permute-start(bf16[32,2048]{1,0:T(8,128)(2,1)S(1)} %get-tuple-element.23), channel_id=1, source_target_pairs={{0,16},{1,17},{2,18},{3,19},{4,20},{5,21},{6,22},{7,23},{8,24},{9,... | collective-permute-start | bytes 393224 | tf_op jit(solution)/shard_map/ppermute | solution.py:363
  13.8 5.1 %collective-permute-done.4.refs_1_.refs_2_ = f32[8,128]{1,0:T(8,128)S(1)} collective-permute-done((f32[8,128]{1,0:T(8,128)S(1)}, f32[8,128]{1,0:T(8,128)S(1)}, u32[]{:S(2)}, u32[]{:S(2)}) %collective-permute-start.4) | collective-permute-done | bytes 4128 | tf_op jit(solution)/shard_map/ppermute | solution.py:363
  18.9 0.0 collective-permute-done.2.refs_0_
  18.9 0.3 %norm.1.refs_0_ = bf16[32,2048]{1,0:T(8,128)(2,1)S(1)} custom-call(bf16[32,2048]{1,0:T(8,128)(2,1)S(1)} %collective-permute-done.2.refs_0_, f32[8,128]{1,0:T(8,128)S(1)} %collective-permute-done.4.refs_1_.refs_2_), custom_call_target="tpu_custom_call" | custom-call | flops 2000000000 | bytes 300000 | tf_op jit(solution)/shard_map/norm/pallas_call | solution.py:307
  19.2 5.4 %collective-permute-start.7 = (bf16[32,2048]{1,0:T(8,128)(2,1)S(1)}, bf16[32,2048]{1,0:T(8,128)(2,1)S(1)}, u32[]{:S(2)}, u32[]{:S(2)}) collective-permute-start(bf16[32,2048]{1,0:T(8,128)(2,1)S(1)} %norm.1.refs_0_), channel_id=1, source_target_pairs={{16,18},{17,19},{18,16},{19,17},{20,22},{21,23},{22,20},{23,21},{2... | collective-permute-start | bytes 393224 | tf_op jit(solution)/shard_map/ppermute | solution.py:363
  24.6 0.0 collective-permute-done.5.refs_0_.refs_8_
  24.6 0.2 squares.5.mine_ref
  24.8 0.0 collective-permute-done.6.other_ref
  24.8 0.8 %collective-permute-done.7.refs_1_ = bf16[32,2048]{1,0:T(8,128)(2,1)S(1)} collective-permute-done((bf16[32,2048]{1,0:T(8,128)(2,1)S(1)}, bf16[32,2048]{1,0:T(8,128)(2,1)S(1)}, u32[]{:S(2)}, u32[]{:S(2)}) %collective-permute-start.7) | collective-permute-done | bytes 131104 | tf_op jit(solution)/shard_map/ppermute | solution.py:363
  25.6 0.4 %project.1 = (bf16[32,6144]{1,0:T(8,128)(2,1)S(1)}, bf16[32,6144]{1,0:T(8,128)(2,1)S(1)}) custom-call(bf16[1,16,128,384]{3,2,1,0:T(8,128)(2,1)S(1)} %get-tuple-element.20.refs_5_.weights_ref, bf16[32,2048]{1,0:T(8,128)(2,1)S(1)} %norm.1.refs_0_, bf16[32,2048]{1,0:T(8,128)(2,1)S(1)} %collective-permute-done.7.refs_1_), custom_call_target="tpu_custom_call" | custom-call | flops 2000000000 | bytes 300000 | tf_op jit(solution)/shard_map/project/pallas_call | solution.py:318
  26.0 0.1 collective-permute-done.3.refs_1_
  26.1 1.7 %layer.3 = bf16[1,2,8,4,2048]{4,3,2,1,0:T(4,128)(2,1)} custom-call(bf16[32,2048]{1,0:T(8,128)(2,1)S(1)} %collective-permute-done.2.refs_0_, bf16[32,2048]{1,0:T(8,128)(2,1)S(1)} %collective-permute-done.3.refs_1_, f32[8,128]{1,0:T(8,128)S(1)} %collective-permute-done.4.refs_1_.refs_2_, f32[2,64,128]{2,1,0:T(8,128)S(1)} %get-tuple-element.18.refs_3_, ...), custom_call_target="tpu_custom_call" | custom-call | flops 402653184 | bytes 4194304 | tf_op jit(solution)/shard_map/layer/pallas_call | solution.py:381
  (2 shorter events, 0.0 us)
Async XLA Ops:
  1.5 1.4 %collective-permute-start = (bf16[32,2048]{1,0:T(8,128)(2,1)S(1)}, bf16[32,2048]{1,0:T(8,128)(2,1)S(1)}, u32[]{:S(2)}, u32[]{:S(2)}) collective-permute-start(bf16[32,2048]{1,0:T(8,128)(2,1)S(1)} %get-tuple-element.17.refs_1_.refs_7_), channel_id=1, source_target_pairs={{2,4},{3,5},{4,2},{5,3},{6,8},{7,9},{8,6},{9,7},{10,12},{11,13},{1... | collective-permute-start | bytes 393224 | tf_op jit(solution)/shard_map/ppermute | solution.py:363
  2.2 0.7 %collective-permute-start.1 = (bf16[32,2048]{1,0:T(8,128)(2,1)S(1)}, bf16[32,2048]{1,0:T(8,128)(2,1)S(1)}, u32[]{:S(2)}, u32[]{:S(2)}) collective-permute-start(bf16[32,2048]{1,0:T(8,128)(2,1)S(1)} %get-tuple-element.16.refs_0_.refs_6_), channel_id=1, source_target_pairs={{0,2},{1,3},{2,0},{3,1},{4,6},{5,7},{6,4},{7,5},{8,10},{9,11},{10,... | collective-permute-start | bytes 393224 | tf_op jit(solution)/shard_map/ppermute | solution.py:363
  7.1 11.8 %collective-permute-start.2 = (bf16[32,2048]{1,0:T(8,128)(2,1)S(1)}, bf16[32,2048]{1,0:T(8,128)(2,1)S(1)}, u32[]{:S(2)}, u32[]{:S(2)}) collective-permute-start(bf16[32,2048]{1,0:T(8,128)(2,1)S(1)} %get-tuple-element.21.refs_0_.refs_6_), channel_id=1, source_target_pairs={{0,16},{1,17},{2,18},{3,19},{4,20},{5,21},{6,22},{7,23},{8,24},{9,... | collective-permute-start | bytes 393224 | tf_op jit(solution)/shard_map/ppermute | solution.py:363
  8.6 10.3 %collective-permute-start.4 = (f32[8,128]{1,0:T(8,128)S(1)}, f32[8,128]{1,0:T(8,128)S(1)}, u32[]{:S(2)}, u32[]{:S(2)}) collective-permute-start(f32[8,128]{1,0:T(8,128)S(1)} %squares.4.squares_ref), channel_id=1, source_target_pairs={{0,17},{1,16},{2,19},{3,18},{4,21},{5,20},{6,23},{7,22},{8,25},{9,... | collective-permute-start | bytes 12296 | tf_op jit(solution)/shard_map/ppermute | solution.py:363
  9.9 14.7 %collective-permute-start.5 = (bf16[32,2048]{1,0:T(8,128)(2,1)S(1)}, bf16[32,2048]{1,0:T(8,128)(2,1)S(1)}, u32[]{:S(2)}, u32[]{:S(2)}) collective-permute-start(bf16[32,2048]{1,0:T(8,128)(2,1)S(1)} %get-tuple-element.22.refs_1_.half_ref.refs_7_), channel_id=1, source_target_pairs={{2,20},{3,21},{4,18},{5,19},{6,24},{7,25},{8,22},{9,23},{10,28},{1... | collective-permute-start | bytes 393224 | tf_op jit(solution)/shard_map/ppermute | solution.py:363
  11.2 13.6 %collective-permute-start.6 = (f32[8,128]{1,0:T(8,128)S(1)}, f32[8,128]{1,0:T(8,128)S(1)}, u32[]{:S(2)}, u32[]{:S(2)}) collective-permute-start(f32[8,128]{1,0:T(8,128)S(1)} %get-tuple-element.24), channel_id=1, source_target_pairs={{2,21},{3,20},{4,19},{5,18},{6,25},{7,24},{8,23},{9,22},{10,29},{1... | collective-permute-start | bytes 12296 | tf_op jit(solution)/shard_map/ppermute | solution.py:363
  12.5 13.6 %collective-permute-start.3 = (bf16[32,2048]{1,0:T(8,128)(2,1)S(1)}, bf16[32,2048]{1,0:T(8,128)(2,1)S(1)}, u32[]{:S(2)}, u32[]{:S(2)}) collective-permute-start(bf16[32,2048]{1,0:T(8,128)(2,1)S(1)} %get-tuple-element.23), channel_id=1, source_target_pairs={{0,16},{1,17},{2,18},{3,19},{4,20},{5,21},{6,22},{7,23},{8,24},{9,... | collective-permute-start | bytes 393224 | tf_op jit(solution)/shard_map/ppermute | solution.py:363
  19.2 6.4 %collective-permute-start.7 = (bf16[32,2048]{1,0:T(8,128)(2,1)S(1)}, bf16[32,2048]{1,0:T(8,128)(2,1)S(1)}, u32[]{:S(2)}, u32[]{:S(2)}) collective-permute-start(bf16[32,2048]{1,0:T(8,128)(2,1)S(1)} %norm.1.refs_0_), channel_id=1, source_target_pairs={{16,18},{17,19},{18,16},{19,17},{20,22},{21,23},{22,20},{23,21},{2... | collective-permute-start | bytes 393224 | tf_op jit(solution)/shard_map/ppermute | solution.py:363

commit v9 on v8

--- a/solution.py
+++ b/solution.py
@@ -81,24 +81,12 @@
         station_ref[m] = jnp.where(same_time & (recorded | same_station), 0.0, -BIG)[:own]
 
 
-def first_kernel(
-    signal_hbm, weights_hbm, first_hbm, pad_hbm, chip_ref, far_ref, weights_ref, time_ref, station_ref,
-    signal_ref, first_ref, pad_ref, arrived, *, total_steps,
-):
-    copies = [
-        pltpu.make_async_copy(signal_hbm, signal_ref, arrived.at[0]),
-        pltpu.make_async_copy(first_hbm, first_ref, arrived.at[1]),
-        pltpu.make_async_copy(pad_hbm, pad_ref, arrived.at[2]),
-        pltpu.make_async_copy(weights_hbm, weights_ref, arrived.at[3]),
-    ]
-    for copy in copies:
-        copy.start()
+def halves_kernel(signal_hbm, chip_ref, far_ref, signal_ref, arrived):
+    copy = pltpu.make_async_copy(signal_hbm, signal_ref, arrived)
+    copy.start()
     micro, _, stations, _ = signal_ref.shape
     edge = WIN * stations
-    copies[1].wait()
-    copies[2].wait()
-    fill_masks(first_ref, pad_ref, time_ref, station_ref, stations, total_steps)
-    copies[0].wait()
+    copy.wait()
     for half, half_ref in ((FAR, far_ref), (CHIP, chip_ref)):
         start = first_step(half)
         for m in range(micro):
@@ -108,7 +96,23 @@
                 half_ref[at : at + 2 * stations, :] = jnp.concatenate(pair, axis=0).astype(
                     jnp.bfloat16
                 )
-    copies[3].wait()
+
+
+def fixed_kernel(
+    weights_hbm, first_hbm, pad_hbm, _, weights_ref, time_ref, station_ref,
+    first_ref, pad_ref, arrived, *, stations, total_steps,
+):
+    copies = [
+        pltpu.make_async_copy(first_hbm, first_ref, arrived.at[0]),
+        pltpu.make_async_copy(pad_hbm, pad_ref, arrived.at[1]),
+        pltpu.make_async_copy(weights_hbm, weights_ref, arrived.at[2]),
+    ]
+    for copy in copies:
+        copy.start()
+    copies[0].wait()
+    copies[1].wait()
+    fill_masks(first_ref, pad_ref, time_ref, station_ref, stations, total_steps)
+    copies[2].wait()
 
 
 def squares_kernel(*refs):
@@ -132,9 +136,10 @@
     )
 
 
-def copy_kernel(squares_ref, half_ref, squares_out_ref, half_out_ref):
-    squares_out_ref[...] = squares_ref[...]
-    half_out_ref[...] = half_ref[...]
+def copy_kernel(*refs):
+    count = len(refs) // 2
+    for source, target in zip(refs[:count], refs[count:]):
+        target[...] = source[...]
 
 
 def add_kernel(mine_ref, other_ref, out_ref):
@@ -176,7 +181,7 @@
     active = lax.axis_index("section") == tick
     projected = [None] * 4
     if tick == 0:
-        next_chip_ref, next_far_ref, *refs = refs
+        next_far_ref, next_chip_ref, *refs = refs
         late = [
             (half, half_ref, squares_ref[half : half + 1, :], True)
             for half, half_ref in enumerate((chip_ref, far_ref, next_far_ref, next_chip_ref))
@@ -314,6 +319,17 @@
             name="norm",
         )(rows, squares)
 
+    def again(*blocks):
+        return pl.pallas_call(
+            copy_kernel,
+            in_specs=[VMEM] * len(blocks),
+            out_specs=[VMEM] * len(blocks),
+            out_shape=[jax.ShapeDtypeStruct(block.shape, block.dtype) for block in blocks],
+            compiler_params=PARAMS,
+            cost_estimate=BUSY,
+            name="copy",
+        )(*blocks)
+
     def project(*halves):
         return pl.pallas_call(
             project_kernel,
@@ -325,27 +341,34 @@
             name="project",
         )(weights, *halves)
 
-    chip, far, weights, time_bias, station_bias = pl.pallas_call(
-        lambda *refs: first_kernel(*refs, total_steps=steps * seq_count),
-        in_specs=[HBM] * 4,
-        out_specs=[VMEM] * 5,
+    chip, far = pl.pallas_call(
+        halves_kernel,
+        in_specs=[HBM],
+        out_specs=[VMEM] * 2,
+        out_shape=[half_shape] * 2,
+        scratch_shapes=[pltpu.VMEM(signal.shape, bf16), pltpu.SemaphoreType.DMA],
+        compiler_params=PARAMS,
+        cost_estimate=cost(signal.size, 2 * signal_bytes),
+        name="halves",
+    )(in_hbm(signal))
+    weights, time_bias, station_bias = pl.pallas_call(
+        lambda *refs: fixed_kernel(*refs, stations=stations, total_steps=steps * seq_count),
+        in_specs=[HBM] * 3 + [VMEM],
+        out_specs=[VMEM] * 3,
         out_shape=[
-            half_shape,
-            half_shape,
             jax.ShapeDtypeStruct(head_proj.shape, bf16),
             jax.ShapeDtypeStruct((micro, reach, GROUP * own), f32),
             jax.ShapeDtypeStruct((micro, own, GROUP * own), f32),
         ],
         scratch_shapes=[
-            pltpu.VMEM(signal.shape, bf16),
             pltpu.SMEM(record_start.shape, jnp.int32),
             pltpu.SMEM(record_pad.shape, jnp.int32),
-            pltpu.SemaphoreType.DMA((4,)),
+            pltpu.SemaphoreType.DMA((3,)),
         ],
         compiler_params=PARAMS,
         cost_estimate=cost(signal.size, 2 * head_proj.size),
-        name="first",
-    )(in_hbm(signal), in_hbm(head_proj), in_hbm(record_start), in_hbm(record_pad))
+        name="fixed",
+    )(in_hbm(head_proj), in_hbm(record_start), in_hbm(record_pad), far)
 
     def moved(block, source, target, hop, other=False):
         route = []
@@ -365,7 +388,7 @@
     next_far = moved(far, 0, 0, 2)
     next_chip = moved(chip, 0, 0, 1)
     squares = lax.psum(squares_of(chip, far, next_far, next_chip), "rep")
-    inputs = (next_chip, next_far)
+    inputs = (next_far, next_chip)
     kept = (chip, far)
     for tick in range(section_count):
         last = tick + 1 == section_count
@@ -401,15 +424,7 @@
         chip = moved(kept[0], tick, tick + 1, 0)
         next_far = moved(kept[1], tick, tick + 1, 2)
         squares = moved(mine, tick, tick + 1, 0, other=True)
-        mine_again, far_again = pl.pallas_call(
-            copy_kernel,
-            in_specs=[VMEM] * 2,
-            out_specs=[VMEM] * 2,
-            out_shape=[squares_shape, half_shape],
-            compiler_params=PARAMS,
-            cost_estimate=BUSY,
-            name="copy",
-        )(mine, kept[1])
+        mine_again, far_again = again(mine, kept[1])
         far = moved(far_again, tick, tick + 1, 0)
         far_squares = moved(mine_again, tick, tick + 1, 2, other=True)
         normed_chip = normed(chip, squares, CHIP)

time: 28.2 us -> 28 us (level)
  waiting for transfers between devices: 5.92 us -> 4.52 us
  Pallas kernels: 4.72 us -> 5.64 us
  starting transfers between devices: 13.2 us -> 13.6 us
    ppermute x8, waiting for transfers between devices: 5.92 us -> 4.52 us  [moved(): return lax.ppermute(block, ('section', 'seq', 'rep'), route)]
    pallas_call x2 -> x3, Pallas kernels: 1.55 us -> 2.47 us  [the longest x1 1.44 us: body(): pl.pallas_call(lambda *refs: fixed_kernel(*refs, stations=stations, total...]
    ppermute x8, starting transfers between devices: 13.2 us -> 13.6 us  [moved(): return lax.ppermute(block, ('section', 'seq', 'rep'), route)]
  transfers between devices with their start and end apart: 8 -> 8, of which waited for: 3 -> 2; matrix products, arithmetic and copies ran while one was open for 0% -> 0% of each run, Pallas kernels for 4% -> 9%
where the time goes in v9:
time: 28 us; the launch traced here: 27.7 us
  starting transfers between devices  13.6 us (49%)
  Pallas kernels  5.64 us (20%)
  waiting for transfers between devices  4.52 us (16%)
  blocking collectives  3.8 us (14%)
    ppermute x8, starting transfers between devices, moved(): return lax.ppermute(block, ('section', 'seq', 'rep'), route)  13.6 us
    ppermute x8, waiting for transfers between devices, moved(): return lax.ppermute(block, ('section', 'seq', 'rep'), route)  4.52 us
    psum x1, blocking collectives, body(): squares = lax.psum(squares_of(chip, far, next_far, next_chip), 'rep')  3.8 us
    pallas_call x2, Pallas kernels, body(): pl.pallas_call(kernel, in_specs=[VMEM] * (8 + len(inputs)), out_specs=[VM...  1.8 us
    pallas_call x1, Pallas kernels, body(): pl.pallas_call(lambda *refs: fixed_kernel(*refs, stations=stations, total...  1.44 us
    pallas_call x1, Pallas kernels, body(): pl.pallas_call(halves_kernel, in_specs=[HBM], out_specs=[VMEM] * 2, out_s...  1.02 us
    pallas_call x3, Pallas kernels, squares_of(): pl.pallas_call(squares_kernel, in_specs=[VMEM] * len(halves), out_specs=V...  0.66 us
  transfers between devices with their start and end apart: 8, of which 2 were waited for; matrix products, arithmetic and copies ran while one was open for 0% of the time, Pallas kernels for 9%

profile of v9, /device:TPU:11, one launch (start us, length us, event | category | flops | bytes accessed | tf_op | source)
XLA Modules:
  0.0 27.7 jit_solution(11612798848555747560)
XLA Ops:
  0.0 1.0 %halves.1 = (bf16[32,2048]{1,0:T(8,128)(2,1)S(1)}, bf16[32,2048]{1,0:T(8,128)(2,1)S(1)}) custom-call(bf16[2,8,4,2048]{3,2,1,0:T(4,128)(2,1)} %signal_hbm.1), custom_call_target="tpu_custom_call" | custom-call | flops 131072 | bytes 524288 | tf_op jit(solution)/shard_map/halves/pallas_call | solution.py:344
  1.0 0.7 %collective-permute-start = (bf16[32,2048]{1,0:T(8,128)(2,1)S(1)}, bf16[32,2048]{1,0:T(8,128)(2,1)S(1)}, u32[]{:S(2)}, u32[]{:S(2)}) collective-permute-start(bf16[32,2048]{1,0:T(8,128)(2,1)S(1)} %get-tuple-element.17.refs_1_.refs_3_.refs_7_), channel_id=1, source_target_pairs={{2,4},{3,5},{4,2},{5,3},{6,8},{7,9},{8,6},{9,7},{10,12},{11,13},{1... | collective-permute-start | bytes 393224 | tf_op jit(solution)/shard_map/ppermute | solution.py:386
  1.7 0.7 %collective-permute-start.1 = (bf16[32,2048]{1,0:T(8,128)(2,1)S(1)}, bf16[32,2048]{1,0:T(8,128)(2,1)S(1)}, u32[]{:S(2)}, u32[]{:S(2)}) collective-permute-start(bf16[32,2048]{1,0:T(8,128)(2,1)S(1)} %get-tuple-element.16.refs_0_.refs_6_), channel_id=1, source_target_pairs={{0,2},{1,3},{2,0},{3,1},{4,6},{5,7},{6,4},{7,5},{8,10},{9,11},{10,... | collective-permute-start | bytes 393224 | tf_op jit(solution)/shard_map/ppermute | solution.py:386
  2.4 1.4 %fixed.1 = (bf16[1,16,128,384]{3,2,1,0:T(8,128)(2,1)S(1)}, f32[2,64,128]{2,1,0:T(8,128)S(1)}, f32[2,32,128]{2,1,0:T(8,128)S(1)}) custom-call(bf16[1,16,128,384]{3,2,1,0:T(8,128)(2,1)} %refs_0_.1, s32[2,4]{1,0:T(2,128)} %refs_1_.1, s32[2,4]{1,0:T(2,128)} %refs_2_.1, bf16[32,2048]{1,0:T(8,128)(2,1)S(1)} %get-tuple-element.17.refs_1_.refs_3_.refs_7_), custom_call_target="tpu_custom_call" | custom-call | flops 131072 | bytes 1572864 | tf_op jit(solution)/shard_map/fixed/pallas_call | solution.py:354
  3.8 0.0 collective-permute-done.refs_2_.refs_8_
  3.8 0.0 collective-permute-done.1.refs_3_.refs_9_
  3.8 0.3 squares.3
  4.1 3.8 %psum.7.refs_2_ = f32[8,128]{1,0:T(8,128)S(1)} all-reduce(f32[8,128]{1,0:T(8,128)S(1)} %squares.3), channel_id=1, replica_groups=mesh['section'=2,'seq'=8,'rep'=2] {'rep'}, use_global_device_ids=true, to_apply=%region_0.0 | all-reduce | flops 1024 | bytes 8192 | tf_op jit(solution)/shard_map/psum | solution.py:390
  7.9 0.1 layer.2
  8.0 1.3 %collective-permute-start.2 = (bf16[32,2048]{1,0:T(8,128)(2,1)S(1)}, bf16[32,2048]{1,0:T(8,128)(2,1)S(1)}, u32[]{:S(2)}, u32[]{:S(2)}) collective-permute-start(bf16[32,2048]{1,0:T(8,128)(2,1)S(1)} %get-tuple-element.21.refs_0_.refs_6_), channel_id=1, source_target_pairs={{0,16},{1,17},{2,18},{3,19},{4,20},{5,21},{6,22},{7,23},{8,24},{9,... | collective-permute-start | bytes 393224 | tf_op jit(solution)/shard_map/ppermute | solution.py:386
  9.3 0.2 squares.4.refs_0_
  9.5 1.3 %collective-permute-start.4 = (f32[8,128]{1,0:T(8,128)S(1)}, f32[8,128]{1,0:T(8,128)S(1)}, u32[]{:S(2)}, u32[]{:S(2)}) collective-permute-start(f32[8,128]{1,0:T(8,128)S(1)} %squares.4.refs_0_), channel_id=1, source_target_pairs={{0,17},{1,16},{2,19},{3,18},{4,21},{5,20},{6,23},{7,22},{8,25},{9,... | collective-permute-start | bytes 12296 | tf_op jit(solution)/shard_map/ppermute | solution.py:386
  10.8 1.3 %collective-permute-start.5 = (bf16[32,2048]{1,0:T(8,128)(2,1)S(1)}, bf16[32,2048]{1,0:T(8,128)(2,1)S(1)}, u32[]{:S(2)}, u32[]{:S(2)}) collective-permute-start(bf16[32,2048]{1,0:T(8,128)(2,1)S(1)} %get-tuple-element.22.refs_1_.refs_7_), channel_id=1, source_target_pairs={{2,20},{3,21},{4,18},{5,19},{6,24},{7,25},{8,22},{9,23},{10,28},{1... | collective-permute-start | bytes 393224 | tf_op jit(solution)/shard_map/ppermute | solution.py:386
  12.1 1.3 %collective-permute-start.6 = (f32[8,128]{1,0:T(8,128)S(1)}, f32[8,128]{1,0:T(8,128)S(1)}, u32[]{:S(2)}, u32[]{:S(2)}) collective-permute-start(f32[8,128]{1,0:T(8,128)S(1)} %get-tuple-element.24), channel_id=1, source_target_pairs={{2,21},{3,20},{4,19},{5,18},{6,25},{7,24},{8,23},{9,22},{10,29},{1... | collective-permute-start | bytes 12296 | tf_op jit(solution)/shard_map/ppermute | solution.py:386
  13.4 1.3 %collective-permute-start.3 = (bf16[32,2048]{1,0:T(8,128)(2,1)S(1)}, bf16[32,2048]{1,0:T(8,128)(2,1)S(1)}, u32[]{:S(2)}, u32[]{:S(2)}) collective-permute-start(bf16[32,2048]{1,0:T(8,128)(2,1)S(1)} %get-tuple-element.23), channel_id=1, source_target_pairs={{0,16},{1,17},{2,18},{3,19},{4,20},{5,21},{6,22},{7,23},{8,24},{9,... | collective-permute-start | bytes 393224 | tf_op jit(solution)/shard_map/ppermute | solution.py:386
  14.7 3.8 %collective-permute-done.4.refs_1_.refs_2_ = f32[8,128]{1,0:T(8,128)S(1)} collective-permute-done((f32[8,128]{1,0:T(8,128)S(1)}, f32[8,128]{1,0:T(8,128)S(1)}, u32[]{:S(2)}, u32[]{:S(2)}) %collective-permute-start.4) | collective-permute-done | bytes 4128 | tf_op jit(solution)/shard_map/ppermute | solution.py:386
  18.5 0.0 collective-permute-done.2.refs_0_
  18.5 0.3 %norm.1.refs_0_ = bf16[32,2048]{1,0:T(8,128)(2,1)S(1)} custom-call(bf16[32,2048]{1,0:T(8,128)(2,1)S(1)} %collective-permute-done.2.refs_0_, f32[8,128]{1,0:T(8,128)S(1)} %collective-permute-done.4.refs_1_.refs_2_), custom_call_target="tpu_custom_call" | custom-call | flops 2000000000 | bytes 300000 | tf_op jit(solution)/shard_map/norm/pallas_call | solution.py:312
  18.8 5.8 %collective-permute-start.7 = (bf16[32,2048]{1,0:T(8,128)(2,1)S(1)}, bf16[32,2048]{1,0:T(8,128)(2,1)S(1)}, u32[]{:S(2)}, u32[]{:S(2)}) collective-permute-start(bf16[32,2048]{1,0:T(8,128)(2,1)S(1)} %norm.1.refs_0_), channel_id=1, source_target_pairs={{16,18},{17,19},{18,16},{19,17},{20,22},{21,23},{22,20},{23,21},{2... | collective-permute-start | bytes 393224 | tf_op jit(solution)/shard_map/ppermute | solution.py:386
  24.5 0.0 collective-permute-done.5.refs_0_.refs_8_
  24.5 0.2 squares.5.mine_ref
  24.7 0.0 collective-permute-done.6.other_ref
  24.7 0.8 %collective-permute-done.7.refs_1_ = bf16[32,2048]{1,0:T(8,128)(2,1)S(1)} collective-permute-done((bf16[32,2048]{1,0:T(8,128)(2,1)S(1)}, bf16[32,2048]{1,0:T(8,128)(2,1)S(1)}, u32[]{:S(2)}, u32[]{:S(2)}) %collective-permute-start.7) | collective-permute-done | bytes 131104 | tf_op jit(solution)/shard_map/ppermute | solution.py:386
  25.5 0.4 %project.1 = (bf16[32,6144]{1,0:T(8,128)(2,1)S(1)}, bf16[32,6144]{1,0:T(8,128)(2,1)S(1)}) custom-call(bf16[1,16,128,384]{3,2,1,0:T(8,128)(2,1)S(1)} %get-tuple-element.20.refs_5_.weights_ref, bf16[32,2048]{1,0:T(8,128)(2,1)S(1)} %norm.1.refs_0_, bf16[32,2048]{1,0:T(8,128)(2,1)S(1)} %collective-permute-done.7.refs_1_), custom_call_target="tpu_custom_call" | custom-call | flops 2000000000 | bytes 300000 | tf_op jit(solution)/shard_map/project/pallas_call | solution.py:334
  25.9 0.0 collective-permute-done.3.refs_1_
  25.9 1.8 %layer.3 = bf16[1,2,8,4,2048]{4,3,2,1,0:T(4,128)(2,1)} custom-call(bf16[32,2048]{1,0:T(8,128)(2,1)S(1)} %collective-permute-done.2.refs_0_, bf16[32,2048]{1,0:T(8,128)(2,1)S(1)} %collective-permute-done.3.refs_1_, f32[8,128]{1,0:T(8,128)S(1)} %collective-permute-done.4.refs_1_.refs_2_, f32[2,64,128]{2,1,0:T(8,128)S(1)} %get-tuple-element.18.refs_3_, ...), custom_call_target="tpu_custom_call" | custom-call | flops 402653184 | bytes 4194304 | tf_op jit(solution)/shard_map/layer/pallas_call | solution.py:404
  (2 shorter events, 0.0 us)
Async XLA Ops:
  1.0 2.8 %collective-permute-start = (bf16[32,2048]{1,0:T(8,128)(2,1)S(1)}, bf16[32,2048]{1,0:T(8,128)(2,1)S(1)}, u32[]{:S(2)}, u32[]{:S(2)}) collective-permute-start(bf16[32,2048]{1,0:T(8,128)(2,1)S(1)} %get-tuple-element.17.refs_1_.refs_3_.refs_7_), channel_id=1, source_target_pairs={{2,4},{3,5},{4,2},{5,3},{6,8},{7,9},{8,6},{9,7},{10,12},{11,13},{1... | collective-permute-start | bytes 393224 | tf_op jit(solution)/shard_map/ppermute | solution.py:386
  1.7 2.1 %collective-permute-start.1 = (bf16[32,2048]{1,0:T(8,128)(2,1)S(1)}, bf16[32,2048]{1,0:T(8,128)(2,1)S(1)}, u32[]{:S(2)}, u32[]{:S(2)}) collective-permute-start(bf16[32,2048]{1,0:T(8,128)(2,1)S(1)} %get-tuple-element.16.refs_0_.refs_6_), channel_id=1, source_target_pairs={{0,2},{1,3},{2,0},{3,1},{4,6},{5,7},{6,4},{7,5},{8,10},{9,11},{10,... | collective-permute-start | bytes 393224 | tf_op jit(solution)/shard_map/ppermute | solution.py:386
  8.0 10.5 %collective-permute-start.2 = (bf16[32,2048]{1,0:T(8,128)(2,1)S(1)}, bf16[32,2048]{1,0:T(8,128)(2,1)S(1)}, u32[]{:S(2)}, u32[]{:S(2)}) collective-permute-start(bf16[32,2048]{1,0:T(8,128)(2,1)S(1)} %get-tuple-element.21.refs_0_.refs_6_), channel_id=1, source_target_pairs={{0,16},{1,17},{2,18},{3,19},{4,20},{5,21},{6,22},{7,23},{8,24},{9,... | collective-permute-start | bytes 393224 | tf_op jit(solution)/shard_map/ppermute | solution.py:386
  9.5 9.0 %collective-permute-start.4 = (f32[8,128]{1,0:T(8,128)S(1)}, f32[8,128]{1,0:T(8,128)S(1)}, u32[]{:S(2)}, u32[]{:S(2)}) collective-permute-start(f32[8,128]{1,0:T(8,128)S(1)} %squares.4.refs_0_), channel_id=1, source_target_pairs={{0,17},{1,16},{2,19},{3,18},{4,21},{5,20},{6,23},{7,22},{8,25},{9,... | collective-permute-start | bytes 12296 | tf_op jit(solution)/shard_map/ppermute | solution.py:386
  10.8 13.7 %collective-permute-start.5 = (bf16[32,2048]{1,0:T(8,128)(2,1)S(1)}, bf16[32,2048]{1,0:T(8,128)(2,1)S(1)}, u32[]{:S(2)}, u32[]{:S(2)}) collective-permute-start(bf16[32,2048]{1,0:T(8,128)(2,1)S(1)} %get-tuple-element.22.refs_1_.refs_7_), channel_id=1, source_target_pairs={{2,20},{3,21},{4,18},{5,19},{6,24},{7,25},{8,22},{9,23},{10,28},{1... | collective-permute-start | bytes 393224 | tf_op jit(solution)/shard_map/ppermute | solution.py:386
  12.1 12.6 %collective-permute-start.6 = (f32[8,128]{1,0:T(8,128)S(1)}, f32[8,128]{1,0:T(8,128)S(1)}, u32[]{:S(2)}, u32[]{:S(2)}) collective-permute-start(f32[8,128]{1,0:T(8,128)S(1)} %get-tuple-element.24), channel_id=1, source_target_pairs={{2,21},{3,20},{4,19},{5,18},{6,25},{7,24},{8,23},{9,22},{10,29},{1... | collective-permute-start | bytes 12296 | tf_op jit(solution)/shard_map/ppermute | solution.py:386
  13.4 12.5 %collective-permute-start.3 = (bf16[32,2048]{1,0:T(8,128)(2,1)S(1)}, bf16[32,2048]{1,0:T(8,128)(2,1)S(1)}, u32[]{:S(2)}, u32[]{:S(2)}) collective-permute-start(bf16[32,2048]{1,0:T(8,128)(2,1)S(1)} %get-tuple-element.23), channel_id=1, source_target_pairs={{0,16},{1,17},{2,18},{3,19},{4,20},{5,21},{6,22},{7,23},{8,24},{9,... | collective-permute-start | bytes 393224 | tf_op jit(solution)/shard_map/ppermute | solution.py:386
  18.8 6.7 %collective-permute-start.7 = (bf16[32,2048]{1,0:T(8,128)(2,1)S(1)}, bf16[32,2048]{1,0:T(8,128)(2,1)S(1)}, u32[]{:S(2)}, u32[]{:S(2)}) collective-permute-start(bf16[32,2048]{1,0:T(8,128)(2,1)S(1)} %norm.1.refs_0_), channel_id=1, source_target_pairs={{16,18},{17,19},{18,16},{19,17},{20,22},{21,23},{22,20},{23,21},{2... | collective-permute-start | bytes 393224 | tf_op jit(solution)/shard_map/ppermute | solution.py:386

commit v10 on v9

--- a/solution.py
+++ b/solution.py
@@ -129,11 +129,10 @@
     return (rows.astype(jnp.float32) * column).astype(jnp.bfloat16)
 
 
-def norm_kernel(half_ref, squares_ref, normed_ref, *, line):
+def norm_kernel(half_ref, mine_ref, squares_ref, normed_ref, *, line):
     rows = half_ref[...]
-    normed_ref[...] = scaled(
-        rows, squares_row(rows) + squares_ref[line : line + 1, 0 : rows.shape[0]]
-    )
+    count = rows.shape[0]
+    normed_ref[...] = scaled(rows, mine_ref[0:1, 0:count] + squares_ref[line : line + 1, 0:count])
 
 
 def copy_kernel(*refs):
@@ -187,14 +186,17 @@
             for half, half_ref in enumerate((chip_ref, far_ref, next_far_ref, next_chip_ref))
         ]
     else:
-        next_far_ref, far_squares_ref, projected[CHIP], projected[NEXT_CHIP], *refs = refs
+        next_far_ref, far_squares_ref, next_chip_ref, projected[CHIP], *refs = refs
         late = [
             (FAR, far_ref, squares_ref[FAR : FAR + 1, :], False),
             (NEXT_FAR, next_far_ref, far_squares_ref[0:1, :], True),
         ]
-    outs, refs = (refs[:1], refs[1:]) if last else (refs[:2], refs[2:])
-    normed = refs[: len(late)]
-    for (half, *_), half_ref in zip(late, refs[len(late) :]):
+    outs, refs = (refs[:1], refs[1:]) if last else (refs[:3], refs[3:])
+    normed, refs = refs[: len(late)], refs[len(late) :]
+    projecting = [half for half, *_ in late]
+    if tick > 0:
+        projecting.append(NEXT_CHIP)
+    for half, half_ref in zip(projecting, refs):
         projected[half] = half_ref
 
     def write(m, lanes, values):
@@ -223,7 +225,9 @@
                     total = total + part * part
             factor = lax.rsqrt(jnp.sum(total, axis=1, keepdims=True) / (HEADS * HEAD) + EPS)
             normed_ref[...] = (half_ref[...].astype(f32) * factor).astype(bf16)
-        project_kernel(weights_ref, *normed, *[projected[half] for half, *_ in late])
+        if tick > 0:
+            normed.append(next_chip_ref)
+        project_kernel(weights_ref, *normed, *[projected[half] for half in projecting])
         pairs = [(g, m) for g in range(heads_dev // GROUP) for m in range(micro)]
         blank = jnp.zeros((own, HEAD), bf16)
         scores = []
@@ -254,6 +258,7 @@
             time_weights = softmax_columns(score + time_ref[m])
             station_weights = softmax_columns(score[:own] + station_ref[m])
             mixes.append(jnp.concatenate([time_weights, station_weights], axis=0).T)
+        sums = [jnp.zeros((own, HEAD), f32) for _ in range(micro)]
         for (g, m), mix in zip(pairs, mixes):
             for j in range(GROUP):
                 head = g * GROUP + j
@@ -269,6 +274,17 @@
                 )
                 result = hidden.astype(f32) + mixed
                 write(m, lanes, result)
+                if not last:
+                    rounded = result.astype(bf16).astype(f32)
+                    sums[m] = sums[m] + rounded * rounded
+        if not last:
+            outs[2][...] = jnp.zeros(outs[2].shape, f32)
+            for half in (CHIP, FAR):
+                parts = [part[half * edge : (half + 1) * edge] for part in sums]
+                column = jnp.sum(jnp.concatenate(parts, axis=0), axis=1, keepdims=True)
+                outs[2][half : half + 1, 0 : micro * edge] = jnp.sum(
+                    jnp.where(same(micro * edge), column, 0.0), axis=0, keepdims=True
+                )
 
     @pl.when(jnp.logical_not(active))
     def _():
@@ -279,6 +295,8 @@
                     ref[m * edge : (m + 1) * edge, lanes] for ref in (kept_chip_ref, kept_far_ref)
                 ]
                 write(m, lanes, jnp.concatenate(kept, axis=0).astype(f32))
+        if not last:
+            outs[2][...] = jnp.zeros(outs[2].shape, f32)
 
 
 def body(signal, head_proj, record_start, record_pad):
@@ -311,13 +329,13 @@
     def normed(rows, squares, line):
         return pl.pallas_call(
             lambda *refs: norm_kernel(*refs, line=line),
-            in_specs=[VMEM] * 2,
+            in_specs=[VMEM] * 3,
             out_specs=VMEM,
             out_shape=half_shape,
             compiler_params=PARAMS,
             cost_estimate=BUSY,
             name="norm",
-        )(rows, squares)
+        )(rows, squares_of(rows), squares)
 
     def again(*blocks):
         return pl.pallas_call(
@@ -368,7 +386,7 @@
         compiler_params=PARAMS,
         cost_estimate=cost(signal.size, 2 * head_proj.size),
         name="fixed",
-    )(in_hbm(head_proj), in_hbm(record_start), in_hbm(record_pad), far)
+    )(in_hbm(head_proj), in_hbm(record_start), in_hbm(record_pad), chip)
 
     def moved(block, source, target, hop, other=False):
         route = []
@@ -399,7 +417,7 @@
         out_shape = (
             [jax.ShapeDtypeStruct((1,) + signal.shape, bf16)]
             if last
-            else [half_shape, half_shape]
+            else [half_shape, half_shape, squares_shape]
         )
         outputs = pl.pallas_call(
             kernel,
@@ -408,8 +426,8 @@
             out_shape=out_shape,
             scratch_shapes=[
                 pltpu.VMEM(shape.shape, bf16)
-                for shape in (half_shape, projected_shape)
-                for _ in range(4 if tick == 0 else 2)
+                for shape, count in zip((half_shape, projected_shape), (4, 4) if tick == 0 else (2, 3))
+                for _ in range(count)
             ],
             compiler_params=PARAMS,
             cost_estimate=cost(8 * signal.size * 3 * HEAD, 16 * signal_bytes),
@@ -419,8 +437,7 @@
         )
         if last:
             return outputs[0]
-        kept = outputs
-        mine = squares_of(*kept)
+        *kept, mine = outputs
         chip = moved(kept[0], tick, tick + 1, 0)
         next_far = moved(kept[1], tick, tick + 1, 2)
         squares = moved(mine, tick, tick + 1, 0, other=True)
@@ -438,7 +455,7 @@
             cost_estimate=BUSY,
             name="add",
         )(squares_of(next_far), far_squares)
-        inputs = (next_far, far_squares, *project(normed_chip, next_chip))
+        inputs = (next_far, far_squares, next_chip, *project(normed_chip))
 
 
 def solution(mesh):

time: 28 us -> 29.8 us (1.064)
  the two profiles are of different devices: /device:TPU:11 before, /device:TPU:23 now
where the time goes in v10:
time: 29.8 us; the launch traced here: 29.5 us
  starting transfers between devices  13.6 us (46%)
  waiting for transfers between devices  6.47 us (22%)
  Pallas kernels  5.44 us (18%)
  blocking collectives  3.8 us (13%)
    ppermute x8, starting transfers between devices, moved(): return lax.ppermute(block, ('section', 'seq', 'rep'), route)  13.6 us
    ppermute x8, waiting for transfers between devices, moved(): return lax.ppermute(block, ('section', 'seq', 'rep'), route)  6.47 us
    psum x1, blocking collectives, body(): squares = lax.psum(squares_of(chip, far, next_far, next_chip), 'rep')  3.8 us
    pallas_call x2, Pallas kernels, body(): pl.pallas_call(kernel, in_specs=[VMEM] * (8 + len(inputs)), out_specs=[VM...  1.86 us
    pallas_call x1, Pallas kernels, body(): pl.pallas_call(lambda *refs: fixed_kernel(*refs, stations=stations, total...  1.44 us
    pallas_call x1, Pallas kernels, body(): pl.pallas_call(halves_kernel, in_specs=[HBM], out_specs=[VMEM] * 2, out_s...  1.02 us
    pallas_call x3, Pallas kernels, squares_of(): pl.pallas_call(squares_kernel, in_specs=[VMEM] * len(halves), out_specs=V...  0.62 us
  transfers between devices with their start and end apart: 8, of which 2 were waited for; matrix products, arithmetic and copies ran while one was open for 0% of the time, Pallas kernels for 8%

profile of v10, /device:TPU:23, one launch (start us, length us, event | category | flops | bytes accessed | tf_op | source)
XLA Modules:
  0.0 29.5 jit_solution(8242411491122852373)
XLA Ops:
  0.0 1.0 %halves.1 = (bf16[32,2048]{1,0:T(8,128)(2,1)S(1)}, bf16[32,2048]{1,0:T(8,128)(2,1)S(1)}) custom-call(bf16[2,8,4,2048]{3,2,1,0:T(4,128)(2,1)} %signal_hbm.1), custom_call_target="tpu_custom_call" | custom-call | flops 131072 | bytes 524288 | tf_op jit(solution)/shard_map/halves/pallas_call | solution.py:362
  1.0 0.7 %collective-permute-start = (bf16[32,2048]{1,0:T(8,128)(2,1)S(1)}, bf16[32,2048]{1,0:T(8,128)(2,1)S(1)}, u32[]{:S(2)}, u32[]{:S(2)}) collective-permute-start(bf16[32,2048]{1,0:T(8,128)(2,1)S(1)} %get-tuple-element.16.refs_1_.refs_7_), channel_id=1, source_target_pairs={{2,4},{3,5},{4,2},{5,3},{6,8},{7,9},{8,6},{9,7},{10,12},{11,13},{1... | collective-permute-start | bytes 393224 | tf_op jit(solution)/shard_map/ppermute | solution.py:404
  1.7 0.7 %collective-permute-start.1 = (bf16[32,2048]{1,0:T(8,128)(2,1)S(1)}, bf16[32,2048]{1,0:T(8,128)(2,1)S(1)}, u32[]{:S(2)}, u32[]{:S(2)}) collective-permute-start(bf16[32,2048]{1,0:T(8,128)(2,1)S(1)} %get-tuple-element.15.refs_0_.refs_3_.refs_6_), channel_id=1, source_target_pairs={{0,2},{1,3},{2,0},{3,1},{4,6},{5,7},{6,4},{7,5},{8,10},{9,11},{10,... | collective-permute-start | bytes 393224 | tf_op jit(solution)/shard_map/ppermute | solution.py:404
  2.4 1.4 %fixed.1 = (bf16[1,16,128,384]{3,2,1,0:T(8,128)(2,1)S(1)}, f32[2,64,128]{2,1,0:T(8,128)S(1)}, f32[2,32,128]{2,1,0:T(8,128)S(1)}) custom-call(bf16[1,16,128,384]{3,2,1,0:T(8,128)(2,1)} %refs_0_.1, s32[2,4]{1,0:T(2,128)} %refs_1_.1, s32[2,4]{1,0:T(2,128)} %refs_2_.1, bf16[32,2048]{1,0:T(8,128)(2,1)S(1)} %get-tuple-element.15.refs_0_.refs_3_.refs_6_), custom_call_target="tpu_custom_call" | custom-call | flops 131072 | bytes 1572864 | tf_op jit(solution)/shard_map/fixed/pallas_call | solution.py:372
  3.8 0.0 collective-permute-done.refs_2_.refs_8_
  3.8 0.0 collective-permute-done.1.refs_3_.refs_9_
  3.8 0.3 squares.3
  4.1 3.8 %psum.7.refs_2_ = f32[8,128]{1,0:T(8,128)S(1)} all-reduce(f32[8,128]{1,0:T(8,128)S(1)} %squares.3), channel_id=1, replica_groups=mesh['section'=2,'seq'=8,'rep'=2] {'rep'}, use_global_device_ids=true, to_apply=%region_0.0 | all-reduce | flops 1024 | bytes 8192 | tf_op jit(solution)/shard_map/psum | solution.py:408
  7.9 0.1 layer.2
  8.0 1.3 %collective-permute-start.4 = (f32[8,128]{1,0:T(8,128)S(1)}, f32[8,128]{1,0:T(8,128)S(1)}, u32[]{:S(2)}, u32[]{:S(2)}) collective-permute-start(f32[8,128]{1,0:T(8,128)S(1)} %get-tuple-element.21.refs_0_), channel_id=1, source_target_pairs={{0,17},{1,16},{2,19},{3,18},{4,21},{5,20},{6,23},{7,22},{8,25},{9,... | collective-permute-start | bytes 12296 | tf_op jit(solution)/shard_map/ppermute | solution.py:404
  9.3 1.3 %collective-permute-start.2 = (bf16[32,2048]{1,0:T(8,128)(2,1)S(1)}, bf16[32,2048]{1,0:T(8,128)(2,1)S(1)}, u32[]{:S(2)}, u32[]{:S(2)}) collective-permute-start(bf16[32,2048]{1,0:T(8,128)(2,1)S(1)} %get-tuple-element.20.refs_6_), channel_id=1, source_target_pairs={{0,16},{1,17},{2,18},{3,19},{4,20},{5,21},{6,22},{7,23},{8,24},{9,... | collective-permute-start | bytes 393224 | tf_op jit(solution)/shard_map/ppermute | solution.py:404
  10.6 1.3 %collective-permute-start.5 = (bf16[32,2048]{1,0:T(8,128)(2,1)S(1)}, bf16[32,2048]{1,0:T(8,128)(2,1)S(1)}, u32[]{:S(2)}, u32[]{:S(2)}) collective-permute-start(bf16[32,2048]{1,0:T(8,128)(2,1)S(1)} %get-tuple-element.22.refs_1_.refs_7_), channel_id=1, source_target_pairs={{2,20},{3,21},{4,18},{5,19},{6,24},{7,25},{8,22},{9,23},{10,28},{1... | collective-permute-start | bytes 393224 | tf_op jit(solution)/shard_map/ppermute | solution.py:404
  11.9 1.3 %collective-permute-start.6 = (f32[8,128]{1,0:T(8,128)S(1)}, f32[8,128]{1,0:T(8,128)S(1)}, u32[]{:S(2)}, u32[]{:S(2)}) collective-permute-start(f32[8,128]{1,0:T(8,128)S(1)} %get-tuple-element.24), channel_id=1, source_target_pairs={{2,21},{3,20},{4,19},{5,18},{6,25},{7,24},{8,23},{9,22},{10,29},{1... | collective-permute-start | bytes 12296 | tf_op jit(solution)/shard_map/ppermute | solution.py:404
  13.2 1.3 %collective-permute-start.3 = (bf16[32,2048]{1,0:T(8,128)(2,1)S(1)}, bf16[32,2048]{1,0:T(8,128)(2,1)S(1)}, u32[]{:S(2)}, u32[]{:S(2)}) collective-permute-start(bf16[32,2048]{1,0:T(8,128)(2,1)S(1)} %get-tuple-element.23), channel_id=1, source_target_pairs={{0,16},{1,17},{2,18},{3,19},{4,20},{5,21},{6,22},{7,23},{8,24},{9,... | collective-permute-start | bytes 393224 | tf_op jit(solution)/shard_map/ppermute | solution.py:404
  14.5 6.1 %collective-permute-done.2.refs_0_ = bf16[32,2048]{1,0:T(8,128)(2,1)S(1)} collective-permute-done((bf16[32,2048]{1,0:T(8,128)(2,1)S(1)}, bf16[32,2048]{1,0:T(8,128)(2,1)S(1)}, u32[]{:S(2)}, u32[]{:S(2)}) %collective-permute-start.2) | collective-permute-done | bytes 131104 | tf_op jit(solution)/shard_map/ppermute | solution.py:404
  20.6 0.2 squares.5.refs_1_
  20.8 0.0 collective-permute-done.4.refs_2_
  20.8 0.1 norm.1.refs_0_
  20.9 5.8 %collective-permute-start.7 = (bf16[32,2048]{1,0:T(8,128)(2,1)S(1)}, bf16[32,2048]{1,0:T(8,128)(2,1)S(1)}, u32[]{:S(2)}, u32[]{:S(2)}) collective-permute-start(bf16[32,2048]{1,0:T(8,128)(2,1)S(1)} %norm.1.refs_0_), channel_id=1, source_target_pairs={{16,18},{17,19},{18,16},{19,17},{20,22},{21,23},{22,20},{23,21},{2... | collective-permute-start | bytes 393224 | tf_op jit(solution)/shard_map/ppermute | solution.py:404
  26.7 0.4 %project.1.refs_11_ = bf16[32,6144]{1,0:T(8,128)(2,1)S(1)} custom-call(bf16[1,16,128,384]{3,2,1,0:T(8,128)(2,1)S(1)} %get-tuple-element.19.refs_5_.weights_ref, bf16[32,2048]{1,0:T(8,128)(2,1)S(1)} %norm.1.refs_0_), custom_call_target="tpu_custom_call" | custom-call | flops 2000000000 | bytes 300000 | tf_op jit(solution)/shard_map/project/pallas_call | solution.py:352
  27.1 0.0 collective-permute-done.5.refs_0_.refs_8_
  27.1 0.2 squares.4.mine_ref
  27.3 0.0 collective-permute-done.6.other_ref
  27.3 0.0 collective-permute-done.3.refs_1_
  27.3 0.4 %collective-permute-done.7.refs_10_ = bf16[32,2048]{1,0:T(8,128)(2,1)S(1)} collective-permute-done((bf16[32,2048]{1,0:T(8,128)(2,1)S(1)}, bf16[32,2048]{1,0:T(8,128)(2,1)S(1)}, u32[]{:S(2)}, u32[]{:S(2)}) %collective-permute-start.7) | collective-permute-done | bytes 131104 | tf_op jit(solution)/shard_map/ppermute | solution.py:404
  27.7 1.8 %layer.3 = bf16[1,2,8,4,2048]{4,3,2,1,0:T(4,128)(2,1)} custom-call(bf16[32,2048]{1,0:T(8,128)(2,1)S(1)} %collective-permute-done.2.refs_0_, bf16[32,2048]{1,0:T(8,128)(2,1)S(1)} %collective-permute-done.3.refs_1_, f32[8,128]{1,0:T(8,128)S(1)} %collective-permute-done.4.refs_2_, f32[2,64,128]{2,1,0:T(8,128)S(1)} %get-tuple-element.17.refs_3_, ...), custom_call_target="tpu_custom_call" | custom-call | flops 402653184 | bytes 4194304 | tf_op jit(solution)/shard_map/layer/pallas_call | solution.py:422
  (2 shorter events, 0.0 us)
Async XLA Ops:
  1.0 2.8 %collective-permute-start = (bf16[32,2048]{1,0:T(8,128)(2,1)S(1)}, bf16[32,2048]{1,0:T(8,128)(2,1)S(1)}, u32[]{:S(2)}, u32[]{:S(2)}) collective-permute-start(bf16[32,2048]{1,0:T(8,128)(2,1)S(1)} %get-tuple-element.16.refs_1_.refs_7_), channel_id=1, source_target_pairs={{2,4},{3,5},{4,2},{5,3},{6,8},{7,9},{8,6},{9,7},{10,12},{11,13},{1... | collective-permute-start | bytes 393224 | tf_op jit(solution)/shard_map/ppermute | solution.py:404
  1.7 2.1 %collective-permute-start.1 = (bf16[32,2048]{1,0:T(8,128)(2,1)S(1)}, bf16[32,2048]{1,0:T(8,128)(2,1)S(1)}, u32[]{:S(2)}, u32[]{:S(2)}) collective-permute-start(bf16[32,2048]{1,0:T(8,128)(2,1)S(1)} %get-tuple-element.15.refs_0_.refs_3_.refs_6_), channel_id=1, source_target_pairs={{0,2},{1,3},{2,0},{3,1},{4,6},{5,7},{6,4},{7,5},{8,10},{9,11},{10,... | collective-permute-start | bytes 393224 | tf_op jit(solution)/shard_map/ppermute | solution.py:404
  8.0 12.8 %collective-permute-start.4 = (f32[8,128]{1,0:T(8,128)S(1)}, f32[8,128]{1,0:T(8,128)S(1)}, u32[]{:S(2)}, u32[]{:S(2)}) collective-permute-start(f32[8,128]{1,0:T(8,128)S(1)} %get-tuple-element.21.refs_0_), channel_id=1, source_target_pairs={{0,17},{1,16},{2,19},{3,18},{4,21},{5,20},{6,23},{7,22},{8,25},{9,... | collective-permute-start | bytes 12296 | tf_op jit(solution)/shard_map/ppermute | solution.py:404
  9.3 11.3 %collective-permute-start.2 = (bf16[32,2048]{1,0:T(8,128)(2,1)S(1)}, bf16[32,2048]{1,0:T(8,128)(2,1)S(1)}, u32[]{:S(2)}, u32[]{:S(2)}) collective-permute-start(bf16[32,2048]{1,0:T(8,128)(2,1)S(1)} %get-tuple-element.20.refs_6_), channel_id=1, source_target_pairs={{0,16},{1,17},{2,18},{3,19},{4,20},{5,21},{6,22},{7,23},{8,24},{9,... | collective-permute-start | bytes 393224 | tf_op jit(solution)/shard_map/ppermute | solution.py:404
  10.6 16.5 %collective-permute-start.5 = (bf16[32,2048]{1,0:T(8,128)(2,1)S(1)}, bf16[32,2048]{1,0:T(8,128)(2,1)S(1)}, u32[]{:S(2)}, u32[]{:S(2)}) collective-permute-start(bf16[32,2048]{1,0:T(8,128)(2,1)S(1)} %get-tuple-element.22.refs_1_.refs_7_), channel_id=1, source_target_pairs={{2,20},{3,21},{4,18},{5,19},{6,24},{7,25},{8,22},{9,23},{10,28},{1... | collective-permute-start | bytes 393224 | tf_op jit(solution)/shard_map/ppermute | solution.py:404
  11.9 15.4 %collective-permute-start.6 = (f32[8,128]{1,0:T(8,128)S(1)}, f32[8,128]{1,0:T(8,128)S(1)}, u32[]{:S(2)}, u32[]{:S(2)}) collective-permute-start(f32[8,128]{1,0:T(8,128)S(1)} %get-tuple-element.24), channel_id=1, source_target_pairs={{2,21},{3,20},{4,19},{5,18},{6,25},{7,24},{8,23},{9,22},{10,29},{1... | collective-permute-start | bytes 12296 | tf_op jit(solution)/shard_map/ppermute | solution.py:404
  13.2 14.1 %collective-permute-start.3 = (bf16[32,2048]{1,0:T(8,128)(2,1)S(1)}, bf16[32,2048]{1,0:T(8,128)(2,1)S(1)}, u32[]{:S(2)}, u32[]{:S(2)}) collective-permute-start(bf16[32,2048]{1,0:T(8,128)(2,1)S(1)} %get-tuple-element.23), channel_id=1, source_target_pairs={{0,16},{1,17},{2,18},{3,19},{4,20},{5,21},{6,22},{7,23},{8,24},{9,... | collective-permute-start | bytes 393224 | tf_op jit(solution)/shard_map/ppermute | solution.py:404
  20.9 6.7 %collective-permute-start.7 = (bf16[32,2048]{1,0:T(8,128)(2,1)S(1)}, bf16[32,2048]{1,0:T(8,128)(2,1)S(1)}, u32[]{:S(2)}, u32[]{:S(2)}) collective-permute-start(bf16[32,2048]{1,0:T(8,128)(2,1)S(1)} %norm.1.refs_0_), channel_id=1, source_target_pairs={{16,18},{17,19},{18,16},{19,17},{20,22},{21,23},{22,20},{23,21},{2... | collective-permute-start | bytes 393224 | tf_op jit(solution)/shard_map/ppermute | solution.py:404

commit v11 on v10

--- a/solution.py
+++ b/solution.py
@@ -180,9 +180,14 @@
     active = lax.axis_index("section") == tick
     projected = [None] * 4
     if tick == 0:
-        next_far_ref, next_chip_ref, *refs = refs
+        next_far_ref, next_chip_ref, other_squares_ref, *refs = refs
         late = [
-            (half, half_ref, squares_ref[half : half + 1, :], True)
+            (
+                half,
+                half_ref,
+                squares_ref[half : half + 1, :] + other_squares_ref[half : half + 1, :],
+                True,
+            )
             for half, half_ref in enumerate((chip_ref, far_ref, next_far_ref, next_chip_ref))
         ]
     else:
@@ -191,7 +196,7 @@
             (FAR, far_ref, squares_ref[FAR : FAR + 1, :], False),
             (NEXT_FAR, next_far_ref, far_squares_ref[0:1, :], True),
         ]
-    outs, refs = (refs[:1], refs[1:]) if last else (refs[:3], refs[3:])
+    outs, refs = (refs[:1], refs[1:]) if last else (refs[:2], refs[2:])
     normed, refs = refs[: len(late)], refs[len(late) :]
     projecting = [half for half, *_ in late]
     if tick > 0:
@@ -258,7 +263,6 @@
             time_weights = softmax_columns(score + time_ref[m])
             station_weights = softmax_columns(score[:own] + station_ref[m])
             mixes.append(jnp.concatenate([time_weights, station_weights], axis=0).T)
-        sums = [jnp.zeros((own, HEAD), f32) for _ in range(micro)]
         for (g, m), mix in zip(pairs, mixes):
             for j in range(GROUP):
                 head = g * GROUP + j
@@ -274,17 +278,6 @@
                 )
                 result = hidden.astype(f32) + mixed
                 write(m, lanes, result)
-                if not last:
-                    rounded = result.astype(bf16).astype(f32)
-                    sums[m] = sums[m] + rounded * rounded
-        if not last:
-            outs[2][...] = jnp.zeros(outs[2].shape, f32)
-            for half in (CHIP, FAR):
-                parts = [part[half * edge : (half + 1) * edge] for part in sums]
-                column = jnp.sum(jnp.concatenate(parts, axis=0), axis=1, keepdims=True)
-                outs[2][half : half + 1, 0 : micro * edge] = jnp.sum(
-                    jnp.where(same(micro * edge), column, 0.0), axis=0, keepdims=True
-                )
 
     @pl.when(jnp.logical_not(active))
     def _():
@@ -295,8 +288,6 @@
                     ref[m * edge : (m + 1) * edge, lanes] for ref in (kept_chip_ref, kept_far_ref)
                 ]
                 write(m, lanes, jnp.concatenate(kept, axis=0).astype(f32))
-        if not last:
-            outs[2][...] = jnp.zeros(outs[2].shape, f32)
 
 
 def body(signal, head_proj, record_start, record_pad):
@@ -369,6 +360,25 @@
         cost_estimate=cost(signal.size, 2 * signal_bytes),
         name="halves",
     )(in_hbm(signal))
+    def moved(block, source, target, hop, other=False):
+        route = []
+        for i in range(seq_count):
+            to = i if hop == 0 else i + 1 - 2 * (i % 2) if hop == 1 else i - 1 + 2 * (i % 2)
+            if 0 <= to < seq_count:
+                for r in range(rep_count):
+                    route.append(
+                        (
+                            (source * seq_count + i) * rep_count + r,
+                            (target * seq_count + to) * rep_count
+                            + ((r + 1) % rep_count if other else r),
+                        )
+                    )
+        return lax.ppermute(block, ("section", "seq", "rep"), route)
+
+    next_far = moved(far, 0, 0, 2)
+    next_chip = moved(chip, 0, 0, 1)
+    squares = squares_of(chip, far, next_far, next_chip)
+    other_squares = moved(squares, 0, 0, 0, other=True)
     weights, time_bias, station_bias = pl.pallas_call(
         lambda *refs: fixed_kernel(*refs, stations=stations, total_steps=steps * seq_count),
         in_specs=[HBM] * 3 + [VMEM],
@@ -387,26 +397,7 @@
         cost_estimate=cost(signal.size, 2 * head_proj.size),
         name="fixed",
     )(in_hbm(head_proj), in_hbm(record_start), in_hbm(record_pad), chip)
-
-    def moved(block, source, target, hop, other=False):
-        route = []
-        for i in range(seq_count):
-            to = i if hop == 0 else i + 1 - 2 * (i % 2) if hop == 1 else i - 1 + 2 * (i % 2)
-            if 0 <= to < seq_count:
-                for r in range(rep_count):
-                    route.append(
-                        (
-                            (source * seq_count + i) * rep_count + r,
-                            (target * seq_count + to) * rep_count
-                            + ((r + 1) % rep_count if other else r),
-                        )
-                    )
-        return lax.ppermute(block, ("section", "seq", "rep"), route)
-
-    next_far = moved(far, 0, 0, 2)
-    next_chip = moved(chip, 0, 0, 1)
-    squares = lax.psum(squares_of(chip, far, next_far, next_chip), "rep")
-    inputs = (next_far, next_chip)
+    inputs = (next_far, next_chip, other_squares)
     kept = (chip, far)
     for tick in range(section_count):
         last = tick + 1 == section_count
@@ -417,7 +408,7 @@
         out_shape = (
             [jax.ShapeDtypeStruct((1,) + signal.shape, bf16)]
             if last
-            else [half_shape, half_shape, squares_shape]
+            else [half_shape, half_shape]
         )
         outputs = pl.pallas_call(
             kernel,
@@ -437,7 +428,8 @@
         )
         if last:
             return outputs[0]
-        *kept, mine = outputs
+        kept = outputs
+        mine = squares_of(*kept)
         chip = moved(kept[0], tick, tick + 1, 0)
         next_far = moved(kept[1], tick, tick + 1, 2)
         squares = moved(mine, tick, tick + 1, 0, other=True)

time: 29.8 us -> 28.4 us (0.953)
  the two profiles are of different devices: /device:TPU:23 before, /device:TPU:11 now
where the time goes in v11:
time: 28.4 us; the launch traced here: 27.9 us
  starting transfers between devices  13.9 us (49%)
  waiting for transfers between devices  8.19 us (29%)
  Pallas kernels  5.68 us (20%)
    ppermute x9, starting transfers between devices, moved(): return lax.ppermute(block, ('section', 'seq', 'rep'), route)  13.9 us
    ppermute x9, waiting for transfers between devices, moved(): return lax.ppermute(block, ('section', 'seq', 'rep'), route)  8.19 us
    pallas_call x2, Pallas kernels, body(): pl.pallas_call(kernel, in_specs=[VMEM] * (8 + len(inputs)), out_specs=[VM...  1.88 us
    pallas_call x1, Pallas kernels, body(): pl.pallas_call(lambda *refs: fixed_kernel(*refs, stations=stations, total...  1.44 us
    pallas_call x1, Pallas kernels, body(): pl.pallas_call(halves_kernel, in_specs=[HBM], out_specs=[VMEM] * 2, out_s...  1.02 us
    pallas_call x4, Pallas kernels, squares_of(): pl.pallas_call(squares_kernel, in_specs=[VMEM] * len(halves), out_specs=V...  0.83 us
  transfers between devices with their start and end apart: 9, of which 3 were waited for; matrix products, arithmetic and copies ran while one was open for 0% of the time, Pallas kernels for 9%

profile of v11, /device:TPU:11, one launch (start us, length us, event | category | flops | bytes accessed | tf_op | source)
XLA Modules:
  0.0 27.9 jit_solution(1092747879278364003)
XLA Ops:
  0.0 1.0 %halves.1 = (bf16[32,2048]{1,0:T(8,128)(2,1)S(1)}, bf16[32,2048]{1,0:T(8,128)(2,1)S(1)}) custom-call(bf16[2,8,4,2048]{3,2,1,0:T(4,128)(2,1)} %signal_hbm.1), custom_call_target="tpu_custom_call" | custom-call | flops 131072 | bytes 524288 | tf_op jit(solution)/shard_map/halves/pallas_call | solution.py:353
  1.0 0.7 %collective-permute-start = (bf16[32,2048]{1,0:T(8,128)(2,1)S(1)}, bf16[32,2048]{1,0:T(8,128)(2,1)S(1)}, u32[]{:S(2)}, u32[]{:S(2)}) collective-permute-start(bf16[32,2048]{1,0:T(8,128)(2,1)S(1)} %get-tuple-element.15.refs_1_.refs_7_), channel_id=1, source_target_pairs={{2,4},{3,5},{4,2},{5,3},{6,8},{7,9},{8,6},{9,7},{10,12},{11,13},{1... | collective-permute-start | bytes 393224 | tf_op jit(solution)/shard_map/ppermute | solution.py:376
  1.7 0.7 %collective-permute-start.1 = (bf16[32,2048]{1,0:T(8,128)(2,1)S(1)}, bf16[32,2048]{1,0:T(8,128)(2,1)S(1)}, u32[]{:S(2)}, u32[]{:S(2)}) collective-permute-start(bf16[32,2048]{1,0:T(8,128)(2,1)S(1)} %get-tuple-element.14.refs_0_.refs_3_.refs_6_), channel_id=1, source_target_pairs={{0,2},{1,3},{2,0},{3,1},{4,6},{5,7},{6,4},{7,5},{8,10},{9,11},{10,... | collective-permute-start | bytes 393224 | tf_op jit(solution)/shard_map/ppermute | solution.py:376
  2.4 0.0 collective-permute-done.refs_2_.refs_8_
  2.4 0.0 collective-permute-done.1.refs_3_.refs_9_
  2.4 0.3 squares.4.refs_2_
  2.7 0.7 %collective-permute-start.2 = (f32[8,128]{1,0:T(8,128)S(1)}, f32[8,128]{1,0:T(8,128)S(1)}, u32[]{:S(2)}, u32[]{:S(2)}) collective-permute-start(f32[8,128]{1,0:T(8,128)S(1)} %squares.4.refs_2_), channel_id=1, source_target_pairs={{0,1},{1,0},{2,3},{3,2},{4,5},{5,4},{6,7},{7,6},{8,9},{9,8},{10,11... | collective-permute-start | bytes 12296 | tf_op jit(solution)/shard_map/ppermute | solution.py:376
  3.4 1.4 %fixed.1 = (bf16[1,16,128,384]{3,2,1,0:T(8,128)(2,1)S(1)}, f32[2,64,128]{2,1,0:T(8,128)S(1)}, f32[2,32,128]{2,1,0:T(8,128)S(1)}) custom-call(bf16[1,16,128,384]{3,2,1,0:T(8,128)(2,1)} %refs_0_.1, s32[2,4]{1,0:T(2,128)} %refs_1_.1, s32[2,4]{1,0:T(2,128)} %refs_2_.1, bf16[32,2048]{1,0:T(8,128)(2,1)S(1)} %get-tuple-element.14.refs_0_.refs_3_.refs_6_), custom_call_target="tpu_custom_call" | custom-call | flops 131072 | bytes 1572864 | tf_op jit(solution)/shard_map/fixed/pallas_call | solution.py:382
  4.8 0.0 collective-permute-done.2.refs_10_
  4.8 0.1 layer.2
  4.9 1.3 %collective-permute-start.3 = (bf16[32,2048]{1,0:T(8,128)(2,1)S(1)}, bf16[32,2048]{1,0:T(8,128)(2,1)S(1)}, u32[]{:S(2)}, u32[]{:S(2)}) collective-permute-start(bf16[32,2048]{1,0:T(8,128)(2,1)S(1)} %get-tuple-element.19.refs_0_.refs_6_), channel_id=1, source_target_pairs={{0,16},{1,17},{2,18},{3,19},{4,20},{5,21},{6,22},{7,23},{8,24},{9,... | collective-permute-start | bytes 393224 | tf_op jit(solution)/shard_map/ppermute | solution.py:376
  6.2 0.2 squares.5.refs_0_
  6.4 1.3 %collective-permute-start.5 = (f32[8,128]{1,0:T(8,128)S(1)}, f32[8,128]{1,0:T(8,128)S(1)}, u32[]{:S(2)}, u32[]{:S(2)}) collective-permute-start(f32[8,128]{1,0:T(8,128)S(1)} %squares.5.refs_0_), channel_id=1, source_target_pairs={{0,17},{1,16},{2,19},{3,18},{4,21},{5,20},{6,23},{7,22},{8,25},{9,... | collective-permute-start | bytes 12296 | tf_op jit(solution)/shard_map/ppermute | solution.py:376
  7.7 1.3 %collective-permute-start.6 = (bf16[32,2048]{1,0:T(8,128)(2,1)S(1)}, bf16[32,2048]{1,0:T(8,128)(2,1)S(1)}, u32[]{:S(2)}, u32[]{:S(2)}) collective-permute-start(bf16[32,2048]{1,0:T(8,128)(2,1)S(1)} %get-tuple-element.20.refs_1_.refs_7_), channel_id=1, source_target_pairs={{2,20},{3,21},{4,18},{5,19},{6,24},{7,25},{8,22},{9,23},{10,28},{1... | collective-permute-start | bytes 393224 | tf_op jit(solution)/shard_map/ppermute | solution.py:376
  9.0 1.3 %collective-permute-start.7 = (f32[8,128]{1,0:T(8,128)S(1)}, f32[8,128]{1,0:T(8,128)S(1)}, u32[]{:S(2)}, u32[]{:S(2)}) collective-permute-start(f32[8,128]{1,0:T(8,128)S(1)} %get-tuple-element.22), channel_id=1, source_target_pairs={{2,21},{3,20},{4,19},{5,18},{6,25},{7,24},{8,23},{9,22},{10,29},{1... | collective-permute-start | bytes 12296 | tf_op jit(solution)/shard_map/ppermute | solution.py:376
  10.3 1.3 %collective-permute-start.4 = (bf16[32,2048]{1,0:T(8,128)(2,1)S(1)}, bf16[32,2048]{1,0:T(8,128)(2,1)S(1)}, u32[]{:S(2)}, u32[]{:S(2)}) collective-permute-start(bf16[32,2048]{1,0:T(8,128)(2,1)S(1)} %get-tuple-element.21), channel_id=1, source_target_pairs={{0,16},{1,17},{2,18},{3,19},{4,20},{5,21},{6,22},{7,23},{8,24},{9,... | collective-permute-start | bytes 393224 | tf_op jit(solution)/shard_map/ppermute | solution.py:376
  11.6 6.9 %collective-permute-done.3.refs_0_ = bf16[32,2048]{1,0:T(8,128)(2,1)S(1)} collective-permute-done((bf16[32,2048]{1,0:T(8,128)(2,1)S(1)}, bf16[32,2048]{1,0:T(8,128)(2,1)S(1)}, u32[]{:S(2)}, u32[]{:S(2)}) %collective-permute-start.3) | collective-permute-done | bytes 131104 | tf_op jit(solution)/shard_map/ppermute | solution.py:376
  18.5 0.2 squares.7.refs_1_
  18.7 0.3 collective-permute-done.5.refs_2_
  18.9 0.1 norm.1.refs_0_
  19.0 5.4 %collective-permute-start.8 = (bf16[32,2048]{1,0:T(8,128)(2,1)S(1)}, bf16[32,2048]{1,0:T(8,128)(2,1)S(1)}, u32[]{:S(2)}, u32[]{:S(2)}) collective-permute-start(bf16[32,2048]{1,0:T(8,128)(2,1)S(1)} %norm.1.refs_0_), channel_id=1, source_target_pairs={{16,18},{17,19},{18,16},{19,17},{20,22},{21,23},{22,20},{23,21},{2... | collective-permute-start | bytes 393224 | tf_op jit(solution)/shard_map/ppermute | solution.py:376
  24.5 0.4 %project.1.refs_11_ = bf16[32,6144]{1,0:T(8,128)(2,1)S(1)} custom-call(bf16[1,16,128,384]{3,2,1,0:T(8,128)(2,1)S(1)} %get-tuple-element.18.refs_5_.weights_ref, bf16[32,2048]{1,0:T(8,128)(2,1)S(1)} %norm.1.refs_0_), custom_call_target="tpu_custom_call" | custom-call | flops 2000000000 | bytes 300000 | tf_op jit(solution)/shard_map/project/pallas_call | solution.py:343
  24.9 0.0 collective-permute-done.6.refs_0_.refs_8_
  24.9 0.2 squares.6.mine_ref
  25.0 0.0 collective-permute-done.7.other_ref
  25.1 1.0 %collective-permute-done.4.refs_1_ = bf16[32,2048]{1,0:T(8,128)(2,1)S(1)} collective-permute-done((bf16[32,2048]{1,0:T(8,128)(2,1)S(1)}, bf16[32,2048]{1,0:T(8,128)(2,1)S(1)}, u32[]{:S(2)}, u32[]{:S(2)}) %collective-permute-start.4) | collective-permute-done | bytes 131104 | tf_op jit(solution)/shard_map/ppermute | solution.py:376
  26.1 0.0 collective-permute-done.8.refs_10_
  26.1 1.8 %layer.3 = bf16[1,2,8,4,2048]{4,3,2,1,0:T(4,128)(2,1)} custom-call(bf16[32,2048]{1,0:T(8,128)(2,1)S(1)} %collective-permute-done.3.refs_0_, bf16[32,2048]{1,0:T(8,128)(2,1)S(1)} %collective-permute-done.4.refs_1_, f32[8,128]{1,0:T(8,128)S(1)} %collective-permute-done.5.refs_2_, f32[2,64,128]{2,1,0:T(8,128)S(1)} %get-tuple-element.16.refs_3_, ...), custom_call_target="tpu_custom_call" | custom-call | flops 402653184 | bytes 4194304 | tf_op jit(solution)/shard_map/layer/pallas_call | solution.py:413
  (2 shorter events, 0.0 us)
Async XLA Ops:
  1.0 1.4 %collective-permute-start = (bf16[32,2048]{1,0:T(8,128)(2,1)S(1)}, bf16[32,2048]{1,0:T(8,128)(2,1)S(1)}, u32[]{:S(2)}, u32[]{:S(2)}) collective-permute-start(bf16[32,2048]{1,0:T(8,128)(2,1)S(1)} %get-tuple-element.15.refs_1_.refs_7_), channel_id=1, source_target_pairs={{2,4},{3,5},{4,2},{5,3},{6,8},{7,9},{8,6},{9,7},{10,12},{11,13},{1... | collective-permute-start | bytes 393224 | tf_op jit(solution)/shard_map/ppermute | solution.py:376
  1.7 0.7 %collective-permute-start.1 = (bf16[32,2048]{1,0:T(8,128)(2,1)S(1)}, bf16[32,2048]{1,0:T(8,128)(2,1)S(1)}, u32[]{:S(2)}, u32[]{:S(2)}) collective-permute-start(bf16[32,2048]{1,0:T(8,128)(2,1)S(1)} %get-tuple-element.14.refs_0_.refs_3_.refs_6_), channel_id=1, source_target_pairs={{0,2},{1,3},{2,0},{3,1},{4,6},{5,7},{6,4},{7,5},{8,10},{9,11},{10,... | collective-permute-start | bytes 393224 | tf_op jit(solution)/shard_map/ppermute | solution.py:376
  2.7 2.1 %collective-permute-start.2 = (f32[8,128]{1,0:T(8,128)S(1)}, f32[8,128]{1,0:T(8,128)S(1)}, u32[]{:S(2)}, u32[]{:S(2)}) collective-permute-start(f32[8,128]{1,0:T(8,128)S(1)} %squares.4.refs_2_), channel_id=1, source_target_pairs={{0,1},{1,0},{2,3},{3,2},{4,5},{5,4},{6,7},{7,6},{8,9},{9,8},{10,11... | collective-permute-start | bytes 12296 | tf_op jit(solution)/shard_map/ppermute | solution.py:376
  4.9 13.6 %collective-permute-start.3 = (bf16[32,2048]{1,0:T(8,128)(2,1)S(1)}, bf16[32,2048]{1,0:T(8,128)(2,1)S(1)}, u32[]{:S(2)}, u32[]{:S(2)}) collective-permute-start(bf16[32,2048]{1,0:T(8,128)(2,1)S(1)} %get-tuple-element.19.refs_0_.refs_6_), channel_id=1, source_target_pairs={{0,16},{1,17},{2,18},{3,19},{4,20},{5,21},{6,22},{7,23},{8,24},{9,... | collective-permute-start | bytes 393224 | tf_op jit(solution)/shard_map/ppermute | solution.py:376
  6.4 12.5 %collective-permute-start.5 = (f32[8,128]{1,0:T(8,128)S(1)}, f32[8,128]{1,0:T(8,128)S(1)}, u32[]{:S(2)}, u32[]{:S(2)}) collective-permute-start(f32[8,128]{1,0:T(8,128)S(1)} %squares.5.refs_0_), channel_id=1, source_target_pairs={{0,17},{1,16},{2,19},{3,18},{4,21},{5,20},{6,23},{7,22},{8,25},{9,... | collective-permute-start | bytes 12296 | tf_op jit(solution)/shard_map/ppermute | solution.py:376
  7.7 17.1 %collective-permute-start.6 = (bf16[32,2048]{1,0:T(8,128)(2,1)S(1)}, bf16[32,2048]{1,0:T(8,128)(2,1)S(1)}, u32[]{:S(2)}, u32[]{:S(2)}) collective-permute-start(bf16[32,2048]{1,0:T(8,128)(2,1)S(1)} %get-tuple-element.20.refs_1_.refs_7_), channel_id=1, source_target_pairs={{2,20},{3,21},{4,18},{5,19},{6,24},{7,25},{8,22},{9,23},{10,28},{1... | collective-permute-start | bytes 393224 | tf_op jit(solution)/shard_map/ppermute | solution.py:376
  9.0 16.0 %collective-permute-start.7 = (f32[8,128]{1,0:T(8,128)S(1)}, f32[8,128]{1,0:T(8,128)S(1)}, u32[]{:S(2)}, u32[]{:S(2)}) collective-permute-start(f32[8,128]{1,0:T(8,128)S(1)} %get-tuple-element.22), channel_id=1, source_target_pairs={{2,21},{3,20},{4,19},{5,18},{6,25},{7,24},{8,23},{9,22},{10,29},{1... | collective-permute-start | bytes 12296 | tf_op jit(solution)/shard_map/ppermute | solution.py:376
  10.3 15.8 %collective-permute-start.4 = (bf16[32,2048]{1,0:T(8,128)(2,1)S(1)}, bf16[32,2048]{1,0:T(8,128)(2,1)S(1)}, u32[]{:S(2)}, u32[]{:S(2)}) collective-permute-start(bf16[32,2048]{1,0:T(8,128)(2,1)S(1)} %get-tuple-element.21), channel_id=1, source_target_pairs={{0,16},{1,17},{2,18},{3,19},{4,20},{5,21},{6,22},{7,23},{8,24},{9,... | collective-permute-start | bytes 393224 | tf_op jit(solution)/shard_map/ppermute | solution.py:376
  19.0 7.1 %collective-permute-start.8 = (bf16[32,2048]{1,0:T(8,128)(2,1)S(1)}, bf16[32,2048]{1,0:T(8,128)(2,1)S(1)}, u32[]{:S(2)}, u32[]{:S(2)}) collective-permute-start(bf16[32,2048]{1,0:T(8,128)(2,1)S(1)} %norm.1.refs_0_), channel_id=1, source_target_pairs={{16,18},{17,19},{18,16},{19,17},{20,22},{21,23},{22,20},{23,21},{2... | collective-permute-start | bytes 393224 | tf_op jit(solution)/shard_map/ppermute | solution.py:376

commit v12 on v11

--- a/solution.py
+++ b/solution.py
@@ -180,14 +180,9 @@
     active = lax.axis_index("section") == tick
     projected = [None] * 4
     if tick == 0:
-        next_far_ref, next_chip_ref, other_squares_ref, *refs = refs
+        next_far_ref, next_chip_ref, *refs = refs
         late = [
-            (
-                half,
-                half_ref,
-                squares_ref[half : half + 1, :] + other_squares_ref[half : half + 1, :],
-                True,
-            )
+            (half, half_ref, squares_ref[half : half + 1, :], True)
             for half, half_ref in enumerate((chip_ref, far_ref, next_far_ref, next_chip_ref))
         ]
     else:
@@ -377,8 +372,7 @@
 
     next_far = moved(far, 0, 0, 2)
     next_chip = moved(chip, 0, 0, 1)
-    squares = squares_of(chip, far, next_far, next_chip)
-    other_squares = moved(squares, 0, 0, 0, other=True)
+    squares = lax.psum(squares_of(chip, far, next_far, next_chip), "rep")
     weights, time_bias, station_bias = pl.pallas_call(
         lambda *refs: fixed_kernel(*refs, stations=stations, total_steps=steps * seq_count),
         in_specs=[HBM] * 3 + [VMEM],
@@ -397,7 +391,7 @@
         cost_estimate=cost(signal.size, 2 * head_proj.size),
         name="fixed",
     )(in_hbm(head_proj), in_hbm(record_start), in_hbm(record_pad), chip)
-    inputs = (next_far, next_chip, other_squares)
+    inputs = (next_far, next_chip)
     kept = (chip, far)
     for tick in range(section_count):
         last = tick + 1 == section_count
@@ -433,8 +427,8 @@
         chip = moved(kept[0], tick, tick + 1, 0)
         next_far = moved(kept[1], tick, tick + 1, 2)
         squares = moved(mine, tick, tick + 1, 0, other=True)
-        mine_again, far_again = again(mine, kept[1])
-        far = moved(far_again, tick, tick + 1, 0)
+        (mine_again,) = again(mine)
+        far = moved(kept[1], tick, tick + 1, 0)
         far_squares = moved(mine_again, tick, tick + 1, 2, other=True)
         normed_chip = normed(chip, squares, CHIP)
         next_chip = moved(normed_chip, tick + 1, tick + 1, 1)

time: 28.4 us -> 27.8 us (0.979)
  waiting for transfers between devices: 8.19 us -> 3.97 us
  blocking collectives: 0 us -> 3.8 us
    ppermute x9 -> x8, waiting for transfers between devices: 8.19 us -> 3.97 us  [moved(): return lax.ppermute(block, ('section', 'seq', 'rep'), route)]
    psum x0 -> x1, blocking collectives: none -> 3.8 us  [body(): squares = lax.psum(squares_of(chip, far, next_far, next_chip), 'rep')]
    ppermute x9 -> x8, starting transfers between devices: 13.9 us -> 13.9 us  [moved(): return lax.ppermute(block, ('section', 'seq', 'rep'), route)]
  transfers between devices with their start and end apart: 9 -> 8, of which waited for: 3 -> 4; matrix products, arithmetic and copies ran while one was open for 0% -> 0% of each run, Pallas kernels for 9% -> 9%
where the time goes in v12:
time: 27.8 us; the launch traced here: 27.5 us
  starting transfers between devices  13.9 us (50%)
  Pallas kernels  5.64 us (20%)
  waiting for transfers between devices  3.97 us (14%)
  blocking collectives  3.8 us (14%)
    ppermute x8, starting transfers between devices, moved(): return lax.ppermute(block, ('section', 'seq', 'rep'), route)  13.9 us
    ppermute x8, waiting for transfers between devices, moved(): return lax.ppermute(block, ('section', 'seq', 'rep'), route)  3.97 us
    psum x1, blocking collectives, body(): squares = lax.psum(squares_of(chip, far, next_far, next_chip), 'rep')  3.8 us
    pallas_call x2, Pallas kernels, body(): pl.pallas_call(kernel, in_specs=[VMEM] * (8 + len(inputs)), out_specs=[VM...  1.86 us
    pallas_call x1, Pallas kernels, body(): pl.pallas_call(lambda *refs: fixed_kernel(*refs, stations=stations, total...  1.44 us
    pallas_call x1, Pallas kernels, body(): pl.pallas_call(halves_kernel, in_specs=[HBM], out_specs=[VMEM] * 2, out_s...  1.02 us
    pallas_call x4, Pallas kernels, squares_of(): pl.pallas_call(squares_kernel, in_specs=[VMEM] * len(halves), out_specs=V...  0.83 us
  transfers between devices with their start and end apart: 8, of which 4 were waited for; matrix products, arithmetic and copies ran while one was open for 0% of the time, Pallas kernels for 9%

profile of v12, /device:TPU:11, one launch (start us, length us, event | category | flops | bytes accessed | tf_op | source)
XLA Modules:
  0.0 27.5 jit_solution(7098736133352964926)
XLA Ops:
  0.0 1.0 %halves.1 = (bf16[32,2048]{1,0:T(8,128)(2,1)S(1)}, bf16[32,2048]{1,0:T(8,128)(2,1)S(1)}) custom-call(bf16[2,8,4,2048]{3,2,1,0:T(4,128)(2,1)} %signal_hbm.1), custom_call_target="tpu_custom_call" | custom-call | flops 131072 | bytes 524288 | tf_op jit(solution)/shard_map/halves/pallas_call | solution.py:348
  1.0 0.7 %collective-permute-start = (bf16[32,2048]{1,0:T(8,128)(2,1)S(1)}, bf16[32,2048]{1,0:T(8,128)(2,1)S(1)}, u32[]{:S(2)}, u32[]{:S(2)}) collective-permute-start(bf16[32,2048]{1,0:T(8,128)(2,1)S(1)} %get-tuple-element.13.refs_1_.refs_7_), channel_id=1, source_target_pairs={{2,4},{3,5},{4,2},{5,3},{6,8},{7,9},{8,6},{9,7},{10,12},{11,13},{1... | collective-permute-start | bytes 393224 | tf_op jit(solution)/shard_map/ppermute | solution.py:371
  1.7 0.7 %collective-permute-start.1 = (bf16[32,2048]{1,0:T(8,128)(2,1)S(1)}, bf16[32,2048]{1,0:T(8,128)(2,1)S(1)}, u32[]{:S(2)}, u32[]{:S(2)}) collective-permute-start(bf16[32,2048]{1,0:T(8,128)(2,1)S(1)} %get-tuple-element.12.refs_0_.refs_3_.refs_6_), channel_id=1, source_target_pairs={{0,2},{1,3},{2,0},{3,1},{4,6},{5,7},{6,4},{7,5},{8,10},{9,11},{10,... | collective-permute-start | bytes 393224 | tf_op jit(solution)/shard_map/ppermute | solution.py:371
  2.4 1.4 %fixed.1 = (bf16[1,16,128,384]{3,2,1,0:T(8,128)(2,1)S(1)}, f32[2,64,128]{2,1,0:T(8,128)S(1)}, f32[2,32,128]{2,1,0:T(8,128)S(1)}) custom-call(bf16[1,16,128,384]{3,2,1,0:T(8,128)(2,1)} %refs_0_.1, s32[2,4]{1,0:T(2,128)} %refs_1_.1, s32[2,4]{1,0:T(2,128)} %refs_2_.1, bf16[32,2048]{1,0:T(8,128)(2,1)S(1)} %get-tuple-element.12.refs_0_.refs_3_.refs_6_), custom_call_target="tpu_custom_call" | custom-call | flops 131072 | bytes 1572864 | tf_op jit(solution)/shard_map/fixed/pallas_call | solution.py:376
  3.8 0.0 collective-permute-done.refs_2_.refs_8_
  3.8 0.0 collective-permute-done.1.refs_3_.refs_9_
  3.8 0.3 %squares.4 = f32[8,128]{1,0:T(8,128)S(1)} custom-call(bf16[32,2048]{1,0:T(8,128)(2,1)S(1)} %get-tuple-element.12.refs_0_.refs_3_.refs_6_, bf16[32,2048]{1,0:T(8,128)(2,1)S(1)} %get-tuple-element.13.refs_1_.refs_7_, bf16[32,2048]{1,0:T(8,128)(2,1)S(1)} %collective-permute-done.refs_2_.refs_8_, bf16[32,2048]{1,0:T(8,128)(2,1)S(1)} %collective-permute-done.1.refs_3_.refs_9_), custom_call_target="tpu_custom_call" | custom-call | tf_op jit(solution)/shard_map/squares/pallas_call | solution.py:306
  4.1 3.8 %psum.7.refs_2_ = f32[8,128]{1,0:T(8,128)S(1)} all-reduce(f32[8,128]{1,0:T(8,128)S(1)} %squares.4), channel_id=1, replica_groups=mesh['section'=2,'seq'=8,'rep'=2] {'rep'}, use_global_device_ids=true, to_apply=%region_0.0 | all-reduce | flops 1024 | bytes 8192 | tf_op jit(solution)/shard_map/psum | solution.py:375
  7.9 0.1 layer.2
  8.0 1.3 %collective-permute-start.2 = (bf16[32,2048]{1,0:T(8,128)(2,1)S(1)}, bf16[32,2048]{1,0:T(8,128)(2,1)S(1)}, u32[]{:S(2)}, u32[]{:S(2)}) collective-permute-start(bf16[32,2048]{1,0:T(8,128)(2,1)S(1)} %get-tuple-element.17.refs_0_.refs_6_), channel_id=1, source_target_pairs={{0,16},{1,17},{2,18},{3,19},{4,20},{5,21},{6,22},{7,23},{8,24},{9,... | collective-permute-start | bytes 393224 | tf_op jit(solution)/shard_map/ppermute | solution.py:371
  9.3 0.2 squares.5.refs_0_
  9.5 1.3 %collective-permute-start.4 = (f32[8,128]{1,0:T(8,128)S(1)}, f32[8,128]{1,0:T(8,128)S(1)}, u32[]{:S(2)}, u32[]{:S(2)}) collective-permute-start(f32[8,128]{1,0:T(8,128)S(1)} %squares.5.refs_0_), channel_id=1, source_target_pairs={{0,17},{1,16},{2,19},{3,18},{4,21},{5,20},{6,23},{7,22},{8,25},{9,... | collective-permute-start | bytes 12296 | tf_op jit(solution)/shard_map/ppermute | solution.py:371
  10.8 1.3 %collective-permute-start.5 = (bf16[32,2048]{1,0:T(8,128)(2,1)S(1)}, bf16[32,2048]{1,0:T(8,128)(2,1)S(1)}, u32[]{:S(2)}, u32[]{:S(2)}) collective-permute-start(bf16[32,2048]{1,0:T(8,128)(2,1)S(1)} %get-tuple-element.18.refs_1_.refs_7_), channel_id=1, source_target_pairs={{2,20},{3,21},{4,18},{5,19},{6,24},{7,25},{8,22},{9,23},{10,28},{1... | collective-permute-start | bytes 393224 | tf_op jit(solution)/shard_map/ppermute | solution.py:371
  12.1 1.3 %collective-permute-start.3 = (bf16[32,2048]{1,0:T(8,128)(2,1)S(1)}, bf16[32,2048]{1,0:T(8,128)(2,1)S(1)}, u32[]{:S(2)}, u32[]{:S(2)}) collective-permute-start(bf16[32,2048]{1,0:T(8,128)(2,1)S(1)} %get-tuple-element.18.refs_1_.refs_7_), channel_id=1, source_target_pairs={{0,16},{1,17},{2,18},{3,19},{4,20},{5,21},{6,22},{7,23},{8,24},{9,... | collective-permute-start | bytes 393224 | tf_op jit(solution)/shard_map/ppermute | solution.py:371
  13.4 1.3 %collective-permute-start.6 = (f32[8,128]{1,0:T(8,128)S(1)}, f32[8,128]{1,0:T(8,128)S(1)}, u32[]{:S(2)}, u32[]{:S(2)}) collective-permute-start(f32[8,128]{1,0:T(8,128)S(1)} %copy.6), channel_id=1, source_target_pairs={{2,21},{3,20},{4,19},{5,18},{6,25},{7,24},{8,23},{9,22},{10,29},{1... | collective-permute-start | bytes 12296 | tf_op jit(solution)/shard_map/ppermute | solution.py:371
  14.7 2.6 %collective-permute-done.2.refs_0_ = bf16[32,2048]{1,0:T(8,128)(2,1)S(1)} collective-permute-done((bf16[32,2048]{1,0:T(8,128)(2,1)S(1)}, bf16[32,2048]{1,0:T(8,128)(2,1)S(1)}, u32[]{:S(2)}, u32[]{:S(2)}) %collective-permute-start.2) | collective-permute-done | bytes 131104 | tf_op jit(solution)/shard_map/ppermute | solution.py:371
  17.4 0.2 squares.7.refs_1_
  17.5 0.9 %collective-permute-done.4.refs_2_ = f32[8,128]{1,0:T(8,128)S(1)} collective-permute-done((f32[8,128]{1,0:T(8,128)S(1)}, f32[8,128]{1,0:T(8,128)S(1)}, u32[]{:S(2)}, u32[]{:S(2)}) %collective-permute-start.4) | collective-permute-done | bytes 4128 | tf_op jit(solution)/shard_map/ppermute | solution.py:371
  18.5 0.1 norm.1.refs_0_
  18.6 6.1 %collective-permute-start.7 = (bf16[32,2048]{1,0:T(8,128)(2,1)S(1)}, bf16[32,2048]{1,0:T(8,128)(2,1)S(1)}, u32[]{:S(2)}, u32[]{:S(2)}) collective-permute-start(bf16[32,2048]{1,0:T(8,128)(2,1)S(1)} %norm.1.refs_0_), channel_id=1, source_target_pairs={{16,18},{17,19},{18,16},{19,17},{20,22},{21,23},{22,20},{23,21},{2... | collective-permute-start | bytes 393224 | tf_op jit(solution)/shard_map/ppermute | solution.py:371
  24.7 0.4 %project.1.refs_11_ = bf16[32,6144]{1,0:T(8,128)(2,1)S(1)} custom-call(bf16[1,16,128,384]{3,2,1,0:T(8,128)(2,1)S(1)} %get-tuple-element.16.refs_5_.weights_ref, bf16[32,2048]{1,0:T(8,128)(2,1)S(1)} %norm.1.refs_0_), custom_call_target="tpu_custom_call" | custom-call | flops 2000000000 | bytes 300000 | tf_op jit(solution)/shard_map/project/pallas_call | solution.py:338
  25.1 0.0 collective-permute-done.5.refs_0_.refs_8_
  25.1 0.2 squares.6.mine_ref
  25.3 0.1 collective-permute-done.6.other_ref
  25.3 0.0 collective-permute-done.3.refs_1_
  25.3 0.3 %collective-permute-done.7.refs_10_ = bf16[32,2048]{1,0:T(8,128)(2,1)S(1)} collective-permute-done((bf16[32,2048]{1,0:T(8,128)(2,1)S(1)}, bf16[32,2048]{1,0:T(8,128)(2,1)S(1)}, u32[]{:S(2)}, u32[]{:S(2)}) %collective-permute-start.7) | collective-permute-done | bytes 131104 | tf_op jit(solution)/shard_map/ppermute | solution.py:371
  25.7 1.8 %layer.3 = bf16[1,2,8,4,2048]{4,3,2,1,0:T(4,128)(2,1)} custom-call(bf16[32,2048]{1,0:T(8,128)(2,1)S(1)} %collective-permute-done.2.refs_0_, bf16[32,2048]{1,0:T(8,128)(2,1)S(1)} %collective-permute-done.3.refs_1_, f32[8,128]{1,0:T(8,128)S(1)} %collective-permute-done.4.refs_2_, f32[2,64,128]{2,1,0:T(8,128)S(1)} %get-tuple-element.14.refs_3_, ...), custom_call_target="tpu_custom_call" | custom-call | flops 402653184 | bytes 4194304 | tf_op jit(solution)/shard_map/layer/pallas_call | solution.py:407
  (2 shorter events, 0.0 us)
Async XLA Ops:
  1.0 2.8 %collective-permute-start = (bf16[32,2048]{1,0:T(8,128)(2,1)S(1)}, bf16[32,2048]{1,0:T(8,128)(2,1)S(1)}, u32[]{:S(2)}, u32[]{:S(2)}) collective-permute-start(bf16[32,2048]{1,0:T(8,128)(2,1)S(1)} %get-tuple-element.13.refs_1_.refs_7_), channel_id=1, source_target_pairs={{2,4},{3,5},{4,2},{5,3},{6,8},{7,9},{8,6},{9,7},{10,12},{11,13},{1... | collective-permute-start | bytes 393224 | tf_op jit(solution)/shard_map/ppermute | solution.py:371
  1.7 2.1 %collective-permute-start.1 = (bf16[32,2048]{1,0:T(8,128)(2,1)S(1)}, bf16[32,2048]{1,0:T(8,128)(2,1)S(1)}, u32[]{:S(2)}, u32[]{:S(2)}) collective-permute-start(bf16[32,2048]{1,0:T(8,128)(2,1)S(1)} %get-tuple-element.12.refs_0_.refs_3_.refs_6_), channel_id=1, source_target_pairs={{0,2},{1,3},{2,0},{3,1},{4,6},{5,7},{6,4},{7,5},{8,10},{9,11},{10,... | collective-permute-start | bytes 393224 | tf_op jit(solution)/shard_map/ppermute | solution.py:371
  8.0 9.4 %collective-permute-start.2 = (bf16[32,2048]{1,0:T(8,128)(2,1)S(1)}, bf16[32,2048]{1,0:T(8,128)(2,1)S(1)}, u32[]{:S(2)}, u32[]{:S(2)}) collective-permute-start(bf16[32,2048]{1,0:T(8,128)(2,1)S(1)} %get-tuple-element.17.refs_0_.refs_6_), channel_id=1, source_target_pairs={{0,16},{1,17},{2,18},{3,19},{4,20},{5,21},{6,22},{7,23},{8,24},{9,... | collective-permute-start | bytes 393224 | tf_op jit(solution)/shard_map/ppermute | solution.py:371
  9.5 9.0 %collective-permute-start.4 = (f32[8,128]{1,0:T(8,128)S(1)}, f32[8,128]{1,0:T(8,128)S(1)}, u32[]{:S(2)}, u32[]{:S(2)}) collective-permute-start(f32[8,128]{1,0:T(8,128)S(1)} %squares.5.refs_0_), channel_id=1, source_target_pairs={{0,17},{1,16},{2,19},{3,18},{4,21},{5,20},{6,23},{7,22},{8,25},{9,... | collective-permute-start | bytes 12296 | tf_op jit(solution)/shard_map/ppermute | solution.py:371
  10.8 14.3 %collective-permute-start.5 = (bf16[32,2048]{1,0:T(8,128)(2,1)S(1)}, bf16[32,2048]{1,0:T(8,128)(2,1)S(1)}, u32[]{:S(2)}, u32[]{:S(2)}) collective-permute-start(bf16[32,2048]{1,0:T(8,128)(2,1)S(1)} %get-tuple-element.18.refs_1_.refs_7_), channel_id=1, source_target_pairs={{2,20},{3,21},{4,18},{5,19},{6,24},{7,25},{8,22},{9,23},{10,28},{1... | collective-permute-start | bytes 393224 | tf_op jit(solution)/shard_map/ppermute | solution.py:371
  12.1 13.2 %collective-permute-start.3 = (bf16[32,2048]{1,0:T(8,128)(2,1)S(1)}, bf16[32,2048]{1,0:T(8,128)(2,1)S(1)}, u32[]{:S(2)}, u32[]{:S(2)}) collective-permute-start(bf16[32,2048]{1,0:T(8,128)(2,1)S(1)} %get-tuple-element.18.refs_1_.refs_7_), channel_id=1, source_target_pairs={{0,16},{1,17},{2,18},{3,19},{4,20},{5,21},{6,22},{7,23},{8,24},{9,... | collective-permute-start | bytes 393224 | tf_op jit(solution)/shard_map/ppermute | solution.py:371
  13.4 11.9 %collective-permute-start.6 = (f32[8,128]{1,0:T(8,128)S(1)}, f32[8,128]{1,0:T(8,128)S(1)}, u32[]{:S(2)}, u32[]{:S(2)}) collective-permute-start(f32[8,128]{1,0:T(8,128)S(1)} %copy.6), channel_id=1, source_target_pairs={{2,21},{3,20},{4,19},{5,18},{6,25},{7,24},{8,23},{9,22},{10,29},{1... | collective-permute-start | bytes 12296 | tf_op jit(solution)/shard_map/ppermute | solution.py:371
  18.6 7.1 %collective-permute-start.7 = (bf16[32,2048]{1,0:T(8,128)(2,1)S(1)}, bf16[32,2048]{1,0:T(8,128)(2,1)S(1)}, u32[]{:S(2)}, u32[]{:S(2)}) collective-permute-start(bf16[32,2048]{1,0:T(8,128)(2,1)S(1)} %norm.1.refs_0_), channel_id=1, source_target_pairs={{16,18},{17,19},{18,16},{19,17},{20,22},{21,23},{22,20},{23,21},{2... | collective-permute-start | bytes 393224 | tf_op jit(solution)/shard_map/ppermute | solution.py:371

commit v13 on v12

--- a/solution.py
+++ b/solution.py
@@ -228,51 +228,60 @@
         if tick > 0:
             normed.append(next_chip_ref)
         project_kernel(weights_ref, *normed, *[projected[half] for half in projecting])
-        pairs = [(g, m) for g in range(heads_dev // GROUP) for m in range(micro)]
+        groups = range(heads_dev // GROUP)
         blank = jnp.zeros((own, HEAD), bf16)
-        scores = []
-        for g, m in pairs:
+        columns = GROUP * own
+        scores = {}
+        for g in groups:
             at = [(g * GROUP + j) * width for j in range(GROUP)]
-            queries = [jnp.concatenate(rows_of((CHIP, FAR), m, a), axis=0) for a in at]
-            spread = jnp.concatenate(
-                [
+            spread, keys = [], []
+            for m in range(micro):
+                queries = [jnp.concatenate(rows_of((CHIP, FAR), m, a), axis=0) for a in at]
+                for j in range(GROUP):
+                    spread.append(
+                        jnp.concatenate(
+                            [queries[j] if i == j else blank for i in range(GROUP)], axis=1
+                        )
+                    )
+                keys.append(
                     jnp.concatenate(
-                        [queries[j] if i == j else blank for i in range(GROUP)],
-                        axis=1,
+                        [jnp.concatenate(rows_of(range(4), m, a + HEAD), axis=0) for a in at], axis=1
                     )
-                    for j in range(GROUP)
-                ],
-                axis=0,
+                )
+            score = lax.dot_general(
+                jnp.concatenate(keys, axis=0),
+                jnp.concatenate(spread, axis=0),
+                (((1,), (1,)), ((), ())),
+                preferred_element_type=f32,
             )
-            keys = jnp.concatenate(
-                [jnp.concatenate(rows_of(range(4), m, a + HEAD), axis=0) for a in at], axis=1
-            )
-            scores.append(
-                lax.dot_general(
-                    keys, spread, (((1,), (1,)), ((), ())), preferred_element_type=f32
-                )
-                * (1.0 / math.sqrt(HEAD))
-            )
-        mixes = []
-        for (g, m), score in zip(pairs, scores):
+            for m in range(micro):
+                scores[g, m] = score[
+                    m * 2 * own : (m + 1) * 2 * own, m * columns : (m + 1) * columns
+                ] * (1.0 / math.sqrt(HEAD))
+        mixes = {}
+        for (g, m), score in scores.items():
             time_weights = softmax_columns(score + time_ref[m])
             station_weights = softmax_columns(score[:own] + station_ref[m])
-            mixes.append(jnp.concatenate([time_weights, station_weights], axis=0).T)
-        for (g, m), mix in zip(pairs, mixes):
-            for j in range(GROUP):
-                head = g * GROUP + j
-                at = head * width + 2 * HEAD
+            mixes[g, m] = jnp.concatenate([time_weights, station_weights], axis=0).T
+        for (g, m), mix in mixes.items():
+            for j in range(0, GROUP, 2):
+                pair = [g * GROUP + j, g * GROUP + j + 1]
+                values = [
+                    jnp.concatenate(rows_of((0, 1, 2, 3, CHIP, FAR), m, head * width + 2 * HEAD), axis=0)
+                    for head in pair
+                ]
                 mixed = jnp.dot(
-                    mix[j * own : (j + 1) * own],
-                    jnp.concatenate(rows_of((0, 1, 2, 3, CHIP, FAR), m, at), axis=0),
+                    mix[j * own : (j + 2) * own],
+                    jnp.concatenate(values, axis=1),
                     preferred_element_type=f32,
                 )
-                lanes = slice(head * HEAD, (head + 1) * HEAD)
-                hidden = jnp.concatenate(
-                    [ref[m * edge : (m + 1) * edge, lanes] for ref in (chip_ref, far_ref)], axis=0
-                )
-                result = hidden.astype(f32) + mixed
-                write(m, lanes, result)
+                for i, head in enumerate(pair):
+                    lanes = slice(head * HEAD, (head + 1) * HEAD)
+                    hidden = jnp.concatenate(
+                        [ref[m * edge : (m + 1) * edge, lanes] for ref in (chip_ref, far_ref)], axis=0
+                    )
+                    update = mixed[i * own : (i + 1) * own, i * HEAD : (i + 1) * HEAD]
+                    write(m, lanes, hidden.astype(f32) + update)
 
     @pl.when(jnp.logical_not(active))
     def _():

time: 27.8 us -> 28 us (level)
  no operation moved by 1% of the time
where the time goes in v13:
time: 28 us; the launch traced here: 27.7 us
  starting transfers between devices  13.9 us (50%)
  Pallas kernels  5.8 us (21%)
  waiting for transfers between devices  4.07 us (15%)
  blocking collectives  3.8 us (14%)
    ppermute x8, starting transfers between devices, moved(): return lax.ppermute(block, ('section', 'seq', 'rep'), route)  13.9 us
    ppermute x8, waiting for transfers between devices, moved(): return lax.ppermute(block, ('section', 'seq', 'rep'), route)  4.07 us
    psum x1, blocking collectives, body(): squares = lax.psum(squares_of(chip, far, next_far, next_chip), 'rep')  3.8 us
    pallas_call x2, Pallas kernels, body(): pl.pallas_call(kernel, in_specs=[VMEM] * (8 + len(inputs)), out_specs=[VM...  2.02 us
    pallas_call x1, Pallas kernels, body(): pl.pallas_call(lambda *refs: fixed_kernel(*refs, stations=stations, total...  1.44 us
    pallas_call x1, Pallas kernels, body(): pl.pallas_call(halves_kernel, in_specs=[HBM], out_specs=[VMEM] * 2, out_s...  1.02 us
    pallas_call x4, Pallas kernels, squares_of(): pl.pallas_call(squares_kernel, in_specs=[VMEM] * len(halves), out_specs=V...  0.83 us
  transfers between devices with their start and end apart: 8, of which 4 were waited for; matrix products, arithmetic and copies ran while one was open for 0% of the time, Pallas kernels for 9%

profile of v13, /device:TPU:11, one launch (start us, length us, event | category | flops | bytes accessed | tf_op | source)
XLA Modules:
  0.0 27.7 jit_solution(2316797310018654524)
XLA Ops:
  0.0 1.0 %halves.1 = (bf16[32,2048]{1,0:T(8,128)(2,1)S(1)}, bf16[32,2048]{1,0:T(8,128)(2,1)S(1)}) custom-call(bf16[2,8,4,2048]{3,2,1,0:T(4,128)(2,1)} %signal_hbm.1), custom_call_target="tpu_custom_call" | custom-call | flops 131072 | bytes 524288 | tf_op jit(solution)/shard_map/halves/pallas_call | solution.py:357
  1.0 0.7 %collective-permute-start = (bf16[32,2048]{1,0:T(8,128)(2,1)S(1)}, bf16[32,2048]{1,0:T(8,128)(2,1)S(1)}, u32[]{:S(2)}, u32[]{:S(2)}) collective-permute-start(bf16[32,2048]{1,0:T(8,128)(2,1)S(1)} %get-tuple-element.13.refs_1_.refs_7_), channel_id=1, source_target_pairs={{2,4},{3,5},{4,2},{5,3},{6,8},{7,9},{8,6},{9,7},{10,12},{11,13},{1... | collective-permute-start | bytes 393224 | tf_op jit(solution)/shard_map/ppermute | solution.py:380
  1.7 0.7 %collective-permute-start.1 = (bf16[32,2048]{1,0:T(8,128)(2,1)S(1)}, bf16[32,2048]{1,0:T(8,128)(2,1)S(1)}, u32[]{:S(2)}, u32[]{:S(2)}) collective-permute-start(bf16[32,2048]{1,0:T(8,128)(2,1)S(1)} %get-tuple-element.12.refs_0_.refs_3_.refs_6_), channel_id=1, source_target_pairs={{0,2},{1,3},{2,0},{3,1},{4,6},{5,7},{6,4},{7,5},{8,10},{9,11},{10,... | collective-permute-start | bytes 393224 | tf_op jit(solution)/shard_map/ppermute | solution.py:380
  2.4 1.4 %fixed.1 = (bf16[1,16,128,384]{3,2,1,0:T(8,128)(2,1)S(1)}, f32[2,64,128]{2,1,0:T(8,128)S(1)}, f32[2,32,128]{2,1,0:T(8,128)S(1)}) custom-call(bf16[1,16,128,384]{3,2,1,0:T(8,128)(2,1)} %refs_0_.1, s32[2,4]{1,0:T(2,128)} %refs_1_.1, s32[2,4]{1,0:T(2,128)} %refs_2_.1, bf16[32,2048]{1,0:T(8,128)(2,1)S(1)} %get-tuple-element.12.refs_0_.refs_3_.refs_6_), custom_call_target="tpu_custom_call" | custom-call | flops 131072 | bytes 1572864 | tf_op jit(solution)/shard_map/fixed/pallas_call | solution.py:385
  3.8 0.0 collective-permute-done.refs_2_.refs_8_
  3.8 0.0 collective-permute-done.1.refs_3_.refs_9_
  3.8 0.3 squares.4
  4.1 3.8 %psum.7.refs_2_ = f32[8,128]{1,0:T(8,128)S(1)} all-reduce(f32[8,128]{1,0:T(8,128)S(1)} %squares.4), channel_id=1, replica_groups=mesh['section'=2,'seq'=8,'rep'=2] {'rep'}, use_global_device_ids=true, to_apply=%region_0.0 | all-reduce | flops 1024 | bytes 8192 | tf_op jit(solution)/shard_map/psum | solution.py:384
  7.9 0.1 layer.2
  8.0 1.3 %collective-permute-start.2 = (bf16[32,2048]{1,0:T(8,128)(2,1)S(1)}, bf16[32,2048]{1,0:T(8,128)(2,1)S(1)}, u32[]{:S(2)}, u32[]{:S(2)}) collective-permute-start(bf16[32,2048]{1,0:T(8,128)(2,1)S(1)} %get-tuple-element.17.refs_0_.refs_6_), channel_id=1, source_target_pairs={{0,16},{1,17},{2,18},{3,19},{4,20},{5,21},{6,22},{7,23},{8,24},{9,... | collective-permute-start | bytes 393224 | tf_op jit(solution)/shard_map/ppermute | solution.py:380
  9.3 0.2 squares.5.refs_0_
  9.5 1.3 %collective-permute-start.4 = (f32[8,128]{1,0:T(8,128)S(1)}, f32[8,128]{1,0:T(8,128)S(1)}, u32[]{:S(2)}, u32[]{:S(2)}) collective-permute-start(f32[8,128]{1,0:T(8,128)S(1)} %squares.5.refs_0_), channel_id=1, source_target_pairs={{0,17},{1,16},{2,19},{3,18},{4,21},{5,20},{6,23},{7,22},{8,25},{9,... | collective-permute-start | bytes 12296 | tf_op jit(solution)/shard_map/ppermute | solution.py:380
  10.8 1.3 %collective-permute-start.5 = (bf16[32,2048]{1,0:T(8,128)(2,1)S(1)}, bf16[32,2048]{1,0:T(8,128)(2,1)S(1)}, u32[]{:S(2)}, u32[]{:S(2)}) collective-permute-start(bf16[32,2048]{1,0:T(8,128)(2,1)S(1)} %get-tuple-element.18.refs_1_.refs_7_), channel_id=1, source_target_pairs={{2,20},{3,21},{4,18},{5,19},{6,24},{7,25},{8,22},{9,23},{10,28},{1... | collective-permute-start | bytes 393224 | tf_op jit(solution)/shard_map/ppermute | solution.py:380
  12.1 1.3 %collective-permute-start.3 = (bf16[32,2048]{1,0:T(8,128)(2,1)S(1)}, bf16[32,2048]{1,0:T(8,128)(2,1)S(1)}, u32[]{:S(2)}, u32[]{:S(2)}) collective-permute-start(bf16[32,2048]{1,0:T(8,128)(2,1)S(1)} %get-tuple-element.18.refs_1_.refs_7_), channel_id=1, source_target_pairs={{0,16},{1,17},{2,18},{3,19},{4,20},{5,21},{6,22},{7,23},{8,24},{9,... | collective-permute-start | bytes 393224 | tf_op jit(solution)/shard_map/ppermute | solution.py:380
  13.4 1.3 %collective-permute-start.6 = (f32[8,128]{1,0:T(8,128)S(1)}, f32[8,128]{1,0:T(8,128)S(1)}, u32[]{:S(2)}, u32[]{:S(2)}) collective-permute-start(f32[8,128]{1,0:T(8,128)S(1)} %copy.6), channel_id=1, source_target_pairs={{2,21},{3,20},{4,19},{5,18},{6,25},{7,24},{8,23},{9,22},{10,29},{1... | collective-permute-start | bytes 12296 | tf_op jit(solution)/shard_map/ppermute | solution.py:380
  14.7 2.7 %collective-permute-done.2.refs_0_ = bf16[32,2048]{1,0:T(8,128)(2,1)S(1)} collective-permute-done((bf16[32,2048]{1,0:T(8,128)(2,1)S(1)}, bf16[32,2048]{1,0:T(8,128)(2,1)S(1)}, u32[]{:S(2)}, u32[]{:S(2)}) %collective-permute-start.2) | collective-permute-done | bytes 131104 | tf_op jit(solution)/shard_map/ppermute | solution.py:380
  17.4 0.2 squares.7.refs_1_
  17.6 0.9 %collective-permute-done.4.refs_2_ = f32[8,128]{1,0:T(8,128)S(1)} collective-permute-done((f32[8,128]{1,0:T(8,128)S(1)}, f32[8,128]{1,0:T(8,128)S(1)}, u32[]{:S(2)}, u32[]{:S(2)}) %collective-permute-start.4) | collective-permute-done | bytes 4128 | tf_op jit(solution)/shard_map/ppermute | solution.py:380
  18.6 0.1 norm.1.refs_0_
  18.7 6.1 %collective-permute-start.7 = (bf16[32,2048]{1,0:T(8,128)(2,1)S(1)}, bf16[32,2048]{1,0:T(8,128)(2,1)S(1)}, u32[]{:S(2)}, u32[]{:S(2)}) collective-permute-start(bf16[32,2048]{1,0:T(8,128)(2,1)S(1)} %norm.1.refs_0_), channel_id=1, source_target_pairs={{16,18},{17,19},{18,16},{19,17},{20,22},{21,23},{22,20},{23,21},{2... | collective-permute-start | bytes 393224 | tf_op jit(solution)/shard_map/ppermute | solution.py:380
  24.8 0.4 %project.1.refs_11_ = bf16[32,6144]{1,0:T(8,128)(2,1)S(1)} custom-call(bf16[1,16,128,384]{3,2,1,0:T(8,128)(2,1)S(1)} %get-tuple-element.16.refs_5_.weights_ref, bf16[32,2048]{1,0:T(8,128)(2,1)S(1)} %norm.1.refs_0_), custom_call_target="tpu_custom_call" | custom-call | flops 2000000000 | bytes 300000 | tf_op jit(solution)/shard_map/project/pallas_call | solution.py:347
  25.2 0.0 collective-permute-done.5.refs_0_.refs_8_
  25.2 0.2 squares.6.mine_ref
  25.4 0.1 collective-permute-done.6.other_ref
  25.4 0.0 collective-permute-done.3.refs_1_
  25.4 0.3 %collective-permute-done.7.refs_10_ = bf16[32,2048]{1,0:T(8,128)(2,1)S(1)} collective-permute-done((bf16[32,2048]{1,0:T(8,128)(2,1)S(1)}, bf16[32,2048]{1,0:T(8,128)(2,1)S(1)}, u32[]{:S(2)}, u32[]{:S(2)}) %collective-permute-start.7) | collective-permute-done | bytes 131104 | tf_op jit(solution)/shard_map/ppermute | solution.py:380
  25.8 2.0 %layer.3 = bf16[1,2,8,4,2048]{4,3,2,1,0:T(4,128)(2,1)} custom-call(bf16[32,2048]{1,0:T(8,128)(2,1)S(1)} %collective-permute-done.2.refs_0_, bf16[32,2048]{1,0:T(8,128)(2,1)S(1)} %collective-permute-done.3.refs_1_, f32[8,128]{1,0:T(8,128)S(1)} %collective-permute-done.4.refs_2_, f32[2,64,128]{2,1,0:T(8,128)S(1)} %get-tuple-element.14.refs_3_, ...), custom_call_target="tpu_custom_call" | custom-call | flops 402653184 | bytes 4194304 | tf_op jit(solution)/shard_map/layer/pallas_call | solution.py:416
  (2 shorter events, 0.0 us)
Async XLA Ops:
  1.0 2.8 %collective-permute-start = (bf16[32,2048]{1,0:T(8,128)(2,1)S(1)}, bf16[32,2048]{1,0:T(8,128)(2,1)S(1)}, u32[]{:S(2)}, u32[]{:S(2)}) collective-permute-start(bf16[32,2048]{1,0:T(8,128)(2,1)S(1)} %get-tuple-element.13.refs_1_.refs_7_), channel_id=1, source_target_pairs={{2,4},{3,5},{4,2},{5,3},{6,8},{7,9},{8,6},{9,7},{10,12},{11,13},{1... | collective-permute-start | bytes 393224 | tf_op jit(solution)/shard_map/ppermute | solution.py:380
  1.7 2.1 %collective-permute-start.1 = (bf16[32,2048]{1,0:T(8,128)(2,1)S(1)}, bf16[32,2048]{1,0:T(8,128)(2,1)S(1)}, u32[]{:S(2)}, u32[]{:S(2)}) collective-permute-start(bf16[32,2048]{1,0:T(8,128)(2,1)S(1)} %get-tuple-element.12.refs_0_.refs_3_.refs_6_), channel_id=1, source_target_pairs={{0,2},{1,3},{2,0},{3,1},{4,6},{5,7},{6,4},{7,5},{8,10},{9,11},{10,... | collective-permute-start | bytes 393224 | tf_op jit(solution)/shard_map/ppermute | solution.py:380
  8.0 9.5 %collective-permute-start.2 = (bf16[32,2048]{1,0:T(8,128)(2,1)S(1)}, bf16[32,2048]{1,0:T(8,128)(2,1)S(1)}, u32[]{:S(2)}, u32[]{:S(2)}) collective-permute-start(bf16[32,2048]{1,0:T(8,128)(2,1)S(1)} %get-tuple-element.17.refs_0_.refs_6_), channel_id=1, source_target_pairs={{0,16},{1,17},{2,18},{3,19},{4,20},{5,21},{6,22},{7,23},{8,24},{9,... | collective-permute-start | bytes 393224 | tf_op jit(solution)/shard_map/ppermute | solution.py:380
  9.5 9.1 %collective-permute-start.4 = (f32[8,128]{1,0:T(8,128)S(1)}, f32[8,128]{1,0:T(8,128)S(1)}, u32[]{:S(2)}, u32[]{:S(2)}) collective-permute-start(f32[8,128]{1,0:T(8,128)S(1)} %squares.5.refs_0_), channel_id=1, source_target_pairs={{0,17},{1,16},{2,19},{3,18},{4,21},{5,20},{6,23},{7,22},{8,25},{9,... | collective-permute-start | bytes 12296 | tf_op jit(solution)/shard_map/ppermute | solution.py:380
  10.8 14.4 %collective-permute-start.5 = (bf16[32,2048]{1,0:T(8,128)(2,1)S(1)}, bf16[32,2048]{1,0:T(8,128)(2,1)S(1)}, u32[]{:S(2)}, u32[]{:S(2)}) collective-permute-start(bf16[32,2048]{1,0:T(8,128)(2,1)S(1)} %get-tuple-element.18.refs_1_.refs_7_), channel_id=1, source_target_pairs={{2,20},{3,21},{4,18},{5,19},{6,24},{7,25},{8,22},{9,23},{10,28},{1... | collective-permute-start | bytes 393224 | tf_op jit(solution)/shard_map/ppermute | solution.py:380
  12.1 13.3 %collective-permute-start.3 = (bf16[32,2048]{1,0:T(8,128)(2,1)S(1)}, bf16[32,2048]{1,0:T(8,128)(2,1)S(1)}, u32[]{:S(2)}, u32[]{:S(2)}) collective-permute-start(bf16[32,2048]{1,0:T(8,128)(2,1)S(1)} %get-tuple-element.18.refs_1_.refs_7_), channel_id=1, source_target_pairs={{0,16},{1,17},{2,18},{3,19},{4,20},{5,21},{6,22},{7,23},{8,24},{9,... | collective-permute-start | bytes 393224 | tf_op jit(solution)/shard_map/ppermute | solution.py:380
  13.4 12.0 %collective-permute-start.6 = (f32[8,128]{1,0:T(8,128)S(1)}, f32[8,128]{1,0:T(8,128)S(1)}, u32[]{:S(2)}, u32[]{:S(2)}) collective-permute-start(f32[8,128]{1,0:T(8,128)S(1)} %copy.6), channel_id=1, source_target_pairs={{2,21},{3,20},{4,19},{5,18},{6,25},{7,24},{8,23},{9,22},{10,29},{1... | collective-permute-start | bytes 12296 | tf_op jit(solution)/shard_map/ppermute | solution.py:380
  18.7 7.1 %collective-permute-start.7 = (bf16[32,2048]{1,0:T(8,128)(2,1)S(1)}, bf16[32,2048]{1,0:T(8,128)(2,1)S(1)}, u32[]{:S(2)}, u32[]{:S(2)}) collective-permute-start(bf16[32,2048]{1,0:T(8,128)(2,1)S(1)} %norm.1.refs_0_), channel_id=1, source_target_pairs={{16,18},{17,19},{18,16},{19,17},{20,22},{21,23},{22,20},{23,21},{2... | collective-permute-start | bytes 393224 | tf_op jit(solution)/shard_map/ppermute | solution.py:380

commit v14 on v12

--- a/solution.py
+++ b/solution.py
@@ -11,6 +11,7 @@
 HEAD = 128
 WIN = 4
 GROUP = 4
+WEIGHT_PARTS = 4
 EPS = 1e-06
 BIG = 1e30
 CHIP, FAR, NEXT_FAR, NEXT_CHIP = range(4)
@@ -102,17 +103,25 @@
     weights_hbm, first_hbm, pad_hbm, _, weights_ref, time_ref, station_ref,
     first_ref, pad_ref, arrived, *, stations, total_steps,
 ):
+    part = weights_hbm.shape[1] // WEIGHT_PARTS
     copies = [
         pltpu.make_async_copy(first_hbm, first_ref, arrived.at[0]),
         pltpu.make_async_copy(pad_hbm, pad_ref, arrived.at[1]),
-        pltpu.make_async_copy(weights_hbm, weights_ref, arrived.at[2]),
     ]
+    for i in range(WEIGHT_PARTS):
+        heads = pl.ds(i * part, part)
+        copies.append(
+            pltpu.make_async_copy(
+                weights_hbm.at[:, heads], weights_ref.at[:, heads], arrived.at[2 + i]
+            )
+        )
     for copy in copies:
         copy.start()
     copies[0].wait()
     copies[1].wait()
     fill_masks(first_ref, pad_ref, time_ref, station_ref, stations, total_steps)
-    copies[2].wait()
+    for copy in copies[2:]:
+        copy.wait()
 
 
 def squares_kernel(*refs):
@@ -385,7 +394,7 @@
         scratch_shapes=[
             pltpu.SMEM(record_start.shape, jnp.int32),
             pltpu.SMEM(record_pad.shape, jnp.int32),
-            pltpu.SemaphoreType.DMA((3,)),
+            pltpu.SemaphoreType.DMA((2 + WEIGHT_PARTS,)),
         ],
         compiler_params=PARAMS,
         cost_estimate=cost(signal.size, 2 * head_proj.size),

time: 27.8 us -> 27.7 us (level)
  no operation moved by 1% of the time
where the time goes in v14:
time: 27.7 us; the launch traced here: 27.4 us
  starting transfers between devices  13.9 us (50%)
  Pallas kernels  5.62 us (20%)
  waiting for transfers between devices  3.98 us (14%)
  blocking collectives  3.8 us (14%)
    ppermute x8, starting transfers between devices, moved(): return lax.ppermute(block, ('section', 'seq', 'rep'), route)  13.9 us
    ppermute x8, waiting for transfers between devices, moved(): return lax.ppermute(block, ('section', 'seq', 'rep'), route)  3.98 us
    psum x1, blocking collectives, body(): squares = lax.psum(squares_of(chip, far, next_far, next_chip), 'rep')  3.8 us
    pallas_call x2, Pallas kernels, body(): pl.pallas_call(kernel, in_specs=[VMEM] * (8 + len(inputs)), out_specs=[VM...  1.86 us
    pallas_call x1, Pallas kernels, body(): pl.pallas_call(lambda *refs: fixed_kernel(*refs, stations=stations, total...  1.41 us
    pallas_call x1, Pallas kernels, body(): pl.pallas_call(halves_kernel, in_specs=[HBM], out_specs=[VMEM] * 2, out_s...  1.02 us
    pallas_call x4, Pallas kernels, squares_of(): pl.pallas_call(squares_kernel, in_specs=[VMEM] * len(halves), out_specs=V...  0.83 us
  transfers between devices with their start and end apart: 8, of which 4 were waited for; matrix products, arithmetic and copies ran while one was open for 0% of the time, Pallas kernels for 9%

profile of v14, /device:TPU:11, one launch (start us, length us, event | category | flops | bytes accessed | tf_op | source)
XLA Modules:
  0.0 27.4 jit_solution(10518949982472838458)
XLA Ops:
  0.0 1.0 %halves.1 = (bf16[32,2048]{1,0:T(8,128)(2,1)S(1)}, bf16[32,2048]{1,0:T(8,128)(2,1)S(1)}) custom-call(bf16[2,8,4,2048]{3,2,1,0:T(4,128)(2,1)} %signal_hbm.1), custom_call_target="tpu_custom_call" | custom-call | flops 131072 | bytes 524288 | tf_op jit(solution)/shard_map/halves/pallas_call | solution.py:357
  1.0 0.7 %collective-permute-start = (bf16[32,2048]{1,0:T(8,128)(2,1)S(1)}, bf16[32,2048]{1,0:T(8,128)(2,1)S(1)}, u32[]{:S(2)}, u32[]{:S(2)}) collective-permute-start(bf16[32,2048]{1,0:T(8,128)(2,1)S(1)} %get-tuple-element.13.refs_1_.refs_7_), channel_id=1, source_target_pairs={{2,4},{3,5},{4,2},{5,3},{6,8},{7,9},{8,6},{9,7},{10,12},{11,13},{1... | collective-permute-start | bytes 393224 | tf_op jit(solution)/shard_map/ppermute | solution.py:380
  1.7 0.7 %collective-permute-start.1 = (bf16[32,2048]{1,0:T(8,128)(2,1)S(1)}, bf16[32,2048]{1,0:T(8,128)(2,1)S(1)}, u32[]{:S(2)}, u32[]{:S(2)}) collective-permute-start(bf16[32,2048]{1,0:T(8,128)(2,1)S(1)} %get-tuple-element.12.refs_0_.refs_3_.refs_6_), channel_id=1, source_target_pairs={{0,2},{1,3},{2,0},{3,1},{4,6},{5,7},{6,4},{7,5},{8,10},{9,11},{10,... | collective-permute-start | bytes 393224 | tf_op jit(solution)/shard_map/ppermute | solution.py:380
  2.4 1.4 %fixed.1 = (bf16[1,16,128,384]{3,2,1,0:T(8,128)(2,1)S(1)}, f32[2,64,128]{2,1,0:T(8,128)S(1)}, f32[2,32,128]{2,1,0:T(8,128)S(1)}) custom-call(bf16[1,16,128,384]{3,2,1,0:T(8,128)(2,1)} %refs_0_.1, s32[2,4]{1,0:T(2,128)} %refs_1_.1, s32[2,4]{1,0:T(2,128)} %refs_2_.1, bf16[32,2048]{1,0:T(8,128)(2,1)S(1)} %get-tuple-element.12.refs_0_.refs_3_.refs_6_), custom_call_target="tpu_custom_call" | custom-call | flops 131072 | bytes 1572864 | tf_op jit(solution)/shard_map/fixed/pallas_call | solution.py:385
  3.8 0.0 collective-permute-done.refs_2_.refs_8_
  3.8 0.0 collective-permute-done.1.refs_3_.refs_9_
  3.8 0.3 %squares.4 = f32[8,128]{1,0:T(8,128)S(1)} custom-call(bf16[32,2048]{1,0:T(8,128)(2,1)S(1)} %get-tuple-element.12.refs_0_.refs_3_.refs_6_, bf16[32,2048]{1,0:T(8,128)(2,1)S(1)} %get-tuple-element.13.refs_1_.refs_7_, bf16[32,2048]{1,0:T(8,128)(2,1)S(1)} %collective-permute-done.refs_2_.refs_8_, bf16[32,2048]{1,0:T(8,128)(2,1)S(1)} %collective-permute-done.1.refs_3_.refs_9_), custom_call_target="tpu_custom_call" | custom-call | tf_op jit(solution)/shard_map/squares/pallas_call | solution.py:315
  4.1 3.8 %psum.7.refs_2_ = f32[8,128]{1,0:T(8,128)S(1)} all-reduce(f32[8,128]{1,0:T(8,128)S(1)} %squares.4), channel_id=1, replica_groups=mesh['section'=2,'seq'=8,'rep'=2] {'rep'}, use_global_device_ids=true, to_apply=%region_0.0 | all-reduce | flops 1024 | bytes 8192 | tf_op jit(solution)/shard_map/psum | solution.py:384
  7.9 0.1 layer.2
  8.0 1.3 %collective-permute-start.2 = (bf16[32,2048]{1,0:T(8,128)(2,1)S(1)}, bf16[32,2048]{1,0:T(8,128)(2,1)S(1)}, u32[]{:S(2)}, u32[]{:S(2)}) collective-permute-start(bf16[32,2048]{1,0:T(8,128)(2,1)S(1)} %get-tuple-element.17.refs_0_.refs_6_), channel_id=1, source_target_pairs={{0,16},{1,17},{2,18},{3,19},{4,20},{5,21},{6,22},{7,23},{8,24},{9,... | collective-permute-start | bytes 393224 | tf_op jit(solution)/shard_map/ppermute | solution.py:380
  9.3 0.2 squares.5.refs_0_
  9.5 1.3 %collective-permute-start.4 = (f32[8,128]{1,0:T(8,128)S(1)}, f32[8,128]{1,0:T(8,128)S(1)}, u32[]{:S(2)}, u32[]{:S(2)}) collective-permute-start(f32[8,128]{1,0:T(8,128)S(1)} %squares.5.refs_0_), channel_id=1, source_target_pairs={{0,17},{1,16},{2,19},{3,18},{4,21},{5,20},{6,23},{7,22},{8,25},{9,... | collective-permute-start | bytes 12296 | tf_op jit(solution)/shard_map/ppermute | solution.py:380
  10.8 1.3 %collective-permute-start.5 = (bf16[32,2048]{1,0:T(8,128)(2,1)S(1)}, bf16[32,2048]{1,0:T(8,128)(2,1)S(1)}, u32[]{:S(2)}, u32[]{:S(2)}) collective-permute-start(bf16[32,2048]{1,0:T(8,128)(2,1)S(1)} %get-tuple-element.18.refs_1_.refs_7_), channel_id=1, source_target_pairs={{2,20},{3,21},{4,18},{5,19},{6,24},{7,25},{8,22},{9,23},{10,28},{1... | collective-permute-start | bytes 393224 | tf_op jit(solution)/shard_map/ppermute | solution.py:380
  12.1 1.3 %collective-permute-start.3 = (bf16[32,2048]{1,0:T(8,128)(2,1)S(1)}, bf16[32,2048]{1,0:T(8,128)(2,1)S(1)}, u32[]{:S(2)}, u32[]{:S(2)}) collective-permute-start(bf16[32,2048]{1,0:T(8,128)(2,1)S(1)} %get-tuple-element.18.refs_1_.refs_7_), channel_id=1, source_target_pairs={{0,16},{1,17},{2,18},{3,19},{4,20},{5,21},{6,22},{7,23},{8,24},{9,... | collective-permute-start | bytes 393224 | tf_op jit(solution)/shard_map/ppermute | solution.py:380
  13.4 1.3 %collective-permute-start.6 = (f32[8,128]{1,0:T(8,128)S(1)}, f32[8,128]{1,0:T(8,128)S(1)}, u32[]{:S(2)}, u32[]{:S(2)}) collective-permute-start(f32[8,128]{1,0:T(8,128)S(1)} %copy.6), channel_id=1, source_target_pairs={{2,21},{3,20},{4,19},{5,18},{6,25},{7,24},{8,23},{9,22},{10,29},{1... | collective-permute-start | bytes 12296 | tf_op jit(solution)/shard_map/ppermute | solution.py:380
  14.7 2.6 %collective-permute-done.2.refs_0_ = bf16[32,2048]{1,0:T(8,128)(2,1)S(1)} collective-permute-done((bf16[32,2048]{1,0:T(8,128)(2,1)S(1)}, bf16[32,2048]{1,0:T(8,128)(2,1)S(1)}, u32[]{:S(2)}, u32[]{:S(2)}) %collective-permute-start.2) | collective-permute-done | bytes 131104 | tf_op jit(solution)/shard_map/ppermute | solution.py:380
  17.3 0.2 squares.7.refs_1_
  17.5 0.9 %collective-permute-done.4.refs_2_ = f32[8,128]{1,0:T(8,128)S(1)} collective-permute-done((f32[8,128]{1,0:T(8,128)S(1)}, f32[8,128]{1,0:T(8,128)S(1)}, u32[]{:S(2)}, u32[]{:S(2)}) %collective-permute-start.4) | collective-permute-done | bytes 4128 | tf_op jit(solution)/shard_map/ppermute | solution.py:380
  18.5 0.1 norm.1.refs_0_
  18.6 6.1 %collective-permute-start.7 = (bf16[32,2048]{1,0:T(8,128)(2,1)S(1)}, bf16[32,2048]{1,0:T(8,128)(2,1)S(1)}, u32[]{:S(2)}, u32[]{:S(2)}) collective-permute-start(bf16[32,2048]{1,0:T(8,128)(2,1)S(1)} %norm.1.refs_0_), channel_id=1, source_target_pairs={{16,18},{17,19},{18,16},{19,17},{20,22},{21,23},{22,20},{23,21},{2... | collective-permute-start | bytes 393224 | tf_op jit(solution)/shard_map/ppermute | solution.py:380
  24.7 0.4 %project.1.refs_11_ = bf16[32,6144]{1,0:T(8,128)(2,1)S(1)} custom-call(bf16[1,16,128,384]{3,2,1,0:T(8,128)(2,1)S(1)} %get-tuple-element.16.refs_5_.weights_ref, bf16[32,2048]{1,0:T(8,128)(2,1)S(1)} %norm.1.refs_0_), custom_call_target="tpu_custom_call" | custom-call | flops 2000000000 | bytes 300000 | tf_op jit(solution)/shard_map/project/pallas_call | solution.py:347
  25.1 0.0 collective-permute-done.5.refs_0_.refs_8_
  25.1 0.2 squares.6.mine_ref
  25.2 0.1 collective-permute-done.6.other_ref
  25.3 0.0 collective-permute-done.3.refs_1_
  25.3 0.3 %collective-permute-done.7.refs_10_ = bf16[32,2048]{1,0:T(8,128)(2,1)S(1)} collective-permute-done((bf16[32,2048]{1,0:T(8,128)(2,1)S(1)}, bf16[32,2048]{1,0:T(8,128)(2,1)S(1)}, u32[]{:S(2)}, u32[]{:S(2)}) %collective-permute-start.7) | collective-permute-done | bytes 131104 | tf_op jit(solution)/shard_map/ppermute | solution.py:380
  25.6 1.8 %layer.3 = bf16[1,2,8,4,2048]{4,3,2,1,0:T(4,128)(2,1)} custom-call(bf16[32,2048]{1,0:T(8,128)(2,1)S(1)} %collective-permute-done.2.refs_0_, bf16[32,2048]{1,0:T(8,128)(2,1)S(1)} %collective-permute-done.3.refs_1_, f32[8,128]{1,0:T(8,128)S(1)} %collective-permute-done.4.refs_2_, f32[2,64,128]{2,1,0:T(8,128)S(1)} %get-tuple-element.14.refs_3_, ...), custom_call_target="tpu_custom_call" | custom-call | flops 402653184 | bytes 4194304 | tf_op jit(solution)/shard_map/layer/pallas_call | solution.py:416
  (2 shorter events, 0.0 us)
Async XLA Ops:
  1.0 2.8 %collective-permute-start = (bf16[32,2048]{1,0:T(8,128)(2,1)S(1)}, bf16[32,2048]{1,0:T(8,128)(2,1)S(1)}, u32[]{:S(2)}, u32[]{:S(2)}) collective-permute-start(bf16[32,2048]{1,0:T(8,128)(2,1)S(1)} %get-tuple-element.13.refs_1_.refs_7_), channel_id=1, source_target_pairs={{2,4},{3,5},{4,2},{5,3},{6,8},{7,9},{8,6},{9,7},{10,12},{11,13},{1... | collective-permute-start | bytes 393224 | tf_op jit(solution)/shard_map/ppermute | solution.py:380
  1.7 2.1 %collective-permute-start.1 = (bf16[32,2048]{1,0:T(8,128)(2,1)S(1)}, bf16[32,2048]{1,0:T(8,128)(2,1)S(1)}, u32[]{:S(2)}, u32[]{:S(2)}) collective-permute-start(bf16[32,2048]{1,0:T(8,128)(2,1)S(1)} %get-tuple-element.12.refs_0_.refs_3_.refs_6_), channel_id=1, source_target_pairs={{0,2},{1,3},{2,0},{3,1},{4,6},{5,7},{6,4},{7,5},{8,10},{9,11},{10,... | collective-permute-start | bytes 393224 | tf_op jit(solution)/shard_map/ppermute | solution.py:380
  8.0 9.4 %collective-permute-start.2 = (bf16[32,2048]{1,0:T(8,128)(2,1)S(1)}, bf16[32,2048]{1,0:T(8,128)(2,1)S(1)}, u32[]{:S(2)}, u32[]{:S(2)}) collective-permute-start(bf16[32,2048]{1,0:T(8,128)(2,1)S(1)} %get-tuple-element.17.refs_0_.refs_6_), channel_id=1, source_target_pairs={{0,16},{1,17},{2,18},{3,19},{4,20},{5,21},{6,22},{7,23},{8,24},{9,... | collective-permute-start | bytes 393224 | tf_op jit(solution)/shard_map/ppermute | solution.py:380
  9.5 9.0 %collective-permute-start.4 = (f32[8,128]{1,0:T(8,128)S(1)}, f32[8,128]{1,0:T(8,128)S(1)}, u32[]{:S(2)}, u32[]{:S(2)}) collective-permute-start(f32[8,128]{1,0:T(8,128)S(1)} %squares.5.refs_0_), channel_id=1, source_target_pairs={{0,17},{1,16},{2,19},{3,18},{4,21},{5,20},{6,23},{7,22},{8,25},{9,... | collective-permute-start | bytes 12296 | tf_op jit(solution)/shard_map/ppermute | solution.py:380
  10.8 14.3 %collective-permute-start.5 = (bf16[32,2048]{1,0:T(8,128)(2,1)S(1)}, bf16[32,2048]{1,0:T(8,128)(2,1)S(1)}, u32[]{:S(2)}, u32[]{:S(2)}) collective-permute-start(bf16[32,2048]{1,0:T(8,128)(2,1)S(1)} %get-tuple-element.18.refs_1_.refs_7_), channel_id=1, source_target_pairs={{2,20},{3,21},{4,18},{5,19},{6,24},{7,25},{8,22},{9,23},{10,28},{1... | collective-permute-start | bytes 393224 | tf_op jit(solution)/shard_map/ppermute | solution.py:380
  12.1 13.2 %collective-permute-start.3 = (bf16[32,2048]{1,0:T(8,128)(2,1)S(1)}, bf16[32,2048]{1,0:T(8,128)(2,1)S(1)}, u32[]{:S(2)}, u32[]{:S(2)}) collective-permute-start(bf16[32,2048]{1,0:T(8,128)(2,1)S(1)} %get-tuple-element.18.refs_1_.refs_7_), channel_id=1, source_target_pairs={{0,16},{1,17},{2,18},{3,19},{4,20},{5,21},{6,22},{7,23},{8,24},{9,... | collective-permute-start | bytes 393224 | tf_op jit(solution)/shard_map/ppermute | solution.py:380
  13.4 11.9 %collective-permute-start.6 = (f32[8,128]{1,0:T(8,128)S(1)}, f32[8,128]{1,0:T(8,128)S(1)}, u32[]{:S(2)}, u32[]{:S(2)}) collective-permute-start(f32[8,128]{1,0:T(8,128)S(1)} %copy.6), channel_id=1, source_target_pairs={{2,21},{3,20},{4,19},{5,18},{6,25},{7,24},{8,23},{9,22},{10,29},{1... | collective-permute-start | bytes 12296 | tf_op jit(solution)/shard_map/ppermute | solution.py:380
  18.6 7.1 %collective-permute-start.7 = (bf16[32,2048]{1,0:T(8,128)(2,1)S(1)}, bf16[32,2048]{1,0:T(8,128)(2,1)S(1)}, u32[]{:S(2)}, u32[]{:S(2)}) collective-permute-start(bf16[32,2048]{1,0:T(8,128)(2,1)S(1)} %norm.1.refs_0_), channel_id=1, source_target_pairs={{16,18},{17,19},{18,16},{19,17},{20,22},{21,23},{22,20},{23,21},{2... | collective-permute-start | bytes 393224 | tf_op jit(solution)/shard_map/ppermute | solution.py:380

commit v15 on v14

--- a/solution.py
+++ b/solution.py
@@ -53,7 +53,7 @@
     return jnp.sum(jnp.where(same(rows.shape[0]), gram, 0.0), axis=0, keepdims=True)
 
 
-def fill_masks(first_ref, pad_ref, time_ref, station_ref, stations, total_steps):
+def mask_parts(stations):
     own = 2 * WIN * stations
     keys, columns = 2 * own, GROUP * own
     key = lax.broadcasted_iota(jnp.int32, (keys, columns), 0)
@@ -71,15 +71,22 @@
     same_time = key_time == query_time
     near = jnp.abs(key_time - query_time) <= WIN
     step = lax.axis_index("seq") * (2 * WIN) + key_time
+    return step, key_station, same_station & near, same_time, same_station & same_time
+
+
+def fill_masks(parts, first_ref, pad_ref, time_ref, station_ref, total_steps):
+    step, key_station, near, same_time, itself = parts
     for m in range(time_ref.shape[0]):
-        first = jnp.zeros((keys, columns), jnp.int32)
-        pad = jnp.zeros((keys, columns), jnp.int32)
-        for s in range(stations):
+        first = jnp.zeros(step.shape, jnp.int32)
+        end = jnp.zeros(step.shape, jnp.int32)
+        for s in range(first_ref.shape[1]):
             first = jnp.where(key_station == s, first_ref[m, s], first)
-            pad = jnp.where(key_station == s, pad_ref[m, s], pad)
-        recorded = (step >= first) & (step < total_steps - pad)
-        time_ref[m] = jnp.where(same_station & near & (recorded | same_time), 0.0, -BIG)
-        station_ref[m] = jnp.where(same_time & (recorded | same_station), 0.0, -BIG)[:own]
+            end = jnp.where(key_station == s, total_steps - pad_ref[m, s], end)
+        recorded = (step >= first) & (step < end)
+        time_ref[m] = jnp.where((near & recorded) | itself, 0.0, -BIG)
+        station_ref[m] = jnp.where((same_time & recorded) | itself, 0.0, -BIG)[
+            : station_ref.shape[1]
+        ]
 
 
 def halves_kernel(signal_hbm, chip_ref, far_ref, signal_ref, arrived):
@@ -117,9 +124,10 @@
         )
     for copy in copies:
         copy.start()
+    parts = mask_parts(stations)
     copies[0].wait()
     copies[1].wait()
-    fill_masks(first_ref, pad_ref, time_ref, station_ref, stations, total_steps)
+    fill_masks(parts, first_ref, pad_ref, time_ref, station_ref, total_steps)
     for copy in copies[2:]:
         copy.wait()
 

time: 27.7 us -> 27.7 us (level)
  no operation moved by 1% of the time
where the time goes in v15:
time: 27.7 us; the launch traced here: 27.4 us
  starting transfers between devices  13.9 us (50%)
  Pallas kernels  5.62 us (20%)
  waiting for transfers between devices  3.98 us (14%)
  blocking collectives  3.8 us (14%)
    ppermute x8, starting transfers between devices, moved(): return lax.ppermute(block, ('section', 'seq', 'rep'), route)  13.9 us
    ppermute x8, waiting for transfers between devices, moved(): return lax.ppermute(block, ('section', 'seq', 'rep'), route)  3.98 us
    psum x1, blocking collectives, body(): squares = lax.psum(squares_of(chip, far, next_far, next_chip), 'rep')  3.8 us
    pallas_call x2, Pallas kernels, body(): pl.pallas_call(kernel, in_specs=[VMEM] * (8 + len(inputs)), out_specs=[VM...  1.86 us
    pallas_call x1, Pallas kernels, body(): pl.pallas_call(lambda *refs: fixed_kernel(*refs, stations=stations, total...  1.41 us
    pallas_call x1, Pallas kernels, body(): pl.pallas_call(halves_kernel, in_specs=[HBM], out_specs=[VMEM] * 2, out_s...  1.02 us
    pallas_call x4, Pallas kernels, squares_of(): pl.pallas_call(squares_kernel, in_specs=[VMEM] * len(halves), out_specs=V...  0.83 us
  transfers between devices with their start and end apart: 8, of which 4 were waited for; matrix products, arithmetic and copies ran while one was open for 0% of the time, Pallas kernels for 9%

profile of v15, /device:TPU:11, one launch (start us, length us, event | category | flops | bytes accessed | tf_op | source)
XLA Modules:
  0.0 27.4 jit_solution(5015269704645949414)
XLA Ops:
  0.0 1.0 %halves.1 = (bf16[32,2048]{1,0:T(8,128)(2,1)S(1)}, bf16[32,2048]{1,0:T(8,128)(2,1)S(1)}) custom-call(bf16[2,8,4,2048]{3,2,1,0:T(4,128)(2,1)} %signal_hbm.1), custom_call_target="tpu_custom_call" | custom-call | flops 131072 | bytes 524288 | tf_op jit(solution)/shard_map/halves/pallas_call | solution.py:365
  1.0 0.7 %collective-permute-start = (bf16[32,2048]{1,0:T(8,128)(2,1)S(1)}, bf16[32,2048]{1,0:T(8,128)(2,1)S(1)}, u32[]{:S(2)}, u32[]{:S(2)}) collective-permute-start(bf16[32,2048]{1,0:T(8,128)(2,1)S(1)} %get-tuple-element.13.refs_1_.refs_7_), channel_id=1, source_target_pairs={{2,4},{3,5},{4,2},{5,3},{6,8},{7,9},{8,6},{9,7},{10,12},{11,13},{1... | collective-permute-start | bytes 393224 | tf_op jit(solution)/shard_map/ppermute | solution.py:388
  1.7 0.7 %collective-permute-start.1 = (bf16[32,2048]{1,0:T(8,128)(2,1)S(1)}, bf16[32,2048]{1,0:T(8,128)(2,1)S(1)}, u32[]{:S(2)}, u32[]{:S(2)}) collective-permute-start(bf16[32,2048]{1,0:T(8,128)(2,1)S(1)} %get-tuple-element.12.refs_0_.refs_3_.refs_6_), channel_id=1, source_target_pairs={{0,2},{1,3},{2,0},{3,1},{4,6},{5,7},{6,4},{7,5},{8,10},{9,11},{10,... | collective-permute-start | bytes 393224 | tf_op jit(solution)/shard_map/ppermute | solution.py:388
  2.4 1.4 %fixed.1 = (bf16[1,16,128,384]{3,2,1,0:T(8,128)(2,1)S(1)}, f32[2,64,128]{2,1,0:T(8,128)S(1)}, f32[2,32,128]{2,1,0:T(8,128)S(1)}) custom-call(bf16[1,16,128,384]{3,2,1,0:T(8,128)(2,1)} %refs_0_.1, s32[2,4]{1,0:T(2,128)} %refs_1_.1, s32[2,4]{1,0:T(2,128)} %refs_2_.1, bf16[32,2048]{1,0:T(8,128)(2,1)S(1)} %get-tuple-element.12.refs_0_.refs_3_.refs_6_), custom_call_target="tpu_custom_call" | custom-call | flops 131072 | bytes 1572864 | tf_op jit(solution)/shard_map/fixed/pallas_call | solution.py:393
  3.8 0.0 collective-permute-done.refs_2_.refs_8_
  3.8 0.0 collective-permute-done.1.refs_3_.refs_9_
  3.8 0.3 %squares.4 = f32[8,128]{1,0:T(8,128)S(1)} custom-call(bf16[32,2048]{1,0:T(8,128)(2,1)S(1)} %get-tuple-element.12.refs_0_.refs_3_.refs_6_, bf16[32,2048]{1,0:T(8,128)(2,1)S(1)} %get-tuple-element.13.refs_1_.refs_7_, bf16[32,2048]{1,0:T(8,128)(2,1)S(1)} %collective-permute-done.refs_2_.refs_8_, bf16[32,2048]{1,0:T(8,128)(2,1)S(1)} %collective-permute-done.1.refs_3_.refs_9_), custom_call_target="tpu_custom_call" | custom-call | tf_op jit(solution)/shard_map/squares/pallas_call | solution.py:323
  4.1 3.8 %psum.7.refs_2_ = f32[8,128]{1,0:T(8,128)S(1)} all-reduce(f32[8,128]{1,0:T(8,128)S(1)} %squares.4), channel_id=1, replica_groups=mesh['section'=2,'seq'=8,'rep'=2] {'rep'}, use_global_device_ids=true, to_apply=%region_0.0 | all-reduce | flops 1024 | bytes 8192 | tf_op jit(solution)/shard_map/psum | solution.py:392
  7.9 0.1 layer.2
  8.0 1.3 %collective-permute-start.2 = (bf16[32,2048]{1,0:T(8,128)(2,1)S(1)}, bf16[32,2048]{1,0:T(8,128)(2,1)S(1)}, u32[]{:S(2)}, u32[]{:S(2)}) collective-permute-start(bf16[32,2048]{1,0:T(8,128)(2,1)S(1)} %get-tuple-element.17.refs_0_.refs_6_), channel_id=1, source_target_pairs={{0,16},{1,17},{2,18},{3,19},{4,20},{5,21},{6,22},{7,23},{8,24},{9,... | collective-permute-start | bytes 393224 | tf_op jit(solution)/shard_map/ppermute | solution.py:388
  9.3 0.2 squares.5.refs_0_
  9.5 1.3 %collective-permute-start.4 = (f32[8,128]{1,0:T(8,128)S(1)}, f32[8,128]{1,0:T(8,128)S(1)}, u32[]{:S(2)}, u32[]{:S(2)}) collective-permute-start(f32[8,128]{1,0:T(8,128)S(1)} %squares.5.refs_0_), channel_id=1, source_target_pairs={{0,17},{1,16},{2,19},{3,18},{4,21},{5,20},{6,23},{7,22},{8,25},{9,... | collective-permute-start | bytes 12296 | tf_op jit(solution)/shard_map/ppermute | solution.py:388
  10.8 1.3 %collective-permute-start.5 = (bf16[32,2048]{1,0:T(8,128)(2,1)S(1)}, bf16[32,2048]{1,0:T(8,128)(2,1)S(1)}, u32[]{:S(2)}, u32[]{:S(2)}) collective-permute-start(bf16[32,2048]{1,0:T(8,128)(2,1)S(1)} %get-tuple-element.18.refs_1_.refs_7_), channel_id=1, source_target_pairs={{2,20},{3,21},{4,18},{5,19},{6,24},{7,25},{8,22},{9,23},{10,28},{1... | collective-permute-start | bytes 393224 | tf_op jit(solution)/shard_map/ppermute | solution.py:388
  12.1 1.3 %collective-permute-start.3 = (bf16[32,2048]{1,0:T(8,128)(2,1)S(1)}, bf16[32,2048]{1,0:T(8,128)(2,1)S(1)}, u32[]{:S(2)}, u32[]{:S(2)}) collective-permute-start(bf16[32,2048]{1,0:T(8,128)(2,1)S(1)} %get-tuple-element.18.refs_1_.refs_7_), channel_id=1, source_target_pairs={{0,16},{1,17},{2,18},{3,19},{4,20},{5,21},{6,22},{7,23},{8,24},{9,... | collective-permute-start | bytes 393224 | tf_op jit(solution)/shard_map/ppermute | solution.py:388
  13.4 1.3 %collective-permute-start.6 = (f32[8,128]{1,0:T(8,128)S(1)}, f32[8,128]{1,0:T(8,128)S(1)}, u32[]{:S(2)}, u32[]{:S(2)}) collective-permute-start(f32[8,128]{1,0:T(8,128)S(1)} %copy.6), channel_id=1, source_target_pairs={{2,21},{3,20},{4,19},{5,18},{6,25},{7,24},{8,23},{9,22},{10,29},{1... | collective-permute-start | bytes 12296 | tf_op jit(solution)/shard_map/ppermute | solution.py:388
  14.7 2.6 %collective-permute-done.2.refs_0_ = bf16[32,2048]{1,0:T(8,128)(2,1)S(1)} collective-permute-done((bf16[32,2048]{1,0:T(8,128)(2,1)S(1)}, bf16[32,2048]{1,0:T(8,128)(2,1)S(1)}, u32[]{:S(2)}, u32[]{:S(2)}) %collective-permute-start.2) | collective-permute-done | bytes 131104 | tf_op jit(solution)/shard_map/ppermute | solution.py:388
  17.3 0.2 squares.7.refs_1_
  17.5 0.9 %collective-permute-done.4.refs_2_ = f32[8,128]{1,0:T(8,128)S(1)} collective-permute-done((f32[8,128]{1,0:T(8,128)S(1)}, f32[8,128]{1,0:T(8,128)S(1)}, u32[]{:S(2)}, u32[]{:S(2)}) %collective-permute-start.4) | collective-permute-done | bytes 4128 | tf_op jit(solution)/shard_map/ppermute | solution.py:388
  18.5 0.1 norm.1.refs_0_
  18.6 6.1 %collective-permute-start.7 = (bf16[32,2048]{1,0:T(8,128)(2,1)S(1)}, bf16[32,2048]{1,0:T(8,128)(2,1)S(1)}, u32[]{:S(2)}, u32[]{:S(2)}) collective-permute-start(bf16[32,2048]{1,0:T(8,128)(2,1)S(1)} %norm.1.refs_0_), channel_id=1, source_target_pairs={{16,18},{17,19},{18,16},{19,17},{20,22},{21,23},{22,20},{23,21},{2... | collective-permute-start | bytes 393224 | tf_op jit(solution)/shard_map/ppermute | solution.py:388
  24.7 0.4 %project.1.refs_11_ = bf16[32,6144]{1,0:T(8,128)(2,1)S(1)} custom-call(bf16[1,16,128,384]{3,2,1,0:T(8,128)(2,1)S(1)} %get-tuple-element.16.refs_5_.weights_ref, bf16[32,2048]{1,0:T(8,128)(2,1)S(1)} %norm.1.refs_0_), custom_call_target="tpu_custom_call" | custom-call | flops 2000000000 | bytes 300000 | tf_op jit(solution)/shard_map/project/pallas_call | solution.py:355
  25.1 0.0 collective-permute-done.5.refs_0_.refs_8_
  25.1 0.2 squares.6.mine_ref
  25.2 0.1 collective-permute-done.6.other_ref
  25.3 0.0 collective-permute-done.3.refs_1_
  25.3 0.3 %collective-permute-done.7.refs_10_ = bf16[32,2048]{1,0:T(8,128)(2,1)S(1)} collective-permute-done((bf16[32,2048]{1,0:T(8,128)(2,1)S(1)}, bf16[32,2048]{1,0:T(8,128)(2,1)S(1)}, u32[]{:S(2)}, u32[]{:S(2)}) %collective-permute-start.7) | collective-permute-done | bytes 131104 | tf_op jit(solution)/shard_map/ppermute | solution.py:388
  25.6 1.8 %layer.3 = bf16[1,2,8,4,2048]{4,3,2,1,0:T(4,128)(2,1)} custom-call(bf16[32,2048]{1,0:T(8,128)(2,1)S(1)} %collective-permute-done.2.refs_0_, bf16[32,2048]{1,0:T(8,128)(2,1)S(1)} %collective-permute-done.3.refs_1_, f32[8,128]{1,0:T(8,128)S(1)} %collective-permute-done.4.refs_2_, f32[2,64,128]{2,1,0:T(8,128)S(1)} %get-tuple-element.14.refs_3_, ...), custom_call_target="tpu_custom_call" | custom-call | flops 402653184 | bytes 4194304 | tf_op jit(solution)/shard_map/layer/pallas_call | solution.py:424
  (2 shorter events, 0.0 us)
Async XLA Ops:
  1.0 2.8 %collective-permute-start = (bf16[32,2048]{1,0:T(8,128)(2,1)S(1)}, bf16[32,2048]{1,0:T(8,128)(2,1)S(1)}, u32[]{:S(2)}, u32[]{:S(2)}) collective-permute-start(bf16[32,2048]{1,0:T(8,128)(2,1)S(1)} %get-tuple-element.13.refs_1_.refs_7_), channel_id=1, source_target_pairs={{2,4},{3,5},{4,2},{5,3},{6,8},{7,9},{8,6},{9,7},{10,12},{11,13},{1... | collective-permute-start | bytes 393224 | tf_op jit(solution)/shard_map/ppermute | solution.py:388
  1.7 2.1 %collective-permute-start.1 = (bf16[32,2048]{1,0:T(8,128)(2,1)S(1)}, bf16[32,2048]{1,0:T(8,128)(2,1)S(1)}, u32[]{:S(2)}, u32[]{:S(2)}) collective-permute-start(bf16[32,2048]{1,0:T(8,128)(2,1)S(1)} %get-tuple-element.12.refs_0_.refs_3_.refs_6_), channel_id=1, source_target_pairs={{0,2},{1,3},{2,0},{3,1},{4,6},{5,7},{6,4},{7,5},{8,10},{9,11},{10,... | collective-permute-start | bytes 393224 | tf_op jit(solution)/shard_map/ppermute | solution.py:388
  8.0 9.4 %collective-permute-start.2 = (bf16[32,2048]{1,0:T(8,128)(2,1)S(1)}, bf16[32,2048]{1,0:T(8,128)(2,1)S(1)}, u32[]{:S(2)}, u32[]{:S(2)}) collective-permute-start(bf16[32,2048]{1,0:T(8,128)(2,1)S(1)} %get-tuple-element.17.refs_0_.refs_6_), channel_id=1, source_target_pairs={{0,16},{1,17},{2,18},{3,19},{4,20},{5,21},{6,22},{7,23},{8,24},{9,... | collective-permute-start | bytes 393224 | tf_op jit(solution)/shard_map/ppermute | solution.py:388
  9.5 9.0 %collective-permute-start.4 = (f32[8,128]{1,0:T(8,128)S(1)}, f32[8,128]{1,0:T(8,128)S(1)}, u32[]{:S(2)}, u32[]{:S(2)}) collective-permute-start(f32[8,128]{1,0:T(8,128)S(1)} %squares.5.refs_0_), channel_id=1, source_target_pairs={{0,17},{1,16},{2,19},{3,18},{4,21},{5,20},{6,23},{7,22},{8,25},{9,... | collective-permute-start | bytes 12296 | tf_op jit(solution)/shard_map/ppermute | solution.py:388
  10.8 14.3 %collective-permute-start.5 = (bf16[32,2048]{1,0:T(8,128)(2,1)S(1)}, bf16[32,2048]{1,0:T(8,128)(2,1)S(1)}, u32[]{:S(2)}, u32[]{:S(2)}) collective-permute-start(bf16[32,2048]{1,0:T(8,128)(2,1)S(1)} %get-tuple-element.18.refs_1_.refs_7_), channel_id=1, source_target_pairs={{2,20},{3,21},{4,18},{5,19},{6,24},{7,25},{8,22},{9,23},{10,28},{1... | collective-permute-start | bytes 393224 | tf_op jit(solution)/shard_map/ppermute | solution.py:388
  12.1 13.2 %collective-permute-start.3 = (bf16[32,2048]{1,0:T(8,128)(2,1)S(1)}, bf16[32,2048]{1,0:T(8,128)(2,1)S(1)}, u32[]{:S(2)}, u32[]{:S(2)}) collective-permute-start(bf16[32,2048]{1,0:T(8,128)(2,1)S(1)} %get-tuple-element.18.refs_1_.refs_7_), channel_id=1, source_target_pairs={{0,16},{1,17},{2,18},{3,19},{4,20},{5,21},{6,22},{7,23},{8,24},{9,... | collective-permute-start | bytes 393224 | tf_op jit(solution)/shard_map/ppermute | solution.py:388
  13.4 11.9 %collective-permute-start.6 = (f32[8,128]{1,0:T(8,128)S(1)}, f32[8,128]{1,0:T(8,128)S(1)}, u32[]{:S(2)}, u32[]{:S(2)}) collective-permute-start(f32[8,128]{1,0:T(8,128)S(1)} %copy.6), channel_id=1, source_target_pairs={{2,21},{3,20},{4,19},{5,18},{6,25},{7,24},{8,23},{9,22},{10,29},{1... | collective-permute-start | bytes 12296 | tf_op jit(solution)/shard_map/ppermute | solution.py:388
  18.6 7.1 %collective-permute-start.7 = (bf16[32,2048]{1,0:T(8,128)(2,1)S(1)}, bf16[32,2048]{1,0:T(8,128)(2,1)S(1)}, u32[]{:S(2)}, u32[]{:S(2)}) collective-permute-start(bf16[32,2048]{1,0:T(8,128)(2,1)S(1)} %norm.1.refs_0_), channel_id=1, source_target_pairs={{16,18},{17,19},{18,16},{19,17},{20,22},{21,23},{22,20},{23,21},{2... | collective-permute-start | bytes 393224 | tf_op jit(solution)/shard_map/ppermute | solution.py:388

commit v16 on v15

--- a/solution.py
+++ b/solution.py
@@ -11,7 +11,6 @@
 HEAD = 128
 WIN = 4
 GROUP = 4
-WEIGHT_PARTS = 4
 EPS = 1e-06
 BIG = 1e30
 CHIP, FAR, NEXT_FAR, NEXT_CHIP = range(4)
@@ -89,9 +88,17 @@
         ]
 
 
-def halves_kernel(signal_hbm, chip_ref, far_ref, signal_ref, arrived):
-    copy = pltpu.make_async_copy(signal_hbm, signal_ref, arrived)
+def weights_part(weights_hbm, weights_ref, part, arrived):
+    count = weights_hbm.shape[1] // 2
+    heads = pl.ds(part * count, count)
+    return pltpu.make_async_copy(weights_hbm.at[:, heads], weights_ref.at[:, heads], arrived)
+
+
+def halves_kernel(signal_hbm, weights_hbm, chip_ref, far_ref, weights_ref, signal_ref, arrived):
+    copy = pltpu.make_async_copy(signal_hbm, signal_ref, arrived.at[0])
     copy.start()
+    weights_copy = weights_part(weights_hbm, weights_ref, 0, arrived.at[1])
+    weights_copy.start()
     micro, _, stations, _ = signal_ref.shape
     edge = WIN * stations
     copy.wait()
@@ -104,32 +111,25 @@
                 half_ref[at : at + 2 * stations, :] = jnp.concatenate(pair, axis=0).astype(
                     jnp.bfloat16
                 )
+    weights_copy.wait()
 
 
 def fixed_kernel(
-    weights_hbm, first_hbm, pad_hbm, _, weights_ref, time_ref, station_ref,
+    weights_hbm, first_hbm, pad_hbm, _, __, weights_ref, time_ref, station_ref,
     first_ref, pad_ref, arrived, *, stations, total_steps,
 ):
-    part = weights_hbm.shape[1] // WEIGHT_PARTS
     copies = [
         pltpu.make_async_copy(first_hbm, first_ref, arrived.at[0]),
         pltpu.make_async_copy(pad_hbm, pad_ref, arrived.at[1]),
+        weights_part(weights_hbm, weights_ref, 1, arrived.at[2]),
     ]
-    for i in range(WEIGHT_PARTS):
-        heads = pl.ds(i * part, part)
-        copies.append(
-            pltpu.make_async_copy(
-                weights_hbm.at[:, heads], weights_ref.at[:, heads], arrived.at[2 + i]
-            )
-        )
     for copy in copies:
         copy.start()
     parts = mask_parts(stations)
     copies[0].wait()
     copies[1].wait()
     fill_masks(parts, first_ref, pad_ref, time_ref, station_ref, total_steps)
-    for copy in copies[2:]:
-        copy.wait()
+    copies[2].wait()
 
 
 def squares_kernel(*refs):
@@ -362,16 +362,16 @@
             name="project",
         )(weights, *halves)
 
-    chip, far = pl.pallas_call(
+    chip, far, weights = pl.pallas_call(
         halves_kernel,
-        in_specs=[HBM],
-        out_specs=[VMEM] * 2,
-        out_shape=[half_shape] * 2,
-        scratch_shapes=[pltpu.VMEM(signal.shape, bf16), pltpu.SemaphoreType.DMA],
+        in_specs=[HBM] * 2,
+        out_specs=[VMEM] * 3,
+        out_shape=[half_shape, half_shape, jax.ShapeDtypeStruct(head_proj.shape, bf16)],
+        scratch_shapes=[pltpu.VMEM(signal.shape, bf16), pltpu.SemaphoreType.DMA((2,))],
         compiler_params=PARAMS,
         cost_estimate=cost(signal.size, 2 * signal_bytes),
         name="halves",
-    )(in_hbm(signal))
+    )(in_hbm(signal), in_hbm(head_proj))
     def moved(block, source, target, hop, other=False):
         route = []
         for i in range(seq_count):
@@ -392,7 +392,8 @@
     squares = lax.psum(squares_of(chip, far, next_far, next_chip), "rep")
     weights, time_bias, station_bias = pl.pallas_call(
         lambda *refs: fixed_kernel(*refs, stations=stations, total_steps=steps * seq_count),
-        in_specs=[HBM] * 3 + [VMEM],
+        in_specs=[HBM] * 3 + [VMEM] * 2,
+        input_output_aliases={4: 0},
         out_specs=[VMEM] * 3,
         out_shape=[
             jax.ShapeDtypeStruct(head_proj.shape, bf16),
@@ -402,12 +403,12 @@
         scratch_shapes=[
             pltpu.SMEM(record_start.shape, jnp.int32),
             pltpu.SMEM(record_pad.shape, jnp.int32),
-            pltpu.SemaphoreType.DMA((2 + WEIGHT_PARTS,)),
+            pltpu.SemaphoreType.DMA((3,)),
         ],
         compiler_params=PARAMS,
         cost_estimate=cost(signal.size, 2 * head_proj.size),
         name="fixed",
-    )(in_hbm(head_proj), in_hbm(record_start), in_hbm(record_pad), chip)
+    )(in_hbm(head_proj), in_hbm(record_start), in_hbm(record_pad), chip, weights)
     inputs = (next_far, next_chip)
     kept = (chip, far)
     for tick in range(section_count):

time: 27.7 us -> 27.6 us (level)
  transfers between devices with their start and end apart: 8 -> 8, of which waited for: 4 -> 4; matrix products, arithmetic and copies ran while one was open for 0% -> 0% of each run, Pallas kernels for 9% -> 8%
where the time goes in v16:
time: 27.6 us; the launch traced here: 27.3 us
  starting transfers between devices  13.7 us (50%)
  Pallas kernels  5.59 us (20%)
  waiting for transfers between devices  4.09 us (15%)
  blocking collectives  3.8 us (14%)
    ppermute x8, starting transfers between devices, moved(): return lax.ppermute(block, ('section', 'seq', 'rep'), route)  13.7 us
    ppermute x8, waiting for transfers between devices, moved(): return lax.ppermute(block, ('section', 'seq', 'rep'), route)  4.09 us
    psum x1, blocking collectives, body(): squares = lax.psum(squares_of(chip, far, next_far, next_chip), 'rep')  3.8 us
    pallas_call x2, Pallas kernels, body(): pl.pallas_call(kernel, in_specs=[VMEM] * (8 + len(inputs)), out_specs=[VM...  1.86 us
    pallas_call x1, Pallas kernels, body(): pl.pallas_call(halves_kernel, in_specs=[HBM] * 2, out_specs=[VMEM] * 3, o...  1.23 us
    pallas_call x1, Pallas kernels, body(): pl.pallas_call(lambda *refs: fixed_kernel(*refs, stations=stations, total...  1.17 us
    pallas_call x4, Pallas kernels, squares_of(): pl.pallas_call(squares_kernel, in_specs=[VMEM] * len(halves), out_specs=V...  0.83 us
  transfers between devices with their start and end apart: 8, of which 4 were waited for; matrix products, arithmetic and copies ran while one was open for 0% of the time, Pallas kernels for 8%

profile of v16, /device:TPU:11, one launch (start us, length us, event | category | flops | bytes accessed | tf_op | source)
XLA Modules:
  0.0 27.3 jit_solution(10142231934125604235)
XLA Ops:
  0.0 1.2 %halves.1 = (bf16[32,2048]{1,0:T(8,128)(2,1)S(1)}, bf16[32,2048]{1,0:T(8,128)(2,1)S(1)}, bf16[1,16,128,384]{3,2,1,0:T(8,128)(2,1)S(1)}) custom-call(bf16[2,8,4,2048]{3,2,1,0:T(4,128)(2,1)} %signal_hbm.1, bf16[1,16,128,384]{3,2,1,0:T(8,128)(2,1)} %refs_0_.1), custom_call_target="tpu_custom_call" | custom-call | flops 131072 | bytes 524288 | tf_op jit(solution)/shard_map/halves/pallas_call | solution.py:365
  1.2 0.7 %collective-permute-start = (bf16[32,2048]{1,0:T(8,128)(2,1)S(1)}, bf16[32,2048]{1,0:T(8,128)(2,1)S(1)}, u32[]{:S(2)}, u32[]{:S(2)}) collective-permute-start(bf16[32,2048]{1,0:T(8,128)(2,1)S(1)} %get-tuple-element.14.refs_1_.refs_7_), channel_id=1, source_target_pairs={{2,4},{3,5},{4,2},{5,3},{6,8},{7,9},{8,6},{9,7},{10,12},{11,13},{1... | collective-permute-start | bytes 393224 | tf_op jit(solution)/shard_map/ppermute | solution.py:388
  1.9 0.7 %collective-permute-start.1 = (bf16[32,2048]{1,0:T(8,128)(2,1)S(1)}, bf16[32,2048]{1,0:T(8,128)(2,1)S(1)}, u32[]{:S(2)}, u32[]{:S(2)}) collective-permute-start(bf16[32,2048]{1,0:T(8,128)(2,1)S(1)} %get-tuple-element.13.refs_0_.refs_3_.refs_6_), channel_id=1, source_target_pairs={{0,2},{1,3},{2,0},{3,1},{4,6},{5,7},{6,4},{7,5},{8,10},{9,11},{10,... | collective-permute-start | bytes 393224 | tf_op jit(solution)/shard_map/ppermute | solution.py:388
  2.6 1.2 %fixed.1 = (bf16[1,16,128,384]{3,2,1,0:T(8,128)(2,1)S(1)}, f32[2,64,128]{2,1,0:T(8,128)S(1)}, f32[2,32,128]{2,1,0:T(8,128)S(1)}) custom-call(bf16[1,16,128,384]{3,2,1,0:T(8,128)(2,1)} %refs_0_.1, s32[2,4]{1,0:T(2,128)} %refs_1_.1, s32[2,4]{1,0:T(2,128)} %refs_2_.1, ...), custom_call_target="tpu_custom_call", output_to_operand_aliasing={{0}: (4, {})} | custom-call | flops 131072 | bytes 1572864 | tf_op jit(solution)/shard_map/fixed/pallas_call | solution.py:393
  3.8 0.0 collective-permute-done.refs_2_.refs_8_
  3.8 0.0 collective-permute-done.1.refs_3_.refs_9_
  3.8 0.3 %squares.4 = f32[8,128]{1,0:T(8,128)S(1)} custom-call(bf16[32,2048]{1,0:T(8,128)(2,1)S(1)} %get-tuple-element.13.refs_0_.refs_3_.refs_6_, bf16[32,2048]{1,0:T(8,128)(2,1)S(1)} %get-tuple-element.14.refs_1_.refs_7_, bf16[32,2048]{1,0:T(8,128)(2,1)S(1)} %collective-permute-done.refs_2_.refs_8_, bf16[32,2048]{1,0:T(8,128)(2,1)S(1)} %collective-permute-done.1.refs_3_.refs_9_), custom_call_target="tpu_custom_call" | custom-call | tf_op jit(solution)/shard_map/squares/pallas_call | solution.py:323
  4.1 3.8 %psum.7.refs_2_ = f32[8,128]{1,0:T(8,128)S(1)} all-reduce(f32[8,128]{1,0:T(8,128)S(1)} %squares.4), channel_id=1, replica_groups=mesh['section'=2,'seq'=8,'rep'=2] {'rep'}, use_global_device_ids=true, to_apply=%region_0.0 | all-reduce | flops 1024 | bytes 8192 | tf_op jit(solution)/shard_map/psum | solution.py:392
  7.9 0.1 layer.2
  7.9 1.3 %collective-permute-start.2 = (bf16[32,2048]{1,0:T(8,128)(2,1)S(1)}, bf16[32,2048]{1,0:T(8,128)(2,1)S(1)}, u32[]{:S(2)}, u32[]{:S(2)}) collective-permute-start(bf16[32,2048]{1,0:T(8,128)(2,1)S(1)} %get-tuple-element.19.refs_0_.refs_6_), channel_id=1, source_target_pairs={{0,16},{1,17},{2,18},{3,19},{4,20},{5,21},{6,22},{7,23},{8,24},{9,... | collective-permute-start | bytes 393224 | tf_op jit(solution)/shard_map/ppermute | solution.py:388
  9.2 0.2 squares.5.refs_0_
  9.4 1.3 %collective-permute-start.4 = (f32[8,128]{1,0:T(8,128)S(1)}, f32[8,128]{1,0:T(8,128)S(1)}, u32[]{:S(2)}, u32[]{:S(2)}) collective-permute-start(f32[8,128]{1,0:T(8,128)S(1)} %squares.5.refs_0_), channel_id=1, source_target_pairs={{0,17},{1,16},{2,19},{3,18},{4,21},{5,20},{6,23},{7,22},{8,25},{9,... | collective-permute-start | bytes 12296 | tf_op jit(solution)/shard_map/ppermute | solution.py:388
  10.8 1.3 %collective-permute-start.5 = (bf16[32,2048]{1,0:T(8,128)(2,1)S(1)}, bf16[32,2048]{1,0:T(8,128)(2,1)S(1)}, u32[]{:S(2)}, u32[]{:S(2)}) collective-permute-start(bf16[32,2048]{1,0:T(8,128)(2,1)S(1)} %get-tuple-element.20.refs_1_.refs_7_), channel_id=1, source_target_pairs={{2,20},{3,21},{4,18},{5,19},{6,24},{7,25},{8,22},{9,23},{10,28},{1... | collective-permute-start | bytes 393224 | tf_op jit(solution)/shard_map/ppermute | solution.py:388
  12.1 1.3 %collective-permute-start.3 = (bf16[32,2048]{1,0:T(8,128)(2,1)S(1)}, bf16[32,2048]{1,0:T(8,128)(2,1)S(1)}, u32[]{:S(2)}, u32[]{:S(2)}) collective-permute-start(bf16[32,2048]{1,0:T(8,128)(2,1)S(1)} %get-tuple-element.20.refs_1_.refs_7_), channel_id=1, source_target_pairs={{0,16},{1,17},{2,18},{3,19},{4,20},{5,21},{6,22},{7,23},{8,24},{9,... | collective-permute-start | bytes 393224 | tf_op jit(solution)/shard_map/ppermute | solution.py:388
  13.4 1.3 %collective-permute-start.6 = (f32[8,128]{1,0:T(8,128)S(1)}, f32[8,128]{1,0:T(8,128)S(1)}, u32[]{:S(2)}, u32[]{:S(2)}) collective-permute-start(f32[8,128]{1,0:T(8,128)S(1)} %copy.8), channel_id=1, source_target_pairs={{2,21},{3,20},{4,19},{5,18},{6,25},{7,24},{8,23},{9,22},{10,29},{1... | collective-permute-start | bytes 12296 | tf_op jit(solution)/shard_map/ppermute | solution.py:388
  14.7 2.8 %collective-permute-done.2.refs_0_ = bf16[32,2048]{1,0:T(8,128)(2,1)S(1)} collective-permute-done((bf16[32,2048]{1,0:T(8,128)(2,1)S(1)}, bf16[32,2048]{1,0:T(8,128)(2,1)S(1)}, u32[]{:S(2)}, u32[]{:S(2)}) %collective-permute-start.2) | collective-permute-done | bytes 131104 | tf_op jit(solution)/shard_map/ppermute | solution.py:388
  17.4 0.2 squares.7.refs_1_
  17.6 0.9 %collective-permute-done.4.refs_2_ = f32[8,128]{1,0:T(8,128)S(1)} collective-permute-done((f32[8,128]{1,0:T(8,128)S(1)}, f32[8,128]{1,0:T(8,128)S(1)}, u32[]{:S(2)}, u32[]{:S(2)}) %collective-permute-start.4) | collective-permute-done | bytes 4128 | tf_op jit(solution)/shard_map/ppermute | solution.py:388
  18.5 0.1 norm.1.refs_0_
  18.6 5.9 %collective-permute-start.7 = (bf16[32,2048]{1,0:T(8,128)(2,1)S(1)}, bf16[32,2048]{1,0:T(8,128)(2,1)S(1)}, u32[]{:S(2)}, u32[]{:S(2)}) collective-permute-start(bf16[32,2048]{1,0:T(8,128)(2,1)S(1)} %norm.1.refs_0_), channel_id=1, source_target_pairs={{16,18},{17,19},{18,16},{19,17},{20,22},{21,23},{22,20},{23,21},{2... | collective-permute-start | bytes 393224 | tf_op jit(solution)/shard_map/ppermute | solution.py:388
  24.5 0.4 %project.1.refs_11_ = bf16[32,6144]{1,0:T(8,128)(2,1)S(1)} custom-call(bf16[1,16,128,384]{3,2,1,0:T(8,128)(2,1)S(1)} %get-tuple-element.18.refs_5_.weights_ref, bf16[32,2048]{1,0:T(8,128)(2,1)S(1)} %norm.1.refs_0_), custom_call_target="tpu_custom_call" | custom-call | flops 2000000000 | bytes 300000 | tf_op jit(solution)/shard_map/project/pallas_call | solution.py:355
  24.9 0.0 collective-permute-done.5.refs_0_.refs_8_
  24.9 0.2 squares.6.mine_ref
  25.1 0.2 collective-permute-done.6.other_ref
  25.3 0.0 collective-permute-done.3.refs_1_
  25.3 0.2 collective-permute-done.7.refs_10_
  25.5 1.8 %layer.3 = bf16[1,2,8,4,2048]{4,3,2,1,0:T(4,128)(2,1)} custom-call(bf16[32,2048]{1,0:T(8,128)(2,1)S(1)} %collective-permute-done.2.refs_0_, bf16[32,2048]{1,0:T(8,128)(2,1)S(1)} %collective-permute-done.3.refs_1_, f32[8,128]{1,0:T(8,128)S(1)} %collective-permute-done.4.refs_2_, f32[2,64,128]{2,1,0:T(8,128)S(1)} %get-tuple-element.16.refs_3_, ...), custom_call_target="tpu_custom_call" | custom-call | flops 402653184 | bytes 4194304 | tf_op jit(solution)/shard_map/layer/pallas_call | solution.py:425
  (2 shorter events, 0.0 us)
Async XLA Ops:
  1.2 2.5 %collective-permute-start = (bf16[32,2048]{1,0:T(8,128)(2,1)S(1)}, bf16[32,2048]{1,0:T(8,128)(2,1)S(1)}, u32[]{:S(2)}, u32[]{:S(2)}) collective-permute-start(bf16[32,2048]{1,0:T(8,128)(2,1)S(1)} %get-tuple-element.14.refs_1_.refs_7_), channel_id=1, source_target_pairs={{2,4},{3,5},{4,2},{5,3},{6,8},{7,9},{8,6},{9,7},{10,12},{11,13},{1... | collective-permute-start | bytes 393224 | tf_op jit(solution)/shard_map/ppermute | solution.py:388
  1.9 1.9 %collective-permute-start.1 = (bf16[32,2048]{1,0:T(8,128)(2,1)S(1)}, bf16[32,2048]{1,0:T(8,128)(2,1)S(1)}, u32[]{:S(2)}, u32[]{:S(2)}) collective-permute-start(bf16[32,2048]{1,0:T(8,128)(2,1)S(1)} %get-tuple-element.13.refs_0_.refs_3_.refs_6_), channel_id=1, source_target_pairs={{0,2},{1,3},{2,0},{3,1},{4,6},{5,7},{6,4},{7,5},{8,10},{9,11},{10,... | collective-permute-start | bytes 393224 | tf_op jit(solution)/shard_map/ppermute | solution.py:388
  7.9 9.5 %collective-permute-start.2 = (bf16[32,2048]{1,0:T(8,128)(2,1)S(1)}, bf16[32,2048]{1,0:T(8,128)(2,1)S(1)}, u32[]{:S(2)}, u32[]{:S(2)}) collective-permute-start(bf16[32,2048]{1,0:T(8,128)(2,1)S(1)} %get-tuple-element.19.refs_0_.refs_6_), channel_id=1, source_target_pairs={{0,16},{1,17},{2,18},{3,19},{4,20},{5,21},{6,22},{7,23},{8,24},{9,... | collective-permute-start | bytes 393224 | tf_op jit(solution)/shard_map/ppermute | solution.py:388
  9.4 9.1 %collective-permute-start.4 = (f32[8,128]{1,0:T(8,128)S(1)}, f32[8,128]{1,0:T(8,128)S(1)}, u32[]{:S(2)}, u32[]{:S(2)}) collective-permute-start(f32[8,128]{1,0:T(8,128)S(1)} %squares.5.refs_0_), channel_id=1, source_target_pairs={{0,17},{1,16},{2,19},{3,18},{4,21},{5,20},{6,23},{7,22},{8,25},{9,... | collective-permute-start | bytes 12296 | tf_op jit(solution)/shard_map/ppermute | solution.py:388
  10.8 14.2 %collective-permute-start.5 = (bf16[32,2048]{1,0:T(8,128)(2,1)S(1)}, bf16[32,2048]{1,0:T(8,128)(2,1)S(1)}, u32[]{:S(2)}, u32[]{:S(2)}) collective-permute-start(bf16[32,2048]{1,0:T(8,128)(2,1)S(1)} %get-tuple-element.20.refs_1_.refs_7_), channel_id=1, source_target_pairs={{2,20},{3,21},{4,18},{5,19},{6,24},{7,25},{8,22},{9,23},{10,28},{1... | collective-permute-start | bytes 393224 | tf_op jit(solution)/shard_map/ppermute | solution.py:388
  12.1 13.2 %collective-permute-start.3 = (bf16[32,2048]{1,0:T(8,128)(2,1)S(1)}, bf16[32,2048]{1,0:T(8,128)(2,1)S(1)}, u32[]{:S(2)}, u32[]{:S(2)}) collective-permute-start(bf16[32,2048]{1,0:T(8,128)(2,1)S(1)} %get-tuple-element.20.refs_1_.refs_7_), channel_id=1, source_target_pairs={{0,16},{1,17},{2,18},{3,19},{4,20},{5,21},{6,22},{7,23},{8,24},{9,... | collective-permute-start | bytes 393224 | tf_op jit(solution)/shard_map/ppermute | solution.py:388
  13.4 11.9 %collective-permute-start.6 = (f32[8,128]{1,0:T(8,128)S(1)}, f32[8,128]{1,0:T(8,128)S(1)}, u32[]{:S(2)}, u32[]{:S(2)}) collective-permute-start(f32[8,128]{1,0:T(8,128)S(1)} %copy.8), channel_id=1, source_target_pairs={{2,21},{3,20},{4,19},{5,18},{6,25},{7,24},{8,23},{9,22},{10,29},{1... | collective-permute-start | bytes 12296 | tf_op jit(solution)/shard_map/ppermute | solution.py:388
  18.6 6.8 %collective-permute-start.7 = (bf16[32,2048]{1,0:T(8,128)(2,1)S(1)}, bf16[32,2048]{1,0:T(8,128)(2,1)S(1)}, u32[]{:S(2)}, u32[]{:S(2)}) collective-permute-start(bf16[32,2048]{1,0:T(8,128)(2,1)S(1)} %norm.1.refs_0_), channel_id=1, source_target_pairs={{16,18},{17,19},{18,16},{19,17},{20,22},{21,23},{22,20},{23,21},{2... | collective-permute-start | bytes 393224 | tf_op jit(solution)/shard_map/ppermute | solution.py:388

commit v17 on v12

--- a/solution.py
+++ b/solution.py
@@ -182,7 +182,12 @@
     if tick == 0:
         next_far_ref, next_chip_ref, *refs = refs
         late = [
-            (half, half_ref, squares_ref[half : half + 1, :], True)
+            (
+                half,
+                half_ref,
+                sum(squares_ref[i + half : i + half + 1, :] for i in range(0, squares_ref.shape[0], 8)),
+                True,
+            )
             for half, half_ref in enumerate((chip_ref, far_ref, next_far_ref, next_chip_ref))
         ]
     else:
@@ -372,7 +377,7 @@
 
     next_far = moved(far, 0, 0, 2)
     next_chip = moved(chip, 0, 0, 1)
-    squares = lax.psum(squares_of(chip, far, next_far, next_chip), "rep")
+    squares = lax.all_gather(squares_of(chip, far, next_far, next_chip), "rep", tiled=True)
     weights, time_bias, station_bias = pl.pallas_call(
         lambda *refs: fixed_kernel(*refs, stations=stations, total_steps=steps * seq_count),
         in_specs=[HBM] * 3 + [VMEM],

time: 27.8 us -> 27.2 us (0.978)
  blocking collectives: 3.8 us -> 3.19 us
    psum x1 -> x0, blocking collectives: 3.8 us -> none  [body(): squares = lax.psum(squares_of(chip, far, next_far, next_chip), 'rep')]
    all_gather x0 -> x1, blocking collectives: none -> 3.19 us  [body(): lax.all_gather(squares_of(chip, far, next_far, next_chip), 'rep', tiled=T...]
where the time goes in v17:
time: 27.2 us; the launch traced here: 26.9 us
  starting transfers between devices  13.9 us (51%)
  Pallas kernels  5.65 us (21%)
  waiting for transfers between devices  3.98 us (15%)
  blocking collectives  3.19 us (12%)
    ppermute x8, starting transfers between devices, moved(): return lax.ppermute(block, ('section', 'seq', 'rep'), route)  13.9 us
    ppermute x8, waiting for transfers between devices, moved(): return lax.ppermute(block, ('section', 'seq', 'rep'), route)  3.98 us
    all_gather x1, blocking collectives, body(): lax.all_gather(squares_of(chip, far, next_far, next_chip), 'rep', tiled=T...  3.19 us
    pallas_call x2, Pallas kernels, body(): pl.pallas_call(kernel, in_specs=[VMEM] * (8 + len(inputs)), out_specs=[VM...  1.87 us
    pallas_call x1, Pallas kernels, body(): pl.pallas_call(lambda *refs: fixed_kernel(*refs, stations=stations, total...  1.44 us
    pallas_call x1, Pallas kernels, body(): pl.pallas_call(halves_kernel, in_specs=[HBM], out_specs=[VMEM] * 2, out_s...  1.02 us
    pallas_call x4, Pallas kernels, squares_of(): pl.pallas_call(squares_kernel, in_specs=[VMEM] * len(halves), out_specs=V...  0.83 us
  transfers between devices with their start and end apart: 8, of which 4 were waited for; matrix products, arithmetic and copies ran while one was open for 0% of the time, Pallas kernels for 9%

profile of v17, /device:TPU:11, one launch (start us, length us, event | category | flops | bytes accessed | tf_op | source)
XLA Modules:
  0.0 26.9 jit_solution(16848087997804675355)
XLA Ops:
  0.0 1.0 %halves.1 = (bf16[32,2048]{1,0:T(8,128)(2,1)S(1)}, bf16[32,2048]{1,0:T(8,128)(2,1)S(1)}) custom-call(bf16[2,8,4,2048]{3,2,1,0:T(4,128)(2,1)} %signal_hbm.1), custom_call_target="tpu_custom_call" | custom-call | flops 131072 | bytes 524288 | tf_op jit(solution)/shard_map/halves/pallas_call | solution.py:353
  1.0 0.7 %collective-permute-start = (bf16[32,2048]{1,0:T(8,128)(2,1)S(1)}, bf16[32,2048]{1,0:T(8,128)(2,1)S(1)}, u32[]{:S(2)}, u32[]{:S(2)}) collective-permute-start(bf16[32,2048]{1,0:T(8,128)(2,1)S(1)} %get-tuple-element.13.refs_1_.refs_7_), channel_id=1, source_target_pairs={{2,4},{3,5},{4,2},{5,3},{6,8},{7,9},{8,6},{9,7},{10,12},{11,13},{1... | collective-permute-start | bytes 393224 | tf_op jit(solution)/shard_map/ppermute | solution.py:376
  1.7 0.7 %collective-permute-start.1 = (bf16[32,2048]{1,0:T(8,128)(2,1)S(1)}, bf16[32,2048]{1,0:T(8,128)(2,1)S(1)}, u32[]{:S(2)}, u32[]{:S(2)}) collective-permute-start(bf16[32,2048]{1,0:T(8,128)(2,1)S(1)} %get-tuple-element.12.refs_0_.refs_3_.refs_6_), channel_id=1, source_target_pairs={{0,2},{1,3},{2,0},{3,1},{4,6},{5,7},{6,4},{7,5},{8,10},{9,11},{10,... | collective-permute-start | bytes 393224 | tf_op jit(solution)/shard_map/ppermute | solution.py:376
  2.4 1.4 %fixed.1 = (bf16[1,16,128,384]{3,2,1,0:T(8,128)(2,1)S(1)}, f32[2,64,128]{2,1,0:T(8,128)S(1)}, f32[2,32,128]{2,1,0:T(8,128)S(1)}) custom-call(bf16[1,16,128,384]{3,2,1,0:T(8,128)(2,1)} %refs_0_.1, s32[2,4]{1,0:T(2,128)} %refs_1_.1, s32[2,4]{1,0:T(2,128)} %refs_2_.1, bf16[32,2048]{1,0:T(8,128)(2,1)S(1)} %get-tuple-element.12.refs_0_.refs_3_.refs_6_), custom_call_target="tpu_custom_call" | custom-call | flops 131072 | bytes 1572864 | tf_op jit(solution)/shard_map/fixed/pallas_call | solution.py:381
  3.8 0.0 collective-permute-done.refs_2_.refs_8_
  3.8 0.0 collective-permute-done.1.refs_3_.refs_9_
  3.8 0.3 %squares.4 = f32[8,128]{1,0:T(8,128)S(1)} custom-call(bf16[32,2048]{1,0:T(8,128)(2,1)S(1)} %get-tuple-element.12.refs_0_.refs_3_.refs_6_, bf16[32,2048]{1,0:T(8,128)(2,1)S(1)} %get-tuple-element.13.refs_1_.refs_7_, bf16[32,2048]{1,0:T(8,128)(2,1)S(1)} %collective-permute-done.refs_2_.refs_8_, bf16[32,2048]{1,0:T(8,128)(2,1)S(1)} %collective-permute-done.1.refs_3_.refs_9_), custom_call_target="tpu_custom_call" | custom-call | tf_op jit(solution)/shard_map/squares/pallas_call | solution.py:311
  4.1 3.2 %all_gather.3.refs_2_ = f32[16,128]{1,0:T(8,128)S(1)} all-gather(f32[8,128]{1,0:T(8,128)S(1)} %squares.4), channel_id=1, replica_groups=mesh['section'=2,'seq'=8,'rep'=2] {'rep'}, dimensions={0}, use_global_device_ids=true | all-gather | bytes 12288 | tf_op jit(solution)/shard_map/all_gather | solution.py:380
  7.4 1.3 %collective-permute-start.2 = (bf16[32,2048]{1,0:T(8,128)(2,1)S(1)}, bf16[32,2048]{1,0:T(8,128)(2,1)S(1)}, u32[]{:S(2)}, u32[]{:S(2)}) collective-permute-start(bf16[32,2048]{1,0:T(8,128)(2,1)S(1)} %get-tuple-element.17.refs_0_.refs_6_), channel_id=1, source_target_pairs={{0,16},{1,17},{2,18},{3,19},{4,20},{5,21},{6,22},{7,23},{8,24},{9,... | collective-permute-start | bytes 393224 | tf_op jit(solution)/shard_map/ppermute | solution.py:376
  8.7 0.2 squares.5.refs_0_
  8.9 1.3 %collective-permute-start.4 = (f32[8,128]{1,0:T(8,128)S(1)}, f32[8,128]{1,0:T(8,128)S(1)}, u32[]{:S(2)}, u32[]{:S(2)}) collective-permute-start(f32[8,128]{1,0:T(8,128)S(1)} %squares.5.refs_0_), channel_id=1, source_target_pairs={{0,17},{1,16},{2,19},{3,18},{4,21},{5,20},{6,23},{7,22},{8,25},{9,... | collective-permute-start | bytes 12296 | tf_op jit(solution)/shard_map/ppermute | solution.py:376
  10.2 1.3 %collective-permute-start.5 = (bf16[32,2048]{1,0:T(8,128)(2,1)S(1)}, bf16[32,2048]{1,0:T(8,128)(2,1)S(1)}, u32[]{:S(2)}, u32[]{:S(2)}) collective-permute-start(bf16[32,2048]{1,0:T(8,128)(2,1)S(1)} %get-tuple-element.18.refs_1_.refs_7_), channel_id=1, source_target_pairs={{2,20},{3,21},{4,18},{5,19},{6,24},{7,25},{8,22},{9,23},{10,28},{1... | collective-permute-start | bytes 393224 | tf_op jit(solution)/shard_map/ppermute | solution.py:376
  11.5 1.3 %collective-permute-start.3 = (bf16[32,2048]{1,0:T(8,128)(2,1)S(1)}, bf16[32,2048]{1,0:T(8,128)(2,1)S(1)}, u32[]{:S(2)}, u32[]{:S(2)}) collective-permute-start(bf16[32,2048]{1,0:T(8,128)(2,1)S(1)} %get-tuple-element.18.refs_1_.refs_7_), channel_id=1, source_target_pairs={{0,16},{1,17},{2,18},{3,19},{4,20},{5,21},{6,22},{7,23},{8,24},{9,... | collective-permute-start | bytes 393224 | tf_op jit(solution)/shard_map/ppermute | solution.py:376
  12.8 1.3 %collective-permute-start.6 = (f32[8,128]{1,0:T(8,128)S(1)}, f32[8,128]{1,0:T(8,128)S(1)}, u32[]{:S(2)}, u32[]{:S(2)}) collective-permute-start(f32[8,128]{1,0:T(8,128)S(1)} %copy.6), channel_id=1, source_target_pairs={{2,21},{3,20},{4,19},{5,18},{6,25},{7,24},{8,23},{9,22},{10,29},{1... | collective-permute-start | bytes 12296 | tf_op jit(solution)/shard_map/ppermute | solution.py:376
  14.1 2.7 %collective-permute-done.2.refs_0_ = bf16[32,2048]{1,0:T(8,128)(2,1)S(1)} collective-permute-done((bf16[32,2048]{1,0:T(8,128)(2,1)S(1)}, bf16[32,2048]{1,0:T(8,128)(2,1)S(1)}, u32[]{:S(2)}, u32[]{:S(2)}) %collective-permute-start.2) | collective-permute-done | bytes 131104 | tf_op jit(solution)/shard_map/ppermute | solution.py:376
  16.8 0.2 squares.7.refs_1_
  16.9 0.9 %collective-permute-done.4.refs_2_ = f32[8,128]{1,0:T(8,128)S(1)} collective-permute-done((f32[8,128]{1,0:T(8,128)S(1)}, f32[8,128]{1,0:T(8,128)S(1)}, u32[]{:S(2)}, u32[]{:S(2)}) %collective-permute-start.4) | collective-permute-done | bytes 4128 | tf_op jit(solution)/shard_map/ppermute | solution.py:376
  17.9 0.1 norm.1.refs_0_
  18.0 6.1 %collective-permute-start.7 = (bf16[32,2048]{1,0:T(8,128)(2,1)S(1)}, bf16[32,2048]{1,0:T(8,128)(2,1)S(1)}, u32[]{:S(2)}, u32[]{:S(2)}) collective-permute-start(bf16[32,2048]{1,0:T(8,128)(2,1)S(1)} %norm.1.refs_0_), channel_id=1, source_target_pairs={{16,18},{17,19},{18,16},{19,17},{20,22},{21,23},{22,20},{23,21},{2... | collective-permute-start | bytes 393224 | tf_op jit(solution)/shard_map/ppermute | solution.py:376
  24.1 0.4 %project.1.refs_11_ = bf16[32,6144]{1,0:T(8,128)(2,1)S(1)} custom-call(bf16[1,16,128,384]{3,2,1,0:T(8,128)(2,1)S(1)} %get-tuple-element.16.refs_5_.weights_ref, bf16[32,2048]{1,0:T(8,128)(2,1)S(1)} %norm.1.refs_0_), custom_call_target="tpu_custom_call" | custom-call | flops 2000000000 | bytes 300000 | tf_op jit(solution)/shard_map/project/pallas_call | solution.py:343
  24.5 0.0 collective-permute-done.5.refs_0_.refs_8_
  24.5 0.2 squares.6.mine_ref
  24.7 0.1 collective-permute-done.6.other_ref
  24.7 0.0 collective-permute-done.3.refs_1_
  24.7 0.3 %collective-permute-done.7.refs_10_ = bf16[32,2048]{1,0:T(8,128)(2,1)S(1)} collective-permute-done((bf16[32,2048]{1,0:T(8,128)(2,1)S(1)}, bf16[32,2048]{1,0:T(8,128)(2,1)S(1)}, u32[]{:S(2)}, u32[]{:S(2)}) %collective-permute-start.7) | collective-permute-done | bytes 131104 | tf_op jit(solution)/shard_map/ppermute | solution.py:376
  25.1 1.8 %layer.3 = bf16[1,2,8,4,2048]{4,3,2,1,0:T(4,128)(2,1)} custom-call(bf16[32,2048]{1,0:T(8,128)(2,1)S(1)} %collective-permute-done.2.refs_0_, bf16[32,2048]{1,0:T(8,128)(2,1)S(1)} %collective-permute-done.3.refs_1_, f32[8,128]{1,0:T(8,128)S(1)} %collective-permute-done.4.refs_2_, f32[2,64,128]{2,1,0:T(8,128)S(1)} %get-tuple-element.14.refs_3_, ...), custom_call_target="tpu_custom_call" | custom-call | flops 402653184 | bytes 4194304 | tf_op jit(solution)/shard_map/layer/pallas_call | solution.py:412
  (3 shorter events, 0.1 us)
Async XLA Ops:
  1.0 2.8 %collective-permute-start = (bf16[32,2048]{1,0:T(8,128)(2,1)S(1)}, bf16[32,2048]{1,0:T(8,128)(2,1)S(1)}, u32[]{:S(2)}, u32[]{:S(2)}) collective-permute-start(bf16[32,2048]{1,0:T(8,128)(2,1)S(1)} %get-tuple-element.13.refs_1_.refs_7_), channel_id=1, source_target_pairs={{2,4},{3,5},{4,2},{5,3},{6,8},{7,9},{8,6},{9,7},{10,12},{11,13},{1... | collective-permute-start | bytes 393224 | tf_op jit(solution)/shard_map/ppermute | solution.py:376
  1.7 2.1 %collective-permute-start.1 = (bf16[32,2048]{1,0:T(8,128)(2,1)S(1)}, bf16[32,2048]{1,0:T(8,128)(2,1)S(1)}, u32[]{:S(2)}, u32[]{:S(2)}) collective-permute-start(bf16[32,2048]{1,0:T(8,128)(2,1)S(1)} %get-tuple-element.12.refs_0_.refs_3_.refs_6_), channel_id=1, source_target_pairs={{0,2},{1,3},{2,0},{3,1},{4,6},{5,7},{6,4},{7,5},{8,10},{9,11},{10,... | collective-permute-start | bytes 393224 | tf_op jit(solution)/shard_map/ppermute | solution.py:376
  7.4 9.4 %collective-permute-start.2 = (bf16[32,2048]{1,0:T(8,128)(2,1)S(1)}, bf16[32,2048]{1,0:T(8,128)(2,1)S(1)}, u32[]{:S(2)}, u32[]{:S(2)}) collective-permute-start(bf16[32,2048]{1,0:T(8,128)(2,1)S(1)} %get-tuple-element.17.refs_0_.refs_6_), channel_id=1, source_target_pairs={{0,16},{1,17},{2,18},{3,19},{4,20},{5,21},{6,22},{7,23},{8,24},{9,... | collective-permute-start | bytes 393224 | tf_op jit(solution)/shard_map/ppermute | solution.py:376
  8.9 9.0 %collective-permute-start.4 = (f32[8,128]{1,0:T(8,128)S(1)}, f32[8,128]{1,0:T(8,128)S(1)}, u32[]{:S(2)}, u32[]{:S(2)}) collective-permute-start(f32[8,128]{1,0:T(8,128)S(1)} %squares.5.refs_0_), channel_id=1, source_target_pairs={{0,17},{1,16},{2,19},{3,18},{4,21},{5,20},{6,23},{7,22},{8,25},{9,... | collective-permute-start | bytes 12296 | tf_op jit(solution)/shard_map/ppermute | solution.py:376
  10.2 14.3 %collective-permute-start.5 = (bf16[32,2048]{1,0:T(8,128)(2,1)S(1)}, bf16[32,2048]{1,0:T(8,128)(2,1)S(1)}, u32[]{:S(2)}, u32[]{:S(2)}) collective-permute-start(bf16[32,2048]{1,0:T(8,128)(2,1)S(1)} %get-tuple-element.18.refs_1_.refs_7_), channel_id=1, source_target_pairs={{2,20},{3,21},{4,18},{5,19},{6,24},{7,25},{8,22},{9,23},{10,28},{1... | collective-permute-start | bytes 393224 | tf_op jit(solution)/shard_map/ppermute | solution.py:376
  11.5 13.2 %collective-permute-start.3 = (bf16[32,2048]{1,0:T(8,128)(2,1)S(1)}, bf16[32,2048]{1,0:T(8,128)(2,1)S(1)}, u32[]{:S(2)}, u32[]{:S(2)}) collective-permute-start(bf16[32,2048]{1,0:T(8,128)(2,1)S(1)} %get-tuple-element.18.refs_1_.refs_7_), channel_id=1, source_target_pairs={{0,16},{1,17},{2,18},{3,19},{4,20},{5,21},{6,22},{7,23},{8,24},{9,... | collective-permute-start | bytes 393224 | tf_op jit(solution)/shard_map/ppermute | solution.py:376
  12.8 11.9 %collective-permute-start.6 = (f32[8,128]{1,0:T(8,128)S(1)}, f32[8,128]{1,0:T(8,128)S(1)}, u32[]{:S(2)}, u32[]{:S(2)}) collective-permute-start(f32[8,128]{1,0:T(8,128)S(1)} %copy.6), channel_id=1, source_target_pairs={{2,21},{3,20},{4,19},{5,18},{6,25},{7,24},{8,23},{9,22},{10,29},{1... | collective-permute-start | bytes 12296 | tf_op jit(solution)/shard_map/ppermute | solution.py:376
  18.0 7.1 %collective-permute-start.7 = (bf16[32,2048]{1,0:T(8,128)(2,1)S(1)}, bf16[32,2048]{1,0:T(8,128)(2,1)S(1)}, u32[]{:S(2)}, u32[]{:S(2)}) collective-permute-start(bf16[32,2048]{1,0:T(8,128)(2,1)S(1)} %norm.1.refs_0_), channel_id=1, source_target_pairs={{16,18},{17,19},{18,16},{19,17},{20,22},{21,23},{22,20},{23,21},{2... | collective-permute-start | bytes 393224 | tf_op jit(solution)/shard_map/ppermute | solution.py:376

commit v18 on v17

--- a/solution.py
+++ b/solution.py
@@ -231,7 +231,9 @@
             factor = lax.rsqrt(jnp.sum(total, axis=1, keepdims=True) / (HEADS * HEAD) + EPS)
             normed_ref[...] = (half_ref[...].astype(f32) * factor).astype(bf16)
         if tick > 0:
-            normed.append(next_chip_ref)
+            rows = micro * edge
+            other = pl.multiple_of((1 - odd_device()) * rows, rows)
+            normed.append(next_chip_ref.at[pl.ds(other, rows)])
         project_kernel(weights_ref, *normed, *[projected[half] for half in projecting])
         pairs = [(g, m) for g in range(heads_dev // GROUP) for m in range(micro)]
         blank = jnp.zeros((own, HEAD), bf16)
@@ -436,7 +438,12 @@
         far = moved(kept[1], tick, tick + 1, 0)
         far_squares = moved(mine_again, tick, tick + 1, 2, other=True)
         normed_chip = normed(chip, squares, CHIP)
-        next_chip = moved(normed_chip, tick + 1, tick + 1, 1)
+        next_chip = lax.all_gather(
+            normed_chip,
+            "seq",
+            axis_index_groups=[[i, i + 1] for i in range(0, seq_count, 2)],
+            tiled=True,
+        )
         far_squares = pl.pallas_call(
             add_kernel,
             in_specs=[VMEM] * 2,

time: 27.2 us -> 26.9 us (0.989)
  starting transfers between devices: 13.9 us -> 7.8 us
  blocking collectives: 3.19 us -> 9.03 us
    ppermute x8 -> x7, starting transfers between devices: 13.9 us -> 7.8 us  [moved(): return lax.ppermute(block, ('section', 'seq', 'rep'), route)]
    all_gather x0 -> x1, blocking collectives: none -> 5.83 us  [body(): lax.all_gather(normed_chip, 'seq', axis_index_groups=[[i, i + 1] for i in...]
    ppermute x8 -> x7, waiting for transfers between devices: 3.98 us -> 3.94 us  [moved(): return lax.ppermute(block, ('section', 'seq', 'rep'), route)]
  transfers between devices with their start and end apart: 8 -> 7, of which waited for: 4 -> 3; matrix products, arithmetic and copies ran while one was open for 0% -> 0% of each run, Pallas kernels for 9% -> 9%
where the time goes in v18:
time: 26.9 us; the launch traced here: 26.6 us
  blocking collectives  9.03 us (34%)
  starting transfers between devices  7.8 us (29%)
  Pallas kernels  5.66 us (21%)
  waiting for transfers between devices  3.94 us (15%)
    ppermute x7, starting transfers between devices, moved(): return lax.ppermute(block, ('section', 'seq', 'rep'), route)  7.8 us
    all_gather x1, blocking collectives, body(): lax.all_gather(normed_chip, 'seq', axis_index_groups=[[i, i + 1] for i in...  5.83 us
    ppermute x7, waiting for transfers between devices, moved(): return lax.ppermute(block, ('section', 'seq', 'rep'), route)  3.94 us
    all_gather x1, blocking collectives, body(): lax.all_gather(squares_of(chip, far, next_far, next_chip), 'rep', tiled=T...  3.19 us
    pallas_call x2, Pallas kernels, body(): pl.pallas_call(kernel, in_specs=[VMEM] * (8 + len(inputs)), out_specs=[VM...  1.87 us
    pallas_call x1, Pallas kernels, body(): pl.pallas_call(lambda *refs: fixed_kernel(*refs, stations=stations, total...  1.44 us
    pallas_call x1, Pallas kernels, body(): pl.pallas_call(halves_kernel, in_specs=[HBM], out_specs=[VMEM] * 2, out_s...  1.02 us
    pallas_call x4, Pallas kernels, squares_of(): pl.pallas_call(squares_kernel, in_specs=[VMEM] * len(halves), out_specs=V...  0.83 us
  transfers between devices with their start and end apart: 7, of which 3 were waited for; matrix products, arithmetic and copies ran while one was open for 0% of the time, Pallas kernels for 9%

profile of v18, /device:TPU:11, one launch (start us, length us, event | category | flops | bytes accessed | tf_op | source)
XLA Modules:
  0.0 26.6 jit_solution(2411898087537041426)
XLA Ops:
  0.0 1.0 %halves.1 = (bf16[32,2048]{1,0:T(8,128)(2,1)S(1)}, bf16[32,2048]{1,0:T(8,128)(2,1)S(1)}) custom-call(bf16[2,8,4,2048]{3,2,1,0:T(4,128)(2,1)} %signal_hbm.1), custom_call_target="tpu_custom_call" | custom-call | flops 131072 | bytes 524288 | tf_op jit(solution)/shard_map/halves/pallas_call | solution.py:355
  1.0 0.7 %collective-permute-start = (bf16[32,2048]{1,0:T(8,128)(2,1)S(1)}, bf16[32,2048]{1,0:T(8,128)(2,1)S(1)}, u32[]{:S(2)}, u32[]{:S(2)}) collective-permute-start(bf16[32,2048]{1,0:T(8,128)(2,1)S(1)} %get-tuple-element.13.refs_1_.refs_7_), channel_id=1, source_target_pairs={{2,4},{3,5},{4,2},{5,3},{6,8},{7,9},{8,6},{9,7},{10,12},{11,13},{1... | collective-permute-start | bytes 393224 | tf_op jit(solution)/shard_map/ppermute | solution.py:378
  1.7 0.7 %collective-permute-start.1 = (bf16[32,2048]{1,0:T(8,128)(2,1)S(1)}, bf16[32,2048]{1,0:T(8,128)(2,1)S(1)}, u32[]{:S(2)}, u32[]{:S(2)}) collective-permute-start(bf16[32,2048]{1,0:T(8,128)(2,1)S(1)} %get-tuple-element.12.refs_0_.refs_3_.refs_6_), channel_id=1, source_target_pairs={{0,2},{1,3},{2,0},{3,1},{4,6},{5,7},{6,4},{7,5},{8,10},{9,11},{10,... | collective-permute-start | bytes 393224 | tf_op jit(solution)/shard_map/ppermute | solution.py:378
  2.4 1.4 %fixed.1 = (bf16[1,16,128,384]{3,2,1,0:T(8,128)(2,1)S(1)}, f32[2,64,128]{2,1,0:T(8,128)S(1)}, f32[2,32,128]{2,1,0:T(8,128)S(1)}) custom-call(bf16[1,16,128,384]{3,2,1,0:T(8,128)(2,1)} %refs_0_.1, s32[2,4]{1,0:T(2,128)} %refs_1_.1, s32[2,4]{1,0:T(2,128)} %refs_2_.1, bf16[32,2048]{1,0:T(8,128)(2,1)S(1)} %get-tuple-element.12.refs_0_.refs_3_.refs_6_), custom_call_target="tpu_custom_call" | custom-call | flops 131072 | bytes 1572864 | tf_op jit(solution)/shard_map/fixed/pallas_call | solution.py:383
  3.8 0.0 collective-permute-done.refs_2_.refs_8_
  3.8 0.0 collective-permute-done.1.refs_3_.refs_9_
  3.8 0.3 %squares.4 = f32[8,128]{1,0:T(8,128)S(1)} custom-call(bf16[32,2048]{1,0:T(8,128)(2,1)S(1)} %get-tuple-element.12.refs_0_.refs_3_.refs_6_, bf16[32,2048]{1,0:T(8,128)(2,1)S(1)} %get-tuple-element.13.refs_1_.refs_7_, bf16[32,2048]{1,0:T(8,128)(2,1)S(1)} %collective-permute-done.refs_2_.refs_8_, bf16[32,2048]{1,0:T(8,128)(2,1)S(1)} %collective-permute-done.1.refs_3_.refs_9_), custom_call_target="tpu_custom_call" | custom-call | tf_op jit(solution)/shard_map/squares/pallas_call | solution.py:313
  4.1 3.2 %all_gather.6.refs_2_ = f32[16,128]{1,0:T(8,128)S(1)} all-gather(f32[8,128]{1,0:T(8,128)S(1)} %squares.4), channel_id=1, replica_groups=mesh['section'=2,'seq'=8,'rep'=2] {'rep'}, dimensions={0}, use_global_device_ids=true | all-gather | bytes 12288 | tf_op jit(solution)/shard_map/all_gather | solution.py:382
  7.4 1.3 %collective-permute-start.2 = (bf16[32,2048]{1,0:T(8,128)(2,1)S(1)}, bf16[32,2048]{1,0:T(8,128)(2,1)S(1)}, u32[]{:S(2)}, u32[]{:S(2)}) collective-permute-start(bf16[32,2048]{1,0:T(8,128)(2,1)S(1)} %get-tuple-element.17.refs_0_.refs_6_), channel_id=1, source_target_pairs={{0,16},{1,17},{2,18},{3,19},{4,20},{5,21},{6,22},{7,23},{8,24},{9,... | collective-permute-start | bytes 393224 | tf_op jit(solution)/shard_map/ppermute | solution.py:378
  8.7 0.2 squares.5.refs_0_
  8.9 1.3 %collective-permute-start.4 = (f32[8,128]{1,0:T(8,128)S(1)}, f32[8,128]{1,0:T(8,128)S(1)}, u32[]{:S(2)}, u32[]{:S(2)}) collective-permute-start(f32[8,128]{1,0:T(8,128)S(1)} %squares.5.refs_0_), channel_id=1, source_target_pairs={{0,17},{1,16},{2,19},{3,18},{4,21},{5,20},{6,23},{7,22},{8,25},{9,... | collective-permute-start | bytes 12296 | tf_op jit(solution)/shard_map/ppermute | solution.py:378
  10.2 1.3 %collective-permute-start.5 = (bf16[32,2048]{1,0:T(8,128)(2,1)S(1)}, bf16[32,2048]{1,0:T(8,128)(2,1)S(1)}, u32[]{:S(2)}, u32[]{:S(2)}) collective-permute-start(bf16[32,2048]{1,0:T(8,128)(2,1)S(1)} %get-tuple-element.18.refs_1_.refs_7_), channel_id=1, source_target_pairs={{2,20},{3,21},{4,18},{5,19},{6,24},{7,25},{8,22},{9,23},{10,28},{1... | collective-permute-start | bytes 393224 | tf_op jit(solution)/shard_map/ppermute | solution.py:378
  11.5 1.3 %collective-permute-start.3 = (bf16[32,2048]{1,0:T(8,128)(2,1)S(1)}, bf16[32,2048]{1,0:T(8,128)(2,1)S(1)}, u32[]{:S(2)}, u32[]{:S(2)}) collective-permute-start(bf16[32,2048]{1,0:T(8,128)(2,1)S(1)} %get-tuple-element.18.refs_1_.refs_7_), channel_id=1, source_target_pairs={{0,16},{1,17},{2,18},{3,19},{4,20},{5,21},{6,22},{7,23},{8,24},{9,... | collective-permute-start | bytes 393224 | tf_op jit(solution)/shard_map/ppermute | solution.py:378
  12.8 1.3 %collective-permute-start.6 = (f32[8,128]{1,0:T(8,128)S(1)}, f32[8,128]{1,0:T(8,128)S(1)}, u32[]{:S(2)}, u32[]{:S(2)}) collective-permute-start(f32[8,128]{1,0:T(8,128)S(1)} %copy.6), channel_id=1, source_target_pairs={{2,21},{3,20},{4,19},{5,18},{6,25},{7,24},{8,23},{9,22},{10,29},{1... | collective-permute-start | bytes 12296 | tf_op jit(solution)/shard_map/ppermute | solution.py:378
  14.1 2.7 %collective-permute-done.2.refs_0_ = bf16[32,2048]{1,0:T(8,128)(2,1)S(1)} collective-permute-done((bf16[32,2048]{1,0:T(8,128)(2,1)S(1)}, bf16[32,2048]{1,0:T(8,128)(2,1)S(1)}, u32[]{:S(2)}, u32[]{:S(2)}) %collective-permute-start.2) | collective-permute-done | bytes 131104 | tf_op jit(solution)/shard_map/ppermute | solution.py:378
  16.8 0.2 squares.7.refs_1_
  16.9 0.9 %collective-permute-done.4.refs_2_ = f32[8,128]{1,0:T(8,128)S(1)} collective-permute-done((f32[8,128]{1,0:T(8,128)S(1)}, f32[8,128]{1,0:T(8,128)S(1)}, u32[]{:S(2)}, u32[]{:S(2)}) %collective-permute-start.4) | collective-permute-done | bytes 4128 | tf_op jit(solution)/shard_map/ppermute | solution.py:378
  17.9 0.1 norm.1.refs_0_
  18.0 0.4 %project.1.refs_11_ = bf16[32,6144]{1,0:T(8,128)(2,1)S(1)} custom-call(bf16[1,16,128,384]{3,2,1,0:T(8,128)(2,1)S(1)} %get-tuple-element.16.refs_5_.weights_ref, bf16[32,2048]{1,0:T(8,128)(2,1)S(1)} %norm.1.refs_0_), custom_call_target="tpu_custom_call" | custom-call | flops 2000000000 | bytes 300000 | tf_op jit(solution)/shard_map/project/pallas_call | solution.py:345
  18.4 5.8 %all_gather.7.refs_10_ = bf16[64,2048]{1,0:T(8,128)(2,1)S(1)} all-gather(bf16[32,2048]{1,0:T(8,128)(2,1)S(1)} %norm.1.refs_0_), channel_id=1, replica_groups={{0,2},{4,6},{8,10},{12,14},{1,3},{5,7},{9,11},{13,15},{16,18},{20,22},{..., dimensions={0}, use_global_device_ids=true | all-gather | bytes 393216 | tf_op jit(solution)/shard_map/all_gather | solution.py:441
  24.2 0.0 collective-permute-done.5.refs_0_.refs_8_
  24.2 0.2 squares.6.mine_ref
  24.4 0.3 %collective-permute-done.6.other_ref = f32[8,128]{1,0:T(8,128)S(1)} collective-permute-done((f32[8,128]{1,0:T(8,128)S(1)}, f32[8,128]{1,0:T(8,128)S(1)}, u32[]{:S(2)}, u32[]{:S(2)}) %collective-permute-start.6) | collective-permute-done | bytes 4128 | tf_op jit(solution)/shard_map/ppermute | solution.py:378
  24.7 0.0 collective-permute-done.3.refs_1_
  24.7 1.8 %layer.3 = bf16[1,2,8,4,2048]{4,3,2,1,0:T(4,128)(2,1)} custom-call(bf16[32,2048]{1,0:T(8,128)(2,1)S(1)} %collective-permute-done.2.refs_0_, bf16[32,2048]{1,0:T(8,128)(2,1)S(1)} %collective-permute-done.3.refs_1_, f32[8,128]{1,0:T(8,128)S(1)} %collective-permute-done.4.refs_2_, f32[2,64,128]{2,1,0:T(8,128)S(1)} %get-tuple-element.14.refs_3_, ...), custom_call_target="tpu_custom_call" | custom-call | flops 402653184 | bytes 4194304 | tf_op jit(solution)/shard_map/layer/pallas_call | solution.py:414
  (3 shorter events, 0.1 us)
Async XLA Ops:
  1.0 2.8 %collective-permute-start = (bf16[32,2048]{1,0:T(8,128)(2,1)S(1)}, bf16[32,2048]{1,0:T(8,128)(2,1)S(1)}, u32[]{:S(2)}, u32[]{:S(2)}) collective-permute-start(bf16[32,2048]{1,0:T(8,128)(2,1)S(1)} %get-tuple-element.13.refs_1_.refs_7_), channel_id=1, source_target_pairs={{2,4},{3,5},{4,2},{5,3},{6,8},{7,9},{8,6},{9,7},{10,12},{11,13},{1... | collective-permute-start | bytes 393224 | tf_op jit(solution)/shard_map/ppermute | solution.py:378
  1.7 2.1 %collective-permute-start.1 = (bf16[32,2048]{1,0:T(8,128)(2,1)S(1)}, bf16[32,2048]{1,0:T(8,128)(2,1)S(1)}, u32[]{:S(2)}, u32[]{:S(2)}) collective-permute-start(bf16[32,2048]{1,0:T(8,128)(2,1)S(1)} %get-tuple-element.12.refs_0_.refs_3_.refs_6_), channel_id=1, source_target_pairs={{0,2},{1,3},{2,0},{3,1},{4,6},{5,7},{6,4},{7,5},{8,10},{9,11},{10,... | collective-permute-start | bytes 393224 | tf_op jit(solution)/shard_map/ppermute | solution.py:378
  7.4 9.4 %collective-permute-start.2 = (bf16[32,2048]{1,0:T(8,128)(2,1)S(1)}, bf16[32,2048]{1,0:T(8,128)(2,1)S(1)}, u32[]{:S(2)}, u32[]{:S(2)}) collective-permute-start(bf16[32,2048]{1,0:T(8,128)(2,1)S(1)} %get-tuple-element.17.refs_0_.refs_6_), channel_id=1, source_target_pairs={{0,16},{1,17},{2,18},{3,19},{4,20},{5,21},{6,22},{7,23},{8,24},{9,... | collective-permute-start | bytes 393224 | tf_op jit(solution)/shard_map/ppermute | solution.py:378
  8.9 9.0 %collective-permute-start.4 = (f32[8,128]{1,0:T(8,128)S(1)}, f32[8,128]{1,0:T(8,128)S(1)}, u32[]{:S(2)}, u32[]{:S(2)}) collective-permute-start(f32[8,128]{1,0:T(8,128)S(1)} %squares.5.refs_0_), channel_id=1, source_target_pairs={{0,17},{1,16},{2,19},{3,18},{4,21},{5,20},{6,23},{7,22},{8,25},{9,... | collective-permute-start | bytes 12296 | tf_op jit(solution)/shard_map/ppermute | solution.py:378
  10.2 14.0 %collective-permute-start.5 = (bf16[32,2048]{1,0:T(8,128)(2,1)S(1)}, bf16[32,2048]{1,0:T(8,128)(2,1)S(1)}, u32[]{:S(2)}, u32[]{:S(2)}) collective-permute-start(bf16[32,2048]{1,0:T(8,128)(2,1)S(1)} %get-tuple-element.18.refs_1_.refs_7_), channel_id=1, source_target_pairs={{2,20},{3,21},{4,18},{5,19},{6,24},{7,25},{8,22},{9,23},{10,28},{1... | collective-permute-start | bytes 393224 | tf_op jit(solution)/shard_map/ppermute | solution.py:378
  11.5 13.2 %collective-permute-start.3 = (bf16[32,2048]{1,0:T(8,128)(2,1)S(1)}, bf16[32,2048]{1,0:T(8,128)(2,1)S(1)}, u32[]{:S(2)}, u32[]{:S(2)}) collective-permute-start(bf16[32,2048]{1,0:T(8,128)(2,1)S(1)} %get-tuple-element.18.refs_1_.refs_7_), channel_id=1, source_target_pairs={{0,16},{1,17},{2,18},{3,19},{4,20},{5,21},{6,22},{7,23},{8,24},{9,... | collective-permute-start | bytes 393224 | tf_op jit(solution)/shard_map/ppermute | solution.py:378
  12.8 11.9 %collective-permute-start.6 = (f32[8,128]{1,0:T(8,128)S(1)}, f32[8,128]{1,0:T(8,128)S(1)}, u32[]{:S(2)}, u32[]{:S(2)}) collective-permute-start(f32[8,128]{1,0:T(8,128)S(1)} %copy.6), channel_id=1, source_target_pairs={{2,21},{3,20},{4,19},{5,18},{6,25},{7,24},{8,23},{9,22},{10,29},{1... | collective-permute-start | bytes 12296 | tf_op jit(solution)/shard_map/ppermute | solution.py:378

commit v19 on v18

--- a/solution.py
+++ b/solution.py
@@ -341,16 +341,16 @@
             name="copy",
         )(*blocks)
 
-    def project(*halves):
+    def project(half, after):
         return pl.pallas_call(
-            project_kernel,
-            in_specs=[VMEM] * (1 + len(halves)),
-            out_specs=[VMEM] * len(halves),
-            out_shape=[projected_shape] * len(halves),
+            lambda weights_ref, half_ref, _, out_ref: project_kernel(weights_ref, half_ref, out_ref),
+            in_specs=[VMEM] * 3,
+            out_specs=VMEM,
+            out_shape=projected_shape,
             compiler_params=PARAMS,
             cost_estimate=BUSY,
             name="project",
-        )(weights, *halves)
+        )(weights, half, after)
 
     chip, far = pl.pallas_call(
         halves_kernel,
@@ -453,7 +453,7 @@
             cost_estimate=BUSY,
             name="add",
         )(squares_of(next_far), far_squares)
-        inputs = (next_far, far_squares, next_chip, *project(normed_chip))
+        inputs = (next_far, far_squares, next_chip, project(normed_chip, next_chip))
 
 
 def solution(mesh):

time: 26.9 us -> 26.9 us (level)
  no operation moved by 1% of the time
where the time goes in v19:
time: 26.9 us; the launch traced here: 26.6 us
  blocking collectives  9.02 us (34%)
  starting transfers between devices  7.8 us (29%)
  Pallas kernels  5.66 us (21%)
  waiting for transfers between devices  3.94 us (15%)
    ppermute x7, starting transfers between devices, moved(): return lax.ppermute(block, ('section', 'seq', 'rep'), route)  7.8 us
    all_gather x1, blocking collectives, body(): lax.all_gather(normed_chip, 'seq', axis_index_groups=[[i, i + 1] for i in...  5.83 us
    ppermute x7, waiting for transfers between devices, moved(): return lax.ppermute(block, ('section', 'seq', 'rep'), route)  3.94 us
    all_gather x1, blocking collectives, body(): lax.all_gather(squares_of(chip, far, next_far, next_chip), 'rep', tiled=T...  3.19 us
    pallas_call x2, Pallas kernels, body(): pl.pallas_call(kernel, in_specs=[VMEM] * (8 + len(inputs)), out_specs=[VM...  1.87 us
    pallas_call x1, Pallas kernels, body(): pl.pallas_call(lambda *refs: fixed_kernel(*refs, stations=stations, total...  1.44 us
    pallas_call x1, Pallas kernels, body(): pl.pallas_call(halves_kernel, in_specs=[HBM], out_specs=[VMEM] * 2, out_s...  1.02 us
    pallas_call x4, Pallas kernels, squares_of(): pl.pallas_call(squares_kernel, in_specs=[VMEM] * len(halves), out_specs=V...  0.83 us
  transfers between devices with their start and end apart: 7, of which 3 were waited for; matrix products, arithmetic and copies ran while one was open for 0% of the time, Pallas kernels for 9%

profile of v19, /device:TPU:11, one launch (start us, length us, event | category | flops | bytes accessed | tf_op | source)
XLA Modules:
  0.0 26.6 jit_solution(14551517207226546189)
XLA Ops:
  0.0 1.0 %halves.1 = (bf16[32,2048]{1,0:T(8,128)(2,1)S(1)}, bf16[32,2048]{1,0:T(8,128)(2,1)S(1)}) custom-call(bf16[2,8,4,2048]{3,2,1,0:T(4,128)(2,1)} %signal_hbm.1), custom_call_target="tpu_custom_call" | custom-call | flops 131072 | bytes 524288 | tf_op jit(solution)/shard_map/halves/pallas_call | solution.py:355
  1.0 0.7 %collective-permute-start = (bf16[32,2048]{1,0:T(8,128)(2,1)S(1)}, bf16[32,2048]{1,0:T(8,128)(2,1)S(1)}, u32[]{:S(2)}, u32[]{:S(2)}) collective-permute-start(bf16[32,2048]{1,0:T(8,128)(2,1)S(1)} %get-tuple-element.13.refs_1_.refs_7_), channel_id=1, source_target_pairs={{2,4},{3,5},{4,2},{5,3},{6,8},{7,9},{8,6},{9,7},{10,12},{11,13},{1... | collective-permute-start | bytes 393224 | tf_op jit(solution)/shard_map/ppermute | solution.py:378
  1.7 0.7 %collective-permute-start.1 = (bf16[32,2048]{1,0:T(8,128)(2,1)S(1)}, bf16[32,2048]{1,0:T(8,128)(2,1)S(1)}, u32[]{:S(2)}, u32[]{:S(2)}) collective-permute-start(bf16[32,2048]{1,0:T(8,128)(2,1)S(1)} %get-tuple-element.12.refs_0_.refs_3_.refs_6_), channel_id=1, source_target_pairs={{0,2},{1,3},{2,0},{3,1},{4,6},{5,7},{6,4},{7,5},{8,10},{9,11},{10,... | collective-permute-start | bytes 393224 | tf_op jit(solution)/shard_map/ppermute | solution.py:378
  2.4 1.4 %fixed.1 = (bf16[1,16,128,384]{3,2,1,0:T(8,128)(2,1)S(1)}, f32[2,64,128]{2,1,0:T(8,128)S(1)}, f32[2,32,128]{2,1,0:T(8,128)S(1)}) custom-call(bf16[1,16,128,384]{3,2,1,0:T(8,128)(2,1)} %refs_0_.1, s32[2,4]{1,0:T(2,128)} %refs_1_.1, s32[2,4]{1,0:T(2,128)} %refs_2_.1, bf16[32,2048]{1,0:T(8,128)(2,1)S(1)} %get-tuple-element.12.refs_0_.refs_3_.refs_6_), custom_call_target="tpu_custom_call" | custom-call | flops 131072 | bytes 1572864 | tf_op jit(solution)/shard_map/fixed/pallas_call | solution.py:383
  3.8 0.0 collective-permute-done.refs_2_.refs_8_
  3.8 0.0 collective-permute-done.1.refs_3_.refs_9_
  3.8 0.3 %squares.4 = f32[8,128]{1,0:T(8,128)S(1)} custom-call(bf16[32,2048]{1,0:T(8,128)(2,1)S(1)} %get-tuple-element.12.refs_0_.refs_3_.refs_6_, bf16[32,2048]{1,0:T(8,128)(2,1)S(1)} %get-tuple-element.13.refs_1_.refs_7_, bf16[32,2048]{1,0:T(8,128)(2,1)S(1)} %collective-permute-done.refs_2_.refs_8_, bf16[32,2048]{1,0:T(8,128)(2,1)S(1)} %collective-permute-done.1.refs_3_.refs_9_), custom_call_target="tpu_custom_call" | custom-call | tf_op jit(solution)/shard_map/squares/pallas_call | solution.py:313
  4.1 3.2 %all_gather.6.refs_2_ = f32[16,128]{1,0:T(8,128)S(1)} all-gather(f32[8,128]{1,0:T(8,128)S(1)} %squares.4), channel_id=1, replica_groups=mesh['section'=2,'seq'=8,'rep'=2] {'rep'}, dimensions={0}, use_global_device_ids=true | all-gather | bytes 12288 | tf_op jit(solution)/shard_map/all_gather | solution.py:382
  7.4 1.3 %collective-permute-start.2 = (bf16[32,2048]{1,0:T(8,128)(2,1)S(1)}, bf16[32,2048]{1,0:T(8,128)(2,1)S(1)}, u32[]{:S(2)}, u32[]{:S(2)}) collective-permute-start(bf16[32,2048]{1,0:T(8,128)(2,1)S(1)} %get-tuple-element.17.refs_0_.refs_6_), channel_id=1, source_target_pairs={{0,16},{1,17},{2,18},{3,19},{4,20},{5,21},{6,22},{7,23},{8,24},{9,... | collective-permute-start | bytes 393224 | tf_op jit(solution)/shard_map/ppermute | solution.py:378
  8.7 0.2 squares.5.refs_0_
  8.9 1.3 %collective-permute-start.4 = (f32[8,128]{1,0:T(8,128)S(1)}, f32[8,128]{1,0:T(8,128)S(1)}, u32[]{:S(2)}, u32[]{:S(2)}) collective-permute-start(f32[8,128]{1,0:T(8,128)S(1)} %squares.5.refs_0_), channel_id=1, source_target_pairs={{0,17},{1,16},{2,19},{3,18},{4,21},{5,20},{6,23},{7,22},{8,25},{9,... | collective-permute-start | bytes 12296 | tf_op jit(solution)/shard_map/ppermute | solution.py:378
  10.2 1.3 %collective-permute-start.5 = (bf16[32,2048]{1,0:T(8,128)(2,1)S(1)}, bf16[32,2048]{1,0:T(8,128)(2,1)S(1)}, u32[]{:S(2)}, u32[]{:S(2)}) collective-permute-start(bf16[32,2048]{1,0:T(8,128)(2,1)S(1)} %get-tuple-element.18.refs_1_.refs_7_), channel_id=1, source_target_pairs={{2,20},{3,21},{4,18},{5,19},{6,24},{7,25},{8,22},{9,23},{10,28},{1... | collective-permute-start | bytes 393224 | tf_op jit(solution)/shard_map/ppermute | solution.py:378
  11.5 1.3 %collective-permute-start.3 = (bf16[32,2048]{1,0:T(8,128)(2,1)S(1)}, bf16[32,2048]{1,0:T(8,128)(2,1)S(1)}, u32[]{:S(2)}, u32[]{:S(2)}) collective-permute-start(bf16[32,2048]{1,0:T(8,128)(2,1)S(1)} %get-tuple-element.18.refs_1_.refs_7_), channel_id=1, source_target_pairs={{0,16},{1,17},{2,18},{3,19},{4,20},{5,21},{6,22},{7,23},{8,24},{9,... | collective-permute-start | bytes 393224 | tf_op jit(solution)/shard_map/ppermute | solution.py:378
  12.8 1.3 %collective-permute-start.6 = (f32[8,128]{1,0:T(8,128)S(1)}, f32[8,128]{1,0:T(8,128)S(1)}, u32[]{:S(2)}, u32[]{:S(2)}) collective-permute-start(f32[8,128]{1,0:T(8,128)S(1)} %copy.6), channel_id=1, source_target_pairs={{2,21},{3,20},{4,19},{5,18},{6,25},{7,24},{8,23},{9,22},{10,29},{1... | collective-permute-start | bytes 12296 | tf_op jit(solution)/shard_map/ppermute | solution.py:378
  14.1 2.7 %collective-permute-done.2.refs_0_ = bf16[32,2048]{1,0:T(8,128)(2,1)S(1)} collective-permute-done((bf16[32,2048]{1,0:T(8,128)(2,1)S(1)}, bf16[32,2048]{1,0:T(8,128)(2,1)S(1)}, u32[]{:S(2)}, u32[]{:S(2)}) %collective-permute-start.2) | collective-permute-done | bytes 131104 | tf_op jit(solution)/shard_map/ppermute | solution.py:378
  16.8 0.2 squares.7.refs_1_
  16.9 0.9 %collective-permute-done.4.refs_2_ = f32[8,128]{1,0:T(8,128)S(1)} collective-permute-done((f32[8,128]{1,0:T(8,128)S(1)}, f32[8,128]{1,0:T(8,128)S(1)}, u32[]{:S(2)}, u32[]{:S(2)}) %collective-permute-start.4) | collective-permute-done | bytes 4128 | tf_op jit(solution)/shard_map/ppermute | solution.py:378
  17.9 0.1 norm.1.half_ref
  18.0 5.8 %all_gather.7._.refs_10_ = bf16[64,2048]{1,0:T(8,128)(2,1)S(1)} all-gather(bf16[32,2048]{1,0:T(8,128)(2,1)S(1)} %norm.1.half_ref), channel_id=1, replica_groups={{0,2},{4,6},{8,10},{12,14},{1,3},{5,7},{9,11},{13,15},{16,18},{20,22},{..., dimensions={0}, use_global_device_ids=true | all-gather | bytes 393216 | tf_op jit(solution)/shard_map/all_gather | solution.py:441
  23.8 0.4 %project.1.refs_11_ = bf16[32,6144]{1,0:T(8,128)(2,1)S(1)} custom-call(bf16[1,16,128,384]{3,2,1,0:T(8,128)(2,1)S(1)} %get-tuple-element.16.refs_5_.weights_ref, bf16[32,2048]{1,0:T(8,128)(2,1)S(1)} %norm.1.half_ref, bf16[64,2048]{1,0:T(8,128)(2,1)S(1)} %all_gather.7._.refs_10_), custom_call_target="tpu_custom_call" | custom-call | flops 2000000000 | bytes 300000 | tf_op jit(solution)/shard_map/project/pallas_call | solution.py:345
  24.2 0.0 collective-permute-done.5.refs_0_.refs_8_
  24.2 0.2 squares.6.mine_ref
  24.4 0.3 %collective-permute-done.6.other_ref = f32[8,128]{1,0:T(8,128)S(1)} collective-permute-done((f32[8,128]{1,0:T(8,128)S(1)}, f32[8,128]{1,0:T(8,128)S(1)}, u32[]{:S(2)}, u32[]{:S(2)}) %collective-permute-start.6) | collective-permute-done | bytes 4128 | tf_op jit(solution)/shard_map/ppermute | solution.py:378
  24.7 0.0 collective-permute-done.3.refs_1_
  24.7 1.8 %layer.3 = bf16[1,2,8,4,2048]{4,3,2,1,0:T(4,128)(2,1)} custom-call(bf16[32,2048]{1,0:T(8,128)(2,1)S(1)} %collective-permute-done.2.refs_0_, bf16[32,2048]{1,0:T(8,128)(2,1)S(1)} %collective-permute-done.3.refs_1_, f32[8,128]{1,0:T(8,128)S(1)} %collective-permute-done.4.refs_2_, f32[2,64,128]{2,1,0:T(8,128)S(1)} %get-tuple-element.14.refs_3_, ...), custom_call_target="tpu_custom_call" | custom-call | flops 402653184 | bytes 4194304 | tf_op jit(solution)/shard_map/layer/pallas_call | solution.py:414
  (3 shorter events, 0.1 us)
Async XLA Ops:
  1.0 2.8 %collective-permute-start = (bf16[32,2048]{1,0:T(8,128)(2,1)S(1)}, bf16[32,2048]{1,0:T(8,128)(2,1)S(1)}, u32[]{:S(2)}, u32[]{:S(2)}) collective-permute-start(bf16[32,2048]{1,0:T(8,128)(2,1)S(1)} %get-tuple-element.13.refs_1_.refs_7_), channel_id=1, source_target_pairs={{2,4},{3,5},{4,2},{5,3},{6,8},{7,9},{8,6},{9,7},{10,12},{11,13},{1... | collective-permute-start | bytes 393224 | tf_op jit(solution)/shard_map/ppermute | solution.py:378
  1.7 2.1 %collective-permute-start.1 = (bf16[32,2048]{1,0:T(8,128)(2,1)S(1)}, bf16[32,2048]{1,0:T(8,128)(2,1)S(1)}, u32[]{:S(2)}, u32[]{:S(2)}) collective-permute-start(bf16[32,2048]{1,0:T(8,128)(2,1)S(1)} %get-tuple-element.12.refs_0_.refs_3_.refs_6_), channel_id=1, source_target_pairs={{0,2},{1,3},{2,0},{3,1},{4,6},{5,7},{6,4},{7,5},{8,10},{9,11},{10,... | collective-permute-start | bytes 393224 | tf_op jit(solution)/shard_map/ppermute | solution.py:378
  7.4 9.4 %collective-permute-start.2 = (bf16[32,2048]{1,0:T(8,128)(2,1)S(1)}, bf16[32,2048]{1,0:T(8,128)(2,1)S(1)}, u32[]{:S(2)}, u32[]{:S(2)}) collective-permute-start(bf16[32,2048]{1,0:T(8,128)(2,1)S(1)} %get-tuple-element.17.refs_0_.refs_6_), channel_id=1, source_target_pairs={{0,16},{1,17},{2,18},{3,19},{4,20},{5,21},{6,22},{7,23},{8,24},{9,... | collective-permute-start | bytes 393224 | tf_op jit(solution)/shard_map/ppermute | solution.py:378
  8.9 9.0 %collective-permute-start.4 = (f32[8,128]{1,0:T(8,128)S(1)}, f32[8,128]{1,0:T(8,128)S(1)}, u32[]{:S(2)}, u32[]{:S(2)}) collective-permute-start(f32[8,128]{1,0:T(8,128)S(1)} %squares.5.refs_0_), channel_id=1, source_target_pairs={{0,17},{1,16},{2,19},{3,18},{4,21},{5,20},{6,23},{7,22},{8,25},{9,... | collective-permute-start | bytes 12296 | tf_op jit(solution)/shard_map/ppermute | solution.py:378
  10.2 14.0 %collective-permute-start.5 = (bf16[32,2048]{1,0:T(8,128)(2,1)S(1)}, bf16[32,2048]{1,0:T(8,128)(2,1)S(1)}, u32[]{:S(2)}, u32[]{:S(2)}) collective-permute-start(bf16[32,2048]{1,0:T(8,128)(2,1)S(1)} %get-tuple-element.18.refs_1_.refs_7_), channel_id=1, source_target_pairs={{2,20},{3,21},{4,18},{5,19},{6,24},{7,25},{8,22},{9,23},{10,28},{1... | collective-permute-start | bytes 393224 | tf_op jit(solution)/shard_map/ppermute | solution.py:378
  11.5 13.2 %collective-permute-start.3 = (bf16[32,2048]{1,0:T(8,128)(2,1)S(1)}, bf16[32,2048]{1,0:T(8,128)(2,1)S(1)}, u32[]{:S(2)}, u32[]{:S(2)}) collective-permute-start(bf16[32,2048]{1,0:T(8,128)(2,1)S(1)} %get-tuple-element.18.refs_1_.refs_7_), channel_id=1, source_target_pairs={{0,16},{1,17},{2,18},{3,19},{4,20},{5,21},{6,22},{7,23},{8,24},{9,... | collective-permute-start | bytes 393224 | tf_op jit(solution)/shard_map/ppermute | solution.py:378
  12.8 11.9 %collective-permute-start.6 = (f32[8,128]{1,0:T(8,128)S(1)}, f32[8,128]{1,0:T(8,128)S(1)}, u32[]{:S(2)}, u32[]{:S(2)}) collective-permute-start(f32[8,128]{1,0:T(8,128)S(1)} %copy.6), channel_id=1, source_target_pairs={{2,21},{3,20},{4,19},{5,18},{6,25},{7,24},{8,23},{9,22},{10,29},{1... | collective-permute-start | bytes 12296 | tf_op jit(solution)/shard_map/ppermute | solution.py:378

commit v20 on v19

--- a/solution.py
+++ b/solution.py
@@ -146,7 +146,7 @@
     out_ref[0:1, :] = mine_ref[0:1, :] + other_ref[FAR : FAR + 1, :]
 
 
-def project_kernel(weights_ref, *refs):
+def project_kernel(weights_ref, *refs, start=0):
     count = len(refs) // 2
     halves, outs = refs[:count], refs[count:]
     rows = halves[0].shape[0]
@@ -155,11 +155,11 @@
         lanes = slice(head * HEAD, (head + 1) * HEAD)
         projected = jnp.dot(
             jnp.concatenate([half[:, lanes] for half in halves], axis=0),
-            weights_ref[0, head],
+            weights_ref[0, head, :, start:],
             preferred_element_type=jnp.float32,
         ).astype(jnp.bfloat16)
         for i, out in enumerate(outs):
-            out[:, head * width : (head + 1) * width] = projected[i * rows : (i + 1) * rows]
+            out[:, head * width + start : (head + 1) * width] = projected[i * rows : (i + 1) * rows]
 
 
 def softmax_columns(scores):
@@ -234,7 +234,15 @@
             rows = micro * edge
             other = pl.multiple_of((1 - odd_device()) * rows, rows)
             normed.append(next_chip_ref.at[pl.ds(other, rows)])
-        project_kernel(weights_ref, *normed, *[projected[half] for half in projecting])
+        for mine, start in ((True, 0), (False, HEAD)):
+            chosen = [
+                (normed_half, projected[half])
+                for half, normed_half in zip(projecting, normed)
+                if (half in (CHIP, FAR)) == mine
+            ]
+            project_kernel(
+                weights_ref, *[a for a, _ in chosen], *[b for _, b in chosen], start=start
+            )
         pairs = [(g, m) for g in range(heads_dev // GROUP) for m in range(micro)]
         blank = jnp.zeros((own, HEAD), bf16)
         scores = []

time: 26.9 us -> 27 us (level)
  no operation moved by 1% of the time
where the time goes in v20:
time: 27 us; the launch traced here: 26.7 us
  blocking collectives  9.01 us (33%)
  starting transfers between devices  7.8 us (29%)
  Pallas kernels  5.73 us (21%)
  waiting for transfers between devices  3.96 us (15%)
    ppermute x7, starting transfers between devices, moved(): return lax.ppermute(block, ('section', 'seq', 'rep'), route)  7.8 us
    all_gather x1, blocking collectives, body(): lax.all_gather(normed_chip, 'seq', axis_index_groups=[[i, i + 1] for i in...  5.82 us
    ppermute x7, waiting for transfers between devices, moved(): return lax.ppermute(block, ('section', 'seq', 'rep'), route)  3.96 us
    all_gather x1, blocking collectives, body(): lax.all_gather(squares_of(chip, far, next_far, next_chip), 'rep', tiled=T...  3.19 us
    pallas_call x2, Pallas kernels, body(): pl.pallas_call(kernel, in_specs=[VMEM] * (8 + len(inputs)), out_specs=[VM...  1.94 us
    pallas_call x1, Pallas kernels, body(): pl.pallas_call(lambda *refs: fixed_kernel(*refs, stations=stations, total...  1.44 us
    pallas_call x1, Pallas kernels, body(): pl.pallas_call(halves_kernel, in_specs=[HBM], out_specs=[VMEM] * 2, out_s...  1.02 us
    pallas_call x4, Pallas kernels, squares_of(): pl.pallas_call(squares_kernel, in_specs=[VMEM] * len(halves), out_specs=V...  0.83 us
  transfers between devices with their start and end apart: 7, of which 3 were waited for; matrix products, arithmetic and copies ran while one was open for 0% of the time, Pallas kernels for 9%

profile of v20, /device:TPU:11, one launch (start us, length us, event | category | flops | bytes accessed | tf_op | source)
XLA Modules:
  0.0 26.7 jit_solution(8462482138275727875)
XLA Ops:
  0.0 1.0 %halves.1 = (bf16[32,2048]{1,0:T(8,128)(2,1)S(1)}, bf16[32,2048]{1,0:T(8,128)(2,1)S(1)}) custom-call(bf16[2,8,4,2048]{3,2,1,0:T(4,128)(2,1)} %signal_hbm.1), custom_call_target="tpu_custom_call" | custom-call | flops 131072 | bytes 524288 | tf_op jit(solution)/shard_map/halves/pallas_call | solution.py:363
  1.0 0.7 %collective-permute-start = (bf16[32,2048]{1,0:T(8,128)(2,1)S(1)}, bf16[32,2048]{1,0:T(8,128)(2,1)S(1)}, u32[]{:S(2)}, u32[]{:S(2)}) collective-permute-start(bf16[32,2048]{1,0:T(8,128)(2,1)S(1)} %get-tuple-element.13.refs_1_.refs_7_), channel_id=1, source_target_pairs={{2,4},{3,5},{4,2},{5,3},{6,8},{7,9},{8,6},{9,7},{10,12},{11,13},{1... | collective-permute-start | bytes 393224 | tf_op jit(solution)/shard_map/ppermute | solution.py:386
  1.7 0.7 %collective-permute-start.1 = (bf16[32,2048]{1,0:T(8,128)(2,1)S(1)}, bf16[32,2048]{1,0:T(8,128)(2,1)S(1)}, u32[]{:S(2)}, u32[]{:S(2)}) collective-permute-start(bf16[32,2048]{1,0:T(8,128)(2,1)S(1)} %get-tuple-element.12.refs_0_.refs_3_.refs_6_), channel_id=1, source_target_pairs={{0,2},{1,3},{2,0},{3,1},{4,6},{5,7},{6,4},{7,5},{8,10},{9,11},{10,... | collective-permute-start | bytes 393224 | tf_op jit(solution)/shard_map/ppermute | solution.py:386
  2.4 1.4 %fixed.1 = (bf16[1,16,128,384]{3,2,1,0:T(8,128)(2,1)S(1)}, f32[2,64,128]{2,1,0:T(8,128)S(1)}, f32[2,32,128]{2,1,0:T(8,128)S(1)}) custom-call(bf16[1,16,128,384]{3,2,1,0:T(8,128)(2,1)} %refs_0_.1, s32[2,4]{1,0:T(2,128)} %refs_1_.1, s32[2,4]{1,0:T(2,128)} %refs_2_.1, bf16[32,2048]{1,0:T(8,128)(2,1)S(1)} %get-tuple-element.12.refs_0_.refs_3_.refs_6_), custom_call_target="tpu_custom_call" | custom-call | flops 131072 | bytes 1572864 | tf_op jit(solution)/shard_map/fixed/pallas_call | solution.py:391
  3.8 0.0 collective-permute-done.refs_2_.refs_8_
  3.8 0.0 collective-permute-done.1.refs_3_.refs_9_
  3.8 0.3 %squares.4 = f32[8,128]{1,0:T(8,128)S(1)} custom-call(bf16[32,2048]{1,0:T(8,128)(2,1)S(1)} %get-tuple-element.12.refs_0_.refs_3_.refs_6_, bf16[32,2048]{1,0:T(8,128)(2,1)S(1)} %get-tuple-element.13.refs_1_.refs_7_, bf16[32,2048]{1,0:T(8,128)(2,1)S(1)} %collective-permute-done.refs_2_.refs_8_, bf16[32,2048]{1,0:T(8,128)(2,1)S(1)} %collective-permute-done.1.refs_3_.refs_9_), custom_call_target="tpu_custom_call" | custom-call | tf_op jit(solution)/shard_map/squares/pallas_call | solution.py:321
  4.1 3.2 %all_gather.6.refs_2_ = f32[16,128]{1,0:T(8,128)S(1)} all-gather(f32[8,128]{1,0:T(8,128)S(1)} %squares.4), channel_id=1, replica_groups=mesh['section'=2,'seq'=8,'rep'=2] {'rep'}, dimensions={0}, use_global_device_ids=true | all-gather | bytes 12288 | tf_op jit(solution)/shard_map/all_gather | solution.py:390
  7.4 1.3 %collective-permute-start.2 = (bf16[32,2048]{1,0:T(8,128)(2,1)S(1)}, bf16[32,2048]{1,0:T(8,128)(2,1)S(1)}, u32[]{:S(2)}, u32[]{:S(2)}) collective-permute-start(bf16[32,2048]{1,0:T(8,128)(2,1)S(1)} %get-tuple-element.17.refs_0_.refs_6_), channel_id=1, source_target_pairs={{0,16},{1,17},{2,18},{3,19},{4,20},{5,21},{6,22},{7,23},{8,24},{9,... | collective-permute-start | bytes 393224 | tf_op jit(solution)/shard_map/ppermute | solution.py:386
  8.7 0.2 squares.5.refs_0_
  8.9 1.3 %collective-permute-start.4 = (f32[8,128]{1,0:T(8,128)S(1)}, f32[8,128]{1,0:T(8,128)S(1)}, u32[]{:S(2)}, u32[]{:S(2)}) collective-permute-start(f32[8,128]{1,0:T(8,128)S(1)} %squares.5.refs_0_), channel_id=1, source_target_pairs={{0,17},{1,16},{2,19},{3,18},{4,21},{5,20},{6,23},{7,22},{8,25},{9,... | collective-permute-start | bytes 12296 | tf_op jit(solution)/shard_map/ppermute | solution.py:386
  10.2 1.3 %collective-permute-start.5 = (bf16[32,2048]{1,0:T(8,128)(2,1)S(1)}, bf16[32,2048]{1,0:T(8,128)(2,1)S(1)}, u32[]{:S(2)}, u32[]{:S(2)}) collective-permute-start(bf16[32,2048]{1,0:T(8,128)(2,1)S(1)} %get-tuple-element.18.refs_1_.refs_7_), channel_id=1, source_target_pairs={{2,20},{3,21},{4,18},{5,19},{6,24},{7,25},{8,22},{9,23},{10,28},{1... | collective-permute-start | bytes 393224 | tf_op jit(solution)/shard_map/ppermute | solution.py:386
  11.5 1.3 %collective-permute-start.3 = (bf16[32,2048]{1,0:T(8,128)(2,1)S(1)}, bf16[32,2048]{1,0:T(8,128)(2,1)S(1)}, u32[]{:S(2)}, u32[]{:S(2)}) collective-permute-start(bf16[32,2048]{1,0:T(8,128)(2,1)S(1)} %get-tuple-element.18.refs_1_.refs_7_), channel_id=1, source_target_pairs={{0,16},{1,17},{2,18},{3,19},{4,20},{5,21},{6,22},{7,23},{8,24},{9,... | collective-permute-start | bytes 393224 | tf_op jit(solution)/shard_map/ppermute | solution.py:386
  12.8 1.3 %collective-permute-start.6 = (f32[8,128]{1,0:T(8,128)S(1)}, f32[8,128]{1,0:T(8,128)S(1)}, u32[]{:S(2)}, u32[]{:S(2)}) collective-permute-start(f32[8,128]{1,0:T(8,128)S(1)} %copy.6), channel_id=1, source_target_pairs={{2,21},{3,20},{4,19},{5,18},{6,25},{7,24},{8,23},{9,22},{10,29},{1... | collective-permute-start | bytes 12296 | tf_op jit(solution)/shard_map/ppermute | solution.py:386
  14.1 2.7 %collective-permute-done.2.refs_0_ = bf16[32,2048]{1,0:T(8,128)(2,1)S(1)} collective-permute-done((bf16[32,2048]{1,0:T(8,128)(2,1)S(1)}, bf16[32,2048]{1,0:T(8,128)(2,1)S(1)}, u32[]{:S(2)}, u32[]{:S(2)}) %collective-permute-start.2) | collective-permute-done | bytes 131104 | tf_op jit(solution)/shard_map/ppermute | solution.py:386
  16.8 0.2 squares.7.refs_1_
  17.0 0.9 %collective-permute-done.4.refs_2_ = f32[8,128]{1,0:T(8,128)S(1)} collective-permute-done((f32[8,128]{1,0:T(8,128)S(1)}, f32[8,128]{1,0:T(8,128)S(1)}, u32[]{:S(2)}, u32[]{:S(2)}) %collective-permute-start.4) | collective-permute-done | bytes 4128 | tf_op jit(solution)/shard_map/ppermute | solution.py:386
  17.9 0.1 norm.1.half_ref
  18.0 5.8 %all_gather.7._.refs_10_ = bf16[64,2048]{1,0:T(8,128)(2,1)S(1)} all-gather(bf16[32,2048]{1,0:T(8,128)(2,1)S(1)} %norm.1.half_ref), channel_id=1, replica_groups={{0,2},{4,6},{8,10},{12,14},{1,3},{5,7},{9,11},{13,15},{16,18},{20,22},{..., dimensions={0}, use_global_device_ids=true | all-gather | bytes 393216 | tf_op jit(solution)/shard_map/all_gather | solution.py:449
  23.8 0.4 %project.1.refs_11_ = bf16[32,6144]{1,0:T(8,128)(2,1)S(1)} custom-call(bf16[1,16,128,384]{3,2,1,0:T(8,128)(2,1)S(1)} %get-tuple-element.16.refs_5_.weights_ref, bf16[32,2048]{1,0:T(8,128)(2,1)S(1)} %norm.1.half_ref, bf16[64,2048]{1,0:T(8,128)(2,1)S(1)} %all_gather.7._.refs_10_), custom_call_target="tpu_custom_call" | custom-call | flops 2000000000 | bytes 300000 | tf_op jit(solution)/shard_map/project/pallas_call | solution.py:353
  24.2 0.0 collective-permute-done.5.refs_0_.refs_8_
  24.2 0.2 squares.6.mine_ref
  24.4 0.3 %collective-permute-done.6.other_ref = f32[8,128]{1,0:T(8,128)S(1)} collective-permute-done((f32[8,128]{1,0:T(8,128)S(1)}, f32[8,128]{1,0:T(8,128)S(1)}, u32[]{:S(2)}, u32[]{:S(2)}) %collective-permute-start.6) | collective-permute-done | bytes 4128 | tf_op jit(solution)/shard_map/ppermute | solution.py:386
  24.8 0.0 collective-permute-done.3.refs_1_
  24.8 1.9 %layer.3 = bf16[1,2,8,4,2048]{4,3,2,1,0:T(4,128)(2,1)} custom-call(bf16[32,2048]{1,0:T(8,128)(2,1)S(1)} %collective-permute-done.2.refs_0_, bf16[32,2048]{1,0:T(8,128)(2,1)S(1)} %collective-permute-done.3.refs_1_, f32[8,128]{1,0:T(8,128)S(1)} %collective-permute-done.4.refs_2_, f32[2,64,128]{2,1,0:T(8,128)S(1)} %get-tuple-element.14.refs_3_, ...), custom_call_target="tpu_custom_call" | custom-call | flops 402653184 | bytes 4194304 | tf_op jit(solution)/shard_map/layer/pallas_call | solution.py:422
  (3 shorter events, 0.1 us)
Async XLA Ops:
  1.0 2.8 %collective-permute-start = (bf16[32,2048]{1,0:T(8,128)(2,1)S(1)}, bf16[32,2048]{1,0:T(8,128)(2,1)S(1)}, u32[]{:S(2)}, u32[]{:S(2)}) collective-permute-start(bf16[32,2048]{1,0:T(8,128)(2,1)S(1)} %get-tuple-element.13.refs_1_.refs_7_), channel_id=1, source_target_pairs={{2,4},{3,5},{4,2},{5,3},{6,8},{7,9},{8,6},{9,7},{10,12},{11,13},{1... | collective-permute-start | bytes 393224 | tf_op jit(solution)/shard_map/ppermute | solution.py:386
  1.7 2.1 %collective-permute-start.1 = (bf16[32,2048]{1,0:T(8,128)(2,1)S(1)}, bf16[32,2048]{1,0:T(8,128)(2,1)S(1)}, u32[]{:S(2)}, u32[]{:S(2)}) collective-permute-start(bf16[32,2048]{1,0:T(8,128)(2,1)S(1)} %get-tuple-element.12.refs_0_.refs_3_.refs_6_), channel_id=1, source_target_pairs={{0,2},{1,3},{2,0},{3,1},{4,6},{5,7},{6,4},{7,5},{8,10},{9,11},{10,... | collective-permute-start | bytes 393224 | tf_op jit(solution)/shard_map/ppermute | solution.py:386
  7.4 9.4 %collective-permute-start.2 = (bf16[32,2048]{1,0:T(8,128)(2,1)S(1)}, bf16[32,2048]{1,0:T(8,128)(2,1)S(1)}, u32[]{:S(2)}, u32[]{:S(2)}) collective-permute-start(bf16[32,2048]{1,0:T(8,128)(2,1)S(1)} %get-tuple-element.17.refs_0_.refs_6_), channel_id=1, source_target_pairs={{0,16},{1,17},{2,18},{3,19},{4,20},{5,21},{6,22},{7,23},{8,24},{9,... | collective-permute-start | bytes 393224 | tf_op jit(solution)/shard_map/ppermute | solution.py:386
  8.9 9.0 %collective-permute-start.4 = (f32[8,128]{1,0:T(8,128)S(1)}, f32[8,128]{1,0:T(8,128)S(1)}, u32[]{:S(2)}, u32[]{:S(2)}) collective-permute-start(f32[8,128]{1,0:T(8,128)S(1)} %squares.5.refs_0_), channel_id=1, source_target_pairs={{0,17},{1,16},{2,19},{3,18},{4,21},{5,20},{6,23},{7,22},{8,25},{9,... | collective-permute-start | bytes 12296 | tf_op jit(solution)/shard_map/ppermute | solution.py:386
  10.2 14.0 %collective-permute-start.5 = (bf16[32,2048]{1,0:T(8,128)(2,1)S(1)}, bf16[32,2048]{1,0:T(8,128)(2,1)S(1)}, u32[]{:S(2)}, u32[]{:S(2)}) collective-permute-start(bf16[32,2048]{1,0:T(8,128)(2,1)S(1)} %get-tuple-element.18.refs_1_.refs_7_), channel_id=1, source_target_pairs={{2,20},{3,21},{4,18},{5,19},{6,24},{7,25},{8,22},{9,23},{10,28},{1... | collective-permute-start | bytes 393224 | tf_op jit(solution)/shard_map/ppermute | solution.py:386
  11.5 13.3 %collective-permute-start.3 = (bf16[32,2048]{1,0:T(8,128)(2,1)S(1)}, bf16[32,2048]{1,0:T(8,128)(2,1)S(1)}, u32[]{:S(2)}, u32[]{:S(2)}) collective-permute-start(bf16[32,2048]{1,0:T(8,128)(2,1)S(1)} %get-tuple-element.18.refs_1_.refs_7_), channel_id=1, source_target_pairs={{0,16},{1,17},{2,18},{3,19},{4,20},{5,21},{6,22},{7,23},{8,24},{9,... | collective-permute-start | bytes 393224 | tf_op jit(solution)/shard_map/ppermute | solution.py:386
  12.8 11.9 %collective-permute-start.6 = (f32[8,128]{1,0:T(8,128)S(1)}, f32[8,128]{1,0:T(8,128)S(1)}, u32[]{:S(2)}, u32[]{:S(2)}) collective-permute-start(f32[8,128]{1,0:T(8,128)S(1)} %copy.6), channel_id=1, source_target_pairs={{2,21},{3,20},{4,19},{5,18},{6,25},{7,24},{8,23},{9,22},{10,29},{1... | collective-permute-start | bytes 12296 | tf_op jit(solution)/shard_map/ppermute | solution.py:386
